TPU v7x, 32 devices: a whole 2x2x4 slice. The times are simulated.
32 devices in a mesh: dp: 32 (over z, y, x, core).
Axes of the slice: x: 2, y: 2, z: 4, core: 2. Of those that a mesh axis runs over, the one named last changes fastest.
Arguments:
- tokens: bfloat16 [28224, 768], P('dp'), may hold values from -6 to 6
- ln1_gain: bfloat16 [768], P('dp'), may hold values from 0.5 to 1.5
- ln1_bias: bfloat16 [768], P('dp'), may hold values from -1.796875 to 1.796875
- qkv_weight: bfloat16 [768, 2304], P('dp'), may hold values from -0.21875 to 0.21875
- query_bias: bfloat16 [768], P('dp'), may hold values from -3 to 3
- value_bias: bfloat16 [768], P('dp'), may hold values from -0.29882812 to 0.29882812
- out_weight: bfloat16 [768, 768], P('dp'), may hold values from -1.25 to 1.25
- out_bias: bfloat16 [768], P('dp'), may hold values from -1.796875 to 1.796875
- ln2_gain: bfloat16 [768], P('dp'), may hold values from 0.5 to 1.5
- ln2_bias: bfloat16 [768], P('dp'), may hold values from -1.796875 to 1.796875
- fc1_weight: bfloat16 [768, 3072], P('dp'), may hold values from -0.21875 to 0.21875
- fc1_bias: bfloat16 [3072], P('dp'), may hold values from -3 to 3
- fc2_weight: bfloat16 [3072, 768], P('dp'), may hold values from -0.109375 to 0.109375
- fc2_bias: bfloat16 [768], P('dp'), may hold values from -1.796875 to 1.796875
- dec_weight: bfloat16 [768, 512], P('dp'), may hold values from -0.21875 to 0.21875
- dec_bias: bfloat16 [512], P('dp'), may hold values from -1.796875 to 1.796875
- mask_token: bfloat16 [512], P('dp'), may hold values from -4 to 4
- kept_offsets: int32 [4032, 7], P('dp'), may hold values from 0 to 13, as said below
- kept_count: int32 [192], P('dp'), may hold values from 3 to 7, as said below
- res_id: int32 [192], P('dp'), may hold values from 0 to 1, as said below
- dec_owner: int32 [4032], P('dp'), may hold values from 0 to 31, as said below
- dec_cot: bfloat16 [57344, 512], P('dp'), may hold values from -6 to 6
Outputs:
- decoded: bfloat16 [57344, 512], P('dp')
- grad_tokens: bfloat16 [28224, 768], P('dp')
- grad_ln1_gain: float32 [768], P('dp')
- grad_ln1_bias: float32 [768], P('dp')
- grad_qkv_weight: float32 [768, 2304], P('dp')
- grad_query_bias: float32 [768], P('dp')
- grad_value_bias: float32 [768], P('dp')
- grad_out_weight: float32 [768, 768], P('dp')
- grad_out_bias: float32 [768], P('dp')
- grad_ln2_gain: float32 [768], P('dp')
- grad_ln2_bias: float32 [768], P('dp')
- grad_fc1_weight: float32 [768, 3072], P('dp')
- grad_fc1_bias: float32 [3072], P('dp')
- grad_fc2_weight: float32 [3072, 768], P('dp')
- grad_fc2_bias: float32 [768], P('dp')
- grad_dec_weight: float32 [768, 512], P('dp')
- grad_dec_bias: float32 [512], P('dp')
- grad_mask_token: float32 [512], P('dp')
Inputs may be any that keep to these rules, and one draw needn't show every extreme that they name: `kept_offsets`: each row lists 7 different cells of its window in keeping order; only the first k of a window are kept. `kept_count`: every window of an image keeps this many cells; on every device some image keeps 7. `res_id`: 1 marks an image of side 2 * 14, 0 one of side 14; each device holds exactly 1 images marked 1. `dec_owner`: A device gives at most 4 of its windows to any one owner, and exactly 4 to some owner.
All inputs are finite; a program needn't handle non-finite values.
Results may differ from a plain program's by a relative error of at most 0.013.
Values may be sent and summed in bfloat16 or wider, within the bound.
No kernel may reach another device: no remote copies, remote signals or barrier semaphores. Data moves between devices by JAX's collectives and lax.ppermute only.
A program may use at most 256 MiB of HBM per device.

v0:
```python
import jax
import jax.numpy as jnp
from jax import lax
from jax.sharding import PartitionSpec as P

HEADS = 12
GRID = 14
SETS = 1


NORM_EPS = 1e-06
MASK_FILL = -1e30


def layer_norm(values, gain_vec, bias_vec):
    row_mean = jnp.mean(values, axis=-1, keepdims=True)
    centered = values - row_mean
    variance = jnp.mean(centered * centered, axis=-1, keepdims=True)
    return centered * lax.rsqrt(variance + NORM_EPS) * gain_vec + bias_vec


def gelu_exact(values):
    return jax.nn.gelu(values, approximate=False)


def matmul(left, right):
    return jnp.dot(left, right, preferred_element_type=jnp.float32)


def contract_rows(left, right):
    return lax.dot_general(
        left, right, (((0,), (0,)), ((), ())), preferred_element_type=jnp.float32
    )


def times_transposed(left, right):
    return lax.dot_general(
        left, right, (((1,), (1,)), ((), ())), preferred_element_type=jnp.float32
    )


def sincos_table(position, side_len, table_width):
    quarter = table_width // 4
    freq_scale = 1.0 / 10000.0 ** (jnp.arange(quarter, dtype=jnp.float32) / quarter)
    column = (position % side_len).astype(jnp.float32)[..., None] * freq_scale
    row_pos = (position // side_len).astype(jnp.float32)[..., None] * freq_scale
    return jnp.concatenate(
        [jnp.sin(column), jnp.cos(column), jnp.sin(row_pos), jnp.cos(row_pos)], axis=-1
    )


def window_layout(res_vec, count_vec, num_windows):
    per_image = GRID * (1 + 3 * res_vec)
    starts = jnp.cumsum(per_image) - per_image
    window_ids = jnp.arange(num_windows, dtype=jnp.int32)
    image_of = jnp.sum((window_ids[:, None] >= starts[None, :]).astype(jnp.int32), axis=1) - 1
    picker = (image_of[:, None] == jnp.arange(res_vec.shape[0], dtype=jnp.int32)[None, :]).astype(
        jnp.int32
    )
    kept_win = jnp.sum(picker * count_vec[None, :], axis=1)
    side_win = GRID * (1 + jnp.sum(picker * res_vec[None, :], axis=1))
    start_win = jnp.sum(picker * starts[None, :], axis=1)
    return (image_of, kept_win, side_win, window_ids - start_win)


def owner_rank(owner_vec):
    window_ids = jnp.arange(owner_vec.shape[0], dtype=jnp.int32)
    earlier = (owner_vec[:, None] == owner_vec[None, :]) & (
        window_ids[None, :] < window_ids[:, None]
    )
    return jnp.sum(earlier.astype(jnp.int32), axis=1)


def placement(offsets, kept_win):
    slot_ids = jnp.arange(offsets.shape[-1], dtype=jnp.int32)
    cell_ids = jnp.arange(GRID, dtype=jnp.int32)
    live_slot = slot_ids < kept_win[..., None]
    cell_hits = (offsets[..., None, :] == cell_ids[:, None]) & live_slot[..., None, :]
    return cell_hits.astype(jnp.float32)


def decoder_table(window_info, table_width):
    present = window_info[:, 0].astype(jnp.float32)
    cell_hits = placement(window_info[:, 4:], window_info[:, 1])
    mask_cells = present[:, None] * (1.0 - jnp.sum(cell_hits, axis=-1))
    cell_ids = jnp.arange(GRID, dtype=jnp.int32)
    positions = window_info[:, 2:3] * GRID + cell_ids[None, :]
    side_len = jnp.maximum(window_info[:, 3:4], 1)
    pos_table = sincos_table(positions, side_len, table_width) * present[:, None, None]
    return (cell_hits, mask_cells, pos_table)


def attention_forward(qry_rows, key_rows, val_rows, image_rows, live_rows, blocks):
    row_count = qry_rows.shape[0]
    score_scale = qry_rows.shape[2] ** (-0.5)

    def one_block(block_index):
        scores = (
            jnp.einsum("qhd,khd->hqk", qry_rows, key_rows, preferred_element_type=jnp.float32)
            * score_scale
        )
        allowed = (image_rows[:, None] == image_rows[None, :]) & live_rows[None, :]
        scores = jnp.where(allowed[None], scores, MASK_FILL)
        row_top = jnp.max(scores, axis=-1, keepdims=True)
        expo_vals = jnp.exp(scores - row_top)
        row_total = jnp.sum(expo_vals, axis=-1, keepdims=True)
        weights_b = (expo_vals / row_total).astype(jnp.bfloat16)
        attended = jnp.einsum(
            "hqk,khd->qhd", weights_b, val_rows, preferred_element_type=jnp.float32
        )
        return (attended, (row_top + jnp.log(row_total))[..., 0])

    attended, log_total = lax.map(one_block, jnp.arange(blocks))
    return (attended.reshape(row_count, -1), log_total)


def attention_backward(
    qry_rows, key_rows, val_rows, image_rows, live_rows, log_total, grad_att, blocks
):
    score_scale = qry_rows.shape[2] ** (-0.5)

    def one_block(running, block_index):
        grad_keys, grad_vals = running
        scores = (
            jnp.einsum("qhd,khd->hqk", qry_rows, key_rows, preferred_element_type=jnp.float32)
            * score_scale
        )
        allowed = (image_rows[:, None] == image_rows[None, :]) & live_rows[None, :]
        scores = jnp.where(allowed[None], scores, MASK_FILL)
        probs_f = jnp.exp(scores - log_total[block_index][..., None])
        probs_b = probs_f.astype(jnp.bfloat16)
        grad_probs = jnp.einsum(
            "qhd,khd->hqk", grad_att, val_rows, preferred_element_type=jnp.float32
        )
        row_inner = jnp.sum(grad_probs * probs_f, axis=-1, keepdims=True)
        grad_scores = (probs_f * (grad_probs - row_inner)).astype(jnp.bfloat16)
        grad_qry = (
            jnp.einsum("hqk,khd->qhd", grad_scores, key_rows, preferred_element_type=jnp.float32)
            * score_scale
        )
        grad_keys = (
            grad_keys
            + jnp.einsum("hqk,qhd->khd", grad_scores, qry_rows, preferred_element_type=jnp.float32)
            * score_scale
        )
        grad_vals = grad_vals + jnp.einsum(
            "hqk,qhd->khd", probs_b, grad_att, preferred_element_type=jnp.float32
        )
        return ((grad_keys, grad_vals), grad_qry)

    zero_rows = jnp.zeros(qry_rows.shape, jnp.float32)
    (grad_keys, grad_vals), grad_qry = lax.scan(
        one_block, (zero_rows, zero_rows), jnp.arange(blocks)
    )
    return (grad_qry.reshape(qry_rows.shape), grad_keys, grad_vals)


def encoder_forward(tok_rows, weights, image_rows, live_rows):
    (
        gain_one,
        bias_one,
        qkv_weight,
        query_bias,
        value_bias,
        out_weight,
        out_bias,
        gain_two,
        bias_two,
        fc1_weight,
        fc1_bias,
        fc2_weight,
        fc2_bias,
    ) = weights
    row_count, model_width = tok_rows.shape
    head_dim = model_width // HEADS
    normed_b = layer_norm(
        tok_rows, gain_one.astype(jnp.float32), bias_one.astype(jnp.float32)
    ).astype(jnp.bfloat16)
    qkv_bias = jnp.concatenate([query_bias, jnp.zeros_like(query_bias), value_bias]).astype(
        jnp.float32
    )
    qkv_all = (
        (matmul(normed_b, qkv_weight) + qkv_bias)
        .astype(jnp.bfloat16)
        .reshape(row_count, 3, HEADS, head_dim)
    )
    qry_rows, key_rows, val_rows = (qkv_all[:, 0], qkv_all[:, 1], qkv_all[:, 2])
    attended, log_total = attention_forward(
        qry_rows, key_rows, val_rows, image_rows, live_rows, SETS
    )
    attended_b = attended.astype(jnp.bfloat16)
    residual = tok_rows + matmul(attended_b, out_weight) + out_bias.astype(jnp.float32)
    normed_two_b = layer_norm(
        residual, gain_two.astype(jnp.float32), bias_two.astype(jnp.float32)
    ).astype(jnp.bfloat16)
    hidden = matmul(normed_two_b, fc1_weight) + fc1_bias.astype(jnp.float32)
    activated_b = gelu_exact(hidden).astype(jnp.bfloat16)
    output = residual + matmul(activated_b, fc2_weight) + fc2_bias.astype(jnp.float32)
    kept_acts = (
        normed_b,
        qry_rows,
        key_rows,
        val_rows,
        attended_b,
        log_total,
        residual,
        normed_two_b,
        hidden,
        activated_b,
    )
    return (output, kept_acts)


def encoder_backward(tok_rows, weights, image_rows, live_rows, kept_acts, grad_out_b):
    (
        gain_one,
        bias_one,
        qkv_weight,
        query_bias,
        value_bias,
        out_weight,
        out_bias,
        gain_two,
        bias_two,
        fc1_weight,
        fc1_bias,
        fc2_weight,
        fc2_bias,
    ) = weights
    (
        normed_b,
        qry_rows,
        key_rows,
        val_rows,
        attended_b,
        log_total,
        residual,
        normed_two_b,
        hidden,
        activated_b,
    ) = kept_acts
    row_count, model_width = tok_rows.shape
    head_dim = model_width // HEADS
    grad_out = grad_out_b.astype(jnp.float32)
    grad_fc2_weight = contract_rows(activated_b, grad_out_b)
    grad_fc2_bias = jnp.sum(grad_out, axis=0)
    grad_act = times_transposed(grad_out_b, fc2_weight)
    gelu_back = jax.vjp(gelu_exact, hidden)[1]
    grad_hidden_b = gelu_back(grad_act)[0].astype(jnp.bfloat16)
    grad_fc1_bias = jnp.sum(grad_hidden_b.astype(jnp.float32), axis=0)
    grad_fc1_weight = contract_rows(normed_two_b, grad_hidden_b)
    grad_normed_two = times_transposed(grad_hidden_b, fc1_weight)
    norm_back_two = jax.vjp(
        layer_norm, residual, gain_two.astype(jnp.float32), bias_two.astype(jnp.float32)
    )[1]
    grad_resid_norm, grad_gain_two, grad_bias_two = norm_back_two(grad_normed_two)
    grad_resid = grad_out + grad_resid_norm
    grad_resid_b = grad_resid.astype(jnp.bfloat16)
    grad_out_bias = jnp.sum(grad_resid_b.astype(jnp.float32), axis=0)
    grad_out_weight = contract_rows(attended_b, grad_resid_b)
    grad_att_b = (
        times_transposed(grad_resid_b, out_weight)
        .astype(jnp.bfloat16)
        .reshape(row_count, HEADS, head_dim)
    )
    grad_qry, grad_keys, grad_vals = attention_backward(
        qry_rows, key_rows, val_rows, image_rows, live_rows, log_total, grad_att_b, SETS
    )
    grad_qkv_b = (
        jnp.stack([grad_qry, grad_keys, grad_vals], axis=1)
        .astype(jnp.bfloat16)
        .reshape(row_count, 3 * model_width)
    )
    grad_query_bias = jnp.sum(grad_qkv_b[:, :model_width].astype(jnp.float32), axis=0)
    grad_value_bias = jnp.sum(grad_qkv_b[:, 2 * model_width :].astype(jnp.float32), axis=0)
    grad_qkv_weight = contract_rows(normed_b, grad_qkv_b)
    grad_normed = times_transposed(grad_qkv_b, qkv_weight)
    norm_back_one = jax.vjp(
        layer_norm, tok_rows, gain_one.astype(jnp.float32), bias_one.astype(jnp.float32)
    )[1]
    grad_tok_norm, grad_gain_one, grad_bias_one = norm_back_one(grad_normed)
    block_grads = (
        grad_gain_one,
        grad_bias_one,
        grad_qkv_weight,
        grad_query_bias,
        grad_value_bias,
        grad_out_weight,
        grad_out_bias,
        grad_gain_two,
        grad_bias_two,
        grad_fc1_weight,
        grad_fc1_bias,
        grad_fc2_weight,
        grad_fc2_bias,
    )
    return (grad_resid + grad_tok_norm, block_grads)


def local(
    tokens,
    ln1_gain,
    ln1_bias,
    qkv_weight,
    query_bias,
    value_bias,
    out_weight,
    out_bias,
    ln2_gain,
    ln2_bias,
    fc1_weight,
    fc1_bias,
    fc2_weight,
    fc2_bias,
    dec_weight,
    dec_bias,
    mask_token,
    kept_offsets,
    kept_count,
    res_id,
    dec_owner,
    dec_cot,
):
    dev_count = lax.axis_size("dp")
    model_width = tokens.shape[1]
    dec_width = dec_cot.shape[1]
    win_dev = dec_owner.shape[0]
    slot_count = kept_offsets.shape[1]
    per_peer = (win_dev + dev_count - 1) // dev_count
    slot_total = dev_count * per_peer
    gathered = (
        lax.all_gather(ln1_gain, "dp", axis=0, tiled=True),
        lax.all_gather(ln1_bias, "dp", axis=0, tiled=True),
        lax.all_gather(qkv_weight, "dp", axis=0, tiled=True),
        lax.all_gather(query_bias, "dp", axis=0, tiled=True),
        lax.all_gather(value_bias, "dp", axis=0, tiled=True),
        lax.all_gather(out_weight, "dp", axis=0, tiled=True),
        lax.all_gather(out_bias, "dp", axis=0, tiled=True),
        lax.all_gather(ln2_gain, "dp", axis=0, tiled=True),
        lax.all_gather(ln2_bias, "dp", axis=0, tiled=True),
        lax.all_gather(fc1_weight, "dp", axis=0, tiled=True),
        lax.all_gather(fc1_bias, "dp", axis=0, tiled=True),
        lax.all_gather(fc2_weight, "dp", axis=0, tiled=True),
        lax.all_gather(fc2_bias, "dp", axis=0, tiled=True),
        lax.all_gather(dec_weight, "dp", axis=0, tiled=True),
        lax.all_gather(dec_bias, "dp", axis=0, tiled=True),
        lax.all_gather(mask_token, "dp", axis=0, tiled=True),
    )
    image_of, kept_win, side_win, win_in_image = window_layout(res_id, kept_count, win_dev)
    bucket = dec_owner * per_peer + owner_rank(dec_owner)
    slot_ids = jnp.arange(slot_count, dtype=jnp.int32)
    live_rows = (slot_ids[None, :] < kept_win[:, None]).reshape(-1)
    image_rows = jnp.repeat(image_of, slot_count)
    window_info = jnp.concatenate(
        [
            jnp.stack([jnp.ones_like(kept_win), kept_win, win_in_image, side_win], axis=1),
            kept_offsets,
        ],
        axis=1,
    )
    info_send = jnp.zeros((slot_total, window_info.shape[1]), jnp.int32).at[bucket].set(window_info)
    info_send = info_send.reshape(dev_count, per_peer, -1)
    tok_rows = tokens.astype(jnp.float32)
    output = encoder_forward(tok_rows, gathered[:13], image_rows, live_rows)[0]
    output_b = output.astype(jnp.bfloat16)
    send_rows = (
        jnp.zeros((slot_total, slot_count, model_width), jnp.bfloat16)
        .at[bucket]
        .set(output_b.reshape(win_dev, slot_count, model_width))
        .reshape(dev_count, per_peer, slot_count, model_width)
    )
    got_rows, got_info = (
        lax.all_to_all(send_rows, "dp", split_axis=0, concat_axis=0, tiled=True),
        lax.all_to_all(info_send, "dp", split_axis=0, concat_axis=0, tiled=True),
    )
    got_rows = got_rows.reshape(-1, model_width)
    projected_b = (matmul(got_rows, gathered[13]) + gathered[14].astype(jnp.float32)).astype(
        jnp.bfloat16
    )
    cell_hits, mask_cells, pos_table = decoder_table(got_info.reshape(slot_total, -1), dec_width)
    hits_b = cell_hits.astype(jnp.bfloat16)
    placed = jnp.einsum(
        "sgk,skd->sgd",
        hits_b,
        projected_b.reshape(slot_total, slot_count, dec_width),
        preferred_element_type=jnp.float32,
    )
    decoded = placed + mask_cells[..., None] * gathered[15].astype(jnp.float32) + pos_table
    decoded = decoded.astype(jnp.bfloat16).reshape(-1, dec_width)
    back_weights = (
        lax.all_gather(ln1_gain, "dp", axis=0, tiled=True),
        lax.all_gather(ln1_bias, "dp", axis=0, tiled=True),
        lax.all_gather(qkv_weight, "dp", axis=0, tiled=True),
        lax.all_gather(query_bias, "dp", axis=0, tiled=True),
        lax.all_gather(value_bias, "dp", axis=0, tiled=True),
        lax.all_gather(out_weight, "dp", axis=0, tiled=True),
        lax.all_gather(out_bias, "dp", axis=0, tiled=True),
        lax.all_gather(ln2_gain, "dp", axis=0, tiled=True),
        lax.all_gather(ln2_bias, "dp", axis=0, tiled=True),
        lax.all_gather(fc1_weight, "dp", axis=0, tiled=True),
        lax.all_gather(fc1_bias, "dp", axis=0, tiled=True),
        lax.all_gather(fc2_weight, "dp", axis=0, tiled=True),
        lax.all_gather(fc2_bias, "dp", axis=0, tiled=True),
        lax.all_gather(dec_weight, "dp", axis=0, tiled=True),
        lax.all_gather(dec_bias, "dp", axis=0, tiled=True),
        lax.all_gather(mask_token, "dp", axis=0, tiled=True),
    )
    cot_rows = dec_cot.reshape(slot_total, GRID, dec_width)
    grad_proj = jnp.einsum("sgk,sgd->skd", hits_b, cot_rows, preferred_element_type=jnp.float32)
    grad_mask_token = jnp.sum(mask_cells[..., None] * cot_rows.astype(jnp.float32), axis=(0, 1))
    grad_dec_bias = jnp.sum(grad_proj, axis=(0, 1))
    grad_proj_b = grad_proj.astype(jnp.bfloat16).reshape(-1, dec_width)
    grad_dec_weight = contract_rows(got_rows, grad_proj_b)
    grad_rows_b = times_transposed(grad_proj_b, back_weights[13]).astype(jnp.bfloat16)
    returned = lax.all_to_all(
        grad_rows_b.reshape(dev_count, per_peer, slot_count, model_width),
        "dp",
        split_axis=0,
        concat_axis=0,
        tiled=True,
    )
    grad_out_b = returned.reshape(slot_total, slot_count, model_width)[bucket].reshape(
        -1, model_width
    )
    kept_acts = encoder_forward(tok_rows, back_weights[:13], image_rows, live_rows)[1]
    grad_tok, block_grads = encoder_backward(
        tok_rows, back_weights[:13], image_rows, live_rows, kept_acts, grad_out_b
    )
    (
        grad_gain_one,
        grad_bias_one,
        grad_qkv_weight,
        grad_query_bias,
        grad_value_bias,
        grad_out_weight,
        grad_out_bias,
        grad_gain_two,
        grad_bias_two,
        grad_fc1_weight,
        grad_fc1_bias,
        grad_fc2_weight,
        grad_fc2_bias,
    ) = block_grads
    reduced = (
        lax.psum_scatter(grad_gain_one, "dp", scatter_dimension=0, tiled=True),
        lax.psum_scatter(grad_bias_one, "dp", scatter_dimension=0, tiled=True),
        lax.psum_scatter(grad_qkv_weight, "dp", scatter_dimension=0, tiled=True),
        lax.psum_scatter(grad_query_bias, "dp", scatter_dimension=0, tiled=True),
        lax.psum_scatter(grad_value_bias, "dp", scatter_dimension=0, tiled=True),
        lax.psum_scatter(grad_out_weight, "dp", scatter_dimension=0, tiled=True),
        lax.psum_scatter(grad_out_bias, "dp", scatter_dimension=0, tiled=True),
        lax.psum_scatter(grad_gain_two, "dp", scatter_dimension=0, tiled=True),
        lax.psum_scatter(grad_bias_two, "dp", scatter_dimension=0, tiled=True),
        lax.psum_scatter(grad_fc1_weight, "dp", scatter_dimension=0, tiled=True),
        lax.psum_scatter(grad_fc1_bias, "dp", scatter_dimension=0, tiled=True),
        lax.psum_scatter(grad_fc2_weight, "dp", scatter_dimension=0, tiled=True),
        lax.psum_scatter(grad_fc2_bias, "dp", scatter_dimension=0, tiled=True),
        lax.psum_scatter(grad_dec_weight, "dp", scatter_dimension=0, tiled=True),
        lax.psum_scatter(grad_dec_bias, "dp", scatter_dimension=0, tiled=True),
        lax.psum_scatter(grad_mask_token, "dp", scatter_dimension=0, tiled=True),
    )
    return (decoded, grad_tok.astype(jnp.bfloat16)) + tuple(reduced)


def solution(mesh):
    in_specs = (
        P("dp", None),
        P("dp"),
        P("dp"),
        P("dp", None),
        P("dp"),
        P("dp"),
        P("dp", None),
        P("dp"),
        P("dp"),
        P("dp"),
        P("dp", None),
        P("dp"),
        P("dp", None),
        P("dp"),
        P("dp", None),
        P("dp"),
        P("dp"),
        P("dp", None),
        P("dp"),
        P("dp"),
        P("dp"),
        P("dp", None),
    )
    out_specs = (
        P("dp", None),
        P("dp", None),
        P("dp"),
        P("dp"),
        P("dp", None),
        P("dp"),
        P("dp"),
        P("dp", None),
        P("dp"),
        P("dp"),
        P("dp"),
        P("dp", None),
        P("dp"),
        P("dp", None),
        P("dp"),
        P("dp", None),
        P("dp"),
        P("dp"),
    )
    return jax.shard_map(local, mesh=mesh, in_specs=in_specs, out_specs=out_specs, check_vma=False)
```

profile of v0, /device:TPU:0, one launch (start us, length us, event | category | flops | bytes accessed | tf_op | source)
XLA Modules:
  0.0 979.3 jit_solution(550161364683107842)
XLA Ops:
  15.8 7.3 all-to-all-start
  23.1 47.4 %all_gather.74 = bf16[768,512]{1,0:T(8,128)(2,1)} all-gather(bf16[24,512]{1,0:T(8,128)(2,1)} %param.36), channel_id=1, replica_groups=mesh['dp'=32] {'dp'}, dimensions={0}, use_global_device_ids=true | all-gather | bytes 811008 | tf_op jit(solution)/shard_map/all_gather | solution.py:345
  89.2 53.0 %all-reduce.23 = (bf16[768]{0:T(1024)(128)(2,1)S(1)}, bf16[768]{0:T(1024)(128)(2,1)S(1)}, bf16[768]{0:T(1024)(128)(2,1)S(1)}, bf16[768]{0:T(1024)(128)(2,1)S(1)}...) all-reduce(bf16[768]{0:T(1024)(128)(2,1)S(1)} %dynamic-update-slice, ...), channel_id=1, replica_groups=mesh['dp'=32] {'dp'}, use_global_device_ids=true, to_apply=%add.3 | all-reduce | flops 10240 | bytes 40960
  151.1 7.3 add_convert_fusion.1
  158.4 6.5 copy.99
  164.9 17.6 %fusion.71 = (f32[12,882]{1,0:T(8,128)S(1)}, f32[12,882,882]{1,2,0:T(8,128)}) fusion(bf16[882,3,12,64]{0,3,2,1:T(8,128)(2,1)} %bitcast.83, pred[882,882]{0,1:T(8,128)(4,1)S(1)} %copy-done.11), kind=kOutput, calls=%fused_computation.159 | convolution fusion | flops 1222885888 | bytes 40913124 | tf_op jit(solution)/shard_map/while/body/eval_jaxpr/qhd,khd->hqk/dot_general | solution.py:99
  182.5 15.0 %fusion = f32[12,882]{1,0:T(8,128)S(1)} fusion(f32[12,882,882]{1,2,0:T(8,128)} %get-tuple-element.153, f32[12,882]{1,0:T(8,128)S(1)} %get-tuple-element.152), kind=kLoop, calls=%fused_computation.9 | loop fusion | flops 18659592 | bytes 37425024 | tf_op jit(solution)/shard_map/while/body/eval_jaxpr/reduce_sum | solution.py:106
  197.5 17.4 %fusion.30 = bf16[12,64,882]{2,1,0:T(8,128)(2,1)} fusion(f32[12,882,882]{1,2,0:T(8,128)} %get-tuple-element.153, f32[12,882]{1,0:T(8,128)S(1)} %fusion, f32[12,882]{1,0:T(8,128)S(1)} %get-tuple-element.152, bf16[882,3,12,64]{0,3,2,1:T(8,128)(2,1)} %bitcast.84), kind=kOutput, calls=%fused_computation.73 | convolution fusion | flops 1223573888 | bytes 41006784 | tf_op jit(solution)/shard_map/while/body/eval_jaxpr/hqk,khd->qhd/dot_general | solution.py:108
  214.9 3.5 fusion.72
  219.6 9.8 fusion.65
  229.3 36.6 %all-gather.11.cloned.1.call-done = bf16[3072,768]{1,0:T(8,128)(2,1)} async-done(((bf16[96,768]{1,0:T(8,128)(2,1)}), bf16[3072,768]{1,0:T(8,128)(2,1)}) %all-gather.11.cloned.1.call-update) | async-done | bytes 4718608 | tf_op jit(solution)/shard_map/all_gather | solution.py:343
  265.9 33.6 %convert_reduce_fusion = (f32[3072]{0:T(1024)}, bf16[882,3072]{1,0:T(8,128)(2,1)}, f32[882,3072]{1,0:T(8,128)S(1)}) fusion(f32[882,3072]{1,0:T(8,128)} %fusion.65, f32[3072]{0:T(1024)S(1)} %convert_element_type.196, bf16[882,768]{1,0:T(8,128)(2,1)} %reshape.525, bf16[3072,768]{1,0:T(8,128)(2,1)} %all-gather.11.cloned.1.call-done), kind=kOutput, calls=%fused_computation.16 | convolution fusion | flops 4365007872 | bytes 33192960 | tf_op jit(solution)/shard_map/dot_general | solution.py:37
  299.6 9.6 multiply_reduce_fusion.2
  317.4 5.6 add_convert_fusion.3
  327.5 17.3 %scatter_fusion = bf16[128,7,768]{2,1,0:T(8,128)(2,1)} fusion(bf16[128,7,768]{2,1,0:T(8,128)(2,1)} %broadcast_in_dim.72, s32[126]{0:T(128)S(1)} %copy-done.54, bf16[126,7,768]{2,1,0:T(8,128)(2,1)} %reshape.547), kind=kCustom, calls=%fused_computation.2 | custom fusion | bytes 4064760 | tf_op jit(solution)/shard_map/scatter | solution.py:369
  359.0 4.0 convolution_convert_fusion.1
  365.5 29.7 %multiply_reduce_fusion = (f32[12,882]{1,0:T(8,128)S(1)}, f32[12,882,882]{1,2,0:T(8,128)}) fusion(f32[12,882,882]{1,2,0:T(8,128)} %get-tuple-element.153, f32[12,882]{1,0:T(8,128)S(1)} %copy-done.15, bf16[882,12,64]{0,2,1:T(8,128)(2,1)} %bitcast.88, bf16[882,3,12,64]{0,3,2,1:T(8,128)(2,1)} %bitcast.85), kind=kOutput, calls=%fused_computation.4 | convolution fusion | flops 1222885888 | bytes 78368640 | tf_op jit(solution)/shard_map/while/body/eval_jaxpr/qhd,khd->hqk/dot_general | solution.py:132
  395.2 31.8 %multiply_convert_fusion = bf16[12,882,882]{1,2,0:T(8,128)(2,1)} fusion(f32[12,882,882]{1,2,0:T(8,128)} %get-tuple-element.159, f32[12,882,882]{1,2,0:T(8,128)} %get-tuple-element.153, f32[12,882]{1,0:T(8,128)S(1)} %get-tuple-element.158, f32[12,882]{1,0:T(8,128)S(1)} %copy-done.15), kind=kLoop, calls=%fused_computation.3 | loop fusion | flops 37340352 | bytes 93435552 | tf_op jit(solution)/shard_map/while/body/eval_jaxpr/convert_element_type | solution.py:136
  427.0 12.5 %fusion.35 = bf16[882,1,12,64]{0,3,2,1:T(8,128)(2,1)} fusion(bf16[12,882,882]{1,2,0:T(8,128)(2,1)} %multiply_convert_fusion, bf16[882,3,12,64]{0,3,2,1:T(8,128)(2,1)} %bitcast.86), kind=kOutput, calls=%fused_computation.81 | convolution fusion | flops 1196246016 | bytes 21826560 | tf_op jit(solution)/shard_map/while/body/eval_jaxpr/hqk,qhd->khd/dot_general | solution.py:143
  439.5 15.8 %fusion.31 = bf16[882,1,12,64]{0,3,2,1:T(8,128)(2,1)} fusion(bf16[882,12,64]{0,2,1:T(8,128)(2,1)} %bitcast.89, f32[12,882,882]{1,2,0:T(8,128)} %get-tuple-element.153, f32[12,882]{1,0:T(8,128)S(1)} %copy-done.15), kind=kOutput, calls=%fused_computation.79 | convolution fusion | flops 1214238848 | bytes 40092192 | tf_op jit(solution)/shard_map/while/body/eval_jaxpr/hqk,qhd->khd/dot_general | solution.py:146
  461.5 3.8 fusion.75
  465.6 10.3 %fusion.34 = bf16[882,1,12,64]{0,3,2,1:T(8,128)(2,1)S(1)} fusion(bf16[12,882,882]{1,2,0:T(8,128)(2,1)} %multiply_convert_fusion, bf16[882,3,12,64]{0,3,2,1:T(8,128)(2,1)} %bitcast.87), kind=kOutput, calls=%fused_computation.80 | convolution fusion | flops 1196246016 | bytes 21826560 | tf_op jit(solution)/shard_map/while/body/eval_jaxpr/hqk,khd->qhd/dot_general | solution.py:138
  478.7 6.7 fusion.60
  486.1 10.4 %fusion.64 = f32[768,3072]{1,0:T(8,128)} fusion(bf16[882,3072]{1,0:T(8,128)(2,1)} %get-tuple-element.136, f32[882,768]{1,0:T(8,128)S(1)} %get-tuple-element.156, f32[768]{0:T(1024)S(1)} %copy-done.30, f32[768]{0:T(1024)S(1)} %convert_element_type.193, f32[882]{0:T(1024)S(1)} %fusion.58, f32[882]{0:T(1024)S(1)} %broadcast_multiply_fusion), kind=kOutput, calls=%fused_computation.154 | convolution fusion | flops 4165185024 | bytes 17578896 | tf_op jit(solution)/shard_map/dot_general | solution.py:31
  497.9 10.2 %fusion.74 = f32[3072,768]{1,0:T(8,128)} fusion(bf16[882,3072]{1,0:T(8,128)(2,1)} %copy-done.14, bf16[882,768]{1,0:T(8,128)(2,1)S(1)} %copy-done.6), kind=kOutput, calls=%fused_computation.162 | convolution fusion | flops 4161798144 | bytes 16210944 | tf_op jit(solution)/shard_map/dot_general | solution.py:31
  511.5 8.7 multiply_sine_fusion.1
  520.6 6.0 fusion.66
  528.5 41.8 %all-reduce.22 = (f32[768]{0:T(1024)S(1)}, f32[768]{0:T(1024)S(1)}, f32[768]{0:T(1024)S(1)}, f32[768]{0:T(1024)S(1)}, f32[768]{0:T(1024)S(1)}, /*index=5*/f32[76...) all-reduce(f32[768]{0:T(1024)S(1)} %get-tuple-element.89, ...), channel_id=2, replica_groups=mesh['dp'=32] {'dp'}, use_global_device_ids=true, to_apply=%region_21.22.clone | all-reduce | flops 10240 | bytes 81920
  576.8 4.4 add_convert_fusion.2
  588.4 100.5 %reduce-scatter.6.cloned.1.call-done = f32[24,2304]{1,0:T(8,128)} async-done(((f32[768,2304]{1,0:T(8,128)}), f32[24,2304]{1,0:T(8,128)}) %reduce-scatter.6.cloned.1.call-update) | async-done | bytes 221200 | tf_op jit(solution)/shard_map/reduce_scatter | solution.py:447
  688.9 141.3 %reduce-scatter.10.cloned.1.call-done = f32[24,3072]{1,0:T(8,128)} async-done(((f32[768,3072]{1,0:T(8,128)}), f32[24,3072]{1,0:T(8,128)}) %reduce-scatter.10.cloned.1.call-update) | async-done | bytes 294928 | tf_op jit(solution)/shard_map/reduce_scatter | solution.py:454
  830.2 142.1 %reduce-scatter.12.cloned.1.call-done = f32[96,768]{1,0:T(8,128)} async-done(((f32[3072,768]{1,0:T(8,128)}), f32[96,768]{1,0:T(8,128)}) %reduce-scatter.12.cloned.1.call-update) | async-done | bytes 294928 | tf_op jit(solution)/shard_map/reduce_scatter | solution.py:456
  (288 shorter events, 96.5 us)
Async XLA Ops:
  7.2 143.9 %all-gather.5.cloned.1.call-start = ((), (), s32[]{:S(2)}) async-start(), calls=%async_computation.8 | async-start | bytes 3649536 | tf_op jit(solution)/shard_map/all_gather | solution.py:334
  7.9 207.0 %all-gather.7.cloned.1.call-start = ((), (), s32[]{:S(2)}) async-start(), calls=%async_computation.9 | async-start | bytes 1216512 | tf_op jit(solution)/shard_map/all_gather | solution.py:337
  8.7 210.9 %all-gather.9.cloned.1.call-start = ((), (), s32[]{:S(2)}) async-start(), calls=%async_computation.10 | async-start | bytes 4866048 | tf_op jit(solution)/shard_map/all_gather | solution.py:341
  14.3 129.1 %copy-start.53 = (s32[126]{0:T(128)}, s32[126]{0:T(128)S(1)}, u32[]{:S(2)}) copy-start(s32[126]{0:T(128)S(1)} %compare_select_fusion.1) | copy-start | bytes 1516
  15.8 57.3 %all-to-all-start = ((s32[32,4,11]{2,1,0:T(4,128)}), s32[32,4,11]{2,1,0:T(4,128)S(1)}, u32[]{:S(2)}, u32[]{:S(2)}) async-start(s32[32,4,11]{2,1,0:T(4,128)} %bitcast.5), calls=%async_computation | async-start | bytes 131072 | tf_op jit(solution)/shard_map/all_to_all | solution.py:374
  81.6 61.8 %copy-start.1 = (bf16[882,768]{1,0:T(8,128)(2,1)S(1)}, bf16[882,768]{1,0:T(8,128)(2,1)}, u32[]{:S(2)}) copy-start(bf16[882,768]{1,0:T(8,128)(2,1)} %param.22) | copy-start | bytes 4064260
  83.3 62.6 %all-to-all-start.2 = ((bf16[32,4,7,768]{3,1,2,0:T(4,128)(2,1)}), bf16[32,4,7,768]{3,1,2,0:T(4,128)(2,1)S(1)}, u32[]{:S(2)}, u32[]{:S(2)}) async-start(bf16[32,4,7,768]{3,1,2,0:T(4,128)(2,1)} %copy.104), calls=%async_computation.2 | async-start | bytes 2752512 | tf_op jit(solution)/shard_map/all_to_all | solution.py:415
  86.0 179.9 %all-gather.11.cloned.1.call-start = ((), (), s32[]{:S(2)}) async-start(), calls=%async_computation.11 | async-start | bytes 4866048 | tf_op jit(solution)/shard_map/all_gather | solution.py:343
  142.2 8.9 copy-start.31
  142.2 8.9 copy-start.46
  142.2 77.4 %copy-start.29 = (f32[768]{0:T(1024)}, f32[768]{0:T(1024)S(1)}, u32[]{:S(2)}) copy-start(f32[768]{0:T(1024)S(1)} %convert_element_type.194) | copy-start | bytes 9220
  143.7 7.4 copy-start.27
  149.5 8.9 copy-start.4
  218.9 10.4 %copy-start.37 = (f32[882]{0:T(1024)}, f32[882]{0:T(1024)S(1)}, u32[]{:S(2)}) copy-start(f32[882]{0:T(1024)S(1)} %multiply_reduce_fusion.4) | copy-start | bytes 10588
  299.5 9.6 slice-start
  299.6 9.6 copy-start.38
  299.6 9.6 slice-start.1
  299.6 9.6 slice-start.2
  317.4 34.3 %copy-start.39 = (f32[882]{0:T(1024)}, f32[882]{0:T(1024)S(1)}, u32[]{:S(2)}) copy-start(f32[882]{0:T(1024)S(1)} %negate_multiply_fusion.2) | copy-start | bytes 10588
  347.9 107.4 %all-to-all-start.1 = ((bf16[32,4,7,768]{3,1,2,0:T(4,128)(2,1)}), bf16[32,4,7,768]{3,1,2,0:T(4,128)(2,1)}, u32[]{:S(2)}, u32[]{:S(2)}) async-start(bf16[32,4,7,768]{3,1,2,0:T(4,128)(2,1)} %copy.102), calls=%async_computation.1 | async-start | bytes 2752512 | tf_op jit(solution)/shard_map/all_to_all | solution.py:373
  351.5 237.0 %reduce-scatter.8.cloned.1.call-start = ((), (), s32[]{:S(2)}) async-start(), calls=%async_computation.13 | async-start | bytes 2433024 | tf_op jit(solution)/shard_map/reduce_scatter | solution.py:450
  358.9 229.5 %reduce-scatter.14.cloned.1.call-start = ((), (), s32[]{:S(2)}) async-start(), calls=%async_computation.16 | async-start | bytes 1622016 | tf_op jit(solution)/shard_map/reduce_scatter | solution.py:458
  465.3 223.6 %reduce-scatter.6.cloned.1.call-start = ((), (), s32[]{:S(2)}) async-start(), calls=%async_computation.12 | async-start | bytes 7299072 | tf_op jit(solution)/shard_map/reduce_scatter | solution.py:447
  465.6 10.3 %copy-start.12 = (bf16[882,1,12,64]{0,3,2,1:T(8,128)(2,1)S(1)}, bf16[882,1,12,64]{0,3,2,1:T(8,128)(2,1)}, u32[]{:S(2)}) copy-start(bf16[882,1,12,64]{0,3,2,1:T(8,128)(2,1)} %fusion.31) | copy-start | bytes 4064260
  465.6 10.3 %copy-start.13 = (bf16[882,1,12,64]{0,3,2,1:T(8,128)(2,1)S(1)}, bf16[882,1,12,64]{0,3,2,1:T(8,128)(2,1)}, u32[]{:S(2)}) copy-start(bf16[882,1,12,64]{0,3,2,1:T(8,128)(2,1)} %fusion.35) | copy-start | bytes 4064260
  485.4 344.7 %reduce-scatter.10.cloned.1.call-start = ((), (), s32[]{:S(2)}) async-start(), calls=%async_computation.14 | async-start | bytes 9732096 | tf_op jit(solution)/shard_map/reduce_scatter | solution.py:454
  496.5 475.8 %reduce-scatter.12.cloned.1.call-start = ((), (), s32[]{:S(2)}) async-start(), calls=%async_computation.15 | async-start | bytes 9732096 | tf_op jit(solution)/shard_map/reduce_scatter | solution.py:456
  509.6 10.6 %copy-start.5 = (bf16[126,7,768]{2,1,0:T(8,128)(2,1)S(1)}, bf16[126,7,768]{2,1,0:T(8,128)(2,1)}, u32[]{:S(2)}) copy-start(bf16[126,7,768]{2,1,0:T(8,128)(2,1)} %copy-done.4) | copy-start | bytes 4064260
  511.5 9.1 copy-start.3
  511.5 9.1 copy-start.8
  527.1 49.6 %copy-start = (f32[882,768]{1,0:T(8,128)S(1)}, f32[882,768]{1,0:T(8,128)}, u32[]{:S(2)}) copy-start(f32[882,768]{1,0:T(8,128)} %get-tuple-element.141) | copy-start | bytes 8128516
  527.1 49.6 %copy-start.40 = (f32[882]{0:T(1024)S(1)}, f32[882]{0:T(1024)}, u32[]{:S(2)}) copy-start(f32[882]{0:T(1024)} %copy-done.39) | copy-start | bytes 10588
  (53 other events, 175.9 us)
Sparse Core Ops, SparseCore 0:
  10.9 63.9 all-gather.4
  77.8 57.3 all-gather.6
  138.1 62.5 all-gather.8
  203.4 62.4 all-gather.10
  359.0 100.1 reduce-scatter.7
  465.8 97.9 reduce-scatter.13
  570.9 117.9 reduce-scatter.5
  695.4 134.7 reduce-scatter.9
  837.7 134.5 reduce-scatter.11
where the time goes:
time: 987 us; the launch traced here: 979 us
  waiting for transfers between devices  423 us (43%)
  matrix products  226 us (23%)
  blocking collectives  142 us (14%)
  other arithmetic  83 us (8%)
  local copies, waits for them, and re-layouts  75.4 us (8%)
  between operations  15.3 us (2%)
  starting transfers between devices  14.5 us (1%)
    reduce_scatter x1, waiting for transfers between devices, local(): lax.psum_scatter(grad_fc2_weight, 'dp', scatter_dimension=0, tiled=True)  142 us
    reduce_scatter x1, waiting for transfers between devices, local(): lax.psum_scatter(grad_fc1_weight, 'dp', scatter_dimension=0, tiled=True)  141 us
    reduce_scatter x1, waiting for transfers between devices, local(): lax.psum_scatter(grad_qkv_weight, 'dp', scatter_dimension=0, tiled=True)  100 us
    unnamed x2, blocking collectives  94.8 us
    dot_general x5, matrix products, times_transposed(): lax.dot_general(left, right, (((1,), (1,)), ((), ())), preferred_element_...  56.7 us
    all_gather x1, blocking collectives, local(): lax.all_gather(dec_weight, 'dp', axis=0, tiled=True)  47.4 us
    all_gather x1, waiting for transfers between devices, local(): lax.all_gather(fc2_weight, 'dp', axis=0, tiled=True)  36.6 us
    dot_general x5, matrix products, contract_rows(): lax.dot_general(left, right, (((0,), (0,)), ((), ())), preferred_element_...  33.8 us
  transfers between devices with their start and end apart: 12, of which 4 were waited for; matrix products, arithmetic and copies ran while one was open for 30% of the time, Pallas kernels for 0%

commit v1 on v0

v1 whole, which is shorter than its diff:
```python
import functools

import jax
import jax.numpy as jnp
from jax import lax
from jax.experimental import pallas as pl
from jax.experimental.pallas import tpu as pltpu
from jax.sharding import PartitionSpec as P

HEADS = 12
GRID = 14
NORM_EPS = 1e-06
MASK_FILL = -1e30
BF = jnp.bfloat16
F32 = jnp.float32
MIB = 1 << 20


class Slice:
    def __init__(self, count):
        chips = count // 2
        side = 2 if chips <= 16 else 4
        self.count = count
        self.size = {"c": 2, "x": side, "y": side, "z": chips // (side * side)}
        self.stride = {"c": 1, "x": 2, "y": 2 * side, "z": 2 * side * side}

    def coord(self, axis):
        return (lax.axis_index("dp") // self.stride[axis]) % self.size[axis]

    def shift(self, values, axis, steps):
        stride, size = self.stride[axis], self.size[axis]
        pairs = []
        for source in range(self.count):
            place = (source // stride) % size
            pairs.append((source, source + ((place + steps) % size - place) * stride))
        return lax.ppermute(values, "dp", pairs)

    def spread(self, values, axis):
        return jnp.stack(
            [values] + [self.shift(values, axis, k) for k in range(1, self.size[axis])]
        )

    def groups(self, axes):
        seen, found = set(), []
        for first in range(self.count):
            if first in seen:
                continue
            members = [first]
            for axis in axes:
                members = [
                    m + k * self.stride[axis] for m in members for k in range(self.size[axis])
                ]
            found.append(members)
            seen.update(members)
        return found


def cost(flops, moved, trans=0):
    return pl.CostEstimate(
        flops=int(flops), bytes_accessed=int(moved), transcendentals=int(trans)
    )


def params(mib):
    return pltpu.CompilerParams(vmem_limit_bytes=mib * MIB)


def whole(shape):
    zeros = (0,) * len(shape)
    return pl.BlockSpec(shape, lambda *_: zeros)


SMEM = pl.BlockSpec(memory_space=pltpu.SMEM)


def assemble_kernel(sizes, widths, place, part_a, part_b, from_a, from_b, *outs):
    nz, ny, nx = sizes
    own_z, own_y, own_x, own_c = place[0], place[1], place[2], place[3]
    for kz in range(nz):
        at_z = lax.rem(own_z - kz + nz, nz)
        for ky in range(ny):
            at_y = lax.rem(own_y - ky + ny, ny)
            for kx in range(nx):
                at_x = lax.rem(own_x - kx + nx, nx)
                chip = (at_z * ny + at_y) * nx + at_x
                for core, left, right in ((own_c, part_a, part_b), (1 - own_c, from_a, from_b)):
                    row, start = chip * 2 + core, 0
                    for out, width in zip(outs, widths):
                        half = width // 2
                        out[row, :, :half] = left[ky, kx, kz, :, start : start + half]
                        out[row, :, half:] = right[kx, ky, kz, :, start : start + half]
                        start += half


def gather_start(dev, shards):
    if len(shards) == 1:
        local = shards[0]
    else:
        halves = [s.shape[1] // 2 for s in shards]
        local = jnp.concatenate(
            [s[:, :h] for s, h in zip(shards, halves)] + [s[:, h:] for s, h in zip(shards, halves)],
            axis=1,
        )
    return dev.spread(local, "z")


def gather_finish(dev, shards, along_z):
    rows = shards[0].shape[0]
    widths = [s.shape[1] for s in shards]
    half = sum(widths) // 2
    part_a = dev.spread(dev.spread(along_z[:, :, :half], "x"), "y")
    part_b = dev.spread(dev.spread(along_z[:, :, half:], "y"), "x")
    from_a, from_b = dev.shift(part_a, "c", 1), dev.shift(part_b, "c", 1)
    place = jnp.stack([dev.coord(axis) for axis in "zyxc"]).astype(jnp.int32)
    sizes = (dev.size["z"], dev.size["y"], dev.size["x"])
    kind = shards[0].dtype
    outs = pl.pallas_call(
        functools.partial(assemble_kernel, sizes, widths),
        name="assemble",
        out_shape=[jax.ShapeDtypeStruct((dev.count, rows, w), kind) for w in widths],
        in_specs=[SMEM] + [pl.BlockSpec(memory_space=pltpu.VMEM)] * 4,
        out_specs=[pl.BlockSpec(memory_space=pltpu.VMEM)] * len(widths),
        compiler_params=params(40),
        cost_estimate=cost(0, 4 * dev.count * rows * sum(widths)),
    )(place, part_a, part_b, from_a, from_b)
    return [o.reshape(dev.count * rows, w) for o, w in zip(outs, widths)]


def scatter_group(dev, partials):
    count = dev.count
    rows = partials[0].shape[0] // count
    nz, plane = dev.size["z"], dev.size["y"] * dev.size["x"]
    core = dev.coord("c")

    def pick(values, which):
        split = values.reshape(nz, plane, 2, rows, values.shape[1])
        return jnp.where(which == 0, split[:, :, 0], split[:, :, 1])

    sent = jnp.concatenate([pick(v, 1 - core) for v in partials], axis=-1)
    kept = jnp.concatenate([pick(v, core) for v in partials], axis=-1)
    got = dev.shift(sent, "c", 1)
    chip = (kept.astype(F32) + got.astype(F32)).transpose(1, 0, 2, 3).astype(BF)
    chip = chip.reshape(plane, nz * rows, chip.shape[-1])
    chip = lax.all_to_all(chip, "dp", 0, 0, axis_index_groups=dev.groups("yx"), tiled=True)
    line = jnp.sum(chip.astype(F32), axis=0).astype(BF).reshape(nz, rows, -1)
    line = lax.all_to_all(line, "dp", 0, 0, axis_index_groups=dev.groups("z"), tiled=True)
    total = jnp.sum(line.astype(F32), axis=0)
    out, start = [], 0
    for v in partials:
        out.append(total[:, start : start + v.shape[1]])
        start += v.shape[1]
    return out


def dot(left, right):
    return jnp.dot(left, right, preferred_element_type=F32)


def dot_rows(left, right):
    return lax.dot_general(left, right, (((0,), (0,)), ((), ())), preferred_element_type=F32)


def dot_cols(left, right):
    return lax.dot_general(left, right, (((1,), (1,)), ((), ())), preferred_element_type=F32)


def one_hot(column, row):
    return jnp.where(column == row, 1.0, 0.0).astype(BF)


def row_sum(values):
    return jnp.sum(values, axis=0, keepdims=True)


def normalised(values):
    mean = jnp.mean(values, axis=1, keepdims=True)
    centered = values - mean
    variance = jnp.mean(centered * centered, axis=1, keepdims=True)
    scale = lax.rsqrt(variance + NORM_EPS)
    return centered * scale, scale


def norm_back(unit, scale, gain, grad):
    weighted = grad * gain
    first = jnp.mean(weighted, axis=1, keepdims=True)
    second = jnp.mean(weighted * unit, axis=1, keepdims=True)
    return scale * (weighted - first - unit * second)


class Layout:
    def __init__(self, images, slots):
        self.images, self.slots = images, slots
        self.small, self.large = GRID * slots, 4 * GRID * slots
        self.small_pad = -(-self.small // 16) * 16
        self.large_pad = -(-self.large // 16) * 16
        self.starts = [self.large_pad + i * self.small_pad for i in range(images - 1)]
        self.rows = self.large_pad + (images - 1) * self.small_pad

    def describe(self, big, count_vec, bucket):
        row = jnp.arange(self.rows, dtype=jnp.int32)
        small_id = jnp.maximum(row - self.large_pad, 0) // self.small_pad
        in_large = row < self.large_pad
        offset = jnp.where(in_large, row, row - self.large_pad - small_id * self.small_pad)
        real = offset < jnp.where(in_large, self.large, self.small)
        image = jnp.where(in_large, big, small_id + (small_id >= big).astype(jnp.int32))
        window = GRID * image + 3 * GRID * (image > big).astype(jnp.int32) + offset // self.slots
        slot = offset % self.slots
        kept = jnp.sum(
            jnp.where(
                image[:, None] == jnp.arange(self.images, dtype=jnp.int32)[None, :],
                count_vec[None, :],
                0,
            ),
            axis=1,
        )
        live = real & (slot < kept)
        windows = bucket.shape[0]
        target = jnp.sum(
            jnp.where(
                window[:, None] == jnp.arange(windows, dtype=jnp.int32)[None, :], bucket[None, :], 0
            ),
            axis=1,
        )
        source = jnp.where(real, window * self.slots + slot, -1)
        place = jnp.where(live, target * self.slots + slot, -1)
        return source, live, place


def owner_kernel(slots, wins, cot, off_col, live_col, off_row, info_col, present_row, mask_tok,
                 de_out, base_out, sums_out):
    step = pl.program_id(0)
    cells, rows = wins * GRID, wins * slots
    width = cot.shape[1]
    quarter = width // 4
    grads = cot[...]
    slot_row = lax.broadcasted_iota(jnp.int32, (rows, 1), 0)
    cell_lane = lax.broadcasted_iota(jnp.int32, (1, cells), 1)
    want = jnp.where(live_col[...] > 0, (slot_row // slots) * GRID + off_col[...], -1)
    pick = one_hot(want, cell_lane)
    picked = dot(pick, grads)
    de_out[...] = picked.astype(BF)
    taken = jnp.sum(jnp.where(want == cell_lane, 1.0, 0.0), axis=0, keepdims=True)
    masked = present_row[0].astype(F32) - taken
    mask_sum = dot(jnp.broadcast_to(masked, (8, cells)).astype(BF), grads)[:1]

    cell_row = lax.broadcasted_iota(jnp.int32, (cells, 1), 0)
    want_lane = jnp.where(
        off_row[0] >= 0,
        (lax.broadcasted_iota(jnp.int32, (1, rows), 1) // slots) * GRID + off_row[0],
        -1,
    )
    filled = jnp.sum(jnp.where(cell_row == want_lane, 1.0, 0.0), axis=1, keepdims=True)
    present = info_col[:, 0:1]
    along = info_col[:, 1:2]
    across = info_col[:, 2:3]
    depth = 32
    place = lax.broadcasted_iota(jnp.int32, (depth, quarter), 0).astype(F32)
    index = lax.broadcasted_iota(jnp.int32, (depth, quarter), 1).astype(F32) / quarter
    angle = place * (1.0 / jnp.exp(index * jnp.log(F32(10000.0))))
    table = jnp.concatenate([jnp.sin(angle), jnp.cos(angle)], axis=1)
    high = table.astype(BF)
    rest = table - high.astype(F32)
    middle = rest.astype(BF)
    low = (rest - middle.astype(F32)).astype(BF)
    stacked = jnp.concatenate([high, middle, low], axis=0)
    lane = lax.broadcasted_iota(jnp.int32, (1, 3 * depth), 1) % depth
    shown = present > 0
    first = dot(one_hot(jnp.where(shown, along, -1), lane), stacked)
    second = dot(one_hot(jnp.where(shown, across, -1), lane), stacked)
    bare = present.astype(F32) - filled
    base_out[:, : 2 * quarter] = first + bare * mask_tok[:, : 2 * quarter]
    base_out[:, 2 * quarter :] = second + bare * mask_tok[:, 2 * quarter :]

    @pl.when(step == 0)
    def _():
        sums_out[...] = jnp.zeros_like(sums_out)

    sums_out[0:1, :] += mask_sum
    sums_out[1:2, :] += row_sum(picked)


def decode_kernel(slots, wins, got, off_row, base, out):
    cells, rows = wins * GRID, wins * slots
    cell_row = lax.broadcasted_iota(jnp.int32, (cells, 1), 0)
    want_lane = jnp.where(
        off_row[0] >= 0,
        (lax.broadcasted_iota(jnp.int32, (1, rows), 1) // slots) * GRID + off_row[0],
        -1,
    )
    out[...] = (dot(one_hot(cell_row, want_lane), got[...]) + base[...]).astype(BF)


def first_norm_kernel(tokens, source, gain, bias, x_out, h_out):
    lane = lax.broadcasted_iota(jnp.int32, (1, tokens.shape[0]), 1)
    moved = dot(one_hot(source[...], lane), tokens[...])
    x_out[...] = moved.astype(BF)
    unit, _ = normalised(moved)
    h_out[...] = (unit * gain[...] + bias[...]).astype(BF)


def softmax_rows(scores):
    top = jnp.max(scores, axis=1, keepdims=True)
    expo = jnp.exp(scores - top)
    return (expo * (1.0 / jnp.sum(expo, axis=1, keepdims=True))).astype(BF)


def attention_kernel(lay, chunk, head_dim, h_in, w_q, w_k, w_v, b_q, b_v, mask_l, mask_s,
                     q_out, k_out, v_out, pl_out, ps_out, o_out, scores):
    big, small = lay.large_pad, lay.small_pad
    normed = h_in[...]
    q_out[...] = ((dot(normed, w_q[...]) + b_q[...]) * (head_dim**-0.5)).astype(BF)
    k_out[...] = dot(normed, w_k[...]).astype(BF)
    v_out[...] = (dot(normed, w_v[...]) + b_v[...]).astype(BF)
    lane = lax.broadcasted_iota(jnp.int32, (1, 2 * head_dim), 1)
    low = lane < head_dim
    halves = (jnp.where(low, 1.0, 0.0).astype(BF), jnp.where(low, 0.0, 1.0).astype(BF))
    for pair in range(q_out.shape[1] // (2 * head_dim)):
        cols = slice(pair * 2 * head_dim, (pair + 1) * 2 * head_dim)
        first = []
        for half in range(2):
            head = 2 * pair + half
            query = q_out[:big, cols] * halves[half]
            scores[...] = dot_cols(query, k_out[:big, cols])
            for start in range(0, big, chunk):
                part = scores[start : start + chunk, :] + mask_l[...]
                pl_out[head, start : start + chunk, :] = softmax_rows(part)
            outs = [dot(pl_out[head], v_out[:big, cols])]
            for i, start in enumerate(lay.starts):
                rows = slice(start, start + small)
                query = q_out[rows, cols] * halves[half]
                part = dot_cols(query, k_out[rows, cols]) + mask_s[i : i + 1, :]
                weights = softmax_rows(part)
                ps_out[head, i] = weights
                outs.append(dot(weights, v_out[rows, cols]))
            if half == 0:
                first = outs
        spans = [(0, big)] + [(s, small) for s in lay.starts]
        for (start, size), left, right in zip(spans, first, outs):
            o_out[start : start + size, cols] = jnp.where(low, left, right).astype(BF)


def out_kernel(o_in, w_out, bias, x_in, gain, offset, r_out, h_out):
    residual = x_in[...].astype(F32) + dot(o_in[...], w_out[...]) + bias[...]
    r_out[...] = residual
    unit, _ = normalised(residual)
    h_out[...] = (unit * gain[...] + offset[...]).astype(BF)


def fc1_kernel(chunk, h_in, weight, bias, g_out, d_out, hidden):
    hidden[...] = dot(h_in[...], weight[...])
    for start in range(0, hidden.shape[0], chunk):
        rows = slice(start, start + chunk)
        u = hidden[rows, :] + bias[...]
        half = 0.5 + 0.5 * lax.erf(u * (0.5**0.5))
        g_out[rows, :] = (u * half).astype(BF)
        density = jnp.exp(u * u * -0.5) * 0.3989422804014327
        d_out[rows, :] = (half + u * density).astype(BF)


def fc2_kernel(g_in, w_two, b_two, r_in, w_dec, b_dec, place, y_out, e_out, kept):
    step = pl.program_id(0)
    rows = g_in.shape[0]
    y = (r_in[...] + dot(g_in[...], w_two[...]) + b_two[...]).astype(BF)
    y_out[...] = y
    kept[pl.ds(pl.multiple_of(step * rows, rows), rows), :] = (
        dot(y, w_dec[...]) + b_dec[...]
    ).astype(BF)

    @pl.when(step == pl.num_programs(0) - 1)
    def _():
        target = lax.broadcasted_iota(jnp.int32, (e_out.shape[0], 1), 0)
        e_out[...] = dot(one_hot(target, place[...]), kept[...]).astype(BF)


def dec_back_kernel(got, place, w_dec, y_in, dy_out, dw_out, db_out):
    lane = lax.broadcasted_iota(jnp.int32, (1, got.shape[0]), 1)
    grad = dot(one_hot(place[...], lane), got[...]).astype(BF)
    dy = dot_cols(grad, w_dec[...]).astype(BF)
    dy_out[...] = dy
    dw_out[...] = dot_rows(y_in[...], grad).astype(BF)
    db_out[...] = row_sum(dy.astype(F32))


def fc2_back_kernel(dy_in, w_two, g_in, d_in, du_out, dw_out, db_out):
    dy = dy_in[...]
    du = (dot_cols(dy, w_two[...]) * d_in[...].astype(F32)).astype(BF)
    du_out[...] = du
    db_out[...] = row_sum(du.astype(F32))
    dw_out[...] = dot_rows(g_in[...], dy).astype(BF)


def fc1_back_kernel(du_in, w_one, h_in, dh_out, dw_out, turned):
    step = pl.program_id(0)

    @pl.when(step == 0)
    def _():
        turned[...] = h_in[...].T
        dh_out[...] = jnp.zeros_like(dh_out)

    du = du_in[...]
    dw_out[...] = dot(turned[...], du).astype(BF)
    dh_out[...] += dot_cols(du, w_one[...])


def out_back_kernel(dh_in, r_in, dy_in, gain, w_out, o_in, dr_out, do_out, dw_out, sums, total):
    step = pl.program_id(0)
    unit, scale = normalised(r_in[...])
    grad = dh_in[...]
    dr = dy_in[...].astype(F32) + norm_back(unit, scale, gain[...], grad)
    dr_out[...] = dr
    da = dr.astype(BF)
    do_out[...] = dot_cols(da, w_out[...]).astype(BF)

    @pl.when(step == 0)
    def _():
        sums[...] = jnp.zeros_like(sums)
        total[...] = jnp.zeros_like(total)

    sums[0:1, :] += row_sum(grad * unit)
    sums[1:2, :] += row_sum(grad)
    sums[2:3, :] += row_sum(da.astype(F32))
    total[...] += dot_rows(o_in[...], da)

    @pl.when(step == pl.num_programs(0) - 1)
    def _():
        dw_out[...] = total[...].astype(BF)


def attention_back_kernel(lay, chunk, head_dim, h_in, q_in, k_in, v_in, pl_in, ps_in, do_in,
                          dq_out, dk_out, dv_out, wq_out, wk_out, wv_out, sums, turned, scores, ds_big):
    step = pl.program_id(0)
    big, small = lay.large_pad, lay.small_pad

    @pl.when(step == 0)
    def _():
        turned[...] = h_in[...].T

    lane = lax.broadcasted_iota(jnp.int32, (1, 2 * head_dim), 1)
    low = lane < head_dim
    halves = (jnp.where(low, 1.0, 0.0).astype(BF), jnp.where(low, 0.0, 1.0).astype(BF))

    def back_rows(weights, grad):
        p = weights.astype(F32)
        inner = jnp.sum(grad * p, axis=1, keepdims=True)
        return (p * (grad - inner)).astype(BF)

    for pair in range(q_in.shape[1] // (2 * head_dim)):
        cols = slice(pair * 2 * head_dim, (pair + 1) * 2 * head_dim)
        spans = [(0, big)] + [(s, small) for s in lay.starts]
        first = []
        for half in range(2):
            head = 2 * pair + half
            found = []
            for i, (start, size) in enumerate(spans):
                rows = slice(start, start + size)
                grad_o = do_in[rows, cols] * halves[half]
                if i == 0:
                    scores[...] = dot_cols(grad_o, v_in[rows, cols])
                    for s in range(0, big, chunk):
                        ds_big[s : s + chunk, :] = back_rows(
                            pl_in[head, s : s + chunk, :], scores[s : s + chunk, :]
                        )
                    weights, ds = pl_in[head], ds_big[...]
                else:
                    weights = ps_in[head, i - 1]
                    ds = back_rows(weights, dot_cols(grad_o, v_in[rows, cols]))
                found.append(
                    (
                        dot(ds, k_in[rows, cols]),
                        dot_rows(ds, q_in[rows, cols]),
                        dot_rows(weights, do_in[rows, cols]),
                    )
                )
            if half == 0:
                first = found
        for (start, size), left, right in zip(spans, first, found):
            rows = slice(start, start + size)
            dq_out[rows, cols] = (
                jnp.where(low, left[0], right[0]) * (head_dim**-0.5)
            ).astype(BF)
            dk_out[rows, cols] = jnp.where(low, left[1], right[1]).astype(BF)
            dv_out[rows, cols] = jnp.where(low, left[2], right[2]).astype(BF)
    wq_out[...] = dot(turned[...], dq_out[...]).astype(BF)
    wk_out[...] = dot(turned[...], dk_out[...]).astype(BF)
    wv_out[...] = dot(turned[...], dv_out[...]).astype(BF)
    sums[0:1, :] = row_sum(dq_out[...].astype(F32))
    sums[1:2, :] = row_sum(dv_out[...].astype(F32))


def first_back_kernel(dq_in, dk_in, dv_in, w_qkv, x_in, dr_in, gain, source, out, sums, kept):
    step = pl.program_id(0)
    rows, width = x_in.shape
    grad = dot_cols(dq_in[...], w_qkv[:, :width])
    grad += dot_cols(dk_in[...], w_qkv[:, width : 2 * width])
    grad += dot_cols(dv_in[...], w_qkv[:, 2 * width :])
    unit, scale = normalised(x_in[...].astype(F32))
    moved = dr_in[...] + norm_back(unit, scale, gain[...], grad)
    kept[pl.ds(pl.multiple_of(step * rows, rows), rows), :] = moved.astype(BF)

    @pl.when(step == 0)
    def _():
        sums[...] = jnp.zeros_like(sums)

    sums[0:1, :] += row_sum(grad * unit)
    sums[1:2, :] += row_sum(grad)

    @pl.when(step == pl.num_programs(0) - 1)
    def _():
        slot = lax.broadcasted_iota(jnp.int32, (out.shape[0], 1), 0)
        out[...] = dot(one_hot(slot, source[...]), kept[...]).astype(BF)


def owner_rank(owner_vec):
    window_ids = jnp.arange(owner_vec.shape[0], dtype=jnp.int32)
    earlier = (owner_vec[:, None] == owner_vec[None, :]) & (
        window_ids[None, :] < window_ids[:, None]
    )
    return jnp.sum(earlier.astype(jnp.int32), axis=1)


def spec(shape, index):
    return pl.BlockSpec(shape, index)


def local(tokens, ln1_gain, ln1_bias, qkv_weight, query_bias, value_bias, out_weight, out_bias,
          ln2_gain, ln2_bias, fc1_weight, fc1_bias, fc2_weight, fc2_bias, dec_weight, dec_bias,
          mask_token, kept_offsets, kept_count, res_id, dec_owner, dec_cot):
    count = lax.axis_size("dp")
    dev = Slice(count)
    vis, D = tokens.shape
    dec_width = dec_cot.shape[1]
    windows, slots = kept_offsets.shape
    images = res_id.shape[0]
    hidden = fc1_weight.shape[1]
    head_dim = D // HEADS
    per_peer = (windows + count - 1) // count
    total = count * per_peer
    lay = Layout(images, slots)
    R = lay.rows
    sd = jax.ShapeDtypeStruct

    vectors = [ln1_gain, ln1_bias, query_bias, value_bias, out_bias, ln2_gain, ln2_bias, fc1_bias,
               fc2_bias, dec_bias, mask_token]
    packed = jnp.concatenate(vectors)
    packed = lax.all_to_all(
        jnp.broadcast_to(packed[None, :], (count, packed.shape[0])), "dp", 0, 0, tiled=True
    ).astype(F32)
    full, start = [], 0
    for v in vectors:
        full.append(packed[:, start : start + v.shape[0]].reshape(1, -1))
        start += v.shape[0]
    (g1, b1, bq, bv, bo, g2, b2, bf1, bf2, bdec, mask_tok) = full

    group_a, group_b, group_c = [qkv_weight], [out_weight, dec_weight, fc1_weight], [fc2_weight]
    z_a = gather_start(dev, group_a)
    (w_qkv,) = gather_finish(dev, group_a, z_a)
    z_b = gather_start(dev, group_b)
    w_out, w_dec, w_one = gather_finish(dev, group_b, z_b)
    z_c = gather_start(dev, group_c)
    (w_two,) = gather_finish(dev, group_c, z_c)

    image_ids = jnp.arange(images, dtype=jnp.int32)
    big = jnp.sum(image_ids * res_id)
    bucket = dec_owner * per_peer + owner_rank(dec_owner)
    source, live, place = lay.describe(big, kept_count, bucket)
    source_col, source_row = source[:, None], source[None, :]
    place_col, place_row = place[:, None], place[None, :]
    mask_all = jnp.where(live, 0.0, MASK_FILL).astype(F32)
    mask_l = mask_all[None, : lay.large_pad]
    mask_s = mask_all[lay.large_pad :].reshape(images - 1, lay.small_pad)

    win = jnp.arange(windows, dtype=jnp.int32)
    big_start = GRID * big
    in_big = (win >= big_start) & (win < big_start + 4 * GRID)
    after = win >= big_start + 4 * GRID
    image_win = jnp.where(in_big, big, jnp.where(after, win // GRID - 3, win // GRID))
    in_image = jnp.where(in_big, win - big_start, win % GRID)
    kept_win = jnp.sum(
        jnp.where(image_win[:, None] == image_ids[None, :], kept_count[None, :], 0), axis=1
    )
    side_win = jnp.where(in_big, 2 * GRID, GRID)
    info = jnp.concatenate(
        [jnp.stack([jnp.ones_like(win), kept_win, in_image, side_win], axis=1), kept_offsets], axis=1
    )
    slot_of = jnp.arange(total, dtype=jnp.int32)
    info_send = jnp.sum(
        jnp.where((slot_of[:, None] == bucket[None, :])[:, :, None], info[None, :, :], 0), axis=1
    )
    info_got = lax.all_to_all(
        info_send.reshape(count, per_peer, -1), "dp", 0, 0, tiled=True
    ).reshape(total, -1)

    wins = 16
    steps = total // wins
    off_live = jnp.where(
        jnp.arange(slots, dtype=jnp.int32)[None, :] < info_got[:, 1:2], info_got[:, 4:], -1
    )
    off_col = jnp.maximum(off_live, 0).reshape(-1, 1)
    live_col = (off_live >= 0).astype(jnp.int32).reshape(-1, 1)
    off_row = off_live.reshape(steps, 1, wins * slots)
    present_row = jnp.repeat(info_got[:, 0:1], GRID, axis=1).reshape(steps, 1, wins * GRID)
    spot = info_got[:, 2:3] * GRID + jnp.arange(GRID, dtype=jnp.int32)[None, :]
    side = jnp.maximum(info_got[:, 3:4], 1)
    info_col = jnp.stack(
        [jnp.broadcast_to(info_got[:, 0:1], spot.shape), spot % side, spot // side], axis=-1
    ).reshape(total * GRID, 3)
    cells_w, rows_w = wins * GRID, wins * slots
    by_step = lambda shape: spec(shape, lambda i: (i,) + (0,) * (len(shape) - 1))
    de_send, base, owner_sums = pl.pallas_call(
        functools.partial(owner_kernel, slots, wins),
        name="owner_side",
        grid=(steps,),
        in_specs=[by_step((cells_w, dec_width)), by_step((rows_w, 1)), by_step((rows_w, 1)),
                  by_step((1, 1, rows_w)), by_step((cells_w, 3)), by_step((1, 1, cells_w)),
                  whole((1, dec_width))],
        out_specs=[by_step((rows_w, dec_width)), by_step((cells_w, dec_width)), whole((8, dec_width))],
        out_shape=[sd((total * slots, dec_width), BF), sd((total * GRID, dec_width), F32),
                   sd((8, dec_width), F32)],
        compiler_params=params(32),
        cost_estimate=cost(4e9, 8e6, 1e5),
    )(dec_cot, off_col, live_col, off_row, info_col, present_row, mask_tok)
    de_got = lax.all_to_all(
        de_send.reshape(count, per_peer * slots, dec_width), "dp", 0, 0, tiled=True
    ).reshape(total * slots, dec_width)

    tile = R // 3
    rows_of = lambda width: spec((tile, width), lambda i: (i, 0))
    x_rows, h_one = pl.pallas_call(
        first_norm_kernel,
        name="first_norm",
        grid=(3,),
        in_specs=[whole((vis, D)), rows_of(1), whole((1, D)), whole((1, D))],
        out_specs=[rows_of(D), rows_of(D)],
        out_shape=[sd((R, D), BF), sd((R, D), BF)],
        compiler_params=params(32),
        cost_estimate=cost(2 * R * vis * D, 4e6),
    )(tokens, source_col, g1, b1)

    group = 4
    parts = HEADS // group
    gw = group * head_dim
    chunk = lay.large_pad // 5
    col_of = lambda base_: spec((D, gw), lambda i: (0, base_ * parts + i))
    act = spec((R, gw), lambda i: (0, i))
    vec = spec((1, gw), lambda i: (0, i))
    p_big = spec((group, lay.large_pad, lay.large_pad), lambda i: (i, 0, 0))
    p_small = spec((group, images - 1, lay.small_pad, lay.small_pad), lambda i: (i, 0, 0, 0))
    p_big_t = sd((HEADS, lay.large_pad, lay.large_pad), BF)
    p_small_t = sd((HEADS, images - 1, lay.small_pad, lay.small_pad), BF)
    q_rows, k_rows, v_rows, prob_l, prob_s, att = pl.pallas_call(
        functools.partial(attention_kernel, lay, chunk, head_dim),
        name="attention",
        grid=(parts,),
        in_specs=[whole((R, D)), col_of(0), col_of(1), col_of(2), vec, vec,
                  whole((1, lay.large_pad)), whole((images - 1, lay.small_pad))],
        out_specs=[act, act, act, p_big, p_small, act],
        out_shape=[sd((R, D), BF)] * 3 + [p_big_t, p_small_t, sd((R, D), BF)],
        scratch_shapes=[pltpu.VMEM((lay.large_pad, lay.large_pad), F32)],
        compiler_params=params(48),
        cost_estimate=cost(2 * R * D * 3 * D + 4e9, 2e7, 3e6),
    )(h_one, w_qkv, w_qkv, w_qkv, bq, bv, mask_l, mask_s)

    r_one, h_two = pl.pallas_call(
        out_kernel,
        name="out_projection",
        grid=(3,),
        in_specs=[rows_of(D), whole((D, D)), whole((1, D)), rows_of(D), whole((1, D)), whole((1, D))],
        out_specs=[rows_of(D), rows_of(D)],
        out_shape=[sd((R, D), F32), sd((R, D), BF)],
        compiler_params=params(32),
        cost_estimate=cost(2 * R * D * D, 9e6),
    )(att, w_out, bo, x_rows, g2, b2)

    ht = hidden // 6
    act_h, d_gelu = pl.pallas_call(
        functools.partial(fc1_kernel, R // 24),
        name="fc1",
        grid=(6,),
        in_specs=[whole((R, D)), spec((D, ht), lambda i: (0, i)), spec((1, ht), lambda i: (0, i))],
        out_specs=[spec((R, ht), lambda i: (0, i))] * 2,
        out_shape=[sd((R, hidden), BF)] * 2,
        scratch_shapes=[pltpu.VMEM((R, ht), F32)],
        compiler_params=params(32),
        cost_estimate=cost(2 * R * D * hidden, 2e7, 6e6),
    )(h_two, w_one, bf1)

    y_rows, e_send = pl.pallas_call(
        fc2_kernel,
        name="fc2_and_embed",
        grid=(3,),
        in_specs=[rows_of(hidden), whole((hidden, D)), whole((1, D)), rows_of(D),
                  whole((D, dec_width)), whole((1, dec_width)), whole((1, R))],
        out_specs=[rows_of(D), whole((total * slots, dec_width))],
        out_shape=[sd((R, D), BF), sd((total * slots, dec_width), BF)],
        scratch_shapes=[pltpu.VMEM((R, dec_width), BF)],
        compiler_params=params(48),
        cost_estimate=cost(2 * R * D * hidden + 4 * R * D * dec_width, 2e7),
    )(act_h, w_two, bf2, r_one, w_dec, bdec, place_row)

    e_got = lax.all_to_all(
        e_send.reshape(count, per_peer * slots, dec_width), "dp", 0, 0, tiled=True
    ).reshape(total * slots, dec_width)
    decoded = pl.pallas_call(
        functools.partial(decode_kernel, slots, wins),
        name="decode",
        grid=(steps,),
        in_specs=[by_step((rows_w, dec_width)), by_step((1, 1, rows_w)), by_step((cells_w, dec_width))],
        out_specs=by_step((cells_w, dec_width)),
        out_shape=sd((total * GRID, dec_width), BF),
        compiler_params=params(32),
        cost_estimate=cost(1e9, 7e6),
    )(e_got, off_row, base)

    dy, dw_dec, db_two = pl.pallas_call(
        dec_back_kernel,
        name="embed_back",
        in_specs=[pl.BlockSpec(memory_space=pltpu.VMEM)] * 4,
        out_specs=[pl.BlockSpec(memory_space=pltpu.VMEM)] * 3,
        out_shape=[sd((R, D), BF), sd((D, dec_width), BF), sd((1, D), F32)],
        compiler_params=params(40),
        cost_estimate=cost(6 * R * D * dec_width, 7e6),
    )(de_got, place_col, w_dec, y_rows)

    ht = hidden // 4
    du, dw_two, db_one = pl.pallas_call(
        fc2_back_kernel,
        name="fc2_back",
        grid=(4,),
        in_specs=[whole((R, D)), spec((ht, D), lambda i: (i, 0)), spec((R, ht), lambda i: (0, i)),
                  spec((R, ht), lambda i: (0, i))],
        out_specs=[spec((R, ht), lambda i: (0, i)), spec((ht, D), lambda i: (i, 0)),
                   spec((1, ht), lambda i: (0, i))],
        out_shape=[sd((R, hidden), BF), sd((hidden, D), BF), sd((1, hidden), F32)],
        compiler_params=params(48),
        cost_estimate=cost(4 * R * D * hidden, 3e7),
    )(dy, w_two, act_h, d_gelu)

    dh_two, dw_one = pl.pallas_call(
        fc1_back_kernel,
        name="fc1_back",
        grid=(4,),
        in_specs=[spec((R, ht), lambda i: (0, i)), spec((D, ht), lambda i: (0, i)), whole((R, D))],
        out_specs=[whole((R, D)), spec((D, ht), lambda i: (0, i))],
        out_shape=[sd((R, D), F32), sd((D, hidden), BF)],
        scratch_shapes=[pltpu.VMEM((D, R), BF)],
        compiler_params=params(48),
        cost_estimate=cost(4 * R * D * hidden, 2e7),
    )(du, w_one, h_two)

    dr, d_att, dw_out, sums_two = pl.pallas_call(
        out_back_kernel,
        name="out_back",
        grid=(3,),
        in_specs=[rows_of(D), rows_of(D), rows_of(D), whole((1, D)), whole((D, D)), rows_of(D)],
        out_specs=[rows_of(D), rows_of(D), whole((D, D)), whole((8, D))],
        out_shape=[sd((R, D), F32), sd((R, D), BF), sd((D, D), BF), sd((8, D), F32)],
        scratch_shapes=[pltpu.VMEM((D, D), F32)],
        compiler_params=params(40),
        cost_estimate=cost(4 * R * D * D, 2e7),
    )(dh_two, r_one, dy, g2, w_out, att)

    dq, dk, dv, dw_q, dw_k, dw_v, sums_qv = pl.pallas_call(
        functools.partial(attention_back_kernel, lay, chunk, head_dim),
        name="attention_back",
        grid=(parts,),
        in_specs=[whole((R, D)), act, act, act, p_big, p_small, act],
        out_specs=[act, act, act] + [spec((D, gw), lambda i: (0, i))] * 3 + [spec((8, gw), lambda i: (0, i))],
        out_shape=[sd((R, D), BF)] * 3 + [sd((D, D), BF)] * 3 + [sd((8, D), F32)],
        scratch_shapes=[pltpu.VMEM((D, R), BF), pltpu.VMEM((lay.large_pad, lay.large_pad), F32),
                        pltpu.VMEM((lay.large_pad, lay.large_pad), BF)],
        compiler_params=params(56),
        cost_estimate=cost(2 * R * D * 3 * D + 8e9, 3e7),
    )(h_one, q_rows, k_rows, v_rows, prob_l, prob_s, d_att)

    grad_tokens, sums_one = pl.pallas_call(
        first_back_kernel,
        name="first_back",
        grid=(3,),
        in_specs=[rows_of(D), rows_of(D), rows_of(D), whole((D, 3 * D)), rows_of(D), rows_of(D),
                  whole((1, D)), whole((1, R))],
        out_specs=[whole((vis, D)), whole((8, D))],
        out_shape=[sd((vis, D), BF), sd((8, D), F32)],
        scratch_shapes=[pltpu.VMEM((R, D), BF)],
        compiler_params=params(48),
        cost_estimate=cost(2 * R * D * 3 * D + 2 * R * vis * D, 2e7),
    )(dq, dk, dv, w_qkv, x_rows, dr, g1, source_row)

    (grad_two,) = scatter_group(dev, [dw_two])
    grad_one, grad_dec = scatter_group(dev, [dw_one, dw_dec])
    grad_out, grad_q, grad_k, grad_v = scatter_group(dev, [dw_out, dw_q, dw_k, dw_v])
    grad_qkv = jnp.concatenate([grad_q, grad_k, grad_v], axis=1)

    small = [sums_one[0], sums_one[1], sums_qv[0], sums_qv[1], sums_two[2], sums_two[0], sums_two[1],
             db_one[0], db_two[0], owner_sums[1], owner_sums[0]]
    rows = jnp.concatenate([v.reshape(count, -1) for v in small], axis=1)
    rows = jnp.sum(lax.all_to_all(rows, "dp", 0, 0, tiled=True), axis=0)
    vec_grads, start = [], 0
    for v in vectors:
        vec_grads.append(rows[start : start + v.shape[0]])
        start += v.shape[0]
    (gg1, gb1, gbq, gbv, gbo, gg2, gb2, gbf1, gbf2, gbdec, gmask) = vec_grads
    return (decoded, grad_tokens, gg1, gb1, grad_qkv, gbq, gbv, grad_out, gbo, gg2, gb2, grad_one,
            gbf1, grad_two, gbf2, grad_dec, gbdec, gmask)


def solution(mesh):
    mat, vec = P("dp", None), P("dp")
    in_specs = (mat, vec, vec, mat, vec, vec, mat, vec, vec, vec, mat, vec, mat, vec, mat, vec, vec,
                mat, vec, vec, vec, mat)
    out_specs = (mat, mat, vec, vec, mat, vec, vec, mat, vec, vec, vec, mat, vec, mat, vec, mat, vec,
                 vec)
    return jax.shard_map(local, mesh=mesh, in_specs=in_specs, out_specs=out_specs, check_vma=False)
```

time: 987 us -> 579 us (0.59)
  waiting for transfers between devices: 423 us -> 189 us
  matrix products: 226 us -> 0 us
  Pallas kernels: 0 us -> 153 us
  blocking collectives: 142 us -> 0 us
  starting transfers between devices: 14.5 us -> 97.7 us
  other arithmetic: 83 us -> 59.3 us
  between operations: 15.3 us -> 2.95 us
    reduce_scatter x5 -> x0, waiting for transfers between devices: 384 us -> none  [the longest x1 142 us: local(): lax.psum_scatter(grad_fc2_weight, 'dp', scatter_dimension=0, tiled=True)]
    dot_general x23 -> x0, matrix products: 226 us -> none  [the longest x5 56.7 us: times_transposed(): lax.dot_general(left, right, (((1,), (1,)), ((), ())), preferred_element_...]
    pallas_call x0 -> x16, Pallas kernels: none -> 153 us  [the longest x1 34.8 us: local(): pl.pallas_call(functools.partial(attention_back_kernel, lay, chunk, head_...]
    all_to_all x3 -> x11, waiting for transfers between devices: 0.01 us -> 128 us  [the longest x3 73.9 us: scatter_group(): lax.all_to_all(chip, 'dp', 0, 0, axis_index_groups=dev.groups('yx'), tile...]
    unnamed x2 -> x0, blocking collectives: 94.8 us -> none
    ppermute x0 -> x30, waiting for transfers between devices: none -> 60.2 us  [shift(): return lax.ppermute(values, 'dp', pairs)]
    ppermute x0 -> x30, starting transfers between devices: none -> 50.4 us  [shift(): return lax.ppermute(values, 'dp', pairs)]
    all_gather x1 -> x0, blocking collectives: 47.4 us -> none  [local(): lax.all_gather(dec_weight, 'dp', axis=0, tiled=True)]
  transfers between devices with their start and end apart: 12 -> 41, of which waited for: 4 -> 17; matrix products, arithmetic and copies ran while one was open for 30% -> 15% of each run, Pallas kernels for 0% -> 7%
where the time goes in v1:
time: 579 us; the launch traced here: 571 us
  waiting for transfers between devices  189 us (33%)
  Pallas kernels  153 us (26%)
  starting transfers between devices  97.7 us (17%)
  local copies, waits for them, and re-layouts  70 us (12%)
  other arithmetic  59.3 us (10%)
    all_to_all x3, waiting for transfers between devices, scatter_group(): lax.all_to_all(chip, 'dp', 0, 0, axis_index_groups=dev.groups('yx'), tile...  73.9 us
    ppermute x30, waiting for transfers between devices, shift(): return lax.ppermute(values, 'dp', pairs)  60.2 us
    ppermute x30, starting transfers between devices, shift(): return lax.ppermute(values, 'dp', pairs)  50.4 us
    unnamed x130, local copies, waits for them, and re-layouts  42 us
    pallas_call x1, Pallas kernels, local(): pl.pallas_call(functools.partial(attention_back_kernel, lay, chunk, head_...  34.8 us
    all_to_all x3, waiting for transfers between devices, scatter_group(): lax.all_to_all(line, 'dp', 0, 0, axis_index_groups=dev.groups('z'), tiled...  31.2 us
    pallas_call x1, Pallas kernels, local(): pl.pallas_call(functools.partial(attention_kernel, lay, chunk, head_dim),...  25.9 us
    all_to_all x1, waiting for transfers between devices, local(): lax.all_to_all(e_send.reshape(count, per_peer * slots, dec_width), 'dp',...  19.7 us
  transfers between devices with their start and end apart: 41, of which 17 were waited for; matrix products, arithmetic and copies ran while one was open for 15% of the time, Pallas kernels for 7%

profile of v1, /device:TPU:0, one launch (start us, length us, event | category | flops | bytes accessed | tf_op | source)
XLA Modules:
  0.0 571.1 jit_solution(16710051663031176818)
XLA Ops:
  0.8 5.1 collective-permute-start.2
  22.3 4.0 all-to-all-start.2
  34.3 5.8 %all-to-all-start = ((bf16[32,2,160]{2,1,0:T(2,128)(2,1)}), bf16[32,2,160]{2,1,0:T(2,128)(2,1)S(1)}, u32[]{:S(2)}, u32[]{:S(2)}) async-start(bf16[32,2,160]{2,1,0:T(2,128)(2,1)} %reshape.840), calls=%async_computation | async-start | bytes 65536 | tf_op jit(solution)/shard_map/all_to_all | solution.py:545
  49.8 4.0 owner_side.1
  65.9 15.1 %collective-permute-done.20 = bf16[96,768]{1,0:T(8,128)(2,1)S(1)} collective-permute-done((bf16[96,768]{1,0:T(8,128)(2,1)S(1)}, bf16[96,768]{1,0:T(8,128)(2,1)S(1)}, u32[]{:S(2)}, u32[]{:S(2)}) %collective-permute-start.20) | collective-permute-done | bytes 147488 | tf_op jit(solution)/shard_map/ppermute | solution.py:36
  81.0 20.6 %collective-permute-start.9 = (bf16[24,4352]{1,0:T(8,128)(2,1)S(1)}, bf16[24,4352]{1,0:T(8,128)(2,1)S(1)}, u32[]{:S(2)}, u32[]{:S(2)}) collective-permute-start(bf16[24,4352]{1,0:T(8,128)(2,1)S(1)} %slice_dynamic-update-slice_fusion), channel_id=1, source_target_pairs={{0,8},{1,9},{2,10},{3,11},{4,12},{5,13},{6,14},{7,15},{8,16},{9,17... | collective-permute-start | bytes 626696 | tf_op jit(solution)/shard_map/ppermute | solution.py:36
  114.8 10.8 %collective-permute-done.12 = bf16[4,24,2176]{2,1,0:T(8,128)(2,1)S(1)} collective-permute-done((bf16[4,24,2176]{2,1,0:T(8,128)(2,1)S(1)}, bf16[4,24,2176]{2,1,0:T(8,128)(2,1)S(1)}, u32[]{:S(2)}, u32[]{:S(2)}) %collective-permute-start.12) | collective-permute-done | bytes 417824 | tf_op jit(solution)/shard_map/ppermute | solution.py:36
  133.3 4.7 collective-permute-done.4
  139.5 16.4 %collective-permute-done.13 = bf16[2,4,24,2176]{3,2,1,0:T(8,128)(2,1)S(1)} collective-permute-done((bf16[2,4,24,2176]{3,2,1,0:T(8,128)(2,1)S(1)}, bf16[2,4,24,2176]{3,2,1,0:T(8,128)(2,1)S(1)}, u32[]{:S(2)}, u32[]{:S(2)}) %collective-permute-start.13) | collective-permute-done | bytes 835616 | tf_op jit(solution)/shard_map/ppermute | solution.py:36
  158.4 8.5 %collective-permute-done.22 = bf16[2,4,96,384]{3,2,1,0:T(8,128)(2,1)S(1)} collective-permute-done((bf16[2,4,96,384]{3,2,1,0:T(8,128)(2,1)S(1)}, bf16[2,4,96,384]{3,2,1,0:T(8,128)(2,1)S(1)}, u32[]{:S(2)}, u32[]{:S(2)}) %collective-permute-start.22) | collective-permute-done | bytes 589856 | tf_op jit(solution)/shard_map/ppermute | solution.py:36
  190.9 25.9 %attention.1 = (bf16[960,768]{1,0:T(8,128)(2,1)S(1)}, bf16[960,768]{1,0:T(8,128)(2,1)S(1)}, bf16[960,768]{1,0:T(8,128)(2,1)S(1)}, bf16[12,400,400]{2,1,0:T(8,128...) custom-call(bf16[960,768]{1,0:T(8,128)(2,1)} %copy-done.21, bf16[768,2304]{1,0:T(8,128)(2,1)} %bitcast.128, ...), custom_call_target="tpu_custom_call" | custom-call | flops 7397386240 | bytes 20000000 | tf_op jit(solution)/shard_map/attention/pallas_call | solution.py:650
  233.7 10.7 %fc1.1 = (bf16[960,3072]{1,0:T(8,128)(2,1)S(1)}, bf16[960,3072]{1,0:T(8,128)(2,1)S(1)}) custom-call(bf16[960,768]{1,0:T(8,128)(2,1)S(1)} %get-tuple-element.63.h_in, bf16[768,3072]{1,0:T(8,128)(2,1)S(1)} %bitcast.139, f32[1,3072]{1,0:T(1,128)S(1)} %reshape.771.bias), custom_call_target="tpu_custom_call" | custom-call | flops 4529848320 | bytes 20000000 | tf_op jit(solution)/shard_map/fc1/pallas_call | solution.py:675
  249.4 11.4 %fc2_and_embed.1 = (bf16[960,768]{1,0:T(8,128)(2,1)S(1)}, bf16[896,512]{1,0:T(8,128)(2,1)S(1)}) custom-call(bf16[960,3072]{1,0:T(8,128)(2,1)} %copy-done.22, bf16[3072,768]{1,0:T(8,128)(2,1)} %bitcast.126, f32[1,768]{1,0:T(1,128)S(1)} %reshape.773.b_two, f32[960,768]{1,0:T(8,128)S(1)} %get-tuple-element.66.r_in, bf16[768,512]{1,0:T(8,128)(2,1)S(1)} %bitcast.141, ...), custom_call_target="tpu_custom_call" | custom-call | flops 6039797760 | bytes 20000000 | tf_op jit(solution)/shard_map/fc2_and_embed/pallas_call | solution.py:687
  263.8 13.1 %fc2_back.1 = (bf16[960,3072]{1,0:T(8,128)(2,1)}, bf16[3072,768]{1,0:T(8,128)(2,1)S(1)}, f32[1,3072]{1,0:T(1,128)S(1)}) custom-call(bf16[960,768]{1,0:T(8,128)(2,1)S(1)} %get-tuple-element.77.dy_in, bf16[3072,768]{1,0:T(8,128)(2,1)} %bitcast.127, bf16[960,3072]{1,0:T(8,128)(2,1)} %copy-done.22, bf16[960,3072]{1,0:T(8,128)(2,1)} %copy-done.26), custom_call_target="tpu_custom_call" | custom-call | flops 9059696640 | bytes 30000000 | tf_op jit(solution)/shard_map/fc2_back/pallas_call | solution.py:725
  279.1 13.7 %fc1_back.1 = (f32[960,768]{1,0:T(8,128)S(1)}, bf16[768,3072]{1,0:T(8,128)(2,1)}) custom-call(bf16[960,3072]{1,0:T(8,128)(2,1)} %get-tuple-element.79.du_in, bf16[768,3072]{1,0:T(8,128)(2,1)} %bitcast.140, bf16[960,768]{1,0:T(8,128)(2,1)S(1)} %copy-done.20), custom_call_target="tpu_custom_call" | custom-call | flops 9059696640 | bytes 20000000 | tf_op jit(solution)/shard_map/fc1_back/pallas_call | solution.py:738
  292.9 8.4 %out_back.1 = (f32[960,768]{1,0:T(8,128)S(1)}, bf16[960,768]{1,0:T(8,128)(2,1)S(1)}, bf16[768,768]{1,0:T(8,128)(2,1)S(1)}, f32[8,768]{1,0:T(8,128)S(1)}) custom-call(f32[960,768]{1,0:T(8,128)S(1)} %get-tuple-element.80.dh_in, f32[960,768]{1,0:T(8,128)} %copy-done.5, bf16[960,768]{1,0:T(8,128)(2,1)S(1)} %get-tuple-element.77.dy_in, ...), custom_call_target="tpu_custom_call" | custom-call | flops 2264924160 | bytes 20000000 | tf_op jit(solution)/shard_map/out_back/pallas_call | solution.py:750
  303.9 34.8 %attention_back.1 = (bf16[960,768]{1,0:T(8,128)(2,1)}, bf16[960,768]{1,0:T(8,128)(2,1)}, bf16[960,768]{1,0:T(8,128)(2,1)}, bf16[768,768]{1,0:T(8,128)(2,1)}, bf1...) custom-call(bf16[960,768]{1,0:T(8,128)(2,1)} %copy-done.21, bf16[960,768]{1,0:T(8,128)(2,1)} %copy-done.27, ...), custom_call_target="tpu_custom_call" | custom-call | flops 11397386240 | bytes 30000000 | tf_op jit(solution)/shard_map/attention_back/pallas_call | solution.py:762
  342.9 10.7 %first_back.1 = (bf16[882,768]{1,0:T(8,128)(2,1)}, f32[8,768]{1,0:T(8,128)S(1)}) custom-call(bf16[960,768]{1,0:T(8,128)(2,1)S(1)} %copy-done.23, bf16[960,768]{1,0:T(8,128)(2,1)S(1)} %copy-done.24, bf16[960,768]{1,0:T(8,128)(2,1)S(1)} %copy-done.25, bf16[768,2304]{1,0:T(8,128)(2,1)} %bitcast.131, bf16[960,768]{1,0:T(8,128)(2,1)S(1)} %copy-done.18, ...), custom_call_target="tpu_custom_call" | custom-call | flops 4697948160 | bytes 20000000 | tf_op jit(solution)/shard_map/first_back/pallas_call | solution.py:775
  377.7 6.1 %all-to-all-start.1 = ((bf16[32,28,512]{2,1,0:T(8,128)(2,1)}), bf16[32,28,512]{2,1,0:T(8,128)(2,1)}, u32[]{:S(2)}, u32[]{:S(2)}) async-start(bf16[32,28,512]{2,1,0:T(8,128)(2,1)} %reshape.776), calls=%async_computation.1 | async-start | bytes 2097152 | tf_op jit(solution)/shard_map/all_to_all | solution.py:700
  390.2 19.7 %all-to-all-done.1 = bf16[32,28,512]{2,1,0:T(8,128)(2,1)} async-done(((bf16[32,28,512]{2,1,0:T(8,128)(2,1)}), bf16[32,28,512]{2,1,0:T(8,128)(2,1)}, u32[]{:S(2)}, u32[]{:S(2)}) %all-to-all-start.1) | async-done | bytes 917536 | tf_op jit(solution)/shard_map/all_to_all | solution.py:700
  409.9 4.7 all-to-all-start.5
  414.6 4.9 fusion
  419.5 22.8 %all-to-all-done.5 = bf16[4,96,3072]{2,1,0:T(8,128)(2,1)} async-done(((bf16[4,96,3072]{2,1,0:T(8,128)(2,1)}), bf16[4,96,3072]{2,1,0:T(8,128)(2,1)}, u32[]{:S(2)}, u32[]{:S(2)}) %all-to-all-start.5) | async-done | bytes 2359328 | tf_op jit(solution)/shard_map/all_to_all | solution.py:144
  442.3 4.8 all-to-all-start.9
  447.2 4.1 add_convert_fusion
  451.3 22.9 %all-to-all-done.9 = bf16[4,384,768]{2,1,0:T(8,128)(2,1)} async-done(((bf16[4,384,768]{2,1,0:T(8,128)(2,1)}), bf16[4,384,768]{2,1,0:T(8,128)(2,1)}, u32[]{:S(2)}, u32[]{:S(2)}) %all-to-all-start.9) | async-done | bytes 2359328 | tf_op jit(solution)/shard_map/all_to_all | solution.py:144
  480.9 28.3 %all-to-all-done.7 = bf16[4,96,3584]{2,1,0:T(8,128)(2,1)S(1)} async-done(((bf16[4,96,3584]{2,1,0:T(8,128)(2,1)}), bf16[4,96,3584]{2,1,0:T(8,128)(2,1)S(1)}, u32[]{:S(2)}, u32[]{:S(2)}) %all-to-all-start.7) | async-done | bytes 2752544 | tf_op jit(solution)/shard_map/all_to_all | solution.py:144
  509.1 4.4 all-to-all-start.6
  516.6 12.1 %all-to-all-done.6 = bf16[4,24,3072]{2,1,0:T(8,128)(2,1)S(1)} async-done(((bf16[4,24,3072]{2,1,0:T(8,128)(2,1)}), bf16[4,24,3072]{2,1,0:T(8,128)(2,1)S(1)}, u32[]{:S(2)}, u32[]{:S(2)}) %all-to-all-start.6) | async-done | bytes 589856 | tf_op jit(solution)/shard_map/all_to_all | solution.py:146
  528.6 4.2 all-to-all-start.10
  534.3 14.0 %all-to-all-done.10 = bf16[4,96,768]{2,1,0:T(8,128)(2,1)} async-done(((bf16[4,96,768]{2,1,0:T(8,128)(2,1)}), bf16[4,96,768]{2,1,0:T(8,128)(2,1)}, u32[]{:S(2)}, u32[]{:S(2)}) %all-to-all-start.10) | async-done | bytes 589856 | tf_op jit(solution)/shard_map/all_to_all | solution.py:146
  564.0 5.2 all-to-all-done.8
  (341 shorter events, 186.3 us)
Async XLA Ops:
  0.8 59.4 %collective-permute-start.2 = (bf16[24,2304]{1,0:T(8,128)(2,1)}, bf16[24,2304]{1,0:T(8,128)(2,1)S(1)}, u32[]{:S(2)}, u32[]{:S(2)}) collective-permute-start(bf16[24,2304]{1,0:T(8,128)(2,1)} %param.25), channel_id=1, source_target_pairs={{0,24},{1,25},{2,26},{3,27},{4,28},{5,29},{6,30},{7,31},{8,0},{9,1... | collective-permute-start | bytes 331784 | tf_op jit(solution)/shard_map/ppermute | solution.py:36
  5.9 57.9 %collective-permute-start.1 = (bf16[24,2304]{1,0:T(8,128)(2,1)}, bf16[24,2304]{1,0:T(8,128)(2,1)}, u32[]{:S(2)}, u32[]{:S(2)}) collective-permute-start(bf16[24,2304]{1,0:T(8,128)(2,1)} %param.25), channel_id=1, source_target_pairs={{0,16},{1,17},{2,18},{3,19},{4,20},{5,21},{6,22},{7,23},{8,24},{9,... | collective-permute-start | bytes 331784 | tf_op jit(solution)/shard_map/ppermute | solution.py:36
  5.9 57.9 %collective-permute-start = (bf16[24,2304]{1,0:T(8,128)(2,1)}, bf16[24,2304]{1,0:T(8,128)(2,1)}, u32[]{:S(2)}, u32[]{:S(2)}) collective-permute-start(bf16[24,2304]{1,0:T(8,128)(2,1)} %param.25), channel_id=1, source_target_pairs={{0,8},{1,9},{2,10},{3,11},{4,12},{5,13},{6,14},{7,15},{8,16},{9,17... | collective-permute-start | bytes 331784 | tf_op jit(solution)/shard_map/ppermute | solution.py:36
  11.5 95.0 %collective-permute-start.11 = (bf16[24,4352]{1,0:T(8,128)(2,1)S(1)}, bf16[24,4352]{1,0:T(8,128)(2,1)}, u32[]{:S(2)}, u32[]{:S(2)}) collective-permute-start(bf16[24,4352]{1,0:T(8,128)(2,1)S(1)} %slice_dynamic-update-slice_fusion), channel_id=1, source_target_pairs={{0,24},{1,25},{2,26},{3,27},{4,28},{5,29},{6,30},{7,31},{8,0},{9,1... | collective-permute-start | bytes 626696 | tf_op jit(solution)/shard_map/ppermute | solution.py:36
  14.4 92.8 %collective-permute-start.10 = (bf16[24,4352]{1,0:T(8,128)(2,1)S(1)}, bf16[24,4352]{1,0:T(8,128)(2,1)}, u32[]{:S(2)}, u32[]{:S(2)}) collective-permute-start(bf16[24,4352]{1,0:T(8,128)(2,1)S(1)} %slice_dynamic-update-slice_fusion), channel_id=1, source_target_pairs={{0,16},{1,17},{2,18},{3,19},{4,20},{5,21},{6,22},{7,23},{8,24},{9,... | collective-permute-start | bytes 626696 | tf_op jit(solution)/shard_map/ppermute | solution.py:36
  56.7 164.6 %all-to-all-start.3 = ((bf16[32,28,512]{2,1,0:T(8,128)(2,1)}), bf16[32,28,512]{2,1,0:T(8,128)(2,1)}, u32[]{:S(2)}, u32[]{:S(2)}) async-start(bf16[32,28,512]{2,1,0:T(8,128)(2,1)} %reshape.785), calls=%async_computation.3 | async-start | bytes 2097152 | tf_op jit(solution)/shard_map/all_to_all | solution.py:622
  60.2 20.9 %collective-permute-start.20 = (bf16[96,768]{1,0:T(8,128)(2,1)S(1)}, bf16[96,768]{1,0:T(8,128)(2,1)S(1)}, u32[]{:S(2)}, u32[]{:S(2)}) collective-permute-start(bf16[96,768]{1,0:T(8,128)(2,1)S(1)} %copy-done.44), channel_id=1, source_target_pairs={{0,24},{1,25},{2,26},{3,27},{4,28},{5,29},{6,30},{7,31},{8,0},{9,1... | collective-permute-start | bytes 442376 | tf_op jit(solution)/shard_map/ppermute | solution.py:36
  63.8 39.6 %collective-permute-start.19 = (bf16[96,768]{1,0:T(8,128)(2,1)S(1)}, bf16[96,768]{1,0:T(8,128)(2,1)S(1)}, u32[]{:S(2)}, u32[]{:S(2)}) collective-permute-start(bf16[96,768]{1,0:T(8,128)(2,1)S(1)} %copy-done.44), channel_id=1, source_target_pairs={{0,16},{1,17},{2,18},{3,19},{4,20},{5,21},{6,22},{7,23},{8,24},{9,... | collective-permute-start | bytes 442376 | tf_op jit(solution)/shard_map/ppermute | solution.py:36
  63.8 41.1 %collective-permute-start.18 = (bf16[96,768]{1,0:T(8,128)(2,1)S(1)}, bf16[96,768]{1,0:T(8,128)(2,1)S(1)}, u32[]{:S(2)}, u32[]{:S(2)}) collective-permute-start(bf16[96,768]{1,0:T(8,128)(2,1)S(1)} %copy-done.44), channel_id=1, source_target_pairs={{0,8},{1,9},{2,10},{3,11},{4,12},{5,13},{6,14},{7,15},{8,16},{9,17... | collective-permute-start | bytes 442376 | tf_op jit(solution)/shard_map/ppermute | solution.py:36
  81.0 26.6 %collective-permute-start.9 = (bf16[24,4352]{1,0:T(8,128)(2,1)S(1)}, bf16[24,4352]{1,0:T(8,128)(2,1)S(1)}, u32[]{:S(2)}, u32[]{:S(2)}) collective-permute-start(bf16[24,4352]{1,0:T(8,128)(2,1)S(1)} %slice_dynamic-update-slice_fusion), channel_id=1, source_target_pairs={{0,8},{1,9},{2,10},{3,11},{4,12},{5,13},{6,14},{7,15},{8,16},{9,17... | collective-permute-start | bytes 626696 | tf_op jit(solution)/shard_map/ppermute | solution.py:36
  106.5 23.6 %collective-permute-start.21 = (bf16[4,96,384]{2,1,0:T(8,128)(2,1)S(1)}, bf16[4,96,384]{2,1,0:T(8,128)(2,1)S(1)}, u32[]{:S(2)}, u32[]{:S(2)}) collective-permute-start(bf16[4,96,384]{2,1,0:T(8,128)(2,1)S(1)} %get-tuple-element.156), channel_id=1, source_target_pairs={{0,2},{1,3},{2,0},{3,1},{4,6},{5,7},{6,4},{7,5},{8,10},{9,11},{10,... | collective-permute-start | bytes 884744 | tf_op jit(solution)/shard_map/ppermute | solution.py:36
  107.1 24.5 %collective-permute-start.23 = (bf16[4,96,384]{2,1,0:T(8,128)(2,1)S(1)}, bf16[4,96,384]{2,1,0:T(8,128)(2,1)S(1)}, u32[]{:S(2)}, u32[]{:S(2)}) collective-permute-start(bf16[4,96,384]{2,1,0:T(8,128)(2,1)S(1)} %get-tuple-element.155), channel_id=1, source_target_pairs={{0,4},{1,5},{2,6},{3,7},{4,0},{5,1},{6,2},{7,3},{8,12},{9,13},{10,... | collective-permute-start | bytes 884744 | tf_op jit(solution)/shard_map/ppermute | solution.py:36
  113.3 24.7 %collective-permute-start.4 = (bf16[2,4,24,1152]{3,2,1,0:T(8,128)(2,1)S(1)}, bf16[2,4,24,1152]{3,2,1,0:T(8,128)(2,1)S(1)}, u32[]{:S(2)}, u32[]{:S(2)}) collective-permute-start(bf16[2,4,24,1152]{3,2,1,0:T(8,128)(2,1)S(1)} %get-tuple-element.166), channel_id=1, source_target_pairs={{0,4},{1,5},{2,6},{3,7},{4,0},{5,1},{6,2},{7,3},{8,12},{9,13},{10,... | collective-permute-start | bytes 1327112 | tf_op jit(solution)/shard_map/ppermute | solution.py:36
  125.6 31.2 %collective-permute-start.6 = (bf16[2,4,24,1152]{3,2,1,0:T(8,128)(2,1)S(1)}, bf16[2,4,24,1152]{3,2,1,0:T(8,128)(2,1)S(1)}, u32[]{:S(2)}, u32[]{:S(2)}) collective-permute-start(bf16[2,4,24,1152]{3,2,1,0:T(8,128)(2,1)S(1)} %get-tuple-element.160), channel_id=1, source_target_pairs={{0,2},{1,3},{2,0},{3,1},{4,6},{5,7},{6,4},{7,5},{8,10},{9,11},{10,... | collective-permute-start | bytes 1327112 | tf_op jit(solution)/shard_map/ppermute | solution.py:36
  128.5 27.4 %collective-permute-start.13 = (bf16[2,4,24,2176]{3,2,1,0:T(8,128)(2,1)S(1)}, bf16[2,4,24,2176]{3,2,1,0:T(8,128)(2,1)S(1)}, u32[]{:S(2)}, u32[]{:S(2)}) collective-permute-start(bf16[2,4,24,2176]{3,2,1,0:T(8,128)(2,1)S(1)} %get-tuple-element.146), channel_id=1, source_target_pairs={{0,4},{1,5},{2,6},{3,7},{4,0},{5,1},{6,2},{7,3},{8,12},{9,13},{10,... | collective-permute-start | bytes 2506760 | tf_op jit(solution)/shard_map/ppermute | solution.py:36
  130.1 26.5 %collective-permute-start.15 = (bf16[2,4,24,2176]{3,2,1,0:T(8,128)(2,1)S(1)}, bf16[2,4,24,2176]{3,2,1,0:T(8,128)(2,1)S(1)}, u32[]{:S(2)}, u32[]{:S(2)}) collective-permute-start(bf16[2,4,24,2176]{3,2,1,0:T(8,128)(2,1)S(1)} %get-tuple-element.140), channel_id=1, source_target_pairs={{0,2},{1,3},{2,0},{3,1},{4,6},{5,7},{6,4},{7,5},{8,10},{9,11},{10,... | collective-permute-start | bytes 2506760 | tf_op jit(solution)/shard_map/ppermute | solution.py:36
  131.6 35.2 %collective-permute-start.22 = (bf16[2,4,96,384]{3,2,1,0:T(8,128)(2,1)S(1)}, bf16[2,4,96,384]{3,2,1,0:T(8,128)(2,1)S(1)}, u32[]{:S(2)}, u32[]{:S(2)}) collective-permute-start(bf16[2,4,96,384]{3,2,1,0:T(8,128)(2,1)S(1)} %get-tuple-element.158), channel_id=1, source_target_pairs={{0,4},{1,5},{2,6},{3,7},{4,0},{5,1},{6,2},{7,3},{8,12},{9,13},{10,... | collective-permute-start | bytes 1769480 | tf_op jit(solution)/shard_map/ppermute | solution.py:36
  138.0 33.0 %collective-permute-start.24 = (bf16[2,4,96,384]{3,2,1,0:T(8,128)(2,1)}, bf16[2,4,96,384]{3,2,1,0:T(8,128)(2,1)}, u32[]{:S(2)}, u32[]{:S(2)}) collective-permute-start(bf16[2,4,96,384]{3,2,1,0:T(8,128)(2,1)} %get-tuple-element.152), channel_id=1, source_target_pairs={{0,2},{1,3},{2,0},{3,1},{4,6},{5,7},{6,4},{7,5},{8,10},{9,11},{10,... | collective-permute-start | bytes 1769480 | tf_op jit(solution)/shard_map/ppermute | solution.py:36
  156.6 71.8 %collective-permute-start.16 = (bf16[2,2,4,24,2176]{4,3,2,1,0:T(8,128)(2,1)S(1)}, bf16[2,2,4,24,2176]{4,3,2,1,0:T(8,128)(2,1)}, u32[]{:S(2)}, u32[]{:S(2)}) collective-permute-start(bf16[2,2,4,24,2176]{4,3,2,1,0:T(8,128)(2,1)S(1)} %pad_maximum_fusion.2.part_a), channel_id=1, source_target_pairs={{0,1},{1,0},{2,3},{3,2},{4,5},{5,4},{6,7},{7,6},{8,9},{9,8},{10,11... | collective-permute-start | bytes 5013512 | tf_op jit(solution)/shard_map/ppermute | solution.py:36
  156.8 71.5 %collective-permute-start.17 = (bf16[2,2,4,24,2176]{4,3,2,1,0:T(8,128)(2,1)S(1)}, bf16[2,2,4,24,2176]{4,3,2,1,0:T(8,128)(2,1)}, u32[]{:S(2)}, u32[]{:S(2)}) collective-permute-start(bf16[2,2,4,24,2176]{4,3,2,1,0:T(8,128)(2,1)S(1)} %pad_maximum_fusion.3.part_b), channel_id=1, source_target_pairs={{0,1},{1,0},{2,3},{3,2},{4,5},{5,4},{6,7},{7,6},{8,9},{9,8},{10,11... | collective-permute-start | bytes 5013512 | tf_op jit(solution)/shard_map/ppermute | solution.py:36
  170.9 52.5 %collective-permute-start.25 = (bf16[2,2,4,96,384]{4,3,2,1,0:T(8,128)(2,1)}, bf16[2,2,4,96,384]{4,3,2,1,0:T(8,128)(2,1)}, u32[]{:S(2)}, u32[]{:S(2)}) collective-permute-start(bf16[2,2,4,96,384]{4,3,2,1,0:T(8,128)(2,1)} %pad_maximum_fusion.4.part_a), channel_id=1, source_target_pairs={{0,1},{1,0},{2,3},{3,2},{4,5},{5,4},{6,7},{7,6},{8,9},{9,8},{10,11... | collective-permute-start | bytes 3538952 | tf_op jit(solution)/shard_map/ppermute | solution.py:36
  173.7 49.8 %collective-permute-start.26 = (bf16[2,2,4,96,384]{4,3,2,1,0:T(8,128)(2,1)}, bf16[2,2,4,96,384]{4,3,2,1,0:T(8,128)(2,1)}, u32[]{:S(2)}, u32[]{:S(2)}) collective-permute-start(bf16[2,2,4,96,384]{4,3,2,1,0:T(8,128)(2,1)} %pad_maximum_fusion.5.part_b), channel_id=1, source_target_pairs={{0,1},{1,0},{2,3},{3,2},{4,5},{5,4},{6,7},{7,6},{8,9},{9,8},{10,11... | collective-permute-start | bytes 3538952 | tf_op jit(solution)/shard_map/ppermute | solution.py:36
  357.2 20.4 %all-to-all-start.4 = ((f32[32,1,320]{2,1,0:T(1,128)}), f32[32,1,320]{2,1,0:T(1,128)S(1)}, u32[]{:S(2)}, u32[]{:S(2)}) async-start(f32[32,1,320]{2,1,0:T(1,128)} %all_to_all.41), calls=%async_computation.4 | async-start | bytes 98304 | tf_op jit(solution)/shard_map/all_to_all | solution.py:796
  373.7 40.9 %collective-permute-start.29 = (bf16[4,4,96,768]{3,2,0,1:T(8,128)(2,1)}, bf16[4,4,96,768]{3,2,0,1:T(8,128)(2,1)}, u32[]{:S(2)}, u32[]{:S(2)}) collective-permute-start(bf16[4,4,96,768]{3,2,0,1:T(8,128)(2,1)} %select_bitcast_fusion), channel_id=1, source_target_pairs={{0,1},{1,0},{2,3},{3,2},{4,5},{5,4},{6,7},{7,6},{8,9},{9,8},{10,11... | collective-permute-start | bytes 7077896 | tf_op jit(solution)/shard_map/ppermute | solution.py:36
  377.7 32.3 %all-to-all-start.1 = ((bf16[32,28,512]{2,1,0:T(8,128)(2,1)}), bf16[32,28,512]{2,1,0:T(8,128)(2,1)}, u32[]{:S(2)}, u32[]{:S(2)}) async-start(bf16[32,28,512]{2,1,0:T(8,128)(2,1)} %reshape.776), calls=%async_computation.1 | async-start | bytes 2097152 | tf_op jit(solution)/shard_map/all_to_all | solution.py:700
  386.4 60.8 %collective-permute-start.28 = (bf16[4,4,24,3584]{3,2,0,1:T(8,128)(2,1)}, bf16[4,4,24,3584]{3,2,0,1:T(8,128)(2,1)}, u32[]{:S(2)}, u32[]{:S(2)}) collective-permute-start(bf16[4,4,24,3584]{3,2,0,1:T(8,128)(2,1)} %pad_maximum_fusion), channel_id=1, source_target_pairs={{0,1},{1,0},{2,3},{3,2},{4,5},{5,4},{6,7},{7,6},{8,9},{9,8},{10,11... | collective-permute-start | bytes 8257544 | tf_op jit(solution)/shard_map/ppermute | solution.py:36
  409.9 32.4 %all-to-all-start.5 = ((bf16[4,96,3072]{2,1,0:T(8,128)(2,1)}), bf16[4,96,3072]{2,1,0:T(8,128)(2,1)}, u32[]{:S(2)}, u32[]{:S(2)}) async-start(bf16[4,96,3072]{2,1,0:T(8,128)(2,1)} %bitcast.144), calls=%async_computation.5 | async-start | bytes 4718592 | tf_op jit(solution)/shard_map/all_to_all | solution.py:144
  442.3 31.8 %all-to-all-start.9 = ((bf16[4,384,768]{2,1,0:T(8,128)(2,1)}), bf16[4,384,768]{2,1,0:T(8,128)(2,1)}, u32[]{:S(2)}, u32[]{:S(2)}) async-start(bf16[4,384,768]{2,1,0:T(8,128)(2,1)} %bitcast.145), calls=%async_computation.9 | async-start | bytes 4718592 | tf_op jit(solution)/shard_map/all_to_all | solution.py:144
  474.1 35.0 %all-to-all-start.7 = ((bf16[4,96,3584]{2,1,0:T(8,128)(2,1)}), bf16[4,96,3584]{2,1,0:T(8,128)(2,1)S(1)}, u32[]{:S(2)}, u32[]{:S(2)}) async-start(bf16[4,96,3584]{2,1,0:T(8,128)(2,1)} %bitcast.143), calls=%async_computation.7 | async-start | bytes 5505024 | tf_op jit(solution)/shard_map/all_to_all | solution.py:144
  509.1 19.5 %all-to-all-start.6 = ((bf16[4,24,3072]{2,1,0:T(8,128)(2,1)}), bf16[4,24,3072]{2,1,0:T(8,128)(2,1)S(1)}, u32[]{:S(2)}, u32[]{:S(2)}) async-start(bf16[4,24,3072]{2,1,0:T(8,128)(2,1)} %bitcast.152), calls=%async_computation.6 | async-start | bytes 1179648 | tf_op jit(solution)/shard_map/all_to_all | solution.py:146
  528.6 19.6 %all-to-all-start.10 = ((bf16[4,96,768]{2,1,0:T(8,128)(2,1)}), bf16[4,96,768]{2,1,0:T(8,128)(2,1)}, u32[]{:S(2)}, u32[]{:S(2)}) async-start(bf16[4,96,768]{2,1,0:T(8,128)(2,1)} %bitcast.151), calls=%async_computation.10 | async-start | bytes 1179648 | tf_op jit(solution)/shard_map/all_to_all | solution.py:146
  548.2 20.9 %all-to-all-start.8 = ((bf16[4,24,3584]{2,1,0:T(8,128)(2,1)}), bf16[4,24,3584]{2,1,0:T(8,128)(2,1)S(1)}, u32[]{:S(2)}, u32[]{:S(2)}) async-start(bf16[4,24,3584]{2,1,0:T(8,128)(2,1)} %bitcast.77), calls=%async_computation.8 | async-start | bytes 1376256 | tf_op jit(solution)/shard_map/all_to_all | solution.py:146
  (70 other events, 695.9 us)

commit v2 on v1

v2 whole, which is shorter than its diff:
```python
import functools

import jax
import jax.numpy as jnp
from jax import lax
from jax.experimental import pallas as pl
from jax.experimental.pallas import tpu as pltpu
from jax.sharding import PartitionSpec as P

HEADS = 12
GRID = 14
NORM_EPS = 1e-06
MASK_FILL = -1e30
BF = jnp.bfloat16
F32 = jnp.float32
MIB = 1 << 20


class Slice:
    def __init__(self, count):
        chips = count // 2
        side = 2 if chips <= 16 else 4
        self.count = count
        self.size = {"c": 2, "x": side, "y": side, "z": chips // (side * side)}
        self.stride = {"c": 1, "x": 2, "y": 2 * side, "z": 2 * side * side}

    def coord(self, axis):
        return (lax.axis_index("dp") // self.stride[axis]) % self.size[axis]

    def shift(self, values, axis, steps):
        stride, size = self.stride[axis], self.size[axis]
        pairs = []
        for source in range(self.count):
            place = (source // stride) % size
            pairs.append((source, source + ((place + steps) % size - place) * stride))
        return lax.ppermute(values, "dp", pairs)

    def copies(self, values, axis):
        return [values] + [self.shift(values, axis, k) for k in range(1, self.size[axis])]

    def shift_plane(self, values, ky, kx):
        pairs = []
        for source in range(self.count):
            target = source
            for axis, steps in (("y", ky), ("x", kx)):
                stride, size = self.stride[axis], self.size[axis]
                place = (source // stride) % size
                target += ((place + steps) % size - place) * stride
            pairs.append((source, target))
        return lax.ppermute(values, "dp", pairs)

    def groups(self, axes):
        seen, found = set(), []
        for first in range(self.count):
            if first in seen:
                continue
            members = [first]
            for axis in axes:
                members = [
                    m + k * self.stride[axis] for m in members for k in range(self.size[axis])
                ]
            found.append(members)
            seen.update(members)
        return found


def cost(flops, moved, trans=0, weight=1):
    return pl.CostEstimate(
        flops=int(weight * flops), bytes_accessed=int(weight * moved), transcendentals=int(trans)
    )


def params():
    return pltpu.CompilerParams(vmem_limit_bytes=60 * MIB)


def whole(shape):
    zeros = (0,) * len(shape)
    return pl.BlockSpec(shape, lambda *_: zeros)


SMEM = pl.BlockSpec(memory_space=pltpu.SMEM)
VMEM = pl.BlockSpec(memory_space=pltpu.VMEM)


def assemble_kernel(sizes, widths, place, part_a, part_b, from_a, from_b, *outs):
    nz, ny, nx = sizes
    own_z, own_y, own_x, own_c = place[0], place[1], place[2], place[3]
    for kz in range(nz):
        at_z = lax.rem(own_z - kz + nz, nz)
        for ky in range(ny):
            at_y = lax.rem(own_y - ky + ny, ny)
            for kx in range(nx):
                at_x = lax.rem(own_x - kx + nx, nx)
                chip = (at_z * ny + at_y) * nx + at_x
                for core, left, right in ((own_c, part_a, part_b), (1 - own_c, from_a, from_b)):
                    row, start = chip * 2 + core, 0
                    for out, width in zip(outs, widths):
                        half = width // 2
                        out[row, :, :half] = left[ky, kx, kz, :, start : start + half]
                        out[row, :, half:] = right[kx, ky, kz, :, start : start + half]
                        start += half


def held(values, *others):
    others = [o for o in others if o is not None]
    return lax.optimization_barrier((values, others))[0] if others else values


class Gather:
    def __init__(self, dev, shards):
        self.dev = dev
        self.rows = shards[0].shape[0]
        self.widths = [s.shape[1] for s in shards]
        self.half = sum(self.widths) // 2
        if len(shards) == 1:
            self.local = shards[0]
        else:
            halves = [s.shape[1] // 2 for s in shards]
            self.local = jnp.concatenate(
                [s[:, :h] for s, h in zip(shards, halves)]
                + [s[:, h:] for s, h in zip(shards, halves)],
                axis=1,
            )

    def along_z(self, *after):
        self.arrived = self.dev.copies(held(self.local, *after), "z")
        return self.arrived

    def first(self, *after):
        line = jnp.stack(held(self.arrived, *after))
        part_a, part_b = line[:, :, : self.half], line[:, :, self.half :]
        self.sent = [part_a, part_b]
        self.arrived = self.dev.copies(part_a, "x"), self.dev.copies(part_b, "y")
        return self.arrived[0] + self.arrived[1]

    def second(self, *after):
        part_a, part_b = (jnp.stack(v) for v in held(self.arrived, *after))
        self.sent = [part_a, part_b]
        self.arrived = self.dev.copies(part_a, "y"), self.dev.copies(part_b, "x")
        return self.arrived[0] + self.arrived[1]

    def swap(self, *after):
        self.part_a, self.part_b = (jnp.stack(v) for v in held(self.arrived, *after))
        self.sent = [self.part_a, self.part_b]
        self.from_a = self.dev.shift(self.part_a, "c", 1)
        self.from_b = self.dev.shift(self.part_b, "c", 1)
        return [self.from_a, self.from_b]

    def result(self, place):
        dev, rows = self.dev, self.rows
        sizes = (dev.size["z"], dev.size["y"], dev.size["x"])
        kind = self.local.dtype
        outs = pl.pallas_call(
            functools.partial(assemble_kernel, sizes, self.widths),
            name="assemble",
            out_shape=[jax.ShapeDtypeStruct((dev.count, rows, w), kind) for w in self.widths],
            in_specs=[SMEM] + [VMEM] * 4,
            out_specs=[VMEM] * len(self.widths),
            compiler_params=params(),
            cost_estimate=cost(0, 4 * dev.count * rows * sum(self.widths)),
        )(place, self.part_a, self.part_b, self.from_a, self.from_b)
        return [o.reshape(dev.count * rows, w) for o, w in zip(outs, self.widths)]


def chip_sum_kernel(sizes, pairs, place, *refs):
    nz, ny, nx = sizes
    owns, gots, outs = refs[:pairs], refs[pairs : 2 * pairs], refs[2 * pairs :]
    own_y, own_x = place[1], place[2]
    for ky in range(ny):
        for kx in range(nx):
            at = lax.rem(own_y + ky, ny) * nx + lax.rem(own_x + kx, nx)
            for z in range(nz):
                start = 0
                for own, got in zip(owns, gots):
                    width = own.shape[-1]
                    chip = z * ny * nx + at
                    total = own[chip].astype(F32) + got[chip].astype(F32)
                    outs[ky * nx + kx][z, :, start : start + width] = total.astype(BF)
                    start += width


class Scatter:
    def __init__(self, dev, pairs, place):
        self.dev, self.place = dev, place
        self.own = [p[0] for p in pairs]
        self.sent = [p[1] for p in pairs]
        self.rows = self.own[0].shape[1]
        self.widths = [p[0].shape[2] for p in pairs]
        self.got = []

    def swap(self, *after):
        waiting = held(self.sent[len(self.got) :], *after)
        found = [self.dev.shift(v, "c", 1) for v in waiting]
        self.got = self.got + found
        return found

    def more(self, own, sent):
        self.own, self.sent = self.own + [own], self.sent + [sent]
        self.widths = self.widths + [own.shape[2]]

    def add(self, *after):
        self.got = held(self.got, *after)
        dev, rows = self.dev, self.rows
        sizes = (dev.size["z"], dev.size["y"], dev.size["x"])
        plane, width = sizes[1] * sizes[2], sum(self.widths)
        pairs, chips = len(self.own), dev.count // 2
        self.steps = next(n for n in (4, 3, 2, 1) if all(w % (128 * n) == 0 for w in self.widths))
        tiles = [w // self.steps for w in self.widths]
        halves = [pl.BlockSpec((chips, rows, t), lambda i: (0, 0, i)) for t in tiles]
        out_tile = pl.BlockSpec((sizes[0], rows, sum(tiles)), lambda i: (0, 0, i))
        self.blocks = pl.pallas_call(
            functools.partial(chip_sum_kernel, sizes, pairs),
            name="chip_sum",
            grid=(self.steps,),
            out_shape=[jax.ShapeDtypeStruct((sizes[0], rows, width), BF)] * plane,
            in_specs=[SMEM] + halves + halves,
            out_specs=[out_tile] * plane,
            compiler_params=params(),
            cost_estimate=cost(0, 6 * dev.count // 2 * rows * width),
        )(self.place, *self.own, *self.got)
        self.terms = [self.blocks[0]]
        return self.blocks

    def near(self, *after):
        return self._plane(lambda ky, kx: ky == 0 or kx == 0, after)

    def far(self, *after):
        return self._plane(lambda ky, kx: ky > 0 and kx > 0, after)

    def _plane(self, chosen, after):
        dev, ny, nx = self.dev, self.dev.size["y"], self.dev.size["x"]
        blocks = held(self.blocks, *after)
        found = [
            dev.shift_plane(blocks[ky * nx + kx], ky, kx)
            for ky in range(ny)
            for kx in range(nx)
            if (ky or kx) and chosen(ky, kx)
        ]
        self.terms += found
        return found


def line_kernel(nz, counts, place, *refs):
    terms, outs = refs[: sum(counts)], refs[sum(counts) :]
    joined = len(outs) == 1
    rows = outs[0].shape[-2]
    for k in range(nz):
        at, first, start = k if joined else lax.rem(place[0] + k, nz), 0, 0
        out = outs[0].at[k] if joined else outs[k]
        for count in counts:
            group = terms[first : first + count]
            total = group[0][at].astype(F32)
            for term in group[1:]:
                total += term[at].astype(F32)
            first, width = first + count, total.shape[1]
            for piece in range(total.shape[0] // rows):
                out[:, start : start + width] = total[piece * rows : (piece + 1) * rows].astype(BF)
                start += width


def finish(dev, place, scatters, joined, *after):
    nz, rows = dev.size["z"], min(s.rows for s in scatters)
    width = sum(w * (s.rows // rows) for s in scatters for w in s.widths)
    terms = held([t for s in scatters for t in s.terms], *after)
    blocks = pl.pallas_call(
        functools.partial(line_kernel, nz, [len(s.terms) for s in scatters]),
        name="plane_sum",
        out_shape=[jax.ShapeDtypeStruct((nz, rows, width), BF)]
        if joined
        else [jax.ShapeDtypeStruct((rows, width), BF)] * nz,
        in_specs=[SMEM] + [VMEM] * len(terms),
        out_specs=[VMEM] * (1 if joined else nz),
        compiler_params=params(),
        cost_estimate=cost(0, 8 * nz * rows * width),
    )(place, *terms)
    if joined:
        line = lax.all_to_all(
            blocks[0], "dp", 0, 0, axis_index_groups=dev.groups("z"), tiled=True
        )
        return blocks, line
    return blocks, [blocks[0]] + [dev.shift(blocks[k], "z", k) for k in range(1, nz)]


def totals(arrived, scatters):
    if isinstance(arrived, list):
        total = sum(v.astype(F32) for v in arrived)
    else:
        total = jnp.sum(arrived.astype(F32), axis=0)
    rows, start, out = total.shape[0], 0, []
    for s in scatters:
        pieces, width = s.rows // rows, sum(s.widths)
        parts = [total[:, start + i * width : start + (i + 1) * width] for i in range(pieces)]
        whole_rows = parts[0] if pieces == 1 else jnp.concatenate(parts, axis=0)
        start += pieces * width
        tiles, span = [w // s.steps for w in s.widths], width // s.steps
        for t, tile in enumerate(tiles):
            at = sum(tiles[:t])
            found = [whole_rows[:, i * span + at : i * span + at + tile] for i in range(s.steps)]
            out.append(found[0] if len(found) == 1 else jnp.concatenate(found, axis=1))
    return out


def split_cores(value, rows, core, own, sent):
    if rows % 8 == 0:
        parts = value.reshape(-1, 2, rows, value.shape[1])
        own[...] = jnp.where(core == 0, parts[:, 0], parts[:, 1]).astype(BF)
        sent[...] = jnp.where(core == 0, parts[:, 1], parts[:, 0]).astype(BF)
        return
    for chip in range(value.shape[0] // (2 * rows)):
        first = value[2 * chip * rows : (2 * chip + 1) * rows]
        second = value[(2 * chip + 1) * rows : (2 * chip + 2) * rows]
        own[chip] = jnp.where(core == 0, first, second).astype(BF)
        sent[chip] = jnp.where(core == 0, second, first).astype(BF)


def dot(left, right):
    return jnp.dot(left, right, preferred_element_type=F32)


def dot_rows(left, right):
    return lax.dot_general(left, right, (((0,), (0,)), ((), ())), preferred_element_type=F32)


def dot_cols(left, right):
    return lax.dot_general(left, right, (((1,), (1,)), ((), ())), preferred_element_type=F32)


def one_hot(column, row):
    return jnp.where(column == row, 1.0, 0.0).astype(BF)


def row_sum(values):
    return jnp.sum(values, axis=0, keepdims=True)


def normalised(values):
    mean = jnp.mean(values, axis=1, keepdims=True)
    centered = values - mean
    variance = jnp.mean(centered * centered, axis=1, keepdims=True)
    scale = lax.rsqrt(variance + NORM_EPS)
    return centered * scale, scale


def norm_back(unit, scale, gain, grad):
    weighted = grad * gain
    first = jnp.mean(weighted, axis=1, keepdims=True)
    second = jnp.mean(weighted * unit, axis=1, keepdims=True)
    return scale * (weighted - first - unit * second)


class Layout:
    def __init__(self, images, slots):
        self.images, self.slots = images, slots
        self.small, self.large = GRID * slots, 4 * GRID * slots
        self.small_pad = -(-self.small // 16) * 16
        self.large_pad = -(-self.large // 16) * 16
        self.starts = [self.large_pad + i * self.small_pad for i in range(images - 1)]
        self.rows = self.large_pad + (images - 1) * self.small_pad

    def rows_of(self, row, big):
        small_id = jnp.maximum(row - self.large_pad, 0) // self.small_pad
        in_large = row < self.large_pad
        offset = jnp.where(in_large, row, row - self.large_pad - small_id * self.small_pad)
        real = offset < jnp.where(in_large, self.large, self.small)
        image = jnp.where(in_large, big, small_id + jnp.where(small_id >= big, 1, 0))
        window = (
            GRID * image + jnp.where(image > big, 3 * GRID, 0) + offset // self.slots
        )
        return window, offset % self.slots, real

    def source(self, row, big):
        window, slot, real = self.rows_of(row, big)
        return jnp.where(real, window * self.slots + slot, -1)

    def place(self, big, count_vec, bucket, lane_slots):
        row = jnp.arange(self.rows, dtype=jnp.int32)
        window, slot, real = self.rows_of(row, big)
        in_large = row < self.large_pad
        small_id = jnp.maximum(row - self.large_pad, 0) // self.small_pad
        image = jnp.where(in_large, big, small_id + jnp.where(small_id >= big, 1, 0))
        kept = jnp.sum(
            jnp.where(
                image[:, None] == jnp.arange(self.images, dtype=jnp.int32)[None, :],
                count_vec[None, :],
                0,
            ),
            axis=1,
        )
        windows = bucket.shape[0]
        target = jnp.sum(
            jnp.where(
                window[:, None] == jnp.arange(windows, dtype=jnp.int32)[None, :], bucket[None, :], 0
            ),
            axis=1,
        )
        return jnp.where(real & (slot < kept), target * lane_slots + slot, -1)

    def key_mask(self, size, real, kept):
        lane = lax.broadcasted_iota(jnp.int32, (1, size), 1)
        live = (lane < real) & (lane % self.slots < kept)
        return jnp.where(live, 0.0, MASK_FILL)


LANE_SLOTS = 8


def slot_targets(info, slots, wins, axis):
    rows = wins * LANE_SLOTS
    shape = (rows, 1) if axis == 0 else (1, rows)
    spread = (rows, wins) if axis == 0 else (wins, rows)
    owner = lax.broadcasted_iota(jnp.int32, spread, axis) // LANE_SLOTS
    window = lax.broadcasted_iota(jnp.int32, spread, 1 - axis)
    pick = jnp.where(owner == window, 1.0, 0.0).astype(BF)
    fields = dot(pick, info) if axis == 0 else dot_rows(info, pick)
    slot = lax.broadcasted_iota(jnp.int32, shape, axis) % LANE_SLOTS
    field = (lambda i: fields[:, i : i + 1]) if axis == 0 else (lambda i: fields[i : i + 1, :])
    cell = jnp.zeros(shape, F32)
    for j in range(slots):
        cell = cell + jnp.where(slot == j, field(4 + j), 0.0)
    first = (lax.broadcasted_iota(jnp.int32, shape, axis) // LANE_SLOTS) * GRID
    live = slot.astype(F32) < field(1)
    return jnp.where(live, first + cell.astype(jnp.int32), -1)


def owner_kernel(slots, wins, cot, info_in, vec_dec, de_out, base_out, sums_out):
    step = pl.program_id(0)
    cells = wins * GRID
    width = cot.shape[1]
    quarter = width // 4
    grads = cot[...]
    info = info_in[...]
    cell_lane = lax.broadcasted_iota(jnp.int32, (1, cells), 1)
    want = slot_targets(info, slots, wins, 0)
    pick = one_hot(want, cell_lane)
    picked = dot(pick, grads)
    de_out[...] = picked.astype(BF)
    taken = jnp.sum(jnp.where(want == cell_lane, 1.0, 0.0), axis=0, keepdims=True)
    window = lax.broadcasted_iota(jnp.int32, (wins, cells), 0)
    inside = jnp.where(
        window == lax.broadcasted_iota(jnp.int32, (wins, cells), 1) // GRID, 1.0, 0.0
    ).astype(BF)
    present_row = dot_rows(info, inside)[0:1, :]
    mask_sum = dot(jnp.broadcast_to(present_row - taken, (8, cells)).astype(BF), grads)[:1]

    cell_row = lax.broadcasted_iota(jnp.int32, (cells, 1), 0)
    filled = jnp.sum(
        jnp.where(cell_row == slot_targets(info, slots, wins, 1), 1.0, 0.0), axis=1, keepdims=True
    )
    owner = lax.broadcasted_iota(jnp.int32, (cells, wins), 0) // GRID
    fields = dot(one_hot(owner, lax.broadcasted_iota(jnp.int32, (cells, wins), 1)), info)
    present = fields[:, 0:1]
    turn = fields[:, 2:3].astype(jnp.int32)
    wide = fields[:, 3:4] > GRID
    cell = cell_row % GRID
    along = jnp.where(wide, (turn % 2) * GRID + cell, cell)
    across = jnp.where(wide, turn // 2, turn)
    depth = 32
    place = lax.broadcasted_iota(jnp.int32, (depth, quarter), 0).astype(F32)
    index = lax.broadcasted_iota(jnp.int32, (depth, quarter), 1).astype(F32) / quarter
    angle = place * (1.0 / jnp.exp(index * jnp.log(F32(10000.0))))
    table = jnp.concatenate([jnp.sin(angle), jnp.cos(angle)], axis=1)
    high = table.astype(BF)
    rest = table - high.astype(F32)
    middle = rest.astype(BF)
    low = (rest - middle.astype(F32)).astype(BF)
    stacked = jnp.concatenate([high, middle, low], axis=0)
    lane = lax.broadcasted_iota(jnp.int32, (1, 3 * depth), 1) % depth
    shown = present > 0.5
    first = dot(one_hot(jnp.where(shown, along, -1), lane), stacked)
    second = dot(one_hot(jnp.where(shown, across, -1), lane), stacked)
    bare = present - filled
    base_out[:, : 2 * quarter] = first + bare * vec_dec[1:2, : 2 * quarter]
    base_out[:, 2 * quarter :] = second + bare * vec_dec[1:2, 2 * quarter :]

    @pl.when(step == 0)
    def _():
        sums_out[...] = jnp.zeros_like(sums_out)

    sums_out[0:1, :] += row_sum(picked)
    sums_out[1:2, :] += mask_sum


def decode_kernel(slots, wins, got, info_in, base, out):
    cell_row = lax.broadcasted_iota(jnp.int32, (wins * GRID, 1), 0)
    want = slot_targets(info_in[...], slots, wins, 1)
    out[...] = (dot(one_hot(cell_row, want), got[...]) + base[...]).astype(BF)


BIG, KEPT = 4, 5


def first_norm_kernel(lay, meta, tokens, vecs, x_out, h_out):
    rows = x_out.shape[0]
    row = lax.broadcasted_iota(jnp.int32, (rows, 1), 0) + pl.program_id(0) * rows
    lane = lax.broadcasted_iota(jnp.int32, (1, tokens.shape[0]), 1)
    moved = dot(one_hot(lay.source(row, meta[BIG]), lane), tokens[...])
    x_out[...] = moved.astype(BF)
    unit, _ = normalised(moved)
    h_out[...] = (unit * vecs[0:1, :] + vecs[1:2, :]).astype(BF)


def softmax_rows(scores):
    top = jnp.max(scores, axis=1, keepdims=True)
    expo = jnp.exp(scores - top)
    return (expo * (1.0 / jnp.sum(expo, axis=1, keepdims=True))).astype(BF)


def attention_kernel(lay, chunk, head_dim, meta, h_in, w_q, w_k, w_v, vecs,
                     q_out, k_out, v_out, pl_out, ps_out, o_out, scores):
    big, small = lay.large_pad, lay.small_pad
    normed = h_in[...]
    q_out[...] = ((dot(normed, w_q[...]) + vecs[2:3, :]) * (head_dim**-0.5)).astype(BF)
    k_out[...] = dot(normed, w_k[...]).astype(BF)
    v_out[...] = (dot(normed, w_v[...]) + vecs[3:4, :]).astype(BF)
    lane = lax.broadcasted_iota(jnp.int32, (1, 2 * head_dim), 1)
    low = lane < head_dim
    halves = (jnp.where(low, 1.0, 0.0).astype(BF), jnp.where(low, 0.0, 1.0).astype(BF))
    mask_l = lay.key_mask(big, lay.large, meta[KEPT])
    masks = [lay.key_mask(small, lay.small, meta[KEPT + 1 + i]) for i in range(lay.images - 1)]
    for pair in range(q_out.shape[1] // (2 * head_dim)):
        cols = slice(pair * 2 * head_dim, (pair + 1) * 2 * head_dim)
        first = []
        for half in range(2):
            head = 2 * pair + half
            query = q_out[:big, cols] * halves[half]
            scores[...] = dot_cols(query, k_out[:big, cols])
            for start in range(0, big, chunk):
                part = scores[start : start + chunk, :] + mask_l
                pl_out[head, start : start + chunk, :] = softmax_rows(part)
            outs = [dot(pl_out[head], v_out[:big, cols])]
            for i, start in enumerate(lay.starts):
                rows = slice(start, start + small)
                query = q_out[rows, cols] * halves[half]
                part = dot_cols(query, k_out[rows, cols]) + masks[i]
                weights = softmax_rows(part)
                ps_out[head, i] = weights
                outs.append(dot(weights, v_out[rows, cols]))
            if half == 0:
                first = outs
        spans = [(0, big)] + [(s, small) for s in lay.starts]
        for (start, size), left, right in zip(spans, first, outs):
            o_out[start : start + size, cols] = jnp.where(low, left, right).astype(BF)


def out_kernel(parts, *refs):
    o_in = refs[:parts]
    w_out, vecs, x_in, r_out, h_out = refs[parts:]
    residual = x_in[...].astype(F32) + vecs[4:5, :]
    width = o_in[0].shape[1]
    for i, o in enumerate(o_in):
        residual += dot(o[...], w_out[i * width : (i + 1) * width, :])
    r_out[...] = residual
    unit, _ = normalised(residual)
    h_out[...] = (unit * vecs[5:6, :] + vecs[6:7, :]).astype(BF)


def fc1_kernel(chunk, h_in, weight, bias, g_out, d_out, hidden):
    hidden[...] = dot(h_in[...], weight[...])
    for start in range(0, hidden.shape[0], chunk):
        rows = slice(start, start + chunk)
        u = hidden[rows, :] + bias[...]
        half = 0.5 + 0.5 * lax.erf(u * (0.5**0.5))
        g_out[rows, :] = (u * half).astype(BF)
        density = jnp.exp(u * u * -0.5) * 0.3989422804014327
        d_out[rows, :] = (half + u * density).astype(BF)


def fc2_kernel(g_one, g_two, w_two, vecs, r_in, w_dec, w_dec_more, vec_dec, place, y_out, e_out, kept):
    step = pl.program_id(0)
    rows, half = g_one.shape
    y = r_in[...] + dot(g_one[...], w_two[:half, :]) + dot(g_two[...], w_two[half:, :])
    y = (y + vecs[7:8, :]).astype(BF)
    y_out[...] = y
    kept[pl.ds(pl.multiple_of(step * rows, rows), rows), :] = (
        dot(y, jnp.concatenate([w_dec[...], w_dec_more[...]], axis=1)) + vec_dec[0:1, :]
    ).astype(BF)

    @pl.when(step == pl.num_programs(0) - 1)
    def _():
        target = lax.broadcasted_iota(jnp.int32, (e_out.shape[0], 1), 0)
        e_out[...] = dot(one_hot(target, place[...]), kept[...]).astype(BF)


def dec_back_kernel(rows, spot, got, place, w_dec, w_dec_more, y_in, dy_out, own_out, sent_out, db_out):
    target = lax.broadcasted_iota(jnp.int32, (got.shape[0], 1), 0)
    grad = dot_rows(one_hot(target, place[...]), got[...]).astype(BF)
    half = w_dec.shape[1]
    dy = dot_cols(grad[:, :half], w_dec[...]) + dot_cols(grad[:, half:], w_dec_more[...])
    dy = dy.astype(BF)
    dy_out[...] = dy
    split_cores(dot_rows(y_in[...], grad), rows, spot[3], own_out, sent_out)
    db_out[...] = row_sum(dy.astype(F32))


def fc2_back_kernel(rows, spot, dy_in, w_two, g_one, d_one, g_two, d_two, du_out, own_out, sent_out, db_out):
    dy = dy_in[...]
    early = pl.program_id(0) < 2
    slope = jnp.where(early, d_one[...], d_two[...]).astype(F32)
    du = (dot_cols(dy, w_two[...]) * slope).astype(BF)
    du_out[...] = du
    db_out[...] = row_sum(du.astype(F32))
    split_cores(
        dot_rows(jnp.where(early, g_one[...], g_two[...]), dy), rows, spot[3], own_out, sent_out
    )


def fc1_back_kernel(rows, spot, du_in, w_one, h_in, dh_out, own_out, sent_out, turned):
    step = pl.program_id(0)

    @pl.when(step == 0)
    def _():
        turned[...] = h_in[...].T
        dh_out[...] = jnp.zeros_like(dh_out)

    du = du_in[...]
    split_cores(dot(turned[...], du), rows, spot[3], own_out, sent_out)
    dh_out[...] += dot_cols(du, w_one[...])


def out_back_kernel(rows, parts, spot, dh_one, dh_two, r_in, dy_in, vecs, w_out, *refs):
    o_in = refs[:parts]
    dr_out, do_out, own_out, sent_out, sums, total = refs[parts:]
    step = pl.program_id(0)
    unit, scale = normalised(r_in[...])
    grad = dh_one[...] + dh_two[...]
    dr = dy_in[...].astype(F32) + norm_back(unit, scale, vecs[5:6, :], grad)
    dr_out[...] = dr
    da = dr.astype(BF)
    do_out[...] = dot_cols(da, w_out[...]).astype(BF)

    @pl.when(step == 0)
    def _():
        sums[...] = jnp.zeros_like(sums)
        total[...] = jnp.zeros_like(total)

    sums[0:1, :] += row_sum(grad * unit)
    sums[1:2, :] += row_sum(grad)
    sums[2:3, :] += row_sum(da.astype(F32))
    width = o_in[0].shape[1]
    for i, o in enumerate(o_in):
        total[i * width : (i + 1) * width, :] += dot_rows(o[...], da)

    @pl.when(step == pl.num_programs(0) - 1)
    def _():
        split_cores(total[...], rows, spot[3], own_out, sent_out)


def attention_back_kernel(rows_dev, lay, chunk, head_dim, spot, h_in, q_in, k_in, v_in, pl_in, ps_in, do_in,
                          dq_out, dk_out, dv_out, own_out, sent_out, sums, scores, ds_big):
    big, small = lay.large_pad, lay.small_pad
    lane = lax.broadcasted_iota(jnp.int32, (1, 2 * head_dim), 1)
    low = lane < head_dim
    halves = (jnp.where(low, 1.0, 0.0).astype(BF), jnp.where(low, 0.0, 1.0).astype(BF))

    def back_rows(weights, grad):
        p = weights.astype(F32)
        inner = jnp.sum(grad * p, axis=1, keepdims=True)
        return (p * (grad - inner)).astype(BF)

    for pair in range(q_in.shape[1] // (2 * head_dim)):
        cols = slice(pair * 2 * head_dim, (pair + 1) * 2 * head_dim)
        spans = [(0, big)] + [(s, small) for s in lay.starts]
        first = []
        for half in range(2):
            head = 2 * pair + half
            found = []
            for i, (start, size) in enumerate(spans):
                rows = slice(start, start + size)
                grad_o = do_in[rows, cols] * halves[half]
                if i == 0:
                    scores[...] = dot_cols(grad_o, v_in[rows, cols])
                    for s in range(0, big, chunk):
                        ds_big[s : s + chunk, :] = back_rows(
                            pl_in[head, s : s + chunk, :], scores[s : s + chunk, :]
                        )
                    weights, ds = pl_in[head], ds_big[...]
                else:
                    weights = ps_in[head, i - 1]
                    ds = back_rows(weights, dot_cols(grad_o, v_in[rows, cols]))
                found.append(
                    (
                        dot(ds, k_in[rows, cols]),
                        dot_rows(ds, q_in[rows, cols]),
                        dot_rows(weights, do_in[rows, cols]),
                    )
                )
            if half == 0:
                first = found
        for (start, size), left, right in zip(spans, first, found):
            rows = slice(start, start + size)
            dq_out[rows, cols] = (
                jnp.where(low, left[0], right[0]) * (head_dim**-0.5)
            ).astype(BF)
            dk_out[rows, cols] = jnp.where(low, left[1], right[1]).astype(BF)
            dv_out[rows, cols] = jnp.where(low, left[2], right[2]).astype(BF)
    turned = h_in[...].T
    width = dq_out.shape[1]
    for i, grad in enumerate((dq_out, dk_out, dv_out)):
        cols = slice(i * width, (i + 1) * width)
        split_cores(
            dot(turned, grad[...]), rows_dev, spot[3], own_out.at[:, :, cols], sent_out.at[:, :, cols]
        )
    sums[0:1, :] = row_sum(dq_out[...].astype(F32))
    sums[1:2, :] = row_sum(dv_out[...].astype(F32))


def first_back_kernel(lay, parts, meta, *refs):
    grads, more = refs[: 3 * parts], refs[3 * parts : 4 * parts]
    w_qkv, x_in, dr_in, vecs, sums_two, db_two, out, sums, kept = refs[4 * parts :]
    step = pl.program_id(0)
    rows = x_in.shape[0]
    width = grads[0].shape[1]
    grad = dot_cols(grads[0][...], w_qkv[:, :width])
    for i in range(1, 3 * parts):
        grad += dot_cols(grads[i][...], w_qkv[:, i * width : (i + 1) * width])
    unit, scale = normalised(x_in[...].astype(F32))
    moved = dr_in[...] + norm_back(unit, scale, vecs[0:1, :], grad)
    kept[pl.ds(pl.multiple_of(step * rows, rows), rows), :] = moved.astype(BF)

    @pl.when(step == 0)
    def _():
        sums[...] = jnp.zeros_like(sums)
        for i, part in enumerate(more):
            sums[2:4, i * width : (i + 1) * width] = part[0:2, :]
        sums[4:5, :] = sums_two[2:3, :]
        sums[5:7, :] = sums_two[0:2, :]
        sums[7:8, :] = db_two[...]

    sums[0:1, :] += row_sum(grad * unit)
    sums[1:2, :] += row_sum(grad)

    @pl.when(step == pl.num_programs(0) - 1)
    def _():
        slot = lax.broadcasted_iota(jnp.int32, (out.shape[0], 1), 0)
        row = lax.broadcasted_iota(jnp.int32, (1, lay.rows), 1)
        out[...] = dot(one_hot(slot, lay.source(row, meta[BIG])), kept[...]).astype(BF)


def owner_rank(owner_vec):
    window_ids = jnp.arange(owner_vec.shape[0], dtype=jnp.int32)
    earlier = (owner_vec[:, None] == owner_vec[None, :]) & (
        window_ids[None, :] < window_ids[:, None]
    )
    return jnp.sum(earlier.astype(jnp.int32), axis=1)


def spec(shape, index):
    return pl.BlockSpec(shape, index)


def local(tokens, ln1_gain, ln1_bias, qkv_weight, query_bias, value_bias, out_weight, out_bias,
          ln2_gain, ln2_bias, fc1_weight, fc1_bias, fc2_weight, fc2_bias, dec_weight, dec_bias,
          mask_token, kept_offsets, kept_count, res_id, dec_owner, dec_cot):
    count = lax.axis_size("dp")
    dev = Slice(count)
    vis, D = tokens.shape
    dec_width = dec_cot.shape[1]
    windows, slots = kept_offsets.shape
    images = res_id.shape[0]
    hidden = fc1_weight.shape[1]
    head_dim = D // HEADS
    per_peer = (windows + count - 1) // count
    total = count * per_peer
    lay = Layout(images, slots)
    R = lay.rows
    sd = jax.ShapeDtypeStruct

    ga, gc = Gather(dev, [qkv_weight]), Gather(dev, [fc2_weight])
    za = ga.along_z()
    rest = lax.all_gather(
        jnp.concatenate([fc1_weight, out_weight, dec_weight], axis=1), "dp", axis=0, tiled=True
    )
    image_ids = jnp.arange(images, dtype=jnp.int32)
    big = jnp.sum(image_ids * res_id)
    kept_big = jnp.sum(res_id * kept_count)
    kept_small = jnp.where(image_ids[:-1] < big, kept_count[:-1], kept_count[1:])
    meta = jnp.concatenate(
        [jnp.stack([dev.coord(axis) for axis in "zyxc"] + [big, kept_big]), kept_small]
    ).astype(jnp.int32)
    bucket = dec_owner * per_peer + owner_rank(dec_owner)
    place_row = lay.place(big, kept_count, bucket, LANE_SLOTS)[None, :]
    win = jnp.arange(windows, dtype=jnp.int32)
    big_start = GRID * big
    in_big = (win >= big_start) & (win < big_start + 4 * GRID)
    after = win >= big_start + 4 * GRID
    image_win = jnp.where(in_big, big, jnp.where(after, win // GRID - 3, win // GRID))
    in_image = jnp.where(in_big, win - big_start, win % GRID)
    kept_win = jnp.sum(
        jnp.where(image_win[:, None] == image_ids[None, :], kept_count[None, :], 0), axis=1
    )
    side_win = jnp.where(in_big, 2 * GRID, GRID)
    info = jnp.concatenate(
        [jnp.stack([jnp.ones_like(win), kept_win, in_image, side_win], axis=1), kept_offsets], axis=1
    )
    xa = ga.first(bucket)
    bucket = held(bucket, *ga.sent)
    slot_of = jnp.arange(total, dtype=jnp.int32)
    info_send = jnp.sum(
        jnp.where((slot_of[:, None] == bucket[None, :])[:, :, None], info[None, :, :], 0), axis=1
    )
    eight = [ln1_gain, ln1_bias, query_bias, value_bias, out_bias, ln2_gain, ln2_bias, fc2_bias]
    vectors = eight + [fc1_bias, dec_bias, mask_token]
    wide = max(fc1_bias.shape[0], 128)
    line = lambda v: jnp.pad(v, (0, wide - v.shape[0]))[None, :]
    sheet = jnp.concatenate([line(v) for v in vectors], axis=0)
    fields = info_send.shape[1]
    info_block = jnp.pad(info_send.astype(BF), ((0, 0), (0, wide - fields)))
    packed = jnp.concatenate(
        [
            jnp.broadcast_to(sheet[None], (count,) + sheet.shape),
            info_block.reshape(count, per_peer, wide),
        ],
        axis=1,
    )
    ya = ga.second(packed)
    packed = lax.all_to_all(packed, "dp", 0, 0, tiled=True)
    n_vec = eight[0].shape[0]
    vecs = packed[:, :8, :n_vec].transpose(1, 0, 2).reshape(8, D).astype(F32)
    bf1 = packed[:, 8, : fc1_bias.shape[0]].reshape(1, hidden).astype(F32)
    vec_dec = packed[:, 9:11, : dec_bias.shape[0]].transpose(1, 0, 2).reshape(2, dec_width).astype(F32)
    info_got = packed[:, 11:, :fields].reshape(total, fields)

    w_out_spec = spec((D, D), lambda *_: (0, hidden // D))
    first_dec, dec_half = 2 * (hidden + D) // dec_width, dec_width // 2
    w_dec_specs = [spec((D, dec_half), lambda *_, i=i: (0, first_dec + i)) for i in range(2)]
    tile = R // 3
    rows_of = lambda width: spec((tile, width), lambda i: (i, 0))
    x_rows, h_one = pl.pallas_call(
        functools.partial(first_norm_kernel, lay),
        name="first_norm",
        grid=(3,),
        in_specs=[SMEM, whole((vis, D)), whole((8, D))],
        out_specs=[rows_of(D), rows_of(D)],
        out_shape=[sd((R, D), BF), sd((R, D), BF)],
        compiler_params=params(),
        cost_estimate=cost(2 * R * vis * D, 4e6),
    )(meta, held(tokens, za), vecs)

    wins = 16
    steps = total // wins
    cells_w, rows_w = wins * GRID, wins * LANE_SLOTS
    by_step = lambda height, width: spec((height, width), lambda i: (i, 0))
    info_spec = by_step(wins, info_got.shape[1])
    de_send, base, owner_sums = pl.pallas_call(
        functools.partial(owner_kernel, slots, wins),
        name="owner_side",
        grid=(steps,),
        in_specs=[by_step(cells_w, dec_width), info_spec, whole((2, dec_width))],
        out_specs=[by_step(rows_w, dec_width), by_step(cells_w, dec_width), whole((8, dec_width))],
        out_shape=[sd((total * LANE_SLOTS, dec_width), BF), sd((total * GRID, dec_width), F32),
                   sd((8, dec_width), F32)],
        compiler_params=params(),
        cost_estimate=cost(4e9, 8e6, 1e5),
    )(dec_cot, held(info_got, h_one, *xa), vec_dec)

    from_a = ga.swap(de_send, h_one)
    zc = gc.along_z(*ya)
    (w_qkv,) = ga.result(meta)
    de_got = lax.all_to_all(
        held(de_send, *from_a).reshape(count, per_peer * LANE_SLOTS, dec_width), "dp", 0, 0, tiled=True
    ).reshape(total * LANE_SLOTS, dec_width)

    group = 4
    parts = HEADS // group
    gw = group * head_dim
    chunk = lay.large_pad // 5
    p_big_t = sd((group, lay.large_pad, lay.large_pad), BF)
    p_small_t = sd((group, images - 1, lay.small_pad, lay.small_pad), BF)

    def attend(i, h_rows):
        col_of = lambda base_: spec((D, gw), lambda _: (0, base_ * parts + i))
        return pl.pallas_call(
            functools.partial(attention_kernel, lay, chunk, head_dim),
            name="attention",
            grid=(1,),
            in_specs=[SMEM, whole((R, D)), col_of(0), col_of(1), col_of(2),
                      spec((8, gw), lambda _: (0, i))],
            out_specs=[whole((R, gw))] * 3 + [whole(p_big_t.shape), whole(p_small_t.shape), whole((R, gw))],
            out_shape=[sd((R, gw), BF)] * 3 + [p_big_t, p_small_t, sd((R, gw), BF)],
            scratch_shapes=[pltpu.VMEM((lay.large_pad, lay.large_pad), F32)],
            compiler_params=params(),
            cost_estimate=cost(2 * R * D * D + 2e9, 8e6, 1e6),
        )(meta, h_rows, w_qkv, w_qkv, w_qkv, vecs)

    attn = [attend(0, h_one)]
    attn.append(attend(1, held(h_one, attn[0][5])))
    gc.first(attn[1][5])
    attn.append(attend(2, held(h_one, attn[1][5], *gc.sent)))
    gc.second(attn[2][5])
    att = [a[5] for a in attn]

    r_one, h_two = pl.pallas_call(
        functools.partial(out_kernel, parts),
        name="out_projection",
        grid=(3,),
        in_specs=[rows_of(gw)] * parts
        + [w_out_spec, whole((8, D)), rows_of(D)],
        out_specs=[rows_of(D), rows_of(D)],
        out_shape=[sd((R, D), F32), sd((R, D), BF)],
        compiler_params=params(),
        cost_estimate=cost(2 * R * D * D, 9e6),
    )(*att, rest, vecs, held(x_rows, *gc.sent))

    ht = hidden // 6

    def feed(i, h_rows):
        return pl.pallas_call(
            functools.partial(fc1_kernel, R // 24),
            name="fc1",
            grid=(3,),
            in_specs=[whole((R, D)), spec((D, ht), lambda j: (0, 3 * i + j)),
                      spec((1, ht), lambda j: (0, 3 * i + j))],
            out_specs=[spec((R, ht), lambda j: (0, j))] * 2,
            out_shape=[sd((R, hidden // 2), BF)] * 2,
            scratch_shapes=[pltpu.VMEM((R, ht), F32)],
            compiler_params=params(),
            cost_estimate=cost(R * D * hidden, 1e7, 3e6),
        )(h_rows, rest, bf1)

    act_0, gelu_0 = feed(0, h_two)
    gc.swap(act_0)
    act_1, gelu_1 = feed(1, held(h_two, act_0, de_got, *gc.sent))
    (w_two,) = gc.result(meta)

    y_rows, e_send = pl.pallas_call(
        fc2_kernel,
        name="fc2_and_embed",
        grid=(3,),
        in_specs=[rows_of(hidden // 2), rows_of(hidden // 2), whole((hidden, D)), whole((8, D)),
                  rows_of(D), *w_dec_specs, whole((2, dec_width)), whole((1, R))],
        out_specs=[rows_of(D), whole((total * LANE_SLOTS, dec_width))],
        out_shape=[sd((R, D), BF), sd((total * LANE_SLOTS, dec_width), BF)],
        scratch_shapes=[pltpu.VMEM((R, dec_width), BF)],
        compiler_params=params(),
        cost_estimate=cost(2 * R * D * hidden + 4 * R * D * dec_width, 2e7),
    )(act_0, act_1, w_two, vecs, r_one, rest, rest, vec_dec, place_row)

    e_got = lax.all_to_all(
        e_send.reshape(count, per_peer * LANE_SLOTS, dec_width), "dp", 0, 0, tiled=True
    ).reshape(total * LANE_SLOTS, dec_width)

    row_dev, row_two = D // count, hidden // count
    chips = count // 2
    dy, own_dec, sent_dec, db_two = pl.pallas_call(
        functools.partial(dec_back_kernel, row_dev),
        name="embed_back",
        grid=(1,),
        in_specs=[SMEM, whole((total * LANE_SLOTS, dec_width)), whole((1, R)), *w_dec_specs, whole((R, D))],
        out_specs=[whole((R, D)), whole((chips, row_dev, dec_width)),
                   whole((chips, row_dev, dec_width)), whole((1, D))],
        out_shape=[sd((R, D), BF), sd((chips, row_dev, dec_width), BF),
                   sd((chips, row_dev, dec_width), BF), sd((1, D), F32)],
        compiler_params=params(),
        cost_estimate=cost(6 * R * D * dec_width, 7e6, weight=20),
    )(meta, de_got, place_row, rest, rest, y_rows)

    ht = hidden // 4
    held_chips = ht // (2 * row_two)
    grad_spec = spec((held_chips, row_two, D), lambda j: (j, 0, 0))
    half_tile = lambda k: spec((R, ht), lambda j: (0, jnp.clip(j - 2 * k, 0, 1)))
    du, own_two, sent_two, db_one = pl.pallas_call(
        functools.partial(fc2_back_kernel, row_two),
        name="fc2_back",
        grid=(4,),
        in_specs=[SMEM, whole((R, D)), spec((ht, D), lambda j: (j, 0)), half_tile(0), half_tile(0),
                  half_tile(1), half_tile(1)],
        out_specs=[spec((R, ht), lambda j: (0, j)), grad_spec, grad_spec,
                   spec((1, ht), lambda j: (0, j))],
        out_shape=[sd((R, hidden), BF), sd((chips, row_two, D), BF), sd((chips, row_two, D), BF),
                   sd((1, hidden), F32)],
        compiler_params=params(),
        cost_estimate=cost(4 * R * D * hidden, 3e7, weight=20),
    )(meta, dy, w_two, act_0, gelu_0, act_1, gelu_1)
    s_two = Scatter(dev, [(own_two, sent_two)], meta)
    c_two = s_two.swap()

    grad_spec = spec((chips, row_dev, ht), lambda j: (0, 0, j))

    def fc1_back(i, du_rows):
        return pl.pallas_call(
            functools.partial(fc1_back_kernel, row_dev),
            name="fc1_back",
            grid=(2,),
            in_specs=[SMEM, spec((R, ht), lambda j: (0, 2 * i + j)),
                      spec((D, ht), lambda j: (0, 2 * i + j)), whole((R, D))],
            out_specs=[whole((R, D)), grad_spec, grad_spec],
            out_shape=[sd((R, D), F32)] + [sd((chips, row_dev, hidden // 2), BF)] * 2,
            scratch_shapes=[pltpu.VMEM((D, R), BF)],
            compiler_params=params(),
            cost_estimate=cost(2 * R * D * hidden, 1.5e7, weight=20),
        )(meta, du_rows, rest, h_two)

    dh_0, own_f0, sent_f0 = fc1_back(0, du)
    s_two.add(dh_0, *c_two)
    near = s_two.near()
    dh_1, own_f1, sent_f1 = fc1_back(1, held(du, dh_0, s_two.blocks[0]))
    s_one = Scatter(dev, [(own_f0, sent_f0), (own_f1, sent_f1), (own_dec, sent_dec)], meta)
    far = s_two.far(dh_1, *near)
    c_one = s_one.swap(dh_1, *near)

    grad_spec = whole((chips, row_dev, D))
    dr, d_att, own_out, sent_out, sums_two = pl.pallas_call(
        functools.partial(out_back_kernel, row_dev, parts),
        name="out_back",
        grid=(3,),
        in_specs=[SMEM, rows_of(D), rows_of(D), rows_of(D), rows_of(D), whole((8, D)), w_out_spec]
        + [rows_of(gw)] * parts,
        out_specs=[rows_of(D), rows_of(D), grad_spec, grad_spec, whole((8, D))],
        out_shape=[sd((R, D), F32), sd((R, D), BF)] + [sd((chips, row_dev, D), BF)] * 2
        + [sd((8, D), F32)],
        scratch_shapes=[pltpu.VMEM((D, D), F32)],
        compiler_params=params(),
        cost_estimate=cost(4 * R * D * D, 2e7, weight=20),
    )(meta, dh_0, held(dh_1, *near), r_one, dy, vecs, rest, *att)
    s_one.add(dr, *far, *c_one)
    near = s_one.near()

    def attend_back(i, d_att_rows):
        q_rows, k_rows, v_rows, prob_l, prob_s, _ = attn[i]
        grad_shape = (chips, row_dev, 3 * gw)
        return pl.pallas_call(
            functools.partial(attention_back_kernel, row_dev, lay, chunk, head_dim),
            name="attention_back",
            grid=(1,),
            in_specs=[SMEM, whole((R, D))] + [whole((R, gw))] * 3
            + [whole(p_big_t.shape), whole(p_small_t.shape), spec((R, gw), lambda _: (0, i))],
            out_specs=[whole((R, gw))] * 3 + [whole(grad_shape)] * 2 + [whole((8, gw))],
            out_shape=[sd((R, gw), BF)] * 3 + [sd(grad_shape, BF)] * 2 + [sd((8, gw), F32)],
            scratch_shapes=[pltpu.VMEM((lay.large_pad, lay.large_pad), F32),
                            pltpu.VMEM((lay.large_pad, lay.large_pad), BF)],
            compiler_params=params(),
            cost_estimate=cost(2 * R * D * D + 3e9, 1e7, weight=20),
        )(meta, h_one, q_rows, k_rows, v_rows, prob_l, prob_s, d_att_rows)

    back = [attend_back(0, held(d_att, s_one.blocks[0], *far))]
    far = s_one.far(back[0][0], *near)
    s_mid = Scatter(dev, [(own_out, sent_out), back[0][3:5]], meta)
    c_mid = s_mid.swap(back[0][0], *near)
    back.append(attend_back(1, held(d_att, back[0][0], *near)))
    s_mid.add(back[1][0], *far, *c_mid)
    near = s_mid.near()
    lines_early, z_early = finish(dev, meta, [s_two, s_one], True, back[1][0], s_mid.blocks[0])
    s_last = Scatter(dev, [back[1][3:5]], meta)
    c_last = s_last.swap(back[1][0], *far)
    back.append(attend_back(2, held(d_att, back[1][0], s_mid.blocks[0], lines_early[0])))
    s_last.more(*back[2][3:5])
    c_last += s_last.swap(back[2][0], *near, *c_last)
    far = s_mid.far(back[2][0], *near)

    decoded = pl.pallas_call(
        functools.partial(decode_kernel, slots, wins),
        name="decode",
        grid=(steps,),
        in_specs=[by_step(rows_w, dec_width), info_spec, by_step(cells_w, dec_width)],
        out_specs=by_step(cells_w, dec_width),
        out_shape=sd((total * GRID, dec_width), BF),
        compiler_params=params(),
        cost_estimate=cost(1e9, 7e6, weight=20),
    )(held(e_got, back[2][0], *near), info_got, base)
    s_last.add(decoded, *far, *c_last)
    near = s_last.near() + s_last.far()

    dqkv = [b[i] for i in range(3) for b in back]
    grad_tokens, sums = pl.pallas_call(
        functools.partial(first_back_kernel, lay, parts),
        name="first_back",
        grid=(3,),
        in_specs=[SMEM] + [rows_of(gw)] * (3 * parts) + [whole((8, gw))] * parts
        + [whole((D, 3 * D)), rows_of(D), rows_of(D), whole((8, D)), whole((8, D)), whole((1, D))],
        out_specs=[whole((vis, D)), whole((8, D))],
        out_shape=[sd((vis, D), BF), sd((8, D), F32)],
        scratch_shapes=[pltpu.VMEM((R, D), BF)],
        compiler_params=params(),
        cost_estimate=cost(2 * R * D * 3 * D + 2 * R * vis * D, 2e7, weight=20),
    )(meta, *dqkv, *[b[5] for b in back], w_qkv, x_rows, held(dr, s_last.blocks[0], z_early), vecs, sums_two,
      db_two)

    rows = jnp.concatenate(
        [
            sums.reshape(8, count, -1).transpose(1, 0, 2).reshape(count, -1),
            db_one.reshape(count, -1),
            owner_sums[:2].reshape(2, count, -1).transpose(1, 0, 2).reshape(count, -1),
        ],
        axis=1,
    )
    lines_late, z_late = finish(dev, meta, [s_mid, s_last], False, grad_tokens, *near)
    rows = lax.all_to_all(held(rows, lines_late[0]), "dp", 0, 0, tiled=True)
    rows = jnp.sum(rows, axis=0)
    grad_two, grad_f0, grad_f1, grad_dec = totals(z_early, [s_two, s_one])
    grad_one = jnp.concatenate([grad_f0, grad_f1], axis=1)
    grad_out, *grads_qkv = totals(z_late, [s_mid, s_last])
    grad_qkv = jnp.concatenate(
        [g[:, i * gw : (i + 1) * gw] for i in range(3) for g in grads_qkv], axis=1
    )
    vec_grads, start = [], 0
    for v in vectors:
        vec_grads.append(rows[start : start + v.shape[0]])
        start += v.shape[0]
    (gg1, gb1, gbq, gbv, gbo, gg2, gb2, gbf2, gbf1, gbdec, gmask) = vec_grads
    return (decoded, grad_tokens, gg1, gb1, grad_qkv, gbq, gbv, grad_out, gbo, gg2, gb2, grad_one,
            gbf1, grad_two, gbf2, grad_dec, gbdec, gmask)


def solution(mesh):
    mat, vec = P("dp", None), P("dp")
    in_specs = (mat, vec, vec, mat, vec, vec, mat, vec, vec, vec, mat, vec, mat, vec, mat, vec, vec,
                mat, vec, vec, vec, mat)
    out_specs = (mat, mat, vec, vec, mat, vec, vec, mat, vec, vec, vec, mat, vec, mat, vec, mat, vec,
                 vec)
    return jax.shard_map(local, mesh=mesh, in_specs=in_specs, out_specs=out_specs, check_vma=False)
```

time: 579 us -> 390 us (0.67)
  waiting for transfers between devices: 189 us -> 29.3 us
  Pallas kernels: 153 us -> 230 us
  local copies, waits for them, and re-layouts: 70 us -> 25.9 us
  other arithmetic: 59.3 us -> 16.9 us
  starting transfers between devices: 97.7 us -> 66.3 us
  between operations: 2.95 us -> 15.7 us
    all_to_all x11 -> x5, waiting for transfers between devices: 128 us -> 6.19 us  [the longest x1 4.94 us: local(): packed = lax.all_to_all(packed, 'dp', 0, 0, tiled=True)]
    pallas_call x13 -> x24, Pallas kernels: 133 us -> 197 us  [the longest x3 40.7 us: attend_back(): pl.pallas_call(functools.partial(attention_back_kernel, row_dev, lay, chu...]
    ppermute x30 -> x29, waiting for transfers between devices: 60.2 us -> 9.9 us  [shift(): return lax.ppermute(values, 'dp', pairs)]
    unnamed x130 -> x92, local copies, waits for them, and re-layouts: 42 us -> 8.62 us
    all_to_all x11 -> x5, starting transfers between devices: 47.4 us -> 21 us  [the longest x1 5.22 us: local(): lax.all_to_all(e_send.reshape(count, per_peer * LANE_SLOTS, dec_width), '...]
    ppermute x30 -> x29, starting transfers between devices: 50.4 us -> 29.1 us  [shift(): return lax.ppermute(values, 'dp', pairs)]
    ppermute x0 -> x12, starting transfers between devices: none -> 16.2 us  [shift_plane(): return lax.ppermute(values, 'dp', pairs)]
    ppermute x0 -> x12, waiting for transfers between devices: none -> 13.2 us  [shift_plane(): return lax.ppermute(values, 'dp', pairs)]
  transfers between devices with their start and end apart: 41 -> 47, of which waited for: 17 -> 13; matrix products, arithmetic and copies ran while one was open for 15% -> 8% of each run, Pallas kernels for 7% -> 54%
where the time goes in v2:
time: 390 us; the launch traced here: 384 us
  Pallas kernels  230 us (59%)
  starting transfers between devices  66.3 us (17%)
  waiting for transfers between devices  29.3 us (8%)
  local copies, waits for them, and re-layouts  25.9 us (7%)
  other arithmetic  16.9 us (4%)
  between operations  15.7 us (4%)
    pallas_call x3, Pallas kernels, attend_back(): pl.pallas_call(functools.partial(attention_back_kernel, row_dev, lay, chu...  40.7 us
    pallas_call x3, Pallas kernels, attend(): pl.pallas_call(functools.partial(attention_kernel, lay, chunk, head_dim),...  31.1 us
    ppermute x29, starting transfers between devices, shift(): return lax.ppermute(values, 'dp', pairs)  29.1 us
    pallas_call x2, Pallas kernels, fc1_back(): pl.pallas_call(functools.partial(fc1_back_kernel, row_dev), name='fc1_bac...  19.1 us
    pallas_call x4, Pallas kernels, add(): pl.pallas_call(functools.partial(chip_sum_kernel, sizes, pairs), name='ch...  16.6 us
    ppermute x12, starting transfers between devices, shift_plane(): return lax.ppermute(values, 'dp', pairs)  16.2 us
    pallas_call x1, Pallas kernels, local(): pl.pallas_call(functools.partial(fc2_back_kernel, row_two), name='fc2_bac...  16 us
    pallas_call x2, Pallas kernels, feed(): pl.pallas_call(functools.partial(fc1_kernel, R // 24), name='fc1', grid=(...  15.8 us
  transfers between devices with their start and end apart: 47, of which 13 were waited for; matrix products, arithmetic and copies ran while one was open for 8% of the time, Pallas kernels for 54%

profile of v2, /device:TPU:0, one launch (start us, length us, event | category | flops | bytes accessed | tf_op | source)
XLA Modules:
  0.0 383.7 jit_solution(13077575567050833636)
XLA Ops:
  40.4 4.9 %all-to-all-done = bf16[32,15,128]{2,1,0:T(8,128)(2,1)S(1)} async-done(((bf16[32,15,128]{2,1,0:T(8,128)(2,1)}), bf16[32,15,128]{2,1,0:T(8,128)(2,1)S(1)}, u32[]{:S(2)}, u32[]{:S(2)}) %all-to-all-start) | async-done | bytes 122912 | tf_op jit(solution)/shard_map/all_to_all | solution.py:817
  46.8 6.1 %first_norm.1 = (bf16[960,768]{1,0:T(8,128)(2,1)}, bf16[960,768]{1,0:T(8,128)(2,1)}) custom-call(s32[11]{0:T(128)} %concatenate.36.meta.place.spot, bf16[882,768]{1,0:T(8,128)(2,1)} %tokens, f32[8,768]{1,0:T(8,128)} %reshape.339.vecs.refs_4_.refs_15_), custom_call_target="tpu_custom_call" | custom-call | flops 1300561920 | bytes 4000000 | tf_op jit(solution)/shard_map/first_norm/pallas_call | solution.py:829
  53.6 11.9 %owner_side.1 = (bf16[1024,512]{1,0:T(8,128)(2,1)}, f32[1792,512]{1,0:T(8,128)}, f32[8,512]{1,0:T(8,128)}) custom-call(bf16[1792,512]{1,0:T(8,128)(2,1)} %cot.1, bf16[128,11]{1,0:T(8,128)(2,1)} %bitcast.112, f32[2,512]{1,0:T(2,128)} %reshape.340.vec_dec), custom_call_target="tpu_custom_call" | custom-call | flops 4000000000 | bytes 8000000 | tf_op jit(solution)/shard_map/owner_side/pallas_call | solution.py:845
  72.2 4.1 %assemble.2 = bf16[32,24,2304]{2,1,0:T(8,128)(2,1)} custom-call(s32[11]{0:T(128)} %concatenate.36.meta.place.spot, bf16[2,2,4,24,1152]{4,3,2,1,0:T(8,128)(2,1)} %copy-done.2, bf16[2,2,4,24,1152]{4,3,2,1,0:T(8,128)(2,1)} %copy-done.3, bf16[2,2,4,24,1152]{4,3,2,1,0:T(8,128)(2,1)} %copy-done.8, bf16[2,2,4,24,1152]{4,3,2,1,0:T(8,128)(2,1)} %copy-done.9), custom_call_target="tpu_custom_call" | custom-call | bytes 7077888 | tf_op jit(solution)/shard_map/assemble/pallas_call | solution.py:154
  76.2 10.3 %attention.3 = (bf16[960,256]{1,0:T(8,128)(2,1)}, bf16[960,256]{1,0:T(8,128)(2,1)}, bf16[960,256]{1,0:T(8,128)(2,1)}, bf16[4,400,400]{2,1,0:T(8,128)(2,1)}, bf16...) custom-call(s32[11]{0:T(128)} %concatenate.36.meta.place.spot, bf16[960,768]{1,0:T(8,128)(2,1)} %get-tuple-element.208.h_in, ...), custom_call_target="tpu_custom_call" | custom-call | flops 3132462080 | bytes 8000000 | tf_op jit(solution)/shard_map/attention/pallas_call | solution.py:873
  86.6 10.4 %attention.4 = (bf16[960,256]{1,0:T(8,128)(2,1)}, bf16[960,256]{1,0:T(8,128)(2,1)}, bf16[960,256]{1,0:T(8,128)(2,1)}, bf16[4,400,400]{2,1,0:T(8,128)(2,1)}, bf16...) custom-call(s32[11]{0:T(128)} %concatenate.36.meta.place.spot, bf16[960,768]{1,0:T(8,128)(2,1)} %get-tuple-element.208.h_in, ...), custom_call_target="tpu_custom_call" | custom-call | flops 3132462080 | bytes 8000000 | tf_op jit(solution)/shard_map/attention/pallas_call | solution.py:873
  99.5 4.2 %all-to-all-start.1 = ((bf16[32,32,512]{2,1,0:T(8,128)(2,1)}), bf16[32,32,512]{2,1,0:T(8,128)(2,1)}, u32[]{:S(2)}, u32[]{:S(2)}) async-start(bf16[32,32,512]{2,1,0:T(8,128)(2,1)} %bitcast.43), calls=%async_computation.1 | async-start | bytes 2097152 | tf_op jit(solution)/shard_map/all_to_all | solution.py:860
  103.7 10.4 %attention.5 = (bf16[960,256]{1,0:T(8,128)(2,1)}, bf16[960,256]{1,0:T(8,128)(2,1)}, bf16[960,256]{1,0:T(8,128)(2,1)}, bf16[4,400,400]{2,1,0:T(8,128)(2,1)}, bf16...) custom-call(s32[11]{0:T(128)} %concatenate.36.meta.place.spot, bf16[960,768]{1,0:T(8,128)(2,1)} %get-tuple-element.208.h_in, ...), custom_call_target="tpu_custom_call" | custom-call | flops 3132462080 | bytes 8000000 | tf_op jit(solution)/shard_map/attention/pallas_call | solution.py:873
  119.3 5.9 %out_projection.1 = (f32[960,768]{1,0:T(8,128)}, bf16[960,768]{1,0:T(8,128)(2,1)}) custom-call(bf16[960,256]{1,0:T(8,128)(2,1)} %get-tuple-element.200.refs_0_, bf16[960,256]{1,0:T(8,128)(2,1)} %get-tuple-element.202.refs_1_, bf16[960,256]{1,0:T(8,128)(2,1)} %get-tuple-element.209.refs_2_, ...), custom_call_target="tpu_custom_call" | custom-call | flops 1132462080 | bytes 9000000 | tf_op jit(solution)/shard_map/out_projection/pallas_call | solution.py:893
  125.2 7.9 %fc1.2 = (bf16[960,1536]{1,0:T(8,128)(2,1)}, bf16[960,1536]{1,0:T(8,128)(2,1)}) custom-call(bf16[960,768]{1,0:T(8,128)(2,1)} %get-tuple-element.223.h_in, bf16[768,4352]{1,0:T(8,128)(2,1)} %all-gather.2.cloned.1.call-done.refs_3_.weight.w_dec.w_dec_more.w_one.w_out, f32[1,3072]{1,0:T(1,128)} %reshape.341.bias), custom_call_target="tpu_custom_call" | custom-call | flops 2264924160 | bytes 10000000 | tf_op jit(solution)/shard_map/fc1/pallas_call | solution.py:908
  139.5 7.9 %fc1.3 = (bf16[960,1536]{1,0:T(8,128)(2,1)}, bf16[960,1536]{1,0:T(8,128)(2,1)}) custom-call(bf16[960,768]{1,0:T(8,128)(2,1)} %get-tuple-element.223.h_in, bf16[768,4352]{1,0:T(8,128)(2,1)} %all-gather.2.cloned.1.call-done.refs_3_.weight.w_dec.w_dec_more.w_one.w_out, f32[1,3072]{1,0:T(1,128)} %reshape.341.bias), custom_call_target="tpu_custom_call" | custom-call | flops 2264924160 | bytes 10000000 | tf_op jit(solution)/shard_map/fc1/pallas_call | solution.py:908
  148.5 4.9 %assemble.3 = bf16[32,96,768]{2,1,0:T(8,128)(2,1)} custom-call(s32[11]{0:T(128)} %concatenate.36.meta.place.spot, bf16[2,2,4,96,384]{4,3,2,1,0:T(8,128)(2,1)} %copy-done, bf16[2,2,4,96,384]{4,3,2,1,0:T(8,128)(2,1)} %copy-done.1, bf16[2,2,4,96,384]{4,3,2,1,0:T(8,128)(2,1)} %collective-permute-done.16.from_a, bf16[2,2,4,96,384]{4,3,2,1,0:T(8,128)(2,1)} %copy-done.5), custom_call_target="tpu_custom_call" | custom-call | bytes 9437184 | tf_op jit(solution)/shard_map/assemble/pallas_call | solution.py:154
  153.4 13.1 %fc2_and_embed.1 = (bf16[960,768]{1,0:T(8,128)(2,1)}, bf16[1024,512]{1,0:T(8,128)(2,1)}) custom-call(bf16[960,1536]{1,0:T(8,128)(2,1)} %get-tuple-element.217.g_one, bf16[960,1536]{1,0:T(8,128)(2,1)} %get-tuple-element.224.g_two, bf16[3072,768]{1,0:T(8,128)(2,1)} %bitcast.81, f32[8,768]{1,0:T(8,128)} %reshape.339.vecs.refs_4_.refs_15_, ...), custom_call_target="tpu_custom_call" | custom-call | flops 6039797760 | bytes 20000000 | tf_op jit(solution)/shard_map/fc2_and_embed/pallas_call | solution.py:926
  166.6 5.2 %all-to-all-start.2 = ((bf16[32,32,512]{2,1,0:T(8,128)(2,1)}), bf16[32,32,512]{2,1,0:T(8,128)(2,1)}, u32[]{:S(2)}, u32[]{:S(2)}) async-start(bf16[32,32,512]{2,1,0:T(8,128)(2,1)} %bitcast.89), calls=%async_computation.2 | async-start | bytes 2097152 | tf_op jit(solution)/shard_map/all_to_all | solution.py:939
  171.8 6.0 %embed_back.1 = (bf16[960,768]{1,0:T(8,128)(2,1)}, bf16[16,24,512]{2,1,0:T(8,128)(2,1)}, bf16[16,24,512]{2,1,0:T(8,128)(2,1)}, f32[1,768]{1,0:T(1,128)}) custom-call(s32[11]{0:T(128)} %concatenate.36.meta.place.spot, bf16[1024,512]{1,0:T(8,128)(2,1)} %bitcast.44.got, s32[1,960]{1,0:T(1,128)} %and_select_fusion.place, ...), custom_call_target="tpu_custom_call" | custom-call | flops 45298483200 | bytes 140000000 | tf_op jit(solution)/shard_map/embed_back/pallas_call | solution.py:945
  177.8 16.0 %fc2_back.1 = (bf16[960,3072]{1,0:T(8,128)(2,1)}, bf16[16,96,768]{2,1,0:T(8,128)(2,1)}, bf16[16,96,768]{2,1,0:T(8,128)(2,1)}, f32[1,3072]{1,0:T(1,128)}) custom-call(s32[11]{0:T(128)} %concatenate.36.meta.place.spot, bf16[960,768]{1,0:T(8,128)(2,1)} %get-tuple-element.233.dy_in, bf16[3072,768]{1,0:T(8,128)(2,1)} %bitcast.82, ...), custom_call_target="tpu_custom_call" | custom-call | flops 181193932800 | bytes 600000000 | tf_op jit(solution)/shard_map/fc2_back/pallas_call | solution.py:962
  194.2 9.5 %fc1_back.2 = (f32[960,768]{1,0:T(8,128)}, bf16[16,24,1536]{2,1,0:T(8,128)(2,1)}, bf16[16,24,1536]{2,1,0:T(8,128)(2,1)}) custom-call(s32[11]{0:T(128)} %concatenate.36.meta.place.spot, bf16[960,3072]{1,0:T(8,128)(2,1)} %get-tuple-element.242.du_in, bf16[768,4352]{1,0:T(8,128)(2,1)} %all-gather.2.cloned.1.call-done.refs_3_.weight.w_dec.w_dec_more.w_one.w_out, ...), custom_call_target="tpu_custom_call" | custom-call | flops 90596966400 | bytes 300000000 | tf_op jit(solution)/shard_map/fc1_back/pallas_call | solution.py:981
  207.1 4.6 %chip_sum.4 = (bf16[4,96,768]{2,1,0:T(8,128)(2,1)}, bf16[4,96,768]{2,1,0:T(8,128)(2,1)}, bf16[4,96,768]{2,1,0:T(8,128)(2,1)}, bf16[4,96,768]{2,1,0:T(8,128)(2,1)}) custom-call(s32[11]{0:T(128)} %concatenate.36.meta.place.spot, bf16[16,96,768]{2,1,0:T(8,128)(2,1)} %get-tuple-element.238.refs_0_, bf16[16,96,768]{2,1,0:T(8,128)(2,1)} %copy-done.4), custom_call_target="tpu_custom_call" | custom-call | bytes 7077888 | tf_op jit(solution)/shard_map/chip_sum/pallas_call | solution.py:212
  214.8 9.5 %fc1_back.3 = (f32[960,768]{1,0:T(8,128)}, bf16[16,24,1536]{2,1,0:T(8,128)(2,1)}, bf16[16,24,1536]{2,1,0:T(8,128)(2,1)}) custom-call(s32[11]{0:T(128)} %concatenate.36.meta.place.spot, bf16[960,3072]{1,0:T(8,128)(2,1)} %get-tuple-element.242.du_in, bf16[768,4352]{1,0:T(8,128)(2,1)} %all-gather.2.cloned.1.call-done.refs_3_.weight.w_dec.w_dec_more.w_one.w_out, ...), custom_call_target="tpu_custom_call" | custom-call | flops 90596966400 | bytes 300000000 | tf_op jit(solution)/shard_map/fc1_back/pallas_call | solution.py:981
  231.6 12.2 %out_back.1 = (f32[960,768]{1,0:T(8,128)}, bf16[960,768]{1,0:T(8,128)(2,1)}, bf16[16,24,768]{2,1,0:T(8,128)(2,1)}, bf16[16,24,768]{2,1,0:T(8,128)(2,1)}, f32[8,768]{1,0:T(8,128)}) custom-call(s32[11]{0:T(128)} %concatenate.36.meta.place.spot, f32[960,768]{1,0:T(8,128)} %get-tuple-element.237.dh_one, f32[960,768]{1,0:T(8,128)} %get-tuple-element.246.dh_two, ...), custom_call_target="tpu_custom_call" | custom-call | flops 45298483200 | bytes 400000000 | tf_op jit(solution)/shard_map/out_back/pallas_call | solution.py:1003
  248.4 4.7 %chip_sum.5 = (bf16[4,24,3584]{2,1,0:T(8,128)(2,1)}, bf16[4,24,3584]{2,1,0:T(8,128)(2,1)}, bf16[4,24,3584]{2,1,0:T(8,128)(2,1)}, bf16[4,24,3584]{2,1,0:T(8,128)(2,1)}) custom-call(s32[11]{0:T(128)} %concatenate.36.meta.place.spot, bf16[16,24,1536]{2,1,0:T(8,128)(2,1)} %get-tuple-element.258.refs_0_, bf16[16,24,1536]{2,1,0:T(8,128)(2,1)} %get-tuple-element.259.refs_1_, ...), custom_call_target="tpu_custom_call" | custom-call | bytes 8257536 | tf_op jit(solution)/shard_map/chip_sum/pallas_call | solution.py:212
  255.1 13.6 %attention_back.3 = (bf16[960,256]{1,0:T(8,128)(2,1)}, bf16[960,256]{1,0:T(8,128)(2,1)}, bf16[960,256]{1,0:T(8,128)(2,1)}, bf16[16,24,768]{2,1,0:T(8,128)(2,1)},...) custom-call(s32[11]{0:T(128)} %concatenate.36.meta.place.spot, bf16[960,768]{1,0:T(8,128)(2,1)} %get-tuple-element.208.h_in, ...), custom_call_target="tpu_custom_call" | custom-call | flops 82649243648 | bytes 200000000 | tf_op jit(solution)/shard_map/attention_back/pallas_call | solution.py:1022
  273.6 13.6 %attention_back.4 = (bf16[960,256]{1,0:T(8,128)(2,1)}, bf16[960,256]{1,0:T(8,128)(2,1)}, bf16[960,256]{1,0:T(8,128)(2,1)}, bf16[16,24,768]{2,1,0:T(8,128)(2,1)},...) custom-call(s32[11]{0:T(128)} %concatenate.36.meta.place.spot, bf16[960,768]{1,0:T(8,128)(2,1)} %get-tuple-element.208.h_in, ...), custom_call_target="tpu_custom_call" | custom-call | flops 82649243648 | bytes 200000000 | tf_op jit(solution)/shard_map/attention_back/pallas_call | solution.py:1022
  289.4 3.8 chip_sum.6
  293.2 4.2 %plane_sum.2 = bf16[4,24,6656]{2,1,0:T(8,128)(2,1)} custom-call(s32[11]{0:T(128)} %concatenate.36.meta.place.spot, bf16[4,96,768]{2,1,0:T(8,128)(2,1)} %get-tuple-element.291.refs_0_, bf16[4,96,768]{2,1,0:T(8,128)(2,1)} %copy-done.13, bf16[4,96,768]{2,1,0:T(8,128)(2,1)} %copy-done.14, bf16[4,96,768]{2,1,0:T(8,128)(2,1)} %copy-done.15, ...), custom_call_target="tpu_custom_call" | custom-call | bytes 5111808 | tf_op jit(solution)/shard_map/plane_sum/pallas_call | solution.py:266
  300.4 4.6 %all-to-all-start.3 = ((bf16[4,24,6656]{2,1,0:T(8,128)(2,1)}), bf16[4,24,6656]{2,1,0:T(8,128)(2,1)S(1)}, u32[]{:S(2)}, u32[]{:S(2)}) async-start(bf16[4,24,6656]{2,1,0:T(8,128)(2,1)} %plane_sum.2), calls=%async_computation.3 | async-start | bytes 2555904 | tf_op jit(solution)/shard_map/all_to_all | solution.py:278
  305.0 13.5 %attention_back.5 = (bf16[960,256]{1,0:T(8,128)(2,1)}, bf16[960,256]{1,0:T(8,128)(2,1)}, bf16[960,256]{1,0:T(8,128)(2,1)}, bf16[16,24,768]{2,1,0:T(8,128)(2,1)},...) custom-call(s32[11]{0:T(128)} %concatenate.36.meta.place.spot, bf16[960,768]{1,0:T(8,128)(2,1)} %get-tuple-element.208.h_in, ...), custom_call_target="tpu_custom_call" | custom-call | flops 82649243648 | bytes 200000000 | tf_op jit(solution)/shard_map/attention_back/pallas_call | solution.py:1022
  319.2 7.7 %decode.1 = bf16[1792,512]{1,0:T(8,128)(2,1)} custom-call(bf16[1024,512]{1,0:T(8,128)(2,1)} %bitcast.53.got, bf16[128,11]{1,0:T(8,128)(2,1)} %bitcast.113, f32[1792,512]{1,0:T(8,128)} %get-tuple-element.304.base), custom_call_target="tpu_custom_call" | custom-call | flops 20000000000 | bytes 140000000 | tf_op jit(solution)/shard_map/decode/pallas_call | solution.py:1051
  336.8 11.6 %first_back.1 = (bf16[882,768]{1,0:T(8,128)(2,1)}, f32[8,768]{1,0:T(8,128)}) custom-call(s32[11]{0:T(128)} %concatenate.36.meta.place.spot, bf16[960,256]{1,0:T(8,128)(2,1)} %get-tuple-element.275.refs_0_, bf16[960,256]{1,0:T(8,128)(2,1)} %get-tuple-element.279.refs_1_, bf16[960,256]{1,0:T(8,128)(2,1)} %get-tuple-element.300.refs_2_, ...), custom_call_target="tpu_custom_call" | custom-call | flops 93958963200 | bytes 400000000 | tf_op jit(solution)/shard_map/first_back/pallas_call | solution.py:1065
  353.8 4.3 %all-to-all-start.4 = ((f32[32,1,320]{2,1,0:T(1,128)}), f32[32,1,320]{2,1,0:T(1,128)S(1)}, u32[]{:S(2)}, u32[]{:S(2)}) async-start(f32[32,1,320]{2,1,0:T(1,128)} %copy.61), calls=%async_computation.4 | async-start | bytes 98304 | tf_op jit(solution)/shard_map/all_to_all | solution.py:1088
  358.1 3.7 collective-permute-start.40
  367.4 8.3 %collective-permute-done.39 = bf16[24,3072]{1,0:T(8,128)(2,1)S(1)} collective-permute-done((bf16[24,3072]{1,0:T(8,128)(2,1)}, bf16[24,3072]{1,0:T(8,128)(2,1)S(1)}, u32[]{:S(2)}, u32[]{:S(2)}) %collective-permute-start.39) | collective-permute-done | bytes 147488 | tf_op jit(solution)/shard_map/ppermute | solution.py:36
  (259 shorter events, 109.3 us)
Async XLA Ops:
  7.2 112.1 %all-gather.2.cloned.1.call-start = ((), (), s32[]{:S(2)}) async-start(), calls=%async_computation.5 | async-start | bytes 6893568 | tf_op jit(solution)/shard_map/all_gather | solution.py:771
  8.9 20.3 %collective-permute-start = (bf16[24,2304]{1,0:T(8,128)(2,1)}, bf16[24,2304]{1,0:T(8,128)(2,1)S(1)}, u32[]{:S(2)}, u32[]{:S(2)}) collective-permute-start(bf16[24,2304]{1,0:T(8,128)(2,1)} %param.25), channel_id=1, source_target_pairs={{0,8},{1,9},{2,10},{3,11},{4,12},{5,13},{6,14},{7,15},{8,16},{9,17... | collective-permute-start | bytes 331784 | tf_op jit(solution)/shard_map/ppermute | solution.py:36
  12.0 17.2 %collective-permute-start.1 = (bf16[24,2304]{1,0:T(8,128)(2,1)}, bf16[24,2304]{1,0:T(8,128)(2,1)S(1)}, u32[]{:S(2)}, u32[]{:S(2)}) collective-permute-start(bf16[24,2304]{1,0:T(8,128)(2,1)} %param.25), channel_id=1, source_target_pairs={{0,16},{1,17},{2,18},{3,19},{4,20},{5,21},{6,22},{7,23},{8,24},{9,... | collective-permute-start | bytes 331784 | tf_op jit(solution)/shard_map/ppermute | solution.py:36
  14.6 14.6 %collective-permute-start.2 = (bf16[24,2304]{1,0:T(8,128)(2,1)}, bf16[24,2304]{1,0:T(8,128)(2,1)S(1)}, u32[]{:S(2)}, u32[]{:S(2)}) collective-permute-start(bf16[24,2304]{1,0:T(8,128)(2,1)} %param.25), channel_id=1, source_target_pairs={{0,24},{1,25},{2,26},{3,27},{4,28},{5,29},{6,30},{7,31},{8,0},{9,1... | collective-permute-start | bytes 331784 | tf_op jit(solution)/shard_map/ppermute | solution.py:36
  37.8 27.6 %collective-permute-start.5 = (bf16[2,4,24,1152]{3,2,1,0:T(8,128)(2,1)S(1)}, bf16[2,4,24,1152]{3,2,1,0:T(8,128)(2,1)S(1)}, u32[]{:S(2)}, u32[]{:S(2)}) collective-permute-start(bf16[2,4,24,1152]{3,2,1,0:T(8,128)(2,1)S(1)} %pad_maximum_fusion.8), channel_id=1, source_target_pairs={{0,4},{1,5},{2,6},{3,7},{4,0},{5,1},{6,2},{7,3},{8,12},{9,13},{10,... | collective-permute-start | bytes 1327112 | tf_op jit(solution)/shard_map/ppermute | solution.py:36
  39.5 26.0 %collective-permute-start.6 = (bf16[2,4,24,1152]{3,2,1,0:T(8,128)(2,1)S(1)}, bf16[2,4,24,1152]{3,2,1,0:T(8,128)(2,1)S(1)}, u32[]{:S(2)}, u32[]{:S(2)}) collective-permute-start(bf16[2,4,24,1152]{3,2,1,0:T(8,128)(2,1)S(1)} %pad_maximum_fusion.9), channel_id=1, source_target_pairs={{0,2},{1,3},{2,0},{3,1},{4,6},{5,7},{6,4},{7,5},{8,10},{9,11},{10,... | collective-permute-start | bytes 1327112 | tf_op jit(solution)/shard_map/ppermute | solution.py:36
  66.3 30.7 %collective-permute-start.9 = (bf16[96,768]{1,0:T(8,128)(2,1)}, bf16[96,768]{1,0:T(8,128)(2,1)S(1)}, u32[]{:S(2)}, u32[]{:S(2)}) collective-permute-start(bf16[96,768]{1,0:T(8,128)(2,1)} %param.34), channel_id=1, source_target_pairs={{0,8},{1,9},{2,10},{3,11},{4,12},{5,13},{6,14},{7,15},{8,16},{9,17... | collective-permute-start | bytes 442376 | tf_op jit(solution)/shard_map/ppermute | solution.py:36
  67.0 30.0 %collective-permute-start.10 = (bf16[96,768]{1,0:T(8,128)(2,1)}, bf16[96,768]{1,0:T(8,128)(2,1)S(1)}, u32[]{:S(2)}, u32[]{:S(2)}) collective-permute-start(bf16[96,768]{1,0:T(8,128)(2,1)} %param.34), channel_id=1, source_target_pairs={{0,16},{1,17},{2,18},{3,19},{4,20},{5,21},{6,22},{7,23},{8,24},{9,... | collective-permute-start | bytes 442376 | tf_op jit(solution)/shard_map/ppermute | solution.py:36
  68.2 28.8 %collective-permute-start.11 = (bf16[96,768]{1,0:T(8,128)(2,1)}, bf16[96,768]{1,0:T(8,128)(2,1)S(1)}, u32[]{:S(2)}, u32[]{:S(2)}) collective-permute-start(bf16[96,768]{1,0:T(8,128)(2,1)} %param.34), channel_id=1, source_target_pairs={{0,24},{1,25},{2,26},{3,27},{4,28},{5,29},{6,30},{7,31},{8,0},{9,1... | collective-permute-start | bytes 442376 | tf_op jit(solution)/shard_map/ppermute | solution.py:36
  98.1 16.1 %collective-permute-start.12 = (bf16[4,96,384]{2,1,0:T(8,128)(2,1)S(1)}, bf16[4,96,384]{2,1,0:T(8,128)(2,1)S(1)}, u32[]{:S(2)}, u32[]{:S(2)}) collective-permute-start(bf16[4,96,384]{2,1,0:T(8,128)(2,1)S(1)} %get-tuple-element.211), channel_id=1, source_target_pairs={{0,2},{1,3},{2,0},{3,1},{4,6},{5,7},{6,4},{7,5},{8,10},{9,11},{10,... | collective-permute-start | bytes 884744 | tf_op jit(solution)/shard_map/ppermute | solution.py:36
  98.4 15.7 %collective-permute-start.13 = (bf16[4,96,384]{2,1,0:T(8,128)(2,1)S(1)}, bf16[4,96,384]{2,1,0:T(8,128)(2,1)S(1)}, u32[]{:S(2)}, u32[]{:S(2)}) collective-permute-start(bf16[4,96,384]{2,1,0:T(8,128)(2,1)S(1)} %get-tuple-element.213), channel_id=1, source_target_pairs={{0,4},{1,5},{2,6},{3,7},{4,0},{5,1},{6,2},{7,3},{8,12},{9,13},{10,... | collective-permute-start | bytes 884744 | tf_op jit(solution)/shard_map/ppermute | solution.py:36
  99.5 40.0 %all-to-all-start.1 = ((bf16[32,32,512]{2,1,0:T(8,128)(2,1)}), bf16[32,32,512]{2,1,0:T(8,128)(2,1)}, u32[]{:S(2)}, u32[]{:S(2)}) async-start(bf16[32,32,512]{2,1,0:T(8,128)(2,1)} %bitcast.43), calls=%async_computation.1 | async-start | bytes 2097152 | tf_op jit(solution)/shard_map/all_to_all | solution.py:860
  114.2 19.6 %collective-permute-start.14 = (bf16[2,4,96,384]{3,2,1,0:T(8,128)(2,1)S(1)}, bf16[2,4,96,384]{3,2,1,0:T(8,128)(2,1)S(1)}, u32[]{:S(2)}, u32[]{:S(2)}) collective-permute-start(bf16[2,4,96,384]{3,2,1,0:T(8,128)(2,1)S(1)} %pad_maximum_fusion.5), channel_id=1, source_target_pairs={{0,4},{1,5},{2,6},{3,7},{4,0},{5,1},{6,2},{7,3},{8,12},{9,13},{10,... | collective-permute-start | bytes 1769480 | tf_op jit(solution)/shard_map/ppermute | solution.py:36
  116.2 17.7 %collective-permute-start.15 = (bf16[2,4,96,384]{3,2,1,0:T(8,128)(2,1)S(1)}, bf16[2,4,96,384]{3,2,1,0:T(8,128)(2,1)S(1)}, u32[]{:S(2)}, u32[]{:S(2)}) collective-permute-start(bf16[2,4,96,384]{3,2,1,0:T(8,128)(2,1)S(1)} %pad_maximum_fusion.6), channel_id=1, source_target_pairs={{0,2},{1,3},{2,0},{3,1},{4,6},{5,7},{6,4},{7,5},{8,10},{9,11},{10,... | collective-permute-start | bytes 1769480 | tf_op jit(solution)/shard_map/ppermute | solution.py:36
  166.6 133.8 %all-to-all-start.2 = ((bf16[32,32,512]{2,1,0:T(8,128)(2,1)}), bf16[32,32,512]{2,1,0:T(8,128)(2,1)}, u32[]{:S(2)}, u32[]{:S(2)}) async-start(bf16[32,32,512]{2,1,0:T(8,128)(2,1)} %bitcast.89), calls=%async_computation.2 | async-start | bytes 2097152 | tf_op jit(solution)/shard_map/all_to_all | solution.py:939
  211.6 15.7 %collective-permute-start.19 = (bf16[4,96,768]{2,1,0:T(8,128)(2,1)}, bf16[4,96,768]{2,1,0:T(8,128)(2,1)S(1)}, u32[]{:S(2)}, u32[]{:S(2)}) collective-permute-start(bf16[4,96,768]{2,1,0:T(8,128)(2,1)} %get-tuple-element.244), channel_id=1, source_target_pairs={{0,2},{1,3},{2,0},{3,1},{4,6},{5,7},{6,4},{7,5},{8,10},{9,11},{10,... | collective-permute-start | bytes 1769480 | tf_op jit(solution)/shard_map/ppermute | solution.py:50
  213.3 15.5 %collective-permute-start.20 = (bf16[4,96,768]{2,1,0:T(8,128)(2,1)}, bf16[4,96,768]{2,1,0:T(8,128)(2,1)S(1)}, u32[]{:S(2)}, u32[]{:S(2)}) collective-permute-start(bf16[4,96,768]{2,1,0:T(8,128)(2,1)} %get-tuple-element.245), channel_id=1, source_target_pairs={{0,4},{1,5},{2,6},{3,7},{4,0},{5,1},{6,2},{7,3},{8,12},{9,13},{10,... | collective-permute-start | bytes 1769480 | tf_op jit(solution)/shard_map/ppermute | solution.py:50
  229.7 17.2 %collective-permute-start.21 = (bf16[16,24,1536]{2,1,0:T(8,128)(2,1)}, bf16[16,24,1536]{2,1,0:T(8,128)(2,1)S(1)}, u32[]{:S(2)}, u32[]{:S(2)}) collective-permute-start(bf16[16,24,1536]{2,1,0:T(8,128)(2,1)} %get-tuple-element.264), channel_id=1, source_target_pairs={{0,1},{1,0},{2,3},{3,2},{4,5},{5,4},{6,7},{7,6},{8,9},{9,8},{10,11... | collective-permute-start | bytes 3538952 | tf_op jit(solution)/shard_map/ppermute | solution.py:36
  229.7 17.2 %collective-permute-start.22 = (bf16[16,24,1536]{2,1,0:T(8,128)(2,1)}, bf16[16,24,1536]{2,1,0:T(8,128)(2,1)S(1)}, u32[]{:S(2)}, u32[]{:S(2)}) collective-permute-start(bf16[16,24,1536]{2,1,0:T(8,128)(2,1)} %get-tuple-element.265), channel_id=1, source_target_pairs={{0,1},{1,0},{2,3},{3,2},{4,5},{5,4},{6,7},{7,6},{8,9},{9,8},{10,11... | collective-permute-start | bytes 3538952 | tf_op jit(solution)/shard_map/ppermute | solution.py:36
  230.2 16.6 %collective-permute-start.24 = (bf16[4,96,768]{2,1,0:T(8,128)(2,1)S(1)}, bf16[4,96,768]{2,1,0:T(8,128)(2,1)S(1)}, u32[]{:S(2)}, u32[]{:S(2)}) collective-permute-start(bf16[4,96,768]{2,1,0:T(8,128)(2,1)S(1)} %copy-done.37), channel_id=1, source_target_pairs={{0,6},{1,7},{2,4},{3,5},{4,2},{5,3},{6,0},{7,1},{8,14},{9,15},{10,... | collective-permute-start | bytes 1769480 | tf_op jit(solution)/shard_map/ppermute | solution.py:50
  253.1 17.3 %collective-permute-start.25 = (bf16[4,24,3584]{2,1,0:T(8,128)(2,1)}, bf16[4,24,3584]{2,1,0:T(8,128)(2,1)S(1)}, u32[]{:S(2)}, u32[]{:S(2)}) collective-permute-start(bf16[4,24,3584]{2,1,0:T(8,128)(2,1)} %get-tuple-element.276), channel_id=1, source_target_pairs={{0,2},{1,3},{2,0},{3,1},{4,6},{5,7},{6,4},{7,5},{8,10},{9,11},{10,... | collective-permute-start | bytes 2064392 | tf_op jit(solution)/shard_map/ppermute | solution.py:50
  253.6 17.0 %collective-permute-start.26 = (bf16[4,24,3584]{2,1,0:T(8,128)(2,1)}, bf16[4,24,3584]{2,1,0:T(8,128)(2,1)S(1)}, u32[]{:S(2)}, u32[]{:S(2)}) collective-permute-start(bf16[4,24,3584]{2,1,0:T(8,128)(2,1)} %get-tuple-element.277), channel_id=1, source_target_pairs={{0,4},{1,5},{2,6},{3,7},{4,0},{5,1},{6,2},{7,3},{8,12},{9,13},{10,... | collective-permute-start | bytes 2064392 | tf_op jit(solution)/shard_map/ppermute | solution.py:50
  270.6 16.6 %collective-permute-start.27 = (bf16[16,24,768]{2,1,0:T(8,128)(2,1)}, bf16[16,24,768]{2,1,0:T(8,128)(2,1)S(1)}, u32[]{:S(2)}, u32[]{:S(2)}) collective-permute-start(bf16[16,24,768]{2,1,0:T(8,128)(2,1)} %get-tuple-element.284), channel_id=1, source_target_pairs={{0,1},{1,0},{2,3},{3,2},{4,5},{5,4},{6,7},{7,6},{8,9},{9,8},{10,11... | collective-permute-start | bytes 1769480 | tf_op jit(solution)/shard_map/ppermute | solution.py:36
  270.6 16.6 %collective-permute-start.28 = (bf16[16,24,768]{2,1,0:T(8,128)(2,1)}, bf16[16,24,768]{2,1,0:T(8,128)(2,1)S(1)}, u32[]{:S(2)}, u32[]{:S(2)}) collective-permute-start(bf16[16,24,768]{2,1,0:T(8,128)(2,1)} %get-tuple-element.285), channel_id=1, source_target_pairs={{0,1},{1,0},{2,3},{3,2},{4,5},{5,4},{6,7},{7,6},{8,9},{9,8},{10,11... | collective-permute-start | bytes 1769480 | tf_op jit(solution)/shard_map/ppermute | solution.py:36
  271.1 18.2 %collective-permute-start.29 = (bf16[4,24,3584]{2,1,0:T(8,128)(2,1)S(1)}, bf16[4,24,3584]{2,1,0:T(8,128)(2,1)S(1)}, u32[]{:S(2)}, u32[]{:S(2)}) collective-permute-start(bf16[4,24,3584]{2,1,0:T(8,128)(2,1)S(1)} %copy-done.35), channel_id=1, source_target_pairs={{0,6},{1,7},{2,4},{3,5},{4,2},{5,3},{6,0},{7,1},{8,14},{9,15},{10,... | collective-permute-start | bytes 2064392 | tf_op jit(solution)/shard_map/ppermute | solution.py:50
  297.4 21.2 %collective-permute-start.30 = (bf16[4,24,1536]{2,1,0:T(8,128)(2,1)}, bf16[4,24,1536]{2,1,0:T(8,128)(2,1)S(1)}, u32[]{:S(2)}, u32[]{:S(2)}) collective-permute-start(bf16[4,24,1536]{2,1,0:T(8,128)(2,1)} %get-tuple-element.301), channel_id=1, source_target_pairs={{0,2},{1,3},{2,0},{3,1},{4,6},{5,7},{6,4},{7,5},{8,10},{9,11},{10,... | collective-permute-start | bytes 884744 | tf_op jit(solution)/shard_map/ppermute | solution.py:50
  298.9 19.6 %collective-permute-start.31 = (bf16[4,24,1536]{2,1,0:T(8,128)(2,1)S(1)}, bf16[4,24,1536]{2,1,0:T(8,128)(2,1)S(1)}, u32[]{:S(2)}, u32[]{:S(2)}) collective-permute-start(bf16[4,24,1536]{2,1,0:T(8,128)(2,1)S(1)} %copy-done.39), channel_id=1, source_target_pairs={{0,4},{1,5},{2,6},{3,7},{4,0},{5,1},{6,2},{7,3},{8,12},{9,13},{10,... | collective-permute-start | bytes 884744 | tf_op jit(solution)/shard_map/ppermute | solution.py:50
  300.4 18.8 %collective-permute-start.32 = (bf16[16,24,768]{2,1,0:T(8,128)(2,1)S(1)}, bf16[16,24,768]{2,1,0:T(8,128)(2,1)S(1)}, u32[]{:S(2)}, u32[]{:S(2)}) collective-permute-start(bf16[16,24,768]{2,1,0:T(8,128)(2,1)S(1)} %copy-done.36), channel_id=1, source_target_pairs={{0,1},{1,0},{2,3},{3,2},{4,5},{5,4},{6,7},{7,6},{8,9},{9,8},{10,11... | collective-permute-start | bytes 1769480 | tf_op jit(solution)/shard_map/ppermute | solution.py:36
  300.4 36.2 %all-to-all-start.3 = ((bf16[4,24,6656]{2,1,0:T(8,128)(2,1)}), bf16[4,24,6656]{2,1,0:T(8,128)(2,1)S(1)}, u32[]{:S(2)}, u32[]{:S(2)}) async-start(bf16[4,24,6656]{2,1,0:T(8,128)(2,1)} %plane_sum.2), calls=%async_computation.3 | async-start | bytes 2555904 | tf_op jit(solution)/shard_map/all_to_all | solution.py:278
  333.1 16.4 %collective-permute-start.35 = (bf16[4,24,1536]{2,1,0:T(8,128)(2,1)}, bf16[4,24,1536]{2,1,0:T(8,128)(2,1)S(1)}, u32[]{:S(2)}, u32[]{:S(2)}) collective-permute-start(bf16[4,24,1536]{2,1,0:T(8,128)(2,1)} %get-tuple-element.332), channel_id=1, source_target_pairs={{0,2},{1,3},{2,0},{3,1},{4,6},{5,7},{6,4},{7,5},{8,10},{9,11},{10,... | collective-permute-start | bytes 884744 | tf_op jit(solution)/shard_map/ppermute | solution.py:50
  333.7 15.9 %collective-permute-start.36 = (bf16[4,24,1536]{2,1,0:T(8,128)(2,1)}, bf16[4,24,1536]{2,1,0:T(8,128)(2,1)S(1)}, u32[]{:S(2)}, u32[]{:S(2)}) collective-permute-start(bf16[4,24,1536]{2,1,0:T(8,128)(2,1)} %get-tuple-element.333), channel_id=1, source_target_pairs={{0,4},{1,5},{2,6},{3,7},{4,0},{5,1},{6,2},{7,3},{8,12},{9,13},{10,... | collective-permute-start | bytes 884744 | tf_op jit(solution)/shard_map/ppermute | solution.py:50
  334.4 15.2 %collective-permute-start.37 = (bf16[4,24,1536]{2,1,0:T(8,128)(2,1)}, bf16[4,24,1536]{2,1,0:T(8,128)(2,1)S(1)}, u32[]{:S(2)}, u32[]{:S(2)}) collective-permute-start(bf16[4,24,1536]{2,1,0:T(8,128)(2,1)} %get-tuple-element.334), channel_id=1, source_target_pairs={{0,6},{1,7},{2,4},{3,5},{4,2},{5,3},{6,0},{7,1},{8,14},{9,15},{10,... | collective-permute-start | bytes 884744 | tf_op jit(solution)/shard_map/ppermute | solution.py:50
  (55 other events, 453.8 us)
Sparse Core Ops, SparseCore 0:
  11.5 89.3 all-gather.1

commit v3 on v2

--- a/solution.py
+++ b/solution.py
@@ -84,22 +84,20 @@
 
 
 def assemble_kernel(sizes, widths, place, part_a, part_b, from_a, from_b, *outs):
-    nz, ny, nx = sizes
-    own_z, own_y, own_x, own_c = place[0], place[1], place[2], place[3]
-    for kz in range(nz):
-        at_z = lax.rem(own_z - kz + nz, nz)
-        for ky in range(ny):
-            at_y = lax.rem(own_y - ky + ny, ny)
-            for kx in range(nx):
-                at_x = lax.rem(own_x - kx + nx, nx)
-                chip = (at_z * ny + at_y) * nx + at_x
-                for core, left, right in ((own_c, part_a, part_b), (1 - own_c, from_a, from_b)):
-                    row, start = chip * 2 + core, 0
-                    for out, width in zip(outs, widths):
-                        half = width // 2
-                        out[row, :, :half] = left[ky, kx, kz, :, start : start + half]
-                        out[row, :, half:] = right[kx, ky, kz, :, start : start + half]
-                        start += half
+    _, ny, nx = sizes
+    own_y, own_x, own_c = place[1], place[2], place[3]
+    for ky in range(ny):
+        at_y = lax.rem(own_y - ky + ny, ny)
+        for kx in range(nx):
+            at_x = lax.rem(own_x - kx + nx, nx)
+            chip = at_y * nx + at_x
+            for core, left, right in ((own_c, part_a, part_b), (1 - own_c, from_a, from_b)):
+                row, start = chip * 2 + core, 0
+                for out, width in zip(outs, widths):
+                    half = width // 2
+                    out[0, row, :, :half] = left[ky, kx, 0, :, start : start + half]
+                    out[0, row, :, half:] = right[kx, ky, 0, :, start : start + half]
+                    start += half
 
 
 def held(values, *others):
@@ -147,19 +145,30 @@
         self.from_b = self.dev.shift(self.part_b, "c", 1)
         return [self.from_a, self.from_b]
 
-    def result(self, place):
+    def result(self, place, *after):
         dev, rows = self.dev, self.rows
-        sizes = (dev.size["z"], dev.size["y"], dev.size["x"])
+        nz, ny, nx = sizes = (dev.size["z"], dev.size["y"], dev.size["x"])
         kind = self.local.dtype
+        from_a, from_b = held((self.from_a, self.from_b), *after)
+        part = pl.BlockSpec((ny, nx, 1, rows, self.half), lambda k, _: (0, 0, k, 0, 0))
         outs = pl.pallas_call(
             functools.partial(assemble_kernel, sizes, self.widths),
             name="assemble",
-            out_shape=[jax.ShapeDtypeStruct((dev.count, rows, w), kind) for w in self.widths],
-            in_specs=[SMEM] + [VMEM] * 4,
-            out_specs=[VMEM] * len(self.widths),
+            grid_spec=pltpu.PrefetchScalarGridSpec(
+                num_scalar_prefetch=1,
+                grid=(nz,),
+                in_specs=[part] * 4,
+                out_specs=[
+                    pl.BlockSpec(
+                        (1, 2 * ny * nx, rows, w), lambda k, at: (lax.rem(at[0] - k + nz, nz), 0, 0, 0)
+                    )
+                    for w in self.widths
+                ],
+            ),
+            out_shape=[jax.ShapeDtypeStruct((nz, 2 * ny * nx, rows, w), kind) for w in self.widths],
             compiler_params=params(),
             cost_estimate=cost(0, 4 * dev.count * rows * sum(self.widths)),
-        )(place, self.part_a, self.part_b, self.from_a, self.from_b)
+        )(place, self.part_a, self.part_b, from_a, from_b)
         return [o.reshape(dev.count * rows, w) for o, w in zip(outs, self.widths)]
 
 
@@ -175,8 +184,7 @@
                 for own, got in zip(owns, gots):
                     width = own.shape[-1]
                     chip = z * ny * nx + at
-                    total = own[chip].astype(F32) + got[chip].astype(F32)
-                    outs[ky * nx + kx][z, :, start : start + width] = total.astype(BF)
+                    outs[ky * nx + kx][z, :, start : start + width] = own[chip] + got[chip]
                     start += width
 
 
@@ -301,6 +309,47 @@
     return out
 
 
+def last_sums_kernel(moves, *refs):
+    terms, outs = refs[:-2], refs[-2:]
+    for start, width, out, at in moves:
+        total = terms[0][:, start : start + width].astype(F32)
+        for term in terms[1:]:
+            total += term[:, start : start + width].astype(F32)
+        outs[out][:, at : at + width] = total
+
+
+def last_sums(arrived, scatters, model, head_cols):
+    rows, width = arrived[0].shape
+    moves, start, first = [], 0, True
+    part = -1
+    for s in scatters:
+        tiles, span = [w // s.steps for w in s.widths], sum(s.widths) // s.steps
+        for t, tile in enumerate(tiles):
+            part = part if first else part + 1
+            for i in range(s.steps):
+                source = start + i * span + sum(tiles[:t])
+                if first:
+                    moves.append((source, tile, 0, i * tile))
+                    continue
+                piece = min(tile, head_cols)
+                for k in range(0, tile, piece):
+                    block, inside = divmod(i * tile + k, head_cols)
+                    moves.append((source + k, piece, 1, block * model + part * head_cols + inside))
+            if first:
+                part, first = -1, False
+        start += sum(s.widths)
+    shapes = [(rows, model), (rows, 3 * model)]
+    return pl.pallas_call(
+        functools.partial(last_sums_kernel, moves),
+        name="last_sums",
+        grid=(1,),
+        in_specs=[whole((rows, width))] * len(arrived),
+        out_specs=[whole(v) for v in shapes],
+        out_shape=[jax.ShapeDtypeStruct(v, F32) for v in shapes],
+        compiler_params=params(),
+    )(*arrived)
+
+
 def split_cores(value, rows, core, own, sent):
     if rows % 8 == 0:
         parts = value.reshape(-1, 2, rows, value.shape[1])
@@ -373,29 +422,6 @@
         window, slot, real = self.rows_of(row, big)
         return jnp.where(real, window * self.slots + slot, -1)
 
-    def place(self, big, count_vec, bucket, lane_slots):
-        row = jnp.arange(self.rows, dtype=jnp.int32)
-        window, slot, real = self.rows_of(row, big)
-        in_large = row < self.large_pad
-        small_id = jnp.maximum(row - self.large_pad, 0) // self.small_pad
-        image = jnp.where(in_large, big, small_id + jnp.where(small_id >= big, 1, 0))
-        kept = jnp.sum(
-            jnp.where(
-                image[:, None] == jnp.arange(self.images, dtype=jnp.int32)[None, :],
-                count_vec[None, :],
-                0,
-            ),
-            axis=1,
-        )
-        windows = bucket.shape[0]
-        target = jnp.sum(
-            jnp.where(
-                window[:, None] == jnp.arange(windows, dtype=jnp.int32)[None, :], bucket[None, :], 0
-            ),
-            axis=1,
-        )
-        return jnp.where(real & (slot < kept), target * lane_slots + slot, -1)
-
     def key_mask(self, size, real, kept):
         lane = lax.broadcasted_iota(jnp.int32, (1, size), 1)
         live = (lane < real) & (lane % self.slots < kept)
@@ -403,6 +429,67 @@
 
 
 LANE_SLOTS = 8
+BIG, KEPT = 4, 5
+FIELDS = 4
+
+
+def describe_kernel(lay, dims, per_peer, index, counts, sides, owner_in, offsets_in,
+                    meta, place_out, info_out, owners, cells):
+    images, slots = lay.images, lay.slots
+    windows, padded = offsets_in.shape[0], owners.shape[1]
+    _, ny, nx = dims
+    me = index[0]
+    meta[0] = me // (2 * nx * ny)
+    meta[1] = (me // (2 * nx)) % ny
+    meta[2] = (me // 2) % nx
+    meta[3] = me % 2
+    big, kept_big = jnp.int32(0), jnp.int32(0)
+    for i in range(images):
+        big += i * sides[i]
+        kept_big += sides[i] * counts[i]
+    meta[BIG] = big
+    meta[KEPT] = kept_big
+    for i in range(images - 1):
+        meta[KEPT + 1 + i] = jnp.where(i < big, counts[i], counts[i + 1])
+
+    owners[...] = jnp.full(owners.shape, -1.0, F32)
+    owners[:, :windows] = jnp.broadcast_to(owner_in[...], (8, windows)).astype(F32)
+    row = owners[0:1, :]
+    col = owners[...].T[:, 0:1]
+    before = lax.broadcasted_iota(jnp.int32, (padded, padded), 0)
+    after = lax.broadcasted_iota(jnp.int32, (padded, padded), 1)
+    same = jnp.where(col == row, 1.0, 0.0)
+    rank_row = jnp.sum(jnp.where(before < after, same, 0.0), axis=0, keepdims=True)
+    rank_col = jnp.sum(jnp.where(after < before, same, 0.0), axis=1, keepdims=True)
+    bucket_row = jnp.where(row >= 0, row * per_peer + rank_row, -1.0)
+    bucket_col = jnp.where(col >= 0, col * per_peer + rank_col, -1.0)
+
+    win = lax.broadcasted_iota(jnp.int32, (padded, 1), 0)
+    start = GRID * big
+    in_big = (win >= start) & (win < start + 4 * GRID)
+    image = jnp.where(in_big, big, win // GRID - jnp.where(win >= start + 4 * GRID, 3, 0))
+    kept = jnp.zeros((padded, 1), jnp.int32)
+    for i in range(images):
+        kept = jnp.where(image == i, counts[i], kept)
+    cells[...] = jnp.zeros_like(cells)
+    cells[:windows, FIELDS : FIELDS + slots] = offsets_in[...].astype(F32)
+    lane = lax.broadcasted_iota(jnp.int32, cells.shape, 1)
+    turn = jnp.where(in_big, win - start, win % GRID)
+    values = jnp.where(lane == 0, 1.0, cells[...])
+    values = jnp.where(lane == 1, kept.astype(F32), values)
+    values = jnp.where(lane == 2, turn.astype(F32), values)
+    values = jnp.where(lane == 3, jnp.where(in_big, 2.0 * GRID, 1.0 * GRID), values)
+    target = lax.broadcasted_iota(jnp.int32, (info_out.shape[0], padded), 0).astype(F32)
+    info_out[...] = dot(one_hot(target, bucket_row), values.astype(BF)).astype(BF)
+
+    place = lax.broadcasted_iota(jnp.int32, (1, lay.rows), 1)
+    window, slot, real = lay.rows_of(place, big)
+    found = jnp.sum(
+        jnp.where(win == window, bucket_col * LANE_SLOTS, 0.0), axis=0, keepdims=True
+    ).astype(jnp.int32)
+    bound = jnp.sum(jnp.where(win == window, kept.astype(F32), 0.0), axis=0, keepdims=True)
+    live = real & (slot.astype(F32) < bound)
+    place_out[...] = jnp.where(live, found + slot, -1)
 
 
 def slot_targets(info, slots, wins, axis):
@@ -423,11 +510,9 @@
     return jnp.where(live, first + cell.astype(jnp.int32), -1)
 
 
-def owner_kernel(slots, wins, cot, info_in, vec_dec, de_out, base_out, sums_out):
+def owner_kernel(slots, wins, cot, info_in, de_out, sums_out):
     step = pl.program_id(0)
     cells = wins * GRID
-    width = cot.shape[1]
-    quarter = width // 4
     grads = cot[...]
     info = info_in[...]
     cell_lane = lax.broadcasted_iota(jnp.int32, (1, cells), 1)
@@ -443,10 +528,37 @@
     present_row = dot_rows(info, inside)[0:1, :]
     mask_sum = dot(jnp.broadcast_to(present_row - taken, (8, cells)).astype(BF), grads)[:1]
 
+    @pl.when(step == 0)
+    def _():
+        sums_out[...] = jnp.zeros_like(sums_out)
+
+    sums_out[0:1, :] += row_sum(picked)
+    sums_out[1:2, :] += mask_sum
+
+
+def decode_kernel(slots, wins, got, info_in, vec_dec, out, stacked):
+    cells = wins * GRID
+    quarter = out.shape[1] // 4
+    info = info_in[...]
+    depth = stacked.shape[0] // 3
+
+    @pl.when(pl.program_id(0) == 0)
+    def _():
+        place = lax.broadcasted_iota(jnp.int32, (depth, quarter), 0).astype(F32)
+        index = lax.broadcasted_iota(jnp.int32, (depth, quarter), 1).astype(F32) / quarter
+        angle = place * (1.0 / jnp.exp(index * jnp.log(F32(10000.0))))
+        table = jnp.concatenate([jnp.sin(angle), jnp.cos(angle)], axis=1)
+        high = table.astype(BF)
+        rest = table - high.astype(F32)
+        middle = rest.astype(BF)
+        stacked[:depth] = high
+        stacked[depth : 2 * depth] = middle
+        stacked[2 * depth :] = (rest - middle.astype(F32)).astype(BF)
+
     cell_row = lax.broadcasted_iota(jnp.int32, (cells, 1), 0)
-    filled = jnp.sum(
-        jnp.where(cell_row == slot_targets(info, slots, wins, 1), 1.0, 0.0), axis=1, keepdims=True
-    )
+    chosen = one_hot(cell_row, slot_targets(info, slots, wins, 1))
+    filled = jnp.sum(chosen.astype(F32), axis=1, keepdims=True)
+    placed = dot(chosen, got[...])
     owner = lax.broadcasted_iota(jnp.int32, (cells, wins), 0) // GRID
     fields = dot(one_hot(owner, lax.broadcasted_iota(jnp.int32, (cells, wins), 1)), info)
     present = fields[:, 0:1]
@@ -455,39 +567,14 @@
     cell = cell_row % GRID
     along = jnp.where(wide, (turn % 2) * GRID + cell, cell)
     across = jnp.where(wide, turn // 2, turn)
-    depth = 32
-    place = lax.broadcasted_iota(jnp.int32, (depth, quarter), 0).astype(F32)
-    index = lax.broadcasted_iota(jnp.int32, (depth, quarter), 1).astype(F32) / quarter
-    angle = place * (1.0 / jnp.exp(index * jnp.log(F32(10000.0))))
-    table = jnp.concatenate([jnp.sin(angle), jnp.cos(angle)], axis=1)
-    high = table.astype(BF)
-    rest = table - high.astype(F32)
-    middle = rest.astype(BF)
-    low = (rest - middle.astype(F32)).astype(BF)
-    stacked = jnp.concatenate([high, middle, low], axis=0)
     lane = lax.broadcasted_iota(jnp.int32, (1, 3 * depth), 1) % depth
     shown = present > 0.5
-    first = dot(one_hot(jnp.where(shown, along, -1), lane), stacked)
-    second = dot(one_hot(jnp.where(shown, across, -1), lane), stacked)
+    first = dot(one_hot(jnp.where(shown, along, -1), lane), stacked[...])
+    second = dot(one_hot(jnp.where(shown, across, -1), lane), stacked[...])
     bare = present - filled
-    base_out[:, : 2 * quarter] = first + bare * vec_dec[1:2, : 2 * quarter]
-    base_out[:, 2 * quarter :] = second + bare * vec_dec[1:2, 2 * quarter :]
-
-    @pl.when(step == 0)
-    def _():
-        sums_out[...] = jnp.zeros_like(sums_out)
-
-    sums_out[0:1, :] += row_sum(picked)
-    sums_out[1:2, :] += mask_sum
-
-
-def decode_kernel(slots, wins, got, info_in, base, out):
-    cell_row = lax.broadcasted_iota(jnp.int32, (wins * GRID, 1), 0)
-    want = slot_targets(info_in[...], slots, wins, 1)
-    out[...] = (dot(one_hot(cell_row, want), got[...]) + base[...]).astype(BF)
-
-
-BIG, KEPT = 4, 5
+    half = 2 * quarter
+    out[:, :half] = (placed[:, :half] + first + bare * vec_dec[1:2, :half]).astype(BF)
+    out[:, half:] = (placed[:, half:] + second + bare * vec_dec[1:2, half:]).astype(BF)
 
 
 def first_norm_kernel(lay, meta, tokens, vecs, x_out, h_out):
@@ -520,44 +607,42 @@
     masks = [lay.key_mask(small, lay.small, meta[KEPT + 1 + i]) for i in range(lay.images - 1)]
     for pair in range(q_out.shape[1] // (2 * head_dim)):
         cols = slice(pair * 2 * head_dim, (pair + 1) * 2 * head_dim)
-        first = []
+        both = jnp.concatenate([q_out[:big, cols] * h for h in halves], axis=0)
+        scores[...] = dot_cols(both, k_out[:big, cols])
         for half in range(2):
-            head = 2 * pair + half
-            query = q_out[:big, cols] * halves[half]
-            scores[...] = dot_cols(query, k_out[:big, cols])
             for start in range(0, big, chunk):
-                part = scores[start : start + chunk, :] + mask_l
-                pl_out[head, start : start + chunk, :] = softmax_rows(part)
-            outs = [dot(pl_out[head], v_out[:big, cols])]
-            for i, start in enumerate(lay.starts):
-                rows = slice(start, start + small)
-                query = q_out[rows, cols] * halves[half]
-                part = dot_cols(query, k_out[rows, cols]) + masks[i]
-                weights = softmax_rows(part)
-                ps_out[head, i] = weights
-                outs.append(dot(weights, v_out[rows, cols]))
-            if half == 0:
-                first = outs
-        spans = [(0, big)] + [(s, small) for s in lay.starts]
-        for (start, size), left, right in zip(spans, first, outs):
-            o_out[start : start + size, cols] = jnp.where(low, left, right).astype(BF)
-
-
-def out_kernel(parts, *refs):
+                part = scores[half * big + start : half * big + start + chunk, :] + mask_l
+                pl_out[2 * pair + half, start : start + chunk, :] = softmax_rows(part)
+        outs = dot(pl_out[2 * pair : 2 * pair + 2].reshape(2 * big, big), v_out[:big, cols])
+        o_out[:big, cols] = jnp.where(low, outs[:big], outs[big:]).astype(BF)
+        for i, start in enumerate(lay.starts):
+            rows = slice(start, start + small)
+            both = jnp.concatenate([q_out[rows, cols] * h for h in halves], axis=0)
+            weights = softmax_rows(dot_cols(both, k_out[rows, cols]) + masks[i])
+            ps_out[2 * pair, i] = weights[:small]
+            ps_out[2 * pair + 1, i] = weights[small:]
+            outs = dot(weights, v_out[rows, cols])
+            o_out[rows, cols] = jnp.where(low, outs[:small], outs[small:]).astype(BF)
+
+
+def feed_kernel(parts, chunk, *refs):
     o_in = refs[:parts]
-    w_out, vecs, x_in, r_out, h_out = refs[parts:]
-    residual = x_in[...].astype(F32) + vecs[4:5, :]
-    width = o_in[0].shape[1]
-    for i, o in enumerate(o_in):
-        residual += dot(o[...], w_out[i * width : (i + 1) * width, :])
-    r_out[...] = residual
-    unit, _ = normalised(residual)
-    h_out[...] = (unit * vecs[5:6, :] + vecs[6:7, :]).astype(BF)
-
-
-def fc1_kernel(chunk, h_in, weight, bias, g_out, d_out, hidden):
-    hidden[...] = dot(h_in[...], weight[...])
-    for start in range(0, hidden.shape[0], chunk):
+    w_out, vecs, x_in, weight, bias, r_out, h_out, g_out, d_out, hidden = refs[parts:]
+    rows_all, width = x_in.shape[0], o_in[0].shape[1]
+
+    @pl.when(pl.program_id(0) == 0)
+    def _():
+        for start in range(0, rows_all, rows_all // 3):
+            rows = slice(start, start + rows_all // 3)
+            residual = x_in[rows, :].astype(F32) + vecs[4:5, :]
+            for i, o in enumerate(o_in):
+                residual += dot(o[rows, :], w_out[i * width : (i + 1) * width, :])
+            r_out[rows, :] = residual
+            unit, _ = normalised(residual)
+            h_out[rows, :] = (unit * vecs[5:6, :] + vecs[6:7, :]).astype(BF)
+
+    hidden[...] = dot(h_out[...], weight[...])
+    for start in range(0, rows_all, chunk):
         rows = slice(start, start + chunk)
         u = hidden[rows, :] + bias[...]
         half = 0.5 + 0.5 * lax.erf(u * (0.5**0.5))
@@ -566,64 +651,72 @@
         d_out[rows, :] = (half + u * density).astype(BF)
 
 
-def fc2_kernel(g_one, g_two, w_two, vecs, r_in, w_dec, w_dec_more, vec_dec, place, y_out, e_out, kept):
+def join_kernel(rows_dev, sizes, spot, g_in, part_a, part_b, from_a, from_b, vecs, r_in, w_dec, w_dec_more, vec_dec, place, got,
+                w_out, e_out, dy_out, own_out, sent_out, db_out, total):
     step = pl.program_id(0)
-    rows, half = g_one.shape
-    y = r_in[...] + dot(g_one[...], w_two[:half, :]) + dot(g_two[...], w_two[half:, :])
-    y = (y + vecs[7:8, :]).astype(BF)
-    y_out[...] = y
-    kept[pl.ds(pl.multiple_of(step * rows, rows), rows), :] = (
-        dot(y, jnp.concatenate([w_dec[...], w_dec_more[...]], axis=1)) + vec_dec[0:1, :]
-    ).astype(BF)
+
+    @pl.when(step == 0)
+    def _():
+        total[...] = r_in[...] + vecs[7:8, :]
+
+    _, ny, nx = sizes
+    for ky in range(ny):
+        for kx in range(nx):
+            chip = lax.rem(spot[1] - ky + ny, ny) * nx + lax.rem(spot[2] - kx + nx, nx)
+            for core, left, right in ((spot[3], part_a, part_b), (1 - spot[3], from_a, from_b)):
+                half = left.shape[-1]
+                w_out[chip * 2 + core, :, :half] = left[ky, kx, 0]
+                w_out[chip * 2 + core, :, half:] = right[kx, ky, 0]
+    total[...] += dot(g_in[...], w_out[...].reshape(g_in.shape[1], total.shape[1]))
 
     @pl.when(step == pl.num_programs(0) - 1)
     def _():
+        half = w_dec.shape[1]
+        y = total[...].astype(BF)
         target = lax.broadcasted_iota(jnp.int32, (e_out.shape[0], 1), 0)
-        e_out[...] = dot(one_hot(target, place[...]), kept[...]).astype(BF)
-
-
-def dec_back_kernel(rows, spot, got, place, w_dec, w_dec_more, y_in, dy_out, own_out, sent_out, db_out):
-    target = lax.broadcasted_iota(jnp.int32, (got.shape[0], 1), 0)
-    grad = dot_rows(one_hot(target, place[...]), got[...]).astype(BF)
-    half = w_dec.shape[1]
-    dy = dot_cols(grad[:, :half], w_dec[...]) + dot_cols(grad[:, half:], w_dec_more[...])
-    dy = dy.astype(BF)
-    dy_out[...] = dy
-    split_cores(dot_rows(y_in[...], grad), rows, spot[3], own_out, sent_out)
-    db_out[...] = row_sum(dy.astype(F32))
-
-
-def fc2_back_kernel(rows, spot, dy_in, w_two, g_one, d_one, g_two, d_two, du_out, own_out, sent_out, db_out):
-    dy = dy_in[...]
-    early = pl.program_id(0) < 2
-    slope = jnp.where(early, d_one[...], d_two[...]).astype(F32)
-    du = (dot_cols(dy, w_two[...]) * slope).astype(BF)
-    du_out[...] = du
-    db_out[...] = row_sum(du.astype(F32))
-    split_cores(
-        dot_rows(jnp.where(early, g_one[...], g_two[...]), dy), rows, spot[3], own_out, sent_out
-    )
-
-
-def fc1_back_kernel(rows, spot, du_in, w_one, h_in, dh_out, own_out, sent_out, turned):
+        pick = one_hot(target, place[...])
+        grad = dot_rows(pick, got[...]).astype(BF)
+        for i, w in enumerate((w_dec, w_dec_more)):
+            cols = slice(i * half, (i + 1) * half)
+            embedded = (dot(y, w[...]) + vec_dec[0:1, cols]).astype(BF)
+            e_out[:, cols] = dot(pick, embedded).astype(BF)
+        dy = dot_cols(grad[:, :half], w_dec[...]) + dot_cols(grad[:, half:], w_dec_more[...])
+        dy = dy.astype(BF)
+        dy_out[...] = dy
+        split_cores(dot_rows(y, grad), rows_dev, spot[3], own_out, sent_out)
+        db_out[...] = row_sum(dy.astype(F32))
+
+
+def feed_back_kernel(rows_one, rows_two, spot, dy_in, w_two, g_in, d_in, w_one, h_in,
+                     dh_out, own_two, sent_two, own_one, sent_one, db_out, turned):
     step = pl.program_id(0)
 
     @pl.when(step == 0)
     def _():
         turned[...] = h_in[...].T
-        dh_out[...] = jnp.zeros_like(dh_out)
-
-    du = du_in[...]
-    split_cores(dot(turned[...], du), rows, spot[3], own_out, sent_out)
-    dh_out[...] += dot_cols(du, w_one[...])
-
-
-def out_back_kernel(rows, parts, spot, dh_one, dh_two, r_in, dy_in, vecs, w_out, *refs):
+
+    dy = dy_in[...]
+    du = (dot_cols(dy, w_two[...]) * d_in[...].astype(F32)).astype(BF)
+    db_out[...] = row_sum(du.astype(F32))
+    split_cores(dot_rows(g_in[...], dy), rows_two, spot[3], own_two, sent_two)
+    split_cores(dot(turned[...], du), rows_one, spot[3], own_one, sent_one)
+    part = dot_cols(du, w_one[...])
+
+    @pl.when(step == 0)
+    def _():
+        dh_out[...] = part
+
+    @pl.when(step > 0)
+    def _():
+        dh_out[...] += part
+
+
+def out_back_kernel(rows, parts, spot, dh_in, r_in, dy_in, vecs, w_out, *refs):
     o_in = refs[:parts]
     dr_out, do_out, own_out, sent_out, sums, total = refs[parts:]
     step = pl.program_id(0)
     unit, scale = normalised(r_in[...])
-    grad = dh_one[...] + dh_two[...]
+    grad = dh_in[...]
     dr = dy_in[...].astype(F32) + norm_back(unit, scale, vecs[5:6, :], grad)
     dr_out[...] = dr
     da = dr.astype(BF)
@@ -660,40 +753,31 @@
 
     for pair in range(q_in.shape[1] // (2 * head_dim)):
         cols = slice(pair * 2 * head_dim, (pair + 1) * 2 * head_dim)
-        spans = [(0, big)] + [(s, small) for s in lay.starts]
-        first = []
+        both = jnp.concatenate([do_in[:big, cols] * h for h in halves], axis=0)
+        scores[...] = dot_cols(both, v_in[:big, cols])
         for half in range(2):
-            head = 2 * pair + half
-            found = []
-            for i, (start, size) in enumerate(spans):
-                rows = slice(start, start + size)
-                grad_o = do_in[rows, cols] * halves[half]
-                if i == 0:
-                    scores[...] = dot_cols(grad_o, v_in[rows, cols])
-                    for s in range(0, big, chunk):
-                        ds_big[s : s + chunk, :] = back_rows(
-                            pl_in[head, s : s + chunk, :], scores[s : s + chunk, :]
-                        )
-                    weights, ds = pl_in[head], ds_big[...]
-                else:
-                    weights = ps_in[head, i - 1]
-                    ds = back_rows(weights, dot_cols(grad_o, v_in[rows, cols]))
-                found.append(
-                    (
-                        dot(ds, k_in[rows, cols]),
-                        dot_rows(ds, q_in[rows, cols]),
-                        dot_rows(weights, do_in[rows, cols]),
-                    )
-                )
-            if half == 0:
-                first = found
-        for (start, size), left, right in zip(spans, first, found):
-            rows = slice(start, start + size)
-            dq_out[rows, cols] = (
-                jnp.where(low, left[0], right[0]) * (head_dim**-0.5)
-            ).astype(BF)
-            dk_out[rows, cols] = jnp.where(low, left[1], right[1]).astype(BF)
-            dv_out[rows, cols] = jnp.where(low, left[2], right[2]).astype(BF)
+            for at in range(0, big, chunk):
+                rows = slice(half * big + at, half * big + at + chunk)
+                ds_big[rows, :] = back_rows(pl_in[2 * pair + half, at : at + chunk, :], scores[rows, :])
+        spans = [(slice(0, big), None)] + [
+            (slice(start, start + small), i) for i, start in enumerate(lay.starts)
+        ]
+        for rows, i in spans:
+            if i is None:
+                size, ds = big, ds_big[...]
+                weights = (pl_in[2 * pair], pl_in[2 * pair + 1])
+            else:
+                size = small
+                weights = (ps_in[2 * pair, i], ps_in[2 * pair + 1, i])
+                both = jnp.concatenate([do_in[rows, cols] * h for h in halves], axis=0)
+                ds = back_rows(jnp.concatenate(weights, axis=0), dot_cols(both, v_in[rows, cols]))
+            grad = dot(ds, k_in[rows, cols])
+            grad = jnp.where(low, grad[:size], grad[size:]) * (head_dim**-0.5)
+            dq_out[rows, cols] = grad.astype(BF)
+            left, right = dot_rows(ds[:size], q_in[rows, cols]), dot_rows(ds[size:], q_in[rows, cols])
+            dk_out[rows, cols] = jnp.where(low, left, right).astype(BF)
+            left, right = (dot_rows(w, do_in[rows, cols]) for w in weights)
+            dv_out[rows, cols] = jnp.where(low, left, right).astype(BF)
     turned = h_in[...].T
     width = dq_out.shape[1]
     for i, grad in enumerate((dq_out, dk_out, dv_out)):
@@ -768,58 +852,46 @@
 
     ga, gc = Gather(dev, [qkv_weight]), Gather(dev, [fc2_weight])
     za = ga.along_z()
-    rest = lax.all_gather(
-        jnp.concatenate([fc1_weight, out_weight, dec_weight], axis=1), "dp", axis=0, tiled=True
+    xa = ga.first()
+    kept_offsets, kept_count, dec_owner, ln1_gain, dec_bias, fc1_bias = held(
+        (kept_offsets, kept_count, dec_owner, ln1_gain, dec_bias, fc1_bias), *ga.sent
     )
-    image_ids = jnp.arange(images, dtype=jnp.int32)
-    big = jnp.sum(image_ids * res_id)
-    kept_big = jnp.sum(res_id * kept_count)
-    kept_small = jnp.where(image_ids[:-1] < big, kept_count[:-1], kept_count[1:])
-    meta = jnp.concatenate(
-        [jnp.stack([dev.coord(axis) for axis in "zyxc"] + [big, kept_big]), kept_small]
-    ).astype(jnp.int32)
-    bucket = dec_owner * per_peer + owner_rank(dec_owner)
-    place_row = lay.place(big, kept_count, bucket, LANE_SLOTS)[None, :]
-    win = jnp.arange(windows, dtype=jnp.int32)
-    big_start = GRID * big
-    in_big = (win >= big_start) & (win < big_start + 4 * GRID)
-    after = win >= big_start + 4 * GRID
-    image_win = jnp.where(in_big, big, jnp.where(after, win // GRID - 3, win // GRID))
-    in_image = jnp.where(in_big, win - big_start, win % GRID)
-    kept_win = jnp.sum(
-        jnp.where(image_win[:, None] == image_ids[None, :], kept_count[None, :], 0), axis=1
-    )
-    side_win = jnp.where(in_big, 2 * GRID, GRID)
-    info = jnp.concatenate(
-        [jnp.stack([jnp.ones_like(win), kept_win, in_image, side_win], axis=1), kept_offsets], axis=1
-    )
-    xa = ga.first(bucket)
-    bucket = held(bucket, *ga.sent)
-    slot_of = jnp.arange(total, dtype=jnp.int32)
-    info_send = jnp.sum(
-        jnp.where((slot_of[:, None] == bucket[None, :])[:, :, None], info[None, :, :], 0), axis=1
-    )
+    wide = max(fc1_bias.shape[0], 128)
+    sizes = (dev.size["z"], dev.size["y"], dev.size["x"])
+    lanes = -(-windows // 128) * 128
+    meta, place_row, info_send = pl.pallas_call(
+        functools.partial(describe_kernel, lay, sizes, per_peer),
+        name="describe",
+        in_specs=[SMEM, SMEM, SMEM, VMEM, VMEM],
+        out_specs=[SMEM, VMEM, VMEM],
+        out_shape=[sd((16,), jnp.int32), sd((1, R), jnp.int32), sd((total, wide), BF)],
+        scratch_shapes=[pltpu.VMEM((8, lanes), F32), pltpu.VMEM((lanes, wide), F32)],
+        compiler_params=params(),
+    )(lax.axis_index("dp").astype(jnp.int32).reshape(1), kept_count, res_id, dec_owner.reshape(1, windows),
+      kept_offsets)
     eight = [ln1_gain, ln1_bias, query_bias, value_bias, out_bias, ln2_gain, ln2_bias, fc2_bias]
     vectors = eight + [fc1_bias, dec_bias, mask_token]
-    wide = max(fc1_bias.shape[0], 128)
-    line = lambda v: jnp.pad(v, (0, wide - v.shape[0]))[None, :]
-    sheet = jnp.concatenate([line(v) for v in vectors], axis=0)
-    fields = info_send.shape[1]
-    info_block = jnp.pad(info_send.astype(BF), ((0, 0), (0, wide - fields)))
+    line = lambda v: jnp.pad(v, ((0, 0), (0, wide - v.shape[1])))
+    sheet = jnp.concatenate(
+        [line(jnp.stack(eight)), line(fc1_bias[None, :]), line(jnp.stack([dec_bias, mask_token]))], axis=0
+    )
     packed = jnp.concatenate(
-        [
-            jnp.broadcast_to(sheet[None], (count,) + sheet.shape),
-            info_block.reshape(count, per_peer, wide),
-        ],
+        [jnp.broadcast_to(sheet[None], (count,) + sheet.shape), info_send.reshape(count, per_peer, wide)],
         axis=1,
     )
     ya = ga.second(packed)
+    rest = lax.all_gather(
+        held(jnp.concatenate([fc1_weight, out_weight, dec_weight], axis=1), *za),
+        "dp",
+        axis=0,
+        tiled=True,
+    )
     packed = lax.all_to_all(packed, "dp", 0, 0, tiled=True)
     n_vec = eight[0].shape[0]
     vecs = packed[:, :8, :n_vec].transpose(1, 0, 2).reshape(8, D).astype(F32)
     bf1 = packed[:, 8, : fc1_bias.shape[0]].reshape(1, hidden).astype(F32)
     vec_dec = packed[:, 9:11, : dec_bias.shape[0]].transpose(1, 0, 2).reshape(2, dec_width).astype(F32)
-    info_got = packed[:, 11:, :fields].reshape(total, fields)
+    info_got = packed[:, 11:].reshape(total, wide)
 
     w_out_spec = spec((D, D), lambda *_: (0, hidden // D))
     first_dec, dec_half = 2 * (hidden + D) // dec_width, dec_width // 2
@@ -834,33 +906,29 @@
         out_specs=[rows_of(D), rows_of(D)],
         out_shape=[sd((R, D), BF), sd((R, D), BF)],
         compiler_params=params(),
-        cost_estimate=cost(2 * R * vis * D, 4e6),
+        cost_estimate=cost(2 * R * vis * D, 4e6, weight=0.02),
     )(meta, held(tokens, za), vecs)
+
+    from_a = ga.swap(h_one)
 
     wins = 16
     steps = total // wins
     cells_w, rows_w = wins * GRID, wins * LANE_SLOTS
     by_step = lambda height, width: spec((height, width), lambda i: (i, 0))
     info_spec = by_step(wins, info_got.shape[1])
-    de_send, base, owner_sums = pl.pallas_call(
+    de_send, owner_sums = pl.pallas_call(
         functools.partial(owner_kernel, slots, wins),
         name="owner_side",
         grid=(steps,),
-        in_specs=[by_step(cells_w, dec_width), info_spec, whole((2, dec_width))],
-        out_specs=[by_step(rows_w, dec_width), by_step(cells_w, dec_width), whole((8, dec_width))],
-        out_shape=[sd((total * LANE_SLOTS, dec_width), BF), sd((total * GRID, dec_width), F32),
-                   sd((8, dec_width), F32)],
+        in_specs=[by_step(cells_w, dec_width), info_spec],
+        out_specs=[by_step(rows_w, dec_width), whole((8, dec_width))],
+        out_shape=[sd((total * LANE_SLOTS, dec_width), BF), sd((8, dec_width), F32)],
         compiler_params=params(),
-        cost_estimate=cost(4e9, 8e6, 1e5),
-    )(dec_cot, held(info_got, h_one, *xa), vec_dec)
-
-    from_a = ga.swap(de_send, h_one)
-    zc = gc.along_z(*ya)
-    (w_qkv,) = ga.result(meta)
-    de_got = lax.all_to_all(
-        held(de_send, *from_a).reshape(count, per_peer * LANE_SLOTS, dec_width), "dp", 0, 0, tiled=True
-    ).reshape(total * LANE_SLOTS, dec_width)
-
+        cost_estimate=cost(1e9, 3e6, weight=0.02),
+    )(dec_cot, held(info_got, h_one, *ga.sent))
+
+    zc = gc.along_z(*from_a)
+    (w_qkv,) = ga.result(meta, de_send)
     group = 4
     parts = HEADS // group
     gw = group * head_dim
@@ -878,133 +946,99 @@
                       spec((8, gw), lambda _: (0, i))],
             out_specs=[whole((R, gw))] * 3 + [whole(p_big_t.shape), whole(p_small_t.shape), whole((R, gw))],
             out_shape=[sd((R, gw), BF)] * 3 + [p_big_t, p_small_t, sd((R, gw), BF)],
-            scratch_shapes=[pltpu.VMEM((lay.large_pad, lay.large_pad), F32)],
+            scratch_shapes=[pltpu.VMEM((2 * lay.large_pad, lay.large_pad), F32)],
             compiler_params=params(),
             cost_estimate=cost(2 * R * D * D + 2e9, 8e6, 1e6),
         )(meta, h_rows, w_qkv, w_qkv, w_qkv, vecs)
 
     attn = [attend(0, h_one)]
-    attn.append(attend(1, held(h_one, attn[0][5])))
-    gc.first(attn[1][5])
+    gc.first(attn[0][5])
+    attn.append(attend(1, held(h_one, attn[0][5], *gc.sent)))
+    gc.second(attn[1][5])
     attn.append(attend(2, held(h_one, attn[1][5], *gc.sent)))
-    gc.second(attn[2][5])
+    swapped = gc.swap(attn[2][5])
+    de_got = lax.all_to_all(
+        held(de_send, attn[1][5]).reshape(count, per_peer * LANE_SLOTS, dec_width), "dp", 0, 0, tiled=True
+    ).reshape(total * LANE_SLOTS, dec_width)
+
     att = [a[5] for a in attn]
 
-    r_one, h_two = pl.pallas_call(
-        functools.partial(out_kernel, parts),
-        name="out_projection",
-        grid=(3,),
-        in_specs=[rows_of(gw)] * parts
-        + [w_out_spec, whole((8, D)), rows_of(D)],
-        out_specs=[rows_of(D), rows_of(D)],
-        out_shape=[sd((R, D), F32), sd((R, D), BF)],
+    ht = hidden // 6
+    row_dev, row_two = D // count, hidden // count
+    chips = count // 2
+    r_one, h_two, act_h, d_gelu = pl.pallas_call(
+        functools.partial(feed_kernel, parts, R // 24),
+        name="feed",
+        grid=(6,),
+        in_specs=[whole((R, gw))] * parts
+        + [w_out_spec, whole((8, D)), whole((R, D)), spec((D, ht), lambda j: (0, j)),
+           spec((1, ht), lambda j: (0, j))],
+        out_specs=[whole((R, D)), whole((R, D))] + [spec((R, ht), lambda j: (0, j))] * 2,
+        out_shape=[sd((R, D), F32), sd((R, D), BF), sd((R, hidden), BF), sd((R, hidden), BF)],
+        scratch_shapes=[pltpu.VMEM((R, ht), F32)],
         compiler_params=params(),
-        cost_estimate=cost(2 * R * D * D, 9e6),
-    )(*att, rest, vecs, held(x_rows, *gc.sent))
-
-    ht = hidden // 6
-
-    def feed(i, h_rows):
-        return pl.pallas_call(
-            functools.partial(fc1_kernel, R // 24),
-            name="fc1",
-            grid=(3,),
-            in_specs=[whole((R, D)), spec((D, ht), lambda j: (0, 3 * i + j)),
-                      spec((1, ht), lambda j: (0, 3 * i + j))],
-            out_specs=[spec((R, ht), lambda j: (0, j))] * 2,
-            out_shape=[sd((R, hidden // 2), BF)] * 2,
-            scratch_shapes=[pltpu.VMEM((R, ht), F32)],
-            compiler_params=params(),
-            cost_estimate=cost(R * D * hidden, 1e7, 3e6),
-        )(h_rows, rest, bf1)
-
-    act_0, gelu_0 = feed(0, h_two)
-    gc.swap(act_0)
-    act_1, gelu_1 = feed(1, held(h_two, act_0, de_got, *gc.sent))
-    (w_two,) = gc.result(meta)
-
-    y_rows, e_send = pl.pallas_call(
-        fc2_kernel,
-        name="fc2_and_embed",
-        grid=(3,),
-        in_specs=[rows_of(hidden // 2), rows_of(hidden // 2), whole((hidden, D)), whole((8, D)),
-                  rows_of(D), *w_dec_specs, whole((2, dec_width)), whole((1, R))],
-        out_specs=[rows_of(D), whole((total * LANE_SLOTS, dec_width))],
-        out_shape=[sd((R, D), BF), sd((total * LANE_SLOTS, dec_width), BF)],
-        scratch_shapes=[pltpu.VMEM((R, dec_width), BF)],
+        cost_estimate=cost(2 * R * D * (hidden + D), 2.5e7, 6e6),
+    )(*att, rest, vecs, held(x_rows, *gc.sent), rest, bf1)
+
+    ht = hidden // 4
+    nz, ny, nx = sizes
+    part = pl.BlockSpec(
+        (ny, nx, 1, row_two, D // 2), lambda j, at: (0, 0, lax.rem(at[0] - j + nz, nz), 0, 0)
+    )
+    ht = hidden // nz
+    w_two, e_send, dy, own_dec, sent_dec, db_two = pl.pallas_call(
+        functools.partial(join_kernel, row_dev, sizes),
+        name="join",
+        grid_spec=pltpu.PrefetchScalarGridSpec(
+            num_scalar_prefetch=1,
+            grid=(nz,),
+            in_specs=[spec((R, ht), lambda j, _: (0, j)), part, part, part, part, whole((8, D)),
+                      whole((R, D)), *w_dec_specs, whole((2, dec_width)), whole((1, R)),
+                      whole((total * LANE_SLOTS, dec_width))],
+            out_specs=[spec((2 * ny * nx, row_two, D), lambda j, _: (j, 0, 0)),
+                       whole((total * LANE_SLOTS, dec_width)), whole((R, D)),
+                       whole((chips, row_dev, dec_width)), whole((chips, row_dev, dec_width)), whole((1, D))],
+            scratch_shapes=[pltpu.VMEM((R, D), F32)],
+        ),
+        out_shape=[sd((count, row_two, D), BF), sd((total * LANE_SLOTS, dec_width), BF), sd((R, D), BF),
+                   sd((chips, row_dev, dec_width), BF), sd((chips, row_dev, dec_width), BF), sd((1, D), F32)],
         compiler_params=params(),
-        cost_estimate=cost(2 * R * D * hidden + 4 * R * D * dec_width, 2e7),
-    )(act_0, act_1, w_two, vecs, r_one, rest, rest, vec_dec, place_row)
+        cost_estimate=cost(2 * R * D * hidden + 10 * R * D * dec_width, 2e7),
+    )(meta, act_h, gc.part_a, gc.part_b, gc.from_a, gc.from_b, vecs, r_one, rest, rest, vec_dec, place_row,
+      de_got)
+    w_two = w_two.reshape(hidden, D)
+    ht = hidden // 4
 
     e_got = lax.all_to_all(
         e_send.reshape(count, per_peer * LANE_SLOTS, dec_width), "dp", 0, 0, tiled=True
     ).reshape(total * LANE_SLOTS, dec_width)
 
-    row_dev, row_two = D // count, hidden // count
-    chips = count // 2
-    dy, own_dec, sent_dec, db_two = pl.pallas_call(
-        functools.partial(dec_back_kernel, row_dev),
-        name="embed_back",
-        grid=(1,),
-        in_specs=[SMEM, whole((total * LANE_SLOTS, dec_width)), whole((1, R)), *w_dec_specs, whole((R, D))],
-        out_specs=[whole((R, D)), whole((chips, row_dev, dec_width)),
-                   whole((chips, row_dev, dec_width)), whole((1, D))],
-        out_shape=[sd((R, D), BF), sd((chips, row_dev, dec_width), BF),
-                   sd((chips, row_dev, dec_width), BF), sd((1, D), F32)],
+    held_chips = ht // (2 * row_two)
+    tile_two = spec((held_chips, row_two, D), lambda j: (j, 0, 0))
+    tile_one = spec((chips, row_dev, ht), lambda j: (0, 0, j))
+    dh, own_two, sent_two, own_one, sent_one, db_one = pl.pallas_call(
+        functools.partial(feed_back_kernel, row_dev, row_two),
+        name="feed_back",
+        grid=(4,),
+        in_specs=[SMEM, whole((R, D)), spec((ht, D), lambda j: (j, 0)), spec((R, ht), lambda j: (0, j)),
+                  spec((R, ht), lambda j: (0, j)), spec((D, ht), lambda j: (0, j)), whole((R, D))],
+        out_specs=[whole((R, D)), tile_two, tile_two, tile_one, tile_one, spec((1, ht), lambda j: (0, j))],
+        out_shape=[sd((R, D), F32)] + [sd((chips, row_two, D), BF)] * 2
+        + [sd((chips, row_dev, hidden), BF)] * 2 + [sd((1, hidden), F32)],
+        scratch_shapes=[pltpu.VMEM((D, R), BF)],
         compiler_params=params(),
-        cost_estimate=cost(6 * R * D * dec_width, 7e6, weight=20),
-    )(meta, de_got, place_row, rest, rest, y_rows)
-
-    ht = hidden // 4
-    held_chips = ht // (2 * row_two)
-    grad_spec = spec((held_chips, row_two, D), lambda j: (j, 0, 0))
-    half_tile = lambda k: spec((R, ht), lambda j: (0, jnp.clip(j - 2 * k, 0, 1)))
-    du, own_two, sent_two, db_one = pl.pallas_call(
-        functools.partial(fc2_back_kernel, row_two),
-        name="fc2_back",
-        grid=(4,),
-        in_specs=[SMEM, whole((R, D)), spec((ht, D), lambda j: (j, 0)), half_tile(0), half_tile(0),
-                  half_tile(1), half_tile(1)],
-        out_specs=[spec((R, ht), lambda j: (0, j)), grad_spec, grad_spec,
-                   spec((1, ht), lambda j: (0, j))],
-        out_shape=[sd((R, hidden), BF), sd((chips, row_two, D), BF), sd((chips, row_two, D), BF),
-                   sd((1, hidden), F32)],
-        compiler_params=params(),
-        cost_estimate=cost(4 * R * D * hidden, 3e7, weight=20),
-    )(meta, dy, w_two, act_0, gelu_0, act_1, gelu_1)
+        cost_estimate=cost(8 * R * D * hidden, 4e7, weight=20),
+    )(meta, dy, w_two, act_h, d_gelu, rest, h_two)
     s_two = Scatter(dev, [(own_two, sent_two)], meta)
-    c_two = s_two.swap()
-
-    grad_spec = spec((chips, row_dev, ht), lambda j: (0, 0, j))
-
-    def fc1_back(i, du_rows):
-        return pl.pallas_call(
-            functools.partial(fc1_back_kernel, row_dev),
-            name="fc1_back",
-            grid=(2,),
-            in_specs=[SMEM, spec((R, ht), lambda j: (0, 2 * i + j)),
-                      spec((D, ht), lambda j: (0, 2 * i + j)), whole((R, D))],
-            out_specs=[whole((R, D)), grad_spec, grad_spec],
-            out_shape=[sd((R, D), F32)] + [sd((chips, row_dev, hidden // 2), BF)] * 2,
-            scratch_shapes=[pltpu.VMEM((D, R), BF)],
-            compiler_params=params(),
-            cost_estimate=cost(2 * R * D * hidden, 1.5e7, weight=20),
-        )(meta, du_rows, rest, h_two)
-
-    dh_0, own_f0, sent_f0 = fc1_back(0, du)
-    s_two.add(dh_0, *c_two)
-    near = s_two.near()
-    dh_1, own_f1, sent_f1 = fc1_back(1, held(du, dh_0, s_two.blocks[0]))
-    s_one = Scatter(dev, [(own_f0, sent_f0), (own_f1, sent_f1), (own_dec, sent_dec)], meta)
-    far = s_two.far(dh_1, *near)
-    c_one = s_one.swap(dh_1, *near)
+    s_one = Scatter(dev, [(own_one, sent_one), (own_dec, sent_dec)], meta)
+    c_two, c_one = s_two.swap(), s_one.swap()
 
     grad_spec = whole((chips, row_dev, D))
     dr, d_att, own_out, sent_out, sums_two = pl.pallas_call(
         functools.partial(out_back_kernel, row_dev, parts),
         name="out_back",
         grid=(3,),
-        in_specs=[SMEM, rows_of(D), rows_of(D), rows_of(D), rows_of(D), whole((8, D)), w_out_spec]
+        in_specs=[SMEM, rows_of(D), rows_of(D), rows_of(D), whole((8, D)), w_out_spec]
         + [rows_of(gw)] * parts,
         out_specs=[rows_of(D), rows_of(D), grad_spec, grad_spec, whole((8, D))],
         out_shape=[sd((R, D), F32), sd((R, D), BF)] + [sd((chips, row_dev, D), BF)] * 2
@@ -1012,9 +1046,9 @@
         scratch_shapes=[pltpu.VMEM((D, D), F32)],
         compiler_params=params(),
         cost_estimate=cost(4 * R * D * D, 2e7, weight=20),
-    )(meta, dh_0, held(dh_1, *near), r_one, dy, vecs, rest, *att)
-    s_one.add(dr, *far, *c_one)
-    near = s_one.near()
+    )(meta, dh, r_one, dy, vecs, rest, *att)
+    s_two.add(dr, *c_two)
+    near = s_two.near()
 
     def attend_back(i, d_att_rows):
         q_rows, k_rows, v_rows, prob_l, prob_s, _ = attn[i]
@@ -1027,39 +1061,29 @@
             + [whole(p_big_t.shape), whole(p_small_t.shape), spec((R, gw), lambda _: (0, i))],
             out_specs=[whole((R, gw))] * 3 + [whole(grad_shape)] * 2 + [whole((8, gw))],
             out_shape=[sd((R, gw), BF)] * 3 + [sd(grad_shape, BF)] * 2 + [sd((8, gw), F32)],
-            scratch_shapes=[pltpu.VMEM((lay.large_pad, lay.large_pad), F32),
-                            pltpu.VMEM((lay.large_pad, lay.large_pad), BF)],
+            scratch_shapes=[pltpu.VMEM((2 * lay.large_pad, lay.large_pad), F32),
+                            pltpu.VMEM((2 * lay.large_pad, lay.large_pad), BF)],
             compiler_params=params(),
             cost_estimate=cost(2 * R * D * D + 3e9, 1e7, weight=20),
         )(meta, h_one, q_rows, k_rows, v_rows, prob_l, prob_s, d_att_rows)
 
-    back = [attend_back(0, held(d_att, s_one.blocks[0], *far))]
-    far = s_one.far(back[0][0], *near)
+    back = [attend_back(0, held(d_att, s_two.blocks[0], e_got, *c_one))]
+    far = s_two.far(back[0][0], *near)
+    s_one.add(back[0][0], *near)
+    near = s_one.near()
     s_mid = Scatter(dev, [(own_out, sent_out), back[0][3:5]], meta)
-    c_mid = s_mid.swap(back[0][0], *near)
-    back.append(attend_back(1, held(d_att, back[0][0], *near)))
+    c_mid = s_mid.swap(back[0][0])
+    back.append(attend_back(1, held(d_att, back[0][0], s_one.blocks[0])))
     s_mid.add(back[1][0], *far, *c_mid)
-    near = s_mid.near()
-    lines_early, z_early = finish(dev, meta, [s_two, s_one], True, back[1][0], s_mid.blocks[0])
+    lines_two, z_two = finish(dev, meta, [s_two], True, back[1][0])
+    far = s_one.far(back[1][0], *near)
     s_last = Scatter(dev, [back[1][3:5]], meta)
-    c_last = s_last.swap(back[1][0], *far)
-    back.append(attend_back(2, held(d_att, back[1][0], s_mid.blocks[0], lines_early[0])))
+    c_last = s_last.swap(back[1][0])
+    back.append(attend_back(2, held(d_att, back[1][0], s_mid.blocks[0], lines_two[0], *near)))
     s_last.more(*back[2][3:5])
-    c_last += s_last.swap(back[2][0], *near, *c_last)
-    far = s_mid.far(back[2][0], *near)
-
-    decoded = pl.pallas_call(
-        functools.partial(decode_kernel, slots, wins),
-        name="decode",
-        grid=(steps,),
-        in_specs=[by_step(rows_w, dec_width), info_spec, by_step(cells_w, dec_width)],
-        out_specs=by_step(cells_w, dec_width),
-        out_shape=sd((total * GRID, dec_width), BF),
-        compiler_params=params(),
-        cost_estimate=cost(1e9, 7e6, weight=20),
-    )(held(e_got, back[2][0], *near), info_got, base)
-    s_last.add(decoded, *far, *c_last)
-    near = s_last.near() + s_last.far()
+    near = s_mid.near(back[2][0], *far) + s_mid.far(back[2][0], *far)
+    c_last += s_last.swap(back[2][0], *c_last)
+    lines_one, z_one = finish(dev, meta, [s_one], True, back[2][0], *far, z_two)
 
     dqkv = [b[i] for i in range(3) for b in back]
     grad_tokens, sums = pl.pallas_call(
@@ -1073,10 +1097,12 @@
         scratch_shapes=[pltpu.VMEM((R, D), BF)],
         compiler_params=params(),
         cost_estimate=cost(2 * R * D * 3 * D + 2 * R * vis * D, 2e7, weight=20),
-    )(meta, *dqkv, *[b[5] for b in back], w_qkv, x_rows, held(dr, s_last.blocks[0], z_early), vecs, sums_two,
+    )(meta, *dqkv, *[b[5] for b in back], w_qkv, x_rows, held(dr, *lines_one), vecs, sums_two,
       db_two)
-
-    rows = jnp.concatenate(
+    s_last.add(grad_tokens, *near, *c_last)
+    near = s_last.near() + s_last.far()
+
+    rows_sent = jnp.concatenate(
         [
             sums.reshape(8, count, -1).transpose(1, 0, 2).reshape(count, -1),
             db_one.reshape(count, -1),
@@ -1084,15 +1110,25 @@
         ],
         axis=1,
     )
-    lines_late, z_late = finish(dev, meta, [s_mid, s_last], False, grad_tokens, *near)
-    rows = lax.all_to_all(held(rows, lines_late[0]), "dp", 0, 0, tiled=True)
+    rows = lax.all_to_all(held(rows_sent, s_last.blocks[0], z_one), "dp", 0, 0, tiled=True)
+    decoded = pl.pallas_call(
+        functools.partial(decode_kernel, slots, wins),
+        name="decode",
+        grid=(steps,),
+        in_specs=[by_step(rows_w, dec_width), info_spec, whole((2, dec_width))],
+        out_specs=by_step(cells_w, dec_width),
+        out_shape=sd((total * GRID, dec_width), BF),
+        scratch_shapes=[pltpu.VMEM((3 * 32, dec_width // 2), BF)],
+        compiler_params=params(),
+        cost_estimate=cost(1e9, 7e6, weight=20),
+    )(held(e_got, s_last.blocks[0], z_one, rows_sent), info_got, vec_dec)
+
+
+    lines_late, z_late = finish(dev, meta, [s_mid, s_last], False, decoded, rows, *near)
     rows = jnp.sum(rows, axis=0)
-    grad_two, grad_f0, grad_f1, grad_dec = totals(z_early, [s_two, s_one])
-    grad_one = jnp.concatenate([grad_f0, grad_f1], axis=1)
-    grad_out, *grads_qkv = totals(z_late, [s_mid, s_last])
-    grad_qkv = jnp.concatenate(
-        [g[:, i * gw : (i + 1) * gw] for i in range(3) for g in grads_qkv], axis=1
-    )
+    (grad_two,) = totals(z_two, [s_two])
+    grad_one, grad_dec = totals(z_one, [s_one])
+    grad_out, grad_qkv = last_sums(z_late, [s_mid, s_last], D, gw)
     vec_grads, start = [], 0
     for v in vectors:
         vec_grads.append(rows[start : start + v.shape[0]])

time: 390 us -> 363 us (0.931)
  Pallas kernels: 230 us -> 199 us
  waiting for transfers between devices: 29.3 us -> 47.2 us
  local copies, waits for them, and re-layouts: 25.9 us -> 15.5 us
  other arithmetic: 16.9 us -> 10.8 us
    ppermute x29 -> x28, waiting for transfers between devices: 9.9 us -> 28.8 us  [shift(): return lax.ppermute(values, 'dp', pairs)]
    pallas_call x8 -> x5, Pallas kernels: 75.9 us -> 66.1 us  [the longest x1 27.3 us: local(): pl.pallas_call(functools.partial(feed_back_kernel, row_dev, row_two), nam...]
    pallas_call x3, Pallas kernels: 40.7 us -> 32.3 us  [attend_back(): pl.pallas_call(functools.partial(attention_back_kernel, row_dev, lay, chu...]
    pallas_call x3, Pallas kernels: 31.1 us -> 22.8 us  [attend(): pl.pallas_call(functools.partial(attention_kernel, lay, chunk, head_dim),...]
    all_to_all x1 -> x2, starting transfers between devices: 4.64 us -> 9.64 us  [finish(): lax.all_to_all(blocks[0], 'dp', 0, 0, axis_index_groups=dev.groups('z'),...]
    broadcast_in_dim x6 -> x0, local copies, waits for them, and re-layouts: 4.04 us -> none  [local(): line = lambda v: jnp.pad(v, (0, wide - v.shape[0]))[None, :]]
    unnamed x92 -> x84, local copies, waits for them, and re-layouts: 8.62 us -> 4.61 us
    pallas_call x2 -> x1, Pallas kernels: 8.94 us -> 5.26 us  [result(): pl.pallas_call(functools.partial(assemble_kernel, sizes, self.widths), na...]
  transfers between devices with their start and end apart: 47 -> 47, of which waited for: 13 -> 13; matrix products, arithmetic and copies ran while one was open for 8% -> 6% of each run, Pallas kernels for 54% -> 50%
where the time goes in v3:
time: 363 us; the launch traced here: 357 us
  Pallas kernels  199 us (55%)
  starting transfers between devices  69.5 us (19%)
  waiting for transfers between devices  47.2 us (13%)
  local copies, waits for them, and re-layouts  15.5 us (4%)
  between operations  15.1 us (4%)
  other arithmetic  10.8 us (3%)
    pallas_call x3, Pallas kernels, attend_back(): pl.pallas_call(functools.partial(attention_back_kernel, row_dev, lay, chu...  32.3 us
    ppermute x28, starting transfers between devices, shift(): return lax.ppermute(values, 'dp', pairs)  29 us
    ppermute x28, waiting for transfers between devices, shift(): return lax.ppermute(values, 'dp', pairs)  28.8 us
    pallas_call x1, Pallas kernels, local(): pl.pallas_call(functools.partial(feed_back_kernel, row_dev, row_two), nam...  27.3 us
    pallas_call x3, Pallas kernels, attend(): pl.pallas_call(functools.partial(attention_kernel, lay, chunk, head_dim),...  22.8 us
    pallas_call x1, Pallas kernels, local(): pl.pallas_call(functools.partial(join_kernel, row_dev, sizes), name='join...  18.9 us
    pallas_call x4, Pallas kernels, add(): pl.pallas_call(functools.partial(chip_sum_kernel, sizes, pairs), name='ch...  17.1 us
    pallas_call x1, Pallas kernels, local(): pl.pallas_call(functools.partial(feed_kernel, parts, R // 24), name='feed...  16.1 us
  transfers between devices with their start and end apart: 47, of which 13 were waited for; matrix products, arithmetic and copies ran while one was open for 6% of the time, Pallas kernels for 50%

profile of v3, /device:TPU:0, one launch (start us, length us, event | category | flops | bytes accessed | tf_op | source)
XLA Modules:
  0.0 356.7 jit_solution(17985671867555243028)
XLA Ops:
  7.4 5.1 %collective-permute-start.2 = (bf16[24,2304]{1,0:T(8,128)(2,1)}, bf16[24,2304]{1,0:T(8,128)(2,1)S(1)}, u32[]{:S(2)}, u32[]{:S(2)}) collective-permute-start(bf16[24,2304]{1,0:T(8,128)(2,1)} %param.25), channel_id=1, source_target_pairs={{0,24},{1,25},{2,26},{3,27},{4,28},{5,29},{6,30},{7,31},{8,0},{9,1... | collective-permute-start | bytes 331784 | tf_op jit(solution)/shard_map/ppermute | solution.py:36
  16.2 6.1 %collective-permute-done.1 = bf16[24,2304]{1,0:T(8,128)(2,1)S(1)} collective-permute-done((bf16[24,2304]{1,0:T(8,128)(2,1)}, bf16[24,2304]{1,0:T(8,128)(2,1)S(1)}, u32[]{:S(2)}, u32[]{:S(2)}) %collective-permute-start.1) | collective-permute-done | bytes 110624 | tf_op jit(solution)/shard_map/ppermute | solution.py:36
  37.1 5.8 %all-to-all-done = bf16[32,15,128]{2,1,0:T(8,128)(2,1)S(1)} async-done(((bf16[32,15,128]{2,1,0:T(8,128)(2,1)}), bf16[32,15,128]{2,1,0:T(8,128)(2,1)S(1)}, u32[]{:S(2)}, u32[]{:S(2)}) %all-to-all-start) | async-done | bytes 122912 | tf_op jit(solution)/shard_map/all_to_all | solution.py:889
  43.7 6.1 %first_norm.1 = (bf16[960,768]{1,0:T(8,128)(2,1)}, bf16[960,768]{1,0:T(8,128)(2,1)}) custom-call(s32[16]{0:T(128)} %get-tuple-element.183.meta.place.spot, bf16[882,768]{1,0:T(8,128)(2,1)} %tokens, f32[8,768]{1,0:T(8,128)} %reshape.119.vecs.refs_4_.refs_15_), custom_call_target="tpu_custom_call" | custom-call | flops 26011238 | bytes 80000 | tf_op jit(solution)/shard_map/first_norm/pallas_call | solution.py:901
  52.5 8.4 %owner_side.1 = (bf16[1024,512]{1,0:T(8,128)(2,1)}, f32[8,512]{1,0:T(8,128)}) custom-call(bf16[1792,512]{1,0:T(8,128)(2,1)} %cot.1, bf16[128,128]{1,0:T(8,128)(2,1)} %bitcast.86), custom_call_target="tpu_custom_call" | custom-call | flops 20000000 | bytes 60000 | tf_op jit(solution)/shard_map/owner_side/pallas_call | solution.py:919
  65.3 5.3 %assemble.1 = bf16[4,8,24,2304]{3,2,1,0:T(8,128)(2,1)} custom-call(s32[16]{0:T(128)} %get-tuple-element.183.meta.place.spot, bf16[2,2,4,24,1152]{4,3,2,1,0:T(8,128)(2,1)} %copy-done, bf16[2,2,4,24,1152]{4,3,2,1,0:T(8,128)(2,1)} %copy-done.1, bf16[2,2,4,24,1152]{4,3,2,1,0:T(8,128)(2,1)} %copy-done.5, bf16[2,2,4,24,1152]{4,3,2,1,0:T(8,128)(2,1)} %copy-done.6), custom_call_target="tpu_custom_call" | custom-call | bytes 7077888 | tf_op jit(solution)/shard_map/assemble/pallas_call | solution.py:154
  70.5 7.5 %attention.3 = (bf16[960,256]{1,0:T(8,128)(2,1)}, bf16[960,256]{1,0:T(8,128)(2,1)}, bf16[960,256]{1,0:T(8,128)(2,1)}, bf16[4,400,400]{2,1,0:T(8,128)(2,1)}, bf16...) custom-call(s32[16]{0:T(128)} %get-tuple-element.183.meta.place.spot, bf16[960,768]{1,0:T(8,128)(2,1)} %get-tuple-element.214.h_in, ...), custom_call_target="tpu_custom_call" | custom-call | flops 3132462080 | bytes 8000000 | tf_op jit(solution)/shard_map/attention/pallas_call | solution.py:941
  80.3 7.7 %attention.4 = (bf16[960,256]{1,0:T(8,128)(2,1)}, bf16[960,256]{1,0:T(8,128)(2,1)}, bf16[960,256]{1,0:T(8,128)(2,1)}, bf16[4,400,400]{2,1,0:T(8,128)(2,1)}, bf16...) custom-call(s32[16]{0:T(128)} %get-tuple-element.183.meta.place.spot, bf16[960,768]{1,0:T(8,128)(2,1)} %get-tuple-element.214.h_in, ...), custom_call_target="tpu_custom_call" | custom-call | flops 3132462080 | bytes 8000000 | tf_op jit(solution)/shard_map/attention/pallas_call | solution.py:941
  88.0 6.1 %collective-permute-done.12 = bf16[4,96,384]{2,1,0:T(8,128)(2,1)S(1)} collective-permute-done((bf16[4,96,384]{2,1,0:T(8,128)(2,1)S(1)}, bf16[4,96,384]{2,1,0:T(8,128)(2,1)S(1)}, u32[]{:S(2)}, u32[]{:S(2)}) %collective-permute-start.12) | collective-permute-done | bytes 294944 | tf_op jit(solution)/shard_map/ppermute | solution.py:36
  96.8 3.6 all-to-all-start.1
  100.4 7.6 %attention.5 = (bf16[960,256]{1,0:T(8,128)(2,1)}, bf16[960,256]{1,0:T(8,128)(2,1)}, bf16[960,256]{1,0:T(8,128)(2,1)}, bf16[4,400,400]{2,1,0:T(8,128)(2,1)}, bf16...) custom-call(s32[16]{0:T(128)} %get-tuple-element.183.meta.place.spot, bf16[960,768]{1,0:T(8,128)(2,1)} %get-tuple-element.214.h_in, ...), custom_call_target="tpu_custom_call" | custom-call | flops 3132462080 | bytes 8000000 | tf_op jit(solution)/shard_map/attention/pallas_call | solution.py:941
  108.0 6.5 %collective-permute-done.14 = bf16[2,4,96,384]{3,2,1,0:T(8,128)(2,1)S(1)} collective-permute-done((bf16[2,4,96,384]{3,2,1,0:T(8,128)(2,1)S(1)}, bf16[2,4,96,384]{3,2,1,0:T(8,128)(2,1)S(1)}, u32[]{:S(2)}, u32[]{:S(2)}) %collective-permute-start.14) | collective-permute-done | bytes 589856 | tf_op jit(solution)/shard_map/ppermute | solution.py:36
  124.2 16.1 %feed.1 = (f32[960,768]{1,0:T(8,128)}, bf16[960,768]{1,0:T(8,128)(2,1)}, bf16[960,3072]{1,0:T(8,128)(2,1)}, bf16[960,3072]{1,0:T(8,128)(2,1)}) custom-call(bf16[960,256]{1,0:T(8,128)(2,1)} %get-tuple-element.202.refs_0_, bf16[960,256]{1,0:T(8,128)(2,1)} %get-tuple-element.209.refs_1_, bf16[960,256]{1,0:T(8,128)(2,1)} %get-tuple-element.215.refs_2_, ...), custom_call_target="tpu_custom_call" | custom-call | flops 5662310400 | bytes 25000000 | tf_op jit(solution)/shard_map/feed/pallas_call | solution.py:969
  140.3 18.9 %join.1 = (bf16[32,96,768]{2,1,0:T(8,128)(2,1)}, bf16[1024,512]{1,0:T(8,128)(2,1)}, bf16[960,768]{1,0:T(8,128)(2,1)}, bf16[16,24,512]{2,1,0:T(8,128)(2,1)}, bf16...) custom-call(s32[16]{0:T(128)} %get-tuple-element.183.meta.place.spot, bf16[960,3072]{1,0:T(8,128)(2,1)} %get-tuple-element.223.g_in, ...), custom_call_target="tpu_custom_call" | custom-call | flops 8304721920 | bytes 20000000 | tf_op jit(solution)/shard_map/join/pallas_call | solution.py:989
  159.2 3.6 %all-to-all-start.2 = ((bf16[32,32,512]{2,1,0:T(8,128)(2,1)}), bf16[32,32,512]{2,1,0:T(8,128)(2,1)}, u32[]{:S(2)}, u32[]{:S(2)}) async-start(bf16[32,32,512]{2,1,0:T(8,128)(2,1)} %bitcast.69), calls=%async_computation.2 | async-start | bytes 2097152 | tf_op jit(solution)/shard_map/all_to_all | solution.py:1012
  162.8 27.3 %feed_back.1 = (f32[960,768]{1,0:T(8,128)}, bf16[16,96,768]{2,1,0:T(8,128)(2,1)}, bf16[16,96,768]{2,1,0:T(8,128)(2,1)}, bf16[16,24,3072]{2,1,0:T(8,128)(2,1)}, b...) custom-call(s32[16]{0:T(128)} %get-tuple-element.183.meta.place.spot, bf16[960,768]{1,0:T(8,128)(2,1)} %get-tuple-element.233.dy_in, ...), custom_call_target="tpu_custom_call" | custom-call | flops 362387865600 | bytes 800000000 | tf_op jit(solution)/shard_map/feed_back/pallas_call | solution.py:1019
  191.0 11.4 %out_back.1 = (f32[960,768]{1,0:T(8,128)}, bf16[960,768]{1,0:T(8,128)(2,1)}, bf16[16,24,768]{2,1,0:T(8,128)(2,1)}, bf16[16,24,768]{2,1,0:T(8,128)(2,1)}, f32[8,768]{1,0:T(8,128)}) custom-call(s32[16]{0:T(128)} %get-tuple-element.183.meta.place.spot, f32[960,768]{1,0:T(8,128)} %get-tuple-element.237.dh_in, f32[960,768]{1,0:T(8,128)} %get-tuple-element.224.r_in, ...), custom_call_target="tpu_custom_call" | custom-call | flops 45298483200 | bytes 400000000 | tf_op jit(solution)/shard_map/out_back/pallas_call | solution.py:1037
  204.3 4.8 %chip_sum.4 = (bf16[4,96,768]{2,1,0:T(8,128)(2,1)}, bf16[4,96,768]{2,1,0:T(8,128)(2,1)}, bf16[4,96,768]{2,1,0:T(8,128)(2,1)}, bf16[4,96,768]{2,1,0:T(8,128)(2,1)}) custom-call(s32[16]{0:T(128)} %get-tuple-element.183.meta.place.spot, bf16[16,96,768]{2,1,0:T(8,128)(2,1)} %get-tuple-element.244.refs_0_, bf16[16,96,768]{2,1,0:T(8,128)(2,1)} %collective-permute-done.18.refs_1_), custom_call_target="tpu_custom_call" | custom-call | bytes 7077888 | tf_op jit(solution)/shard_map/chip_sum/pallas_call | solution.py:220
  212.4 10.8 %attention_back.3 = (bf16[960,256]{1,0:T(8,128)(2,1)}, bf16[960,256]{1,0:T(8,128)(2,1)}, bf16[960,256]{1,0:T(8,128)(2,1)}, bf16[16,24,768]{2,1,0:T(8,128)(2,1)},...) custom-call(s32[16]{0:T(128)} %get-tuple-element.183.meta.place.spot, bf16[960,768]{1,0:T(8,128)(2,1)} %get-tuple-element.214.h_in, ...), custom_call_target="tpu_custom_call" | custom-call | flops 82649243648 | bytes 200000000 | tf_op jit(solution)/shard_map/attention_back/pallas_call | solution.py:1056
  226.5 5.2 %chip_sum.5 = (bf16[4,24,3584]{2,1,0:T(8,128)(2,1)}, bf16[4,24,3584]{2,1,0:T(8,128)(2,1)}, bf16[4,24,3584]{2,1,0:T(8,128)(2,1)}, bf16[4,24,3584]{2,1,0:T(8,128)(2,1)}) custom-call(s32[16]{0:T(128)} %get-tuple-element.183.meta.place.spot, bf16[16,24,3072]{2,1,0:T(8,128)(2,1)} %get-tuple-element.253.refs_0_, bf16[16,24,512]{2,1,0:T(8,128)(2,1)} %get-tuple-element.254.refs_1_, ...), custom_call_target="tpu_custom_call" | custom-call | bytes 8257536 | tf_op jit(solution)/shard_map/chip_sum/pallas_call | solution.py:220
  235.2 10.8 %attention_back.4 = (bf16[960,256]{1,0:T(8,128)(2,1)}, bf16[960,256]{1,0:T(8,128)(2,1)}, bf16[960,256]{1,0:T(8,128)(2,1)}, bf16[16,24,768]{2,1,0:T(8,128)(2,1)},...) custom-call(s32[16]{0:T(128)} %get-tuple-element.183.meta.place.spot, bf16[960,768]{1,0:T(8,128)(2,1)} %get-tuple-element.214.h_in, ...), custom_call_target="tpu_custom_call" | custom-call | flops 82649243648 | bytes 200000000 | tf_op jit(solution)/shard_map/attention_back/pallas_call | solution.py:1056
  246.1 3.0 collective-permute-done.25.refs_3_
  252.7 4.9 %all-to-all-start.3 = ((bf16[4,96,768]{2,1,0:T(8,128)(2,1)}), bf16[4,96,768]{2,1,0:T(8,128)(2,1)S(1)}, u32[]{:S(2)}, u32[]{:S(2)}) async-start(bf16[4,96,768]{2,1,0:T(8,128)(2,1)} %plane_sum.3), calls=%async_computation.3 | async-start | bytes 1179648 | tf_op jit(solution)/shard_map/all_to_all | solution.py:286
  257.6 3.6 chip_sum.6
  263.8 10.7 %attention_back.5 = (bf16[960,256]{1,0:T(8,128)(2,1)}, bf16[960,256]{1,0:T(8,128)(2,1)}, bf16[960,256]{1,0:T(8,128)(2,1)}, bf16[16,24,768]{2,1,0:T(8,128)(2,1)},...) custom-call(s32[16]{0:T(128)} %get-tuple-element.183.meta.place.spot, bf16[960,768]{1,0:T(8,128)(2,1)} %get-tuple-element.214.h_in, ...), custom_call_target="tpu_custom_call" | custom-call | flops 82649243648 | bytes 200000000 | tf_op jit(solution)/shard_map/attention_back/pallas_call | solution.py:1056
  274.6 5.9 %collective-permute-done.30.refs_3_ = bf16[4,24,3584]{2,1,0:T(8,128)(2,1)S(1)} collective-permute-done((bf16[4,24,3584]{2,1,0:T(8,128)(2,1)}, bf16[4,24,3584]{2,1,0:T(8,128)(2,1)S(1)}, u32[]{:S(2)}, u32[]{:S(2)}) %collective-permute-start.30) | collective-permute-done | bytes 688160 | tf_op jit(solution)/shard_map/ppermute | solution.py:50
  286.9 4.7 %all-to-all-start.4 = ((bf16[4,24,3584]{2,1,0:T(8,128)(2,1)}), bf16[4,24,3584]{2,1,0:T(8,128)(2,1)S(1)}, u32[]{:S(2)}, u32[]{:S(2)}) async-start(bf16[4,24,3584]{2,1,0:T(8,128)(2,1)} %plane_sum.4), calls=%async_computation.4 | async-start | bytes 1376256 | tf_op jit(solution)/shard_map/all_to_all | solution.py:286
  291.7 11.6 %first_back.1 = (bf16[882,768]{1,0:T(8,128)(2,1)}, f32[8,768]{1,0:T(8,128)}) custom-call(s32[16]{0:T(128)} %get-tuple-element.183.meta.place.spot, bf16[960,256]{1,0:T(8,128)(2,1)} %get-tuple-element.252.refs_0_, bf16[960,256]{1,0:T(8,128)(2,1)} %get-tuple-element.267.refs_1_, bf16[960,256]{1,0:T(8,128)(2,1)} %get-tuple-element.290.refs_2_, ...), custom_call_target="tpu_custom_call" | custom-call | flops 93958963200 | bytes 400000000 | tf_op jit(solution)/shard_map/first_back/pallas_call | solution.py:1089
  306.1 3.6 %chip_sum.7 = (bf16[4,24,1536]{2,1,0:T(8,128)(2,1)}, bf16[4,24,1536]{2,1,0:T(8,128)(2,1)}, bf16[4,24,1536]{2,1,0:T(8,128)(2,1)}, bf16[4,24,1536]{2,1,0:T(8,128)(2,1)}) custom-call(s32[16]{0:T(128)} %get-tuple-element.183.meta.place.spot, bf16[16,24,768]{2,1,0:T(8,128)(2,1)} %get-tuple-element.261.refs_0_, bf16[16,24,768]{2,1,0:T(8,128)(2,1)} %get-tuple-element.286.refs_1_, ...), custom_call_target="tpu_custom_call" | custom-call | bytes 3538944 | tf_op jit(solution)/shard_map/chip_sum/pallas_call | solution.py:220
  313.2 9.1 %decode.1 = bf16[1792,512]{1,0:T(8,128)(2,1)} custom-call(bf16[1024,512]{1,0:T(8,128)(2,1)} %bitcast.45.got, bf16[128,128]{1,0:T(8,128)(2,1)} %bitcast.87, f32[2,512]{1,0:T(2,128)} %reshape.121.vec_dec), custom_call_target="tpu_custom_call" | custom-call | flops 20000000000 | bytes 140000000 | tf_op jit(solution)/shard_map/decode/pallas_call | solution.py:1114
  322.9 5.4 %all-to-all-start.5 = ((f32[32,1,320]{2,1,0:T(1,128)}), f32[32,1,320]{2,1,0:T(1,128)S(1)}, u32[]{:S(2)}, u32[]{:S(2)}) async-start(f32[32,1,320]{2,1,0:T(1,128)} %copy.55), calls=%async_computation.5 | async-start | bytes 98304 | tf_op jit(solution)/shard_map/all_to_all | solution.py:1113
  341.5 5.6 %collective-permute-done.38.refs_2_ = bf16[24,3072]{1,0:T(8,128)(2,1)S(1)} collective-permute-done((bf16[24,3072]{1,0:T(8,128)(2,1)}, bf16[24,3072]{1,0:T(8,128)(2,1)S(1)}, u32[]{:S(2)}, u32[]{:S(2)}) %collective-permute-start.38) | collective-permute-done | bytes 147488 | tf_op jit(solution)/shard_map/ppermute | solution.py:36
  (221 shorter events, 88.9 us)
Async XLA Ops:
  7.3 116.9 %all-gather.2.cloned.1.call-start = ((), (), s32[]{:S(2)}) async-start(), calls=%async_computation.6 | async-start | bytes 6893568 | tf_op jit(solution)/shard_map/all_gather | solution.py:883
  33.7 16.1 %collective-permute-start.5 = (bf16[2,4,24,1152]{3,2,1,0:T(8,128)(2,1)S(1)}, bf16[2,4,24,1152]{3,2,1,0:T(8,128)(2,1)S(1)}, u32[]{:S(2)}, u32[]{:S(2)}) collective-permute-start(bf16[2,4,24,1152]{3,2,1,0:T(8,128)(2,1)S(1)} %pad_maximum_fusion.8), channel_id=1, source_target_pairs={{0,4},{1,5},{2,6},{3,7},{4,0},{5,1},{6,2},{7,3},{8,12},{9,13},{10,... | collective-permute-start | bytes 1327112 | tf_op jit(solution)/shard_map/ppermute | solution.py:36
  60.9 17.2 %collective-permute-start.9 = (bf16[96,768]{1,0:T(8,128)(2,1)S(1)}, bf16[96,768]{1,0:T(8,128)(2,1)S(1)}, u32[]{:S(2)}, u32[]{:S(2)}) collective-permute-start(bf16[96,768]{1,0:T(8,128)(2,1)S(1)} %copy-done.22), channel_id=1, source_target_pairs={{0,8},{1,9},{2,10},{3,11},{4,12},{5,13},{6,14},{7,15},{8,16},{9,17... | collective-permute-start | bytes 442376 | tf_op jit(solution)/shard_map/ppermute | solution.py:36
  61.7 16.4 %collective-permute-start.10 = (bf16[96,768]{1,0:T(8,128)(2,1)S(1)}, bf16[96,768]{1,0:T(8,128)(2,1)S(1)}, u32[]{:S(2)}, u32[]{:S(2)}) collective-permute-start(bf16[96,768]{1,0:T(8,128)(2,1)S(1)} %copy-done.22), channel_id=1, source_target_pairs={{0,16},{1,17},{2,18},{3,19},{4,20},{5,21},{6,22},{7,23},{8,24},{9,... | collective-permute-start | bytes 442376 | tf_op jit(solution)/shard_map/ppermute | solution.py:36
  78.2 15.8 %collective-permute-start.12 = (bf16[4,96,384]{2,1,0:T(8,128)(2,1)S(1)}, bf16[4,96,384]{2,1,0:T(8,128)(2,1)S(1)}, u32[]{:S(2)}, u32[]{:S(2)}) collective-permute-start(bf16[4,96,384]{2,1,0:T(8,128)(2,1)S(1)} %get-tuple-element.210), channel_id=1, source_target_pairs={{0,2},{1,3},{2,0},{3,1},{4,6},{5,7},{6,4},{7,5},{8,10},{9,11},{10,... | collective-permute-start | bytes 884744 | tf_op jit(solution)/shard_map/ppermute | solution.py:36
  79.0 15.6 %collective-permute-start.13 = (bf16[4,96,384]{2,1,0:T(8,128)(2,1)S(1)}, bf16[4,96,384]{2,1,0:T(8,128)(2,1)S(1)}, u32[]{:S(2)}, u32[]{:S(2)}) collective-permute-start(bf16[4,96,384]{2,1,0:T(8,128)(2,1)S(1)} %get-tuple-element.212), channel_id=1, source_target_pairs={{0,4},{1,5},{2,6},{3,7},{4,0},{5,1},{6,2},{7,3},{8,12},{9,13},{10,... | collective-permute-start | bytes 884744 | tf_op jit(solution)/shard_map/ppermute | solution.py:36
  94.7 19.7 %collective-permute-start.14 = (bf16[2,4,96,384]{3,2,1,0:T(8,128)(2,1)S(1)}, bf16[2,4,96,384]{3,2,1,0:T(8,128)(2,1)S(1)}, u32[]{:S(2)}, u32[]{:S(2)}) collective-permute-start(bf16[2,4,96,384]{3,2,1,0:T(8,128)(2,1)S(1)} %pad_maximum_fusion.5), channel_id=1, source_target_pairs={{0,4},{1,5},{2,6},{3,7},{4,0},{5,1},{6,2},{7,3},{8,12},{9,13},{10,... | collective-permute-start | bytes 1769480 | tf_op jit(solution)/shard_map/ppermute | solution.py:36
  95.7 21.6 %collective-permute-start.15 = (bf16[2,4,96,384]{3,2,1,0:T(8,128)(2,1)S(1)}, bf16[2,4,96,384]{3,2,1,0:T(8,128)(2,1)S(1)}, u32[]{:S(2)}, u32[]{:S(2)}) collective-permute-start(bf16[2,4,96,384]{3,2,1,0:T(8,128)(2,1)S(1)} %pad_maximum_fusion.6), channel_id=1, source_target_pairs={{0,2},{1,3},{2,0},{3,1},{4,6},{5,7},{6,4},{7,5},{8,10},{9,11},{10,... | collective-permute-start | bytes 1769480 | tf_op jit(solution)/shard_map/ppermute | solution.py:36
  96.8 43.4 %all-to-all-start.1 = ((bf16[32,32,512]{2,1,0:T(8,128)(2,1)}), bf16[32,32,512]{2,1,0:T(8,128)(2,1)}, u32[]{:S(2)}, u32[]{:S(2)}) async-start(bf16[32,32,512]{2,1,0:T(8,128)(2,1)} %bitcast.42), calls=%async_computation.1 | async-start | bytes 2097152 | tf_op jit(solution)/shard_map/all_to_all | solution.py:960
  117.4 22.9 %collective-permute-start.16 = (bf16[2,2,4,96,384]{4,3,2,1,0:T(8,128)(2,1)S(1)}, bf16[2,2,4,96,384]{4,3,2,1,0:T(8,128)(2,1)}, u32[]{:S(2)}, u32[]{:S(2)}) collective-permute-start(bf16[2,2,4,96,384]{4,3,2,1,0:T(8,128)(2,1)S(1)} %pad_maximum_fusion.part_a), channel_id=1, source_target_pairs={{0,1},{1,0},{2,3},{3,2},{4,5},{5,4},{6,7},{7,6},{8,9},{9,8},{10,11... | collective-permute-start | bytes 3538952 | tf_op jit(solution)/shard_map/ppermute | solution.py:36
  119.3 20.9 %collective-permute-start.17 = (bf16[2,2,4,96,384]{4,3,2,1,0:T(8,128)(2,1)S(1)}, bf16[2,2,4,96,384]{4,3,2,1,0:T(8,128)(2,1)}, u32[]{:S(2)}, u32[]{:S(2)}) collective-permute-start(bf16[2,2,4,96,384]{4,3,2,1,0:T(8,128)(2,1)S(1)} %pad_maximum_fusion.1.part_b), channel_id=1, source_target_pairs={{0,1},{1,0},{2,3},{3,2},{4,5},{5,4},{6,7},{7,6},{8,9},{9,8},{10,11... | collective-permute-start | bytes 3538952 | tf_op jit(solution)/shard_map/ppermute | solution.py:36
  159.2 49.9 %all-to-all-start.2 = ((bf16[32,32,512]{2,1,0:T(8,128)(2,1)}), bf16[32,32,512]{2,1,0:T(8,128)(2,1)}, u32[]{:S(2)}, u32[]{:S(2)}) async-start(bf16[32,32,512]{2,1,0:T(8,128)(2,1)} %bitcast.69), calls=%async_computation.2 | async-start | bytes 2097152 | tf_op jit(solution)/shard_map/all_to_all | solution.py:1012
  190.5 18.6 %collective-permute-start.19 = (bf16[16,24,3072]{2,1,0:T(8,128)(2,1)}, bf16[16,24,3072]{2,1,0:T(8,128)(2,1)S(1)}, u32[]{:S(2)}, u32[]{:S(2)}) collective-permute-start(bf16[16,24,3072]{2,1,0:T(8,128)(2,1)} %get-tuple-element.249), channel_id=1, source_target_pairs={{0,1},{1,0},{2,3},{3,2},{4,5},{5,4},{6,7},{7,6},{8,9},{9,8},{10,11... | collective-permute-start | bytes 7077896 | tf_op jit(solution)/shard_map/ppermute | solution.py:36
  190.8 18.3 %collective-permute-start.20 = (bf16[16,24,512]{2,1,0:T(8,128)(2,1)S(1)}, bf16[16,24,512]{2,1,0:T(8,128)(2,1)S(1)}, u32[]{:S(2)}, u32[]{:S(2)}) collective-permute-start(bf16[16,24,512]{2,1,0:T(8,128)(2,1)S(1)} %copy-done.39), channel_id=1, source_target_pairs={{0,1},{1,0},{2,3},{3,2},{4,5},{5,4},{6,7},{7,6},{8,9},{9,8},{10,11... | collective-permute-start | bytes 1179656 | tf_op jit(solution)/shard_map/ppermute | solution.py:36
  209.1 15.8 %collective-permute-start.21 = (bf16[4,96,768]{2,1,0:T(8,128)(2,1)}, bf16[4,96,768]{2,1,0:T(8,128)(2,1)S(1)}, u32[]{:S(2)}, u32[]{:S(2)}) collective-permute-start(bf16[4,96,768]{2,1,0:T(8,128)(2,1)} %get-tuple-element.255), channel_id=1, source_target_pairs={{0,2},{1,3},{2,0},{3,1},{4,6},{5,7},{6,4},{7,5},{8,10},{9,11},{10,... | collective-permute-start | bytes 1769480 | tf_op jit(solution)/shard_map/ppermute | solution.py:50
  223.2 22.8 %collective-permute-start.23 = (bf16[16,24,768]{2,1,0:T(8,128)(2,1)}, bf16[16,24,768]{2,1,0:T(8,128)(2,1)S(1)}, u32[]{:S(2)}, u32[]{:S(2)}) collective-permute-start(bf16[16,24,768]{2,1,0:T(8,128)(2,1)} %get-tuple-element.272), channel_id=1, source_target_pairs={{0,1},{1,0},{2,3},{3,2},{4,5},{5,4},{6,7},{7,6},{8,9},{9,8},{10,11... | collective-permute-start | bytes 1769480 | tf_op jit(solution)/shard_map/ppermute | solution.py:36
  223.3 22.8 %collective-permute-start.24 = (bf16[16,24,768]{2,1,0:T(8,128)(2,1)}, bf16[16,24,768]{2,1,0:T(8,128)(2,1)}, u32[]{:S(2)}, u32[]{:S(2)}) collective-permute-start(bf16[16,24,768]{2,1,0:T(8,128)(2,1)} %get-tuple-element.273), channel_id=1, source_target_pairs={{0,1},{1,0},{2,3},{3,2},{4,5},{5,4},{6,7},{7,6},{8,9},{9,8},{10,11... | collective-permute-start | bytes 1769480 | tf_op jit(solution)/shard_map/ppermute | solution.py:36
  231.6 17.5 %collective-permute-start.25 = (bf16[4,96,768]{2,1,0:T(8,128)(2,1)}, bf16[4,96,768]{2,1,0:T(8,128)(2,1)S(1)}, u32[]{:S(2)}, u32[]{:S(2)}) collective-permute-start(bf16[4,96,768]{2,1,0:T(8,128)(2,1)} %get-tuple-element.275), channel_id=1, source_target_pairs={{0,6},{1,7},{2,4},{3,5},{4,2},{5,3},{6,0},{7,1},{8,14},{9,15},{10,... | collective-permute-start | bytes 1769480 | tf_op jit(solution)/shard_map/ppermute | solution.py:50
  233.2 28.9 %collective-permute-start.26 = (bf16[4,24,3584]{2,1,0:T(8,128)(2,1)}, bf16[4,24,3584]{2,1,0:T(8,128)(2,1)S(1)}, u32[]{:S(2)}, u32[]{:S(2)}) collective-permute-start(bf16[4,24,3584]{2,1,0:T(8,128)(2,1)} %get-tuple-element.283), channel_id=1, source_target_pairs={{0,2},{1,3},{2,0},{3,1},{4,6},{5,7},{6,4},{7,5},{8,10},{9,11},{10,... | collective-permute-start | bytes 2064392 | tf_op jit(solution)/shard_map/ppermute | solution.py:50
  234.7 27.4 %collective-permute-start.27 = (bf16[4,24,3584]{2,1,0:T(8,128)(2,1)}, bf16[4,24,3584]{2,1,0:T(8,128)(2,1)S(1)}, u32[]{:S(2)}, u32[]{:S(2)}) collective-permute-start(bf16[4,24,3584]{2,1,0:T(8,128)(2,1)} %get-tuple-element.284), channel_id=1, source_target_pairs={{0,4},{1,5},{2,6},{3,7},{4,0},{5,1},{6,2},{7,3},{8,12},{9,13},{10,... | collective-permute-start | bytes 2064392 | tf_op jit(solution)/shard_map/ppermute | solution.py:50
  246.0 28.5 %collective-permute-start.28 = (bf16[16,24,768]{2,1,0:T(8,128)(2,1)}, bf16[16,24,768]{2,1,0:T(8,128)(2,1)S(1)}, u32[]{:S(2)}, u32[]{:S(2)}) collective-permute-start(bf16[16,24,768]{2,1,0:T(8,128)(2,1)} %get-tuple-element.288), channel_id=1, source_target_pairs={{0,1},{1,0},{2,3},{3,2},{4,5},{5,4},{6,7},{7,6},{8,9},{9,8},{10,11... | collective-permute-start | bytes 1769480 | tf_op jit(solution)/shard_map/ppermute | solution.py:36
  252.7 31.3 %all-to-all-start.3 = ((bf16[4,96,768]{2,1,0:T(8,128)(2,1)}), bf16[4,96,768]{2,1,0:T(8,128)(2,1)S(1)}, u32[]{:S(2)}, u32[]{:S(2)}) async-start(bf16[4,96,768]{2,1,0:T(8,128)(2,1)} %plane_sum.3), calls=%async_computation.3 | async-start | bytes 1179648 | tf_op jit(solution)/shard_map/all_to_all | solution.py:286
  262.1 18.4 %collective-permute-start.30 = (bf16[4,24,3584]{2,1,0:T(8,128)(2,1)}, bf16[4,24,3584]{2,1,0:T(8,128)(2,1)S(1)}, u32[]{:S(2)}, u32[]{:S(2)}) collective-permute-start(bf16[4,24,3584]{2,1,0:T(8,128)(2,1)} %get-tuple-element.302), channel_id=1, source_target_pairs={{0,6},{1,7},{2,4},{3,5},{4,2},{5,3},{6,0},{7,1},{8,14},{9,15},{10,... | collective-permute-start | bytes 2064392 | tf_op jit(solution)/shard_map/ppermute | solution.py:50
  274.5 30.7 %collective-permute-start.29 = (bf16[16,24,768]{2,1,0:T(8,128)(2,1)}, bf16[16,24,768]{2,1,0:T(8,128)(2,1)S(1)}, u32[]{:S(2)}, u32[]{:S(2)}) collective-permute-start(bf16[16,24,768]{2,1,0:T(8,128)(2,1)} %get-tuple-element.291), channel_id=1, source_target_pairs={{0,1},{1,0},{2,3},{3,2},{4,5},{5,4},{6,7},{7,6},{8,9},{9,8},{10,11... | collective-permute-start | bytes 1769480 | tf_op jit(solution)/shard_map/ppermute | solution.py:36
  280.5 24.8 %collective-permute-start.31 = (bf16[4,24,1536]{2,1,0:T(8,128)(2,1)}, bf16[4,24,1536]{2,1,0:T(8,128)(2,1)S(1)}, u32[]{:S(2)}, u32[]{:S(2)}) collective-permute-start(bf16[4,24,1536]{2,1,0:T(8,128)(2,1)} %get-tuple-element.314), channel_id=1, source_target_pairs={{0,2},{1,3},{2,0},{3,1},{4,6},{5,7},{6,4},{7,5},{8,10},{9,11},{10,... | collective-permute-start | bytes 884744 | tf_op jit(solution)/shard_map/ppermute | solution.py:50
  281.3 24.0 %collective-permute-start.32 = (bf16[4,24,1536]{2,1,0:T(8,128)(2,1)}, bf16[4,24,1536]{2,1,0:T(8,128)(2,1)}, u32[]{:S(2)}, u32[]{:S(2)}) collective-permute-start(bf16[4,24,1536]{2,1,0:T(8,128)(2,1)} %get-tuple-element.315), channel_id=1, source_target_pairs={{0,4},{1,5},{2,6},{3,7},{4,0},{5,1},{6,2},{7,3},{8,12},{9,13},{10,... | collective-permute-start | bytes 884744 | tf_op jit(solution)/shard_map/ppermute | solution.py:50
  282.8 22.5 %collective-permute-start.33 = (bf16[4,24,1536]{2,1,0:T(8,128)(2,1)}, bf16[4,24,1536]{2,1,0:T(8,128)(2,1)}, u32[]{:S(2)}, u32[]{:S(2)}) collective-permute-start(bf16[4,24,1536]{2,1,0:T(8,128)(2,1)} %get-tuple-element.316), channel_id=1, source_target_pairs={{0,6},{1,7},{2,4},{3,5},{4,2},{5,3},{6,0},{7,1},{8,14},{9,15},{10,... | collective-permute-start | bytes 884744 | tf_op jit(solution)/shard_map/ppermute | solution.py:50
  286.9 26.3 %all-to-all-start.4 = ((bf16[4,24,3584]{2,1,0:T(8,128)(2,1)}), bf16[4,24,3584]{2,1,0:T(8,128)(2,1)S(1)}, u32[]{:S(2)}, u32[]{:S(2)}) async-start(bf16[4,24,3584]{2,1,0:T(8,128)(2,1)} %plane_sum.4), calls=%async_computation.4 | async-start | bytes 1376256 | tf_op jit(solution)/shard_map/all_to_all | solution.py:286
  309.7 18.8 %collective-permute-start.34 = (bf16[4,24,1536]{2,1,0:T(8,128)(2,1)}, bf16[4,24,1536]{2,1,0:T(8,128)(2,1)S(1)}, u32[]{:S(2)}, u32[]{:S(2)}) collective-permute-start(bf16[4,24,1536]{2,1,0:T(8,128)(2,1)} %get-tuple-element.325), channel_id=1, source_target_pairs={{0,2},{1,3},{2,0},{3,1},{4,6},{5,7},{6,4},{7,5},{8,10},{9,11},{10,... | collective-permute-start | bytes 884744 | tf_op jit(solution)/shard_map/ppermute | solution.py:50
  310.5 18.0 %collective-permute-start.35 = (bf16[4,24,1536]{2,1,0:T(8,128)(2,1)}, bf16[4,24,1536]{2,1,0:T(8,128)(2,1)S(1)}, u32[]{:S(2)}, u32[]{:S(2)}) collective-permute-start(bf16[4,24,1536]{2,1,0:T(8,128)(2,1)} %get-tuple-element.326), channel_id=1, source_target_pairs={{0,4},{1,5},{2,6},{3,7},{4,0},{5,1},{6,2},{7,3},{8,12},{9,13},{10,... | collective-permute-start | bytes 884744 | tf_op jit(solution)/shard_map/ppermute | solution.py:50
  312.0 16.5 %collective-permute-start.36 = (bf16[4,24,1536]{2,1,0:T(8,128)(2,1)}, bf16[4,24,1536]{2,1,0:T(8,128)(2,1)S(1)}, u32[]{:S(2)}, u32[]{:S(2)}) collective-permute-start(bf16[4,24,1536]{2,1,0:T(8,128)(2,1)} %get-tuple-element.327), channel_id=1, source_target_pairs={{0,6},{1,7},{2,4},{3,5},{4,2},{5,3},{6,0},{7,1},{8,14},{9,15},{10,... | collective-permute-start | bytes 884744 | tf_op jit(solution)/shard_map/ppermute | solution.py:50
  322.9 16.7 %all-to-all-start.5 = ((f32[32,1,320]{2,1,0:T(1,128)}), f32[32,1,320]{2,1,0:T(1,128)S(1)}, u32[]{:S(2)}, u32[]{:S(2)}) async-start(f32[32,1,320]{2,1,0:T(1,128)} %copy.55), calls=%async_computation.5 | async-start | bytes 98304 | tf_op jit(solution)/shard_map/all_to_all | solution.py:1113
  (57 other events, 720.1 us)
Sparse Core Ops, SparseCore 0:
  22.5 84.0 all-gather.1

commit v4 on v3

--- a/solution.py
+++ b/solution.py
@@ -309,18 +309,24 @@
     return out
 
 
-def last_sums_kernel(moves, *refs):
-    terms, outs = refs[:-2], refs[-2:]
+def last_sums_kernel(count, moves, vectors_at, *refs):
+    terms, outs = refs[:count], refs[count:]
     for start, width, out, at in moves:
         total = terms[0][:, start : start + width].astype(F32)
         for term in terms[1:]:
             total += term[:, start : start + width].astype(F32)
         outs[out][:, at : at + width] = total
-
-
-def last_sums(arrived, scatters, model, head_cols):
+    for out, (row, lane) in zip(outs[2:], vectors_at):
+        lanes = slice(lane, lane + out.shape[1])
+        total = terms[0][:, lanes].astype(F32)
+        for term in terms[1:]:
+            total += term[:, lanes].astype(F32)
+        out[...] = total[row : row + 1]
+
+
+def last_sums(arrived, scatters, model, head_cols, lengths):
     rows, width = arrived[0].shape
-    moves, start, first = [], 0, True
+    moves, rides, start, first = [], [], 0, True
     part = -1
     for s in scatters:
         tiles, span = [w // s.steps for w in s.widths], sum(s.widths) // s.steps
@@ -331,6 +337,9 @@
                 if first:
                     moves.append((source, tile, 0, i * tile))
                     continue
+                if s is scatters[-1] and t == len(tiles) - 1:
+                    rides.append(source)
+                    continue
                 piece = min(tile, head_cols)
                 for k in range(0, tile, piece):
                     block, inside = divmod(i * tile + k, head_cols)
@@ -338,9 +347,14 @@
             if first:
                 part, first = -1, False
         start += sum(s.widths)
-    shapes = [(rows, model), (rows, 3 * model)]
+    ride_tile = scatters[-1].widths[-1] // scatters[-1].steps
+    vectors_at = []
+    for i in range(len(lengths)):
+        step, inside = divmod(128 * (i // rows), ride_tile)
+        vectors_at.append((i % rows, rides[step] + inside))
+    shapes = [(rows, model), (rows, 3 * model)] + [(1, n) for n in lengths]
     return pl.pallas_call(
-        functools.partial(last_sums_kernel, moves),
+        functools.partial(last_sums_kernel, len(arrived), moves, vectors_at),
         name="last_sums",
         grid=(1,),
         in_specs=[whole((rows, width))] * len(arrived),
@@ -426,6 +440,34 @@
         lane = lax.broadcasted_iota(jnp.int32, (1, size), 1)
         live = (lane < real) & (lane % self.slots < kept)
         return jnp.where(live, 0.0, MASK_FILL)
+
+
+def spread_lanes(width, full):
+    lane = lax.broadcasted_iota(jnp.int32, (1, full), 1) % width
+    return lax.broadcasted_iota(jnp.int32, (128, 1), 0) == lane
+
+
+def own_lanes(count, width, full):
+    lane = lax.broadcasted_iota(jnp.int32, (1, full), 1) // width
+    return lax.broadcasted_iota(jnp.int32, (count, 1), 0) == lane
+
+
+def pack_rows(count, width, joined, out, first):
+    vectors, full = joined.shape
+    mask = own_lanes(count, width, full)
+    split = jnp.concatenate(
+        [jnp.where(mask, joined[v : v + 1, :], 0.0) for v in range(vectors)], axis=0
+    )
+    high = split.astype(BF)
+    rest = split - high.astype(F32)
+    middle = rest.astype(BF)
+    low = (rest - middle.astype(F32)).astype(BF)
+    lanes = jnp.where(spread_lanes(width, full), 1.0, 0.0).astype(BF)
+    found = dot_cols(jnp.concatenate([high, middle, low], axis=0), lanes)
+    size = vectors * count
+    total = found[:size] + found[size : 2 * size] + found[2 * size :]
+    for v in range(vectors):
+        out[first + v] = total[v * count : (v + 1) * count]
 
 
 LANE_SLOTS = 8
@@ -789,9 +831,9 @@
     sums[1:2, :] = row_sum(dv_out[...].astype(F32))
 
 
-def first_back_kernel(lay, parts, meta, *refs):
+def first_back_kernel(lay, parts, count, widths, meta, *refs):
     grads, more = refs[: 3 * parts], refs[3 * parts : 4 * parts]
-    w_qkv, x_in, dr_in, vecs, sums_two, db_two, out, sums, kept = refs[4 * parts :]
+    w_qkv, x_in, dr_in, vecs, sums_two, db_two, db_one, sums_dec, out, sheet, sums, kept = refs[4 * parts :]
     step = pl.program_id(0)
     rows = x_in.shape[0]
     width = grads[0].shape[1]
@@ -819,6 +861,9 @@
         slot = lax.broadcasted_iota(jnp.int32, (out.shape[0], 1), 0)
         row = lax.broadcasted_iota(jnp.int32, (1, lay.rows), 1)
         out[...] = dot(one_hot(slot, lay.source(row, meta[BIG])), kept[...]).astype(BF)
+        pack_rows(count, widths[0], sums[...], sheet, 0)
+        pack_rows(count, widths[1], db_one[...], sheet, 8)
+        pack_rows(count, widths[2], sums_dec[0:2, :], sheet, 9)
 
 
 def owner_rank(owner_vec):
@@ -1074,43 +1119,47 @@
     s_mid = Scatter(dev, [(own_out, sent_out), back[0][3:5]], meta)
     c_mid = s_mid.swap(back[0][0])
     back.append(attend_back(1, held(d_att, back[0][0], s_one.blocks[0])))
-    s_mid.add(back[1][0], *far, *c_mid)
-    lines_two, z_two = finish(dev, meta, [s_two], True, back[1][0])
+    lines_two, z_two = finish(dev, meta, [s_two], True, back[1][0], *far)
     far = s_one.far(back[1][0], *near)
-    s_last = Scatter(dev, [back[1][3:5]], meta)
-    c_last = s_last.swap(back[1][0])
-    back.append(attend_back(2, held(d_att, back[1][0], s_mid.blocks[0], lines_two[0], *near)))
-    s_last.more(*back[2][3:5])
-    near = s_mid.near(back[2][0], *far) + s_mid.far(back[2][0], *far)
-    c_last += s_last.swap(back[2][0], *c_last)
-    lines_one, z_one = finish(dev, meta, [s_one], True, back[2][0], *far, z_two)
+    s_mid.more(*back[1][3:5])
+    c_mid += s_mid.swap(back[1][0])
+    back.append(attend_back(2, held(d_att, back[1][0], lines_two[0], *near)))
+    s_last = Scatter(dev, [back[2][3:5]], meta)
+    c_last = s_last.swap(back[2][0])
+    s_mid.add(back[2][0], *c_mid)
+    near = s_mid.near() + s_mid.far()
+    lines_one, z_one = finish(dev, meta, [s_one], True, back[2][0], *far, z_two, s_mid.blocks[0])
 
     dqkv = [b[i] for i in range(3) for b in back]
-    grad_tokens, sums = pl.pallas_call(
-        functools.partial(first_back_kernel, lay, parts),
+    widths = (ln1_gain.shape[0], fc1_bias.shape[0], dec_bias.shape[0])
+    grad_tokens, sheet = pl.pallas_call(
+        functools.partial(first_back_kernel, lay, parts, count, widths),
         name="first_back",
         grid=(3,),
         in_specs=[SMEM] + [rows_of(gw)] * (3 * parts) + [whole((8, gw))] * parts
-        + [whole((D, 3 * D)), rows_of(D), rows_of(D), whole((8, D)), whole((8, D)), whole((1, D))],
-        out_specs=[whole((vis, D)), whole((8, D))],
-        out_shape=[sd((vis, D), BF), sd((8, D), F32)],
-        scratch_shapes=[pltpu.VMEM((R, D), BF)],
+        + [whole((D, 3 * D)), rows_of(D), rows_of(D), whole((8, D)), whole((8, D)), whole((1, D)), whole((1, hidden)),
+           whole((8, dec_width))],
+        out_specs=[whole((vis, D)), whole((11, count, 128))],
+        out_shape=[sd((vis, D), BF), sd((11, count, 128), F32)],
+        scratch_shapes=[pltpu.VMEM((8, D), F32), pltpu.VMEM((R, D), BF)],
         compiler_params=params(),
         cost_estimate=cost(2 * R * D * 3 * D + 2 * R * vis * D, 2e7, weight=20),
-    )(meta, *dqkv, *[b[5] for b in back], w_qkv, x_rows, held(dr, *lines_one), vecs, sums_two,
-      db_two)
+    )(meta, *dqkv, *[b[5] for b in back], w_qkv, x_rows, held(dr, s_mid.blocks[0], *lines_one), vecs, sums_two,
+      db_two, db_one, owner_sums)
+    blocks = -(-11 // row_dev)
+    vec_width = -(-128 * blocks // 384) * 384
+    ride = jnp.pad(sheet, ((0, blocks * row_dev - 11), (0, 0), (0, 0)))
+    ride = ride.reshape(blocks, row_dev, count, 128).transpose(2, 1, 0, 3).reshape(count, row_dev, -1)
+    ride = jnp.pad(ride, ((0, 0), (0, 0), (0, vec_width - 128 * blocks))).astype(BF)
+    ride = ride.reshape(chips, 2, row_dev, vec_width)
+    even = dev.coord("c") == 0
+    s_last.more(
+        jnp.where(even, ride[:, 0], ride[:, 1]), jnp.where(even, ride[:, 1], ride[:, 0])
+    )
+    c_last += s_last.swap(grad_tokens)
     s_last.add(grad_tokens, *near, *c_last)
     near = s_last.near() + s_last.far()
 
-    rows_sent = jnp.concatenate(
-        [
-            sums.reshape(8, count, -1).transpose(1, 0, 2).reshape(count, -1),
-            db_one.reshape(count, -1),
-            owner_sums[:2].reshape(2, count, -1).transpose(1, 0, 2).reshape(count, -1),
-        ],
-        axis=1,
-    )
-    rows = lax.all_to_all(held(rows_sent, s_last.blocks[0], z_one), "dp", 0, 0, tiled=True)
     decoded = pl.pallas_call(
         functools.partial(decode_kernel, slots, wins),
         name="decode",
@@ -1121,18 +1170,16 @@
         scratch_shapes=[pltpu.VMEM((3 * 32, dec_width // 2), BF)],
         compiler_params=params(),
         cost_estimate=cost(1e9, 7e6, weight=20),
-    )(held(e_got, s_last.blocks[0], z_one, rows_sent), info_got, vec_dec)
-
-
-    lines_late, z_late = finish(dev, meta, [s_mid, s_last], False, decoded, rows, *near)
-    rows = jnp.sum(rows, axis=0)
+    )(held(e_got, s_last.blocks[0], z_one), info_got, vec_dec)
+
+
+    lines_late, z_late = finish(dev, meta, [s_mid, s_last], False, decoded, *near)
     (grad_two,) = totals(z_two, [s_two])
     grad_one, grad_dec = totals(z_one, [s_one])
-    grad_out, grad_qkv = last_sums(z_late, [s_mid, s_last], D, gw)
-    vec_grads, start = [], 0
-    for v in vectors:
-        vec_grads.append(rows[start : start + v.shape[0]])
-        start += v.shape[0]
+    grad_out, grad_qkv, *vec_grads = last_sums(
+        z_late, [s_mid, s_last], D, gw, [v.shape[0] for v in vectors]
+    )
+    vec_grads = [v.reshape(-1) for v in vec_grads]
     (gg1, gb1, gbq, gbv, gbo, gg2, gb2, gbf2, gbf1, gbdec, gmask) = vec_grads
     return (decoded, grad_tokens, gg1, gb1, grad_qkv, gbq, gbv, grad_out, gbo, gg2, gb2, grad_one,
             gbf1, grad_two, gbf2, grad_dec, gbdec, gmask)

time: 363 us -> 357 us (0.983)
  local copies, waits for them, and re-layouts: 15.5 us -> 9.27 us
    all_to_all x1 -> x0, starting transfers between devices: 5.38 us -> none  [local(): lax.all_to_all(held(rows_sent, s_last.blocks[0], z_one), 'dp', 0, 0, tile...]
    ppermute x28 -> x29, waiting for transfers between devices: 28.8 us -> 29.9 us  [shift(): return lax.ppermute(values, 'dp', pairs)]
    ppermute x28 -> x29, starting transfers between devices: 29 us -> 28.8 us  [shift(): return lax.ppermute(values, 'dp', pairs)]
  transfers between devices with their start and end apart: 47 -> 47, of which waited for: 13 -> 15; matrix products, arithmetic and copies ran while one was open for 6% -> 4% of each run, Pallas kernels for 50% -> 51%
where the time goes in v4:
time: 357 us; the launch traced here: 350 us
  Pallas kernels  201 us (56%)
  starting transfers between devices  67.9 us (19%)
  waiting for transfers between devices  45.8 us (13%)
  between operations  15.1 us (4%)
  other arithmetic  11.6 us (3%)
  local copies, waits for them, and re-layouts  9.27 us (3%)
    pallas_call x3, Pallas kernels, attend_back(): pl.pallas_call(functools.partial(attention_back_kernel, row_dev, lay, chu...  33.2 us
    ppermute x29, waiting for transfers between devices, shift(): return lax.ppermute(values, 'dp', pairs)  29.9 us
    ppermute x29, starting transfers between devices, shift(): return lax.ppermute(values, 'dp', pairs)  28.8 us
    pallas_call x1, Pallas kernels, local(): pl.pallas_call(functools.partial(feed_back_kernel, row_dev, row_two), nam...  27.3 us
    pallas_call x3, Pallas kernels, attend(): pl.pallas_call(functools.partial(attention_kernel, lay, chunk, head_dim),...  22.8 us
    pallas_call x1, Pallas kernels, local(): pl.pallas_call(functools.partial(join_kernel, row_dev, sizes), name='join...  18.9 us
    pallas_call x4, Pallas kernels, add(): pl.pallas_call(functools.partial(chip_sum_kernel, sizes, pairs), name='ch...  17.7 us
    pallas_call x1, Pallas kernels, local(): pl.pallas_call(functools.partial(feed_kernel, parts, R // 24), name='feed...  16 us
  transfers between devices with their start and end apart: 47, of which 15 were waited for; matrix products, arithmetic and copies ran while one was open for 4% of the time, Pallas kernels for 51%

profile of v4, /device:TPU:0, one launch (start us, length us, event | category | flops | bytes accessed | tf_op | source)
XLA Modules:
  0.0 350.4 jit_solution(17173003814210011080)
XLA Ops:
  7.4 5.1 %collective-permute-start.2 = (bf16[24,2304]{1,0:T(8,128)(2,1)}, bf16[24,2304]{1,0:T(8,128)(2,1)S(1)}, u32[]{:S(2)}, u32[]{:S(2)}) collective-permute-start(bf16[24,2304]{1,0:T(8,128)(2,1)} %param.25), channel_id=1, source_target_pairs={{0,24},{1,25},{2,26},{3,27},{4,28},{5,29},{6,30},{7,31},{8,0},{9,1... | collective-permute-start | bytes 331784 | tf_op jit(solution)/shard_map/ppermute | solution.py:36
  16.2 6.1 %collective-permute-done.1 = bf16[24,2304]{1,0:T(8,128)(2,1)S(1)} collective-permute-done((bf16[24,2304]{1,0:T(8,128)(2,1)}, bf16[24,2304]{1,0:T(8,128)(2,1)S(1)}, u32[]{:S(2)}, u32[]{:S(2)}) %collective-permute-start.1) | collective-permute-done | bytes 110624 | tf_op jit(solution)/shard_map/ppermute | solution.py:36
  37.1 5.8 %all-to-all-done = bf16[32,15,128]{2,1,0:T(8,128)(2,1)S(1)} async-done(((bf16[32,15,128]{2,1,0:T(8,128)(2,1)}), bf16[32,15,128]{2,1,0:T(8,128)(2,1)S(1)}, u32[]{:S(2)}, u32[]{:S(2)}) %all-to-all-start) | async-done | bytes 122912 | tf_op jit(solution)/shard_map/all_to_all | solution.py:934
  43.7 6.1 %first_norm.1 = (bf16[960,768]{1,0:T(8,128)(2,1)}, bf16[960,768]{1,0:T(8,128)(2,1)}) custom-call(s32[16]{0:T(128)} %get-tuple-element.192.meta.place.spot, bf16[882,768]{1,0:T(8,128)(2,1)} %tokens, f32[8,768]{1,0:T(8,128)} %reshape.159.vecs.refs_4_.refs_15_), custom_call_target="tpu_custom_call" | custom-call | flops 26011238 | bytes 80000 | tf_op jit(solution)/shard_map/first_norm/pallas_call | solution.py:946
  53.0 8.3 %owner_side.1 = (bf16[1024,512]{1,0:T(8,128)(2,1)}, f32[8,512]{1,0:T(8,128)}) custom-call(bf16[1792,512]{1,0:T(8,128)(2,1)} %cot.1, bf16[128,128]{1,0:T(8,128)(2,1)} %bitcast.115), custom_call_target="tpu_custom_call" | custom-call | flops 20000000 | bytes 60000 | tf_op jit(solution)/shard_map/owner_side/pallas_call | solution.py:964
  64.7 5.2 %assemble.1 = bf16[4,8,24,2304]{3,2,1,0:T(8,128)(2,1)} custom-call(s32[16]{0:T(128)} %get-tuple-element.192.meta.place.spot, bf16[2,2,4,24,1152]{4,3,2,1,0:T(8,128)(2,1)} %copy-done.1, bf16[2,2,4,24,1152]{4,3,2,1,0:T(8,128)(2,1)} %copy-done, bf16[2,2,4,24,1152]{4,3,2,1,0:T(8,128)(2,1)} %copy-done.6, bf16[2,2,4,24,1152]{4,3,2,1,0:T(8,128)(2,1)} %copy-done.5), custom_call_target="tpu_custom_call" | custom-call | bytes 7077888 | tf_op jit(solution)/shard_map/assemble/pallas_call | solution.py:154
  70.0 7.5 %attention.3 = (bf16[960,256]{1,0:T(8,128)(2,1)}, bf16[960,256]{1,0:T(8,128)(2,1)}, bf16[960,256]{1,0:T(8,128)(2,1)}, bf16[4,400,400]{2,1,0:T(8,128)(2,1)}, bf16...) custom-call(s32[16]{0:T(128)} %get-tuple-element.192.meta.place.spot, bf16[960,768]{1,0:T(8,128)(2,1)} %get-tuple-element.223.h_in, ...), custom_call_target="tpu_custom_call" | custom-call | flops 3132462080 | bytes 8000000 | tf_op jit(solution)/shard_map/attention/pallas_call | solution.py:986
  79.6 7.6 %attention.4 = (bf16[960,256]{1,0:T(8,128)(2,1)}, bf16[960,256]{1,0:T(8,128)(2,1)}, bf16[960,256]{1,0:T(8,128)(2,1)}, bf16[4,400,400]{2,1,0:T(8,128)(2,1)}, bf16...) custom-call(s32[16]{0:T(128)} %get-tuple-element.192.meta.place.spot, bf16[960,768]{1,0:T(8,128)(2,1)} %get-tuple-element.223.h_in, ...), custom_call_target="tpu_custom_call" | custom-call | flops 3132462080 | bytes 8000000 | tf_op jit(solution)/shard_map/attention/pallas_call | solution.py:986
  87.3 6.4 %collective-permute-done.13 = bf16[4,96,384]{2,1,0:T(8,128)(2,1)S(1)} collective-permute-done((bf16[4,96,384]{2,1,0:T(8,128)(2,1)S(1)}, bf16[4,96,384]{2,1,0:T(8,128)(2,1)S(1)}, u32[]{:S(2)}, u32[]{:S(2)}) %collective-permute-start.13) | collective-permute-done | bytes 294944 | tf_op jit(solution)/shard_map/ppermute | solution.py:36
  96.6 4.5 %all-to-all-start.1 = ((bf16[32,32,512]{2,1,0:T(8,128)(2,1)}), bf16[32,32,512]{2,1,0:T(8,128)(2,1)}, u32[]{:S(2)}, u32[]{:S(2)}) async-start(bf16[32,32,512]{2,1,0:T(8,128)(2,1)} %bitcast.42), calls=%async_computation.1 | async-start | bytes 2097152 | tf_op jit(solution)/shard_map/all_to_all | solution.py:1005
  101.1 7.6 %attention.5 = (bf16[960,256]{1,0:T(8,128)(2,1)}, bf16[960,256]{1,0:T(8,128)(2,1)}, bf16[960,256]{1,0:T(8,128)(2,1)}, bf16[4,400,400]{2,1,0:T(8,128)(2,1)}, bf16...) custom-call(s32[16]{0:T(128)} %get-tuple-element.192.meta.place.spot, bf16[960,768]{1,0:T(8,128)(2,1)} %get-tuple-element.223.h_in, ...), custom_call_target="tpu_custom_call" | custom-call | flops 3132462080 | bytes 8000000 | tf_op jit(solution)/shard_map/attention/pallas_call | solution.py:986
  108.7 7.2 %collective-permute-done.15 = bf16[2,4,96,384]{3,2,1,0:T(8,128)(2,1)S(1)} collective-permute-done((bf16[2,4,96,384]{3,2,1,0:T(8,128)(2,1)S(1)}, bf16[2,4,96,384]{3,2,1,0:T(8,128)(2,1)S(1)}, u32[]{:S(2)}, u32[]{:S(2)}) %collective-permute-start.15) | collective-permute-done | bytes 589856 | tf_op jit(solution)/shard_map/ppermute | solution.py:36
  120.0 16.0 %feed.1 = (f32[960,768]{1,0:T(8,128)}, bf16[960,768]{1,0:T(8,128)(2,1)}, bf16[960,3072]{1,0:T(8,128)(2,1)}, bf16[960,3072]{1,0:T(8,128)(2,1)}) custom-call(bf16[960,256]{1,0:T(8,128)(2,1)} %get-tuple-element.211.refs_0_, bf16[960,256]{1,0:T(8,128)(2,1)} %get-tuple-element.218.refs_1_, bf16[960,256]{1,0:T(8,128)(2,1)} %get-tuple-element.224.refs_2_, ...), custom_call_target="tpu_custom_call" | custom-call | flops 5662310400 | bytes 25000000 | tf_op jit(solution)/shard_map/feed/pallas_call | solution.py:1014
  136.1 18.9 %join.1 = (bf16[32,96,768]{2,1,0:T(8,128)(2,1)}, bf16[1024,512]{1,0:T(8,128)(2,1)}, bf16[960,768]{1,0:T(8,128)(2,1)}, bf16[16,24,512]{2,1,0:T(8,128)(2,1)}, bf16...) custom-call(s32[16]{0:T(128)} %get-tuple-element.192.meta.place.spot, bf16[960,3072]{1,0:T(8,128)(2,1)} %get-tuple-element.232.g_in, ...), custom_call_target="tpu_custom_call" | custom-call | flops 8304721920 | bytes 20000000 | tf_op jit(solution)/shard_map/join/pallas_call | solution.py:1034
  155.0 6.7 %all-to-all-start.2 = ((bf16[32,32,512]{2,1,0:T(8,128)(2,1)}), bf16[32,32,512]{2,1,0:T(8,128)(2,1)}, u32[]{:S(2)}, u32[]{:S(2)}) async-start(bf16[32,32,512]{2,1,0:T(8,128)(2,1)} %bitcast.100), calls=%async_computation.2 | async-start | bytes 2097152 | tf_op jit(solution)/shard_map/all_to_all | solution.py:1057
  162.1 27.3 %feed_back.1 = (f32[960,768]{1,0:T(8,128)}, bf16[16,96,768]{2,1,0:T(8,128)(2,1)}, bf16[16,96,768]{2,1,0:T(8,128)(2,1)}, bf16[16,24,3072]{2,1,0:T(8,128)(2,1)}, b...) custom-call(s32[16]{0:T(128)} %get-tuple-element.192.meta.place.spot, bf16[960,768]{1,0:T(8,128)(2,1)} %get-tuple-element.242.dy_in, ...), custom_call_target="tpu_custom_call" | custom-call | flops 362387865600 | bytes 800000000 | tf_op jit(solution)/shard_map/feed_back/pallas_call | solution.py:1064
  190.0 11.4 %out_back.1 = (f32[960,768]{1,0:T(8,128)}, bf16[960,768]{1,0:T(8,128)(2,1)}, bf16[16,24,768]{2,1,0:T(8,128)(2,1)}, bf16[16,24,768]{2,1,0:T(8,128)(2,1)}, f32[8,768]{1,0:T(8,128)}) custom-call(s32[16]{0:T(128)} %get-tuple-element.192.meta.place.spot, f32[960,768]{1,0:T(8,128)} %get-tuple-element.246.dh_in, f32[960,768]{1,0:T(8,128)} %get-tuple-element.233.r_in, ...), custom_call_target="tpu_custom_call" | custom-call | flops 45298483200 | bytes 400000000 | tf_op jit(solution)/shard_map/out_back/pallas_call | solution.py:1082
  201.4 4.8 %chip_sum.4 = (bf16[4,96,768]{2,1,0:T(8,128)(2,1)}, bf16[4,96,768]{2,1,0:T(8,128)(2,1)}, bf16[4,96,768]{2,1,0:T(8,128)(2,1)}, bf16[4,96,768]{2,1,0:T(8,128)(2,1)}) custom-call(s32[16]{0:T(128)} %get-tuple-element.192.meta.place.spot, bf16[16,96,768]{2,1,0:T(8,128)(2,1)} %get-tuple-element.258.refs_0_, bf16[16,96,768]{2,1,0:T(8,128)(2,1)} %collective-permute-done.18.refs_1_), custom_call_target="tpu_custom_call" | custom-call | bytes 7077888 | tf_op jit(solution)/shard_map/chip_sum/pallas_call | solution.py:220
  209.4 11.6 %attention_back.3 = (bf16[960,256]{1,0:T(8,128)(2,1)}, bf16[960,256]{1,0:T(8,128)(2,1)}, bf16[960,256]{1,0:T(8,128)(2,1)}, bf16[16,24,768]{2,1,0:T(8,128)(2,1)},...) custom-call(s32[16]{0:T(128)} %get-tuple-element.192.meta.place.spot, bf16[960,768]{1,0:T(8,128)(2,1)} %get-tuple-element.223.h_in, ...), custom_call_target="tpu_custom_call" | custom-call | flops 82649243648 | bytes 200000000 | tf_op jit(solution)/shard_map/attention_back/pallas_call | solution.py:1101
  223.5 5.4 %chip_sum.5 = (bf16[4,24,3584]{2,1,0:T(8,128)(2,1)}, bf16[4,24,3584]{2,1,0:T(8,128)(2,1)}, bf16[4,24,3584]{2,1,0:T(8,128)(2,1)}, bf16[4,24,3584]{2,1,0:T(8,128)(2,1)}) custom-call(s32[16]{0:T(128)} %get-tuple-element.192.meta.place.spot, bf16[16,24,3072]{2,1,0:T(8,128)(2,1)} %get-tuple-element.267.refs_0_, bf16[16,24,512]{2,1,0:T(8,128)(2,1)} %get-tuple-element.268.refs_1_, ...), custom_call_target="tpu_custom_call" | custom-call | bytes 8257536 | tf_op jit(solution)/shard_map/chip_sum/pallas_call | solution.py:220
  232.5 10.8 %attention_back.4 = (bf16[960,256]{1,0:T(8,128)(2,1)}, bf16[960,256]{1,0:T(8,128)(2,1)}, bf16[960,256]{1,0:T(8,128)(2,1)}, bf16[16,24,768]{2,1,0:T(8,128)(2,1)},...) custom-call(s32[16]{0:T(128)} %get-tuple-element.192.meta.place.spot, bf16[960,768]{1,0:T(8,128)(2,1)} %get-tuple-element.223.h_in, ...), custom_call_target="tpu_custom_call" | custom-call | flops 82649243648 | bytes 200000000 | tf_op jit(solution)/shard_map/attention_back/pallas_call | solution.py:1101
  243.3 2.9 collective-permute-done.23.refs_3_
  249.8 4.8 %all-to-all-start.3 = ((bf16[4,96,768]{2,1,0:T(8,128)(2,1)}), bf16[4,96,768]{2,1,0:T(8,128)(2,1)S(1)}, u32[]{:S(2)}, u32[]{:S(2)}) async-start(bf16[4,96,768]{2,1,0:T(8,128)(2,1)} %plane_sum.3), calls=%async_computation.3 | async-start | bytes 1179648 | tf_op jit(solution)/shard_map/all_to_all | solution.py:286
  254.5 4.6 %collective-permute-done.24.refs_1_ = bf16[4,24,3584]{2,1,0:T(8,128)(2,1)S(1)} collective-permute-done((bf16[4,24,3584]{2,1,0:T(8,128)(2,1)}, bf16[4,24,3584]{2,1,0:T(8,128)(2,1)S(1)}, u32[]{:S(2)}, u32[]{:S(2)}) %collective-permute-start.24) | collective-permute-done | bytes 688160 | tf_op jit(solution)/shard_map/ppermute | solution.py:50
  260.8 10.8 %attention_back.5 = (bf16[960,256]{1,0:T(8,128)(2,1)}, bf16[960,256]{1,0:T(8,128)(2,1)}, bf16[960,256]{1,0:T(8,128)(2,1)}, bf16[16,24,768]{2,1,0:T(8,128)(2,1)},...) custom-call(s32[16]{0:T(128)} %get-tuple-element.192.meta.place.spot, bf16[960,768]{1,0:T(8,128)(2,1)} %get-tuple-element.223.h_in, ...), custom_call_target="tpu_custom_call" | custom-call | flops 82649243648 | bytes 200000000 | tf_op jit(solution)/shard_map/attention_back/pallas_call | solution.py:1101
  272.5 4.2 %chip_sum.6 = (bf16[4,24,2304]{2,1,0:T(8,128)(2,1)}, bf16[4,24,2304]{2,1,0:T(8,128)(2,1)}, bf16[4,24,2304]{2,1,0:T(8,128)(2,1)}, bf16[4,24,2304]{2,1,0:T(8,128)(2,1)}) custom-call(s32[16]{0:T(128)} %get-tuple-element.192.meta.place.spot, bf16[16,24,768]{2,1,0:T(8,128)(2,1)} %get-tuple-element.296.refs_0_, bf16[16,24,768]{2,1,0:T(8,128)(2,1)} %get-tuple-element.297.refs_1_, ...), custom_call_target="tpu_custom_call" | custom-call | bytes 5308416 | tf_op jit(solution)/shard_map/chip_sum/pallas_call | solution.py:220
  281.1 2.9 plane_sum.4
  284.0 4.9 %all-to-all-start.4 = ((bf16[4,24,3584]{2,1,0:T(8,128)(2,1)}), bf16[4,24,3584]{2,1,0:T(8,128)(2,1)S(1)}, u32[]{:S(2)}, u32[]{:S(2)}) async-start(bf16[4,24,3584]{2,1,0:T(8,128)(2,1)} %plane_sum.4), calls=%async_computation.4 | async-start | bytes 1376256 | tf_op jit(solution)/shard_map/all_to_all | solution.py:286
  288.8 12.4 %first_back.1 = (bf16[882,768]{1,0:T(8,128)(2,1)}, f32[11,32,128]{2,1,0:T(8,128)}) custom-call(s32[16]{0:T(128)} %get-tuple-element.192.meta.place.spot, bf16[960,256]{1,0:T(8,128)(2,1)} %get-tuple-element.266.refs_0_, bf16[960,256]{1,0:T(8,128)(2,1)} %get-tuple-element.275.refs_1_, bf16[960,256]{1,0:T(8,128)(2,1)} %get-tuple-element.286.refs_2_, ...), custom_call_target="tpu_custom_call" | custom-call | flops 93958963200 | bytes 400000000 | tf_op jit(solution)/shard_map/first_back/pallas_call | solution.py:1135
  305.4 3.3 chip_sum.7
  312.2 9.1 %decode.1 = bf16[1792,512]{1,0:T(8,128)(2,1)} custom-call(bf16[1024,512]{1,0:T(8,128)(2,1)} %bitcast.45.got, bf16[128,128]{1,0:T(8,128)(2,1)} %bitcast.116, f32[2,512]{1,0:T(2,128)} %reshape.161.vec_dec), custom_call_target="tpu_custom_call" | custom-call | flops 20000000000 | bytes 140000000 | tf_op jit(solution)/shard_map/decode/pallas_call | solution.py:1163
  335.6 5.0 %collective-permute-done.39.refs_2_ = bf16[24,3456]{1,0:T(8,128)(2,1)S(1)} collective-permute-done((bf16[24,3456]{1,0:T(8,128)(2,1)}, bf16[24,3456]{1,0:T(8,128)(2,1)S(1)}, u32[]{:S(2)}, u32[]{:S(2)}) %collective-permute-start.39) | collective-permute-done | bytes 165920 | tf_op jit(solution)/shard_map/ppermute | solution.py:36
  (206 shorter events, 79.9 us)
Async XLA Ops:
  7.3 112.7 %all-gather.2.cloned.1.call-start = ((), (), s32[]{:S(2)}) async-start(), calls=%async_computation.5 | async-start | bytes 6893568 | tf_op jit(solution)/shard_map/all_gather | solution.py:928
  33.7 16.1 %collective-permute-start.6 = (bf16[2,4,24,1152]{3,2,1,0:T(8,128)(2,1)S(1)}, bf16[2,4,24,1152]{3,2,1,0:T(8,128)(2,1)S(1)}, u32[]{:S(2)}, u32[]{:S(2)}) collective-permute-start(bf16[2,4,24,1152]{3,2,1,0:T(8,128)(2,1)S(1)} %pad_maximum_fusion.9), channel_id=1, source_target_pairs={{0,2},{1,3},{2,0},{3,1},{4,6},{5,7},{6,4},{7,5},{8,10},{9,11},{10,... | collective-permute-start | bytes 1327112 | tf_op jit(solution)/shard_map/ppermute | solution.py:36
  35.5 14.3 %collective-permute-start.5 = (bf16[2,4,24,1152]{3,2,1,0:T(8,128)(2,1)S(1)}, bf16[2,4,24,1152]{3,2,1,0:T(8,128)(2,1)S(1)}, u32[]{:S(2)}, u32[]{:S(2)}) collective-permute-start(bf16[2,4,24,1152]{3,2,1,0:T(8,128)(2,1)S(1)} %pad_maximum_fusion.8), channel_id=1, source_target_pairs={{0,4},{1,5},{2,6},{3,7},{4,0},{5,1},{6,2},{7,3},{8,12},{9,13},{10,... | collective-permute-start | bytes 1327112 | tf_op jit(solution)/shard_map/ppermute | solution.py:36
  61.4 16.1 %collective-permute-start.11 = (bf16[96,768]{1,0:T(8,128)(2,1)S(1)}, bf16[96,768]{1,0:T(8,128)(2,1)S(1)}, u32[]{:S(2)}, u32[]{:S(2)}) collective-permute-start(bf16[96,768]{1,0:T(8,128)(2,1)S(1)} %copy-done.26), channel_id=1, source_target_pairs={{0,24},{1,25},{2,26},{3,27},{4,28},{5,29},{6,30},{7,31},{8,0},{9,1... | collective-permute-start | bytes 442376 | tf_op jit(solution)/shard_map/ppermute | solution.py:36
  62.8 14.9 %collective-permute-start.10 = (bf16[96,768]{1,0:T(8,128)(2,1)S(1)}, bf16[96,768]{1,0:T(8,128)(2,1)S(1)}, u32[]{:S(2)}, u32[]{:S(2)}) collective-permute-start(bf16[96,768]{1,0:T(8,128)(2,1)S(1)} %copy-done.26), channel_id=1, source_target_pairs={{0,16},{1,17},{2,18},{3,19},{4,20},{5,21},{6,22},{7,23},{8,24},{9,... | collective-permute-start | bytes 442376 | tf_op jit(solution)/shard_map/ppermute | solution.py:36
  63.6 14.1 %collective-permute-start.9 = (bf16[96,768]{1,0:T(8,128)(2,1)S(1)}, bf16[96,768]{1,0:T(8,128)(2,1)S(1)}, u32[]{:S(2)}, u32[]{:S(2)}) collective-permute-start(bf16[96,768]{1,0:T(8,128)(2,1)S(1)} %copy-done.26), channel_id=1, source_target_pairs={{0,8},{1,9},{2,10},{3,11},{4,12},{5,13},{6,14},{7,15},{8,16},{9,17... | collective-permute-start | bytes 442376 | tf_op jit(solution)/shard_map/ppermute | solution.py:36
  77.8 15.9 %collective-permute-start.13 = (bf16[4,96,384]{2,1,0:T(8,128)(2,1)S(1)}, bf16[4,96,384]{2,1,0:T(8,128)(2,1)S(1)}, u32[]{:S(2)}, u32[]{:S(2)}) collective-permute-start(bf16[4,96,384]{2,1,0:T(8,128)(2,1)S(1)} %get-tuple-element.221), channel_id=1, source_target_pairs={{0,4},{1,5},{2,6},{3,7},{4,0},{5,1},{6,2},{7,3},{8,12},{9,13},{10,... | collective-permute-start | bytes 884744 | tf_op jit(solution)/shard_map/ppermute | solution.py:36
  79.1 15.7 %collective-permute-start.12 = (bf16[4,96,384]{2,1,0:T(8,128)(2,1)S(1)}, bf16[4,96,384]{2,1,0:T(8,128)(2,1)S(1)}, u32[]{:S(2)}, u32[]{:S(2)}) collective-permute-start(bf16[4,96,384]{2,1,0:T(8,128)(2,1)S(1)} %get-tuple-element.219), channel_id=1, source_target_pairs={{0,2},{1,3},{2,0},{3,1},{4,6},{5,7},{6,4},{7,5},{8,10},{9,11},{10,... | collective-permute-start | bytes 884744 | tf_op jit(solution)/shard_map/ppermute | solution.py:36
  94.9 21.1 %collective-permute-start.15 = (bf16[2,4,96,384]{3,2,1,0:T(8,128)(2,1)S(1)}, bf16[2,4,96,384]{3,2,1,0:T(8,128)(2,1)S(1)}, u32[]{:S(2)}, u32[]{:S(2)}) collective-permute-start(bf16[2,4,96,384]{3,2,1,0:T(8,128)(2,1)S(1)} %pad_maximum_fusion.6), channel_id=1, source_target_pairs={{0,2},{1,3},{2,0},{3,1},{4,6},{5,7},{6,4},{7,5},{8,10},{9,11},{10,... | collective-permute-start | bytes 1769480 | tf_op jit(solution)/shard_map/ppermute | solution.py:36
  95.5 20.5 %collective-permute-start.14 = (bf16[2,4,96,384]{3,2,1,0:T(8,128)(2,1)S(1)}, bf16[2,4,96,384]{3,2,1,0:T(8,128)(2,1)S(1)}, u32[]{:S(2)}, u32[]{:S(2)}) collective-permute-start(bf16[2,4,96,384]{3,2,1,0:T(8,128)(2,1)S(1)} %pad_maximum_fusion.5), channel_id=1, source_target_pairs={{0,4},{1,5},{2,6},{3,7},{4,0},{5,1},{6,2},{7,3},{8,12},{9,13},{10,... | collective-permute-start | bytes 1769480 | tf_op jit(solution)/shard_map/ppermute | solution.py:36
  96.6 39.5 %all-to-all-start.1 = ((bf16[32,32,512]{2,1,0:T(8,128)(2,1)}), bf16[32,32,512]{2,1,0:T(8,128)(2,1)}, u32[]{:S(2)}, u32[]{:S(2)}) async-start(bf16[32,32,512]{2,1,0:T(8,128)(2,1)} %bitcast.42), calls=%async_computation.1 | async-start | bytes 2097152 | tf_op jit(solution)/shard_map/all_to_all | solution.py:1005
  116.1 19.9 %collective-permute-start.17 = (bf16[2,2,4,96,384]{4,3,2,1,0:T(8,128)(2,1)S(1)}, bf16[2,2,4,96,384]{4,3,2,1,0:T(8,128)(2,1)}, u32[]{:S(2)}, u32[]{:S(2)}) collective-permute-start(bf16[2,2,4,96,384]{4,3,2,1,0:T(8,128)(2,1)S(1)} %pad_maximum_fusion.1.part_b), channel_id=1, source_target_pairs={{0,1},{1,0},{2,3},{3,2},{4,5},{5,4},{6,7},{7,6},{8,9},{9,8},{10,11... | collective-permute-start | bytes 3538952 | tf_op jit(solution)/shard_map/ppermute | solution.py:36
  116.4 19.7 %collective-permute-start.16 = (bf16[2,2,4,96,384]{4,3,2,1,0:T(8,128)(2,1)S(1)}, bf16[2,2,4,96,384]{4,3,2,1,0:T(8,128)(2,1)}, u32[]{:S(2)}, u32[]{:S(2)}) collective-permute-start(bf16[2,2,4,96,384]{4,3,2,1,0:T(8,128)(2,1)S(1)} %pad_maximum_fusion.part_a), channel_id=1, source_target_pairs={{0,1},{1,0},{2,3},{3,2},{4,5},{5,4},{6,7},{7,6},{8,9},{9,8},{10,11... | collective-permute-start | bytes 3538952 | tf_op jit(solution)/shard_map/ppermute | solution.py:36
  155.0 54.4 %all-to-all-start.2 = ((bf16[32,32,512]{2,1,0:T(8,128)(2,1)}), bf16[32,32,512]{2,1,0:T(8,128)(2,1)}, u32[]{:S(2)}, u32[]{:S(2)}) async-start(bf16[32,32,512]{2,1,0:T(8,128)(2,1)} %bitcast.100), calls=%async_computation.2 | async-start | bytes 2097152 | tf_op jit(solution)/shard_map/all_to_all | solution.py:1057
  161.7 47.7 %collective-permute-start.20 = (bf16[16,24,512]{2,1,0:T(8,128)(2,1)}, bf16[16,24,512]{2,1,0:T(8,128)(2,1)}, u32[]{:S(2)}, u32[]{:S(2)}) collective-permute-start(bf16[16,24,512]{2,1,0:T(8,128)(2,1)} %get-tuple-element.264), channel_id=1, source_target_pairs={{0,1},{1,0},{2,3},{3,2},{4,5},{5,4},{6,7},{7,6},{8,9},{9,8},{10,11... | collective-permute-start | bytes 1179656 | tf_op jit(solution)/shard_map/ppermute | solution.py:36
  189.6 19.8 %collective-permute-start.19 = (bf16[16,24,3072]{2,1,0:T(8,128)(2,1)}, bf16[16,24,3072]{2,1,0:T(8,128)(2,1)S(1)}, u32[]{:S(2)}, u32[]{:S(2)}) collective-permute-start(bf16[16,24,3072]{2,1,0:T(8,128)(2,1)} %get-tuple-element.263), channel_id=1, source_target_pairs={{0,1},{1,0},{2,3},{3,2},{4,5},{5,4},{6,7},{7,6},{8,9},{9,8},{10,11... | collective-permute-start | bytes 7077896 | tf_op jit(solution)/shard_map/ppermute | solution.py:36
  206.2 15.8 %collective-permute-start.21 = (bf16[4,96,768]{2,1,0:T(8,128)(2,1)}, bf16[4,96,768]{2,1,0:T(8,128)(2,1)S(1)}, u32[]{:S(2)}, u32[]{:S(2)}) collective-permute-start(bf16[4,96,768]{2,1,0:T(8,128)(2,1)} %get-tuple-element.269), channel_id=1, source_target_pairs={{0,2},{1,3},{2,0},{3,1},{4,6},{5,7},{6,4},{7,5},{8,10},{9,11},{10,... | collective-permute-start | bytes 1769480 | tf_op jit(solution)/shard_map/ppermute | solution.py:50
  207.9 15.5 %collective-permute-start.22 = (bf16[4,96,768]{2,1,0:T(8,128)(2,1)}, bf16[4,96,768]{2,1,0:T(8,128)(2,1)S(1)}, u32[]{:S(2)}, u32[]{:S(2)}) collective-permute-start(bf16[4,96,768]{2,1,0:T(8,128)(2,1)} %get-tuple-element.270), channel_id=1, source_target_pairs={{0,4},{1,5},{2,6},{3,7},{4,0},{5,1},{6,2},{7,3},{8,12},{9,13},{10,... | collective-permute-start | bytes 1769480 | tf_op jit(solution)/shard_map/ppermute | solution.py:50
  221.1 50.5 %collective-permute-start.26 = (bf16[16,24,768]{2,1,0:T(8,128)(2,1)}, bf16[16,24,768]{2,1,0:T(8,128)(2,1)}, u32[]{:S(2)}, u32[]{:S(2)}) collective-permute-start(bf16[16,24,768]{2,1,0:T(8,128)(2,1)} %get-tuple-element.301), channel_id=1, source_target_pairs={{0,1},{1,0},{2,3},{3,2},{4,5},{5,4},{6,7},{7,6},{8,9},{9,8},{10,11... | collective-permute-start | bytes 1769480 | tf_op jit(solution)/shard_map/ppermute | solution.py:36
  221.2 50.5 %collective-permute-start.27 = (bf16[16,24,768]{2,1,0:T(8,128)(2,1)}, bf16[16,24,768]{2,1,0:T(8,128)(2,1)}, u32[]{:S(2)}, u32[]{:S(2)}) collective-permute-start(bf16[16,24,768]{2,1,0:T(8,128)(2,1)} %get-tuple-element.302), channel_id=1, source_target_pairs={{0,1},{1,0},{2,3},{3,2},{4,5},{5,4},{6,7},{7,6},{8,9},{9,8},{10,11... | collective-permute-start | bytes 1769480 | tf_op jit(solution)/shard_map/ppermute | solution.py:36
  228.9 17.3 %collective-permute-start.23 = (bf16[4,96,768]{2,1,0:T(8,128)(2,1)S(1)}, bf16[4,96,768]{2,1,0:T(8,128)(2,1)S(1)}, u32[]{:S(2)}, u32[]{:S(2)}) collective-permute-start(bf16[4,96,768]{2,1,0:T(8,128)(2,1)S(1)} %copy-done.37), channel_id=1, source_target_pairs={{0,6},{1,7},{2,4},{3,5},{4,2},{5,3},{6,0},{7,1},{8,14},{9,15},{10,... | collective-permute-start | bytes 1769480 | tf_op jit(solution)/shard_map/ppermute | solution.py:50
  230.5 28.7 %collective-permute-start.24 = (bf16[4,24,3584]{2,1,0:T(8,128)(2,1)}, bf16[4,24,3584]{2,1,0:T(8,128)(2,1)S(1)}, u32[]{:S(2)}, u32[]{:S(2)}) collective-permute-start(bf16[4,24,3584]{2,1,0:T(8,128)(2,1)} %get-tuple-element.282), channel_id=1, source_target_pairs={{0,2},{1,3},{2,0},{3,1},{4,6},{5,7},{6,4},{7,5},{8,10},{9,11},{10,... | collective-permute-start | bytes 2064392 | tf_op jit(solution)/shard_map/ppermute | solution.py:50
  231.9 27.2 %collective-permute-start.25 = (bf16[4,24,3584]{2,1,0:T(8,128)(2,1)}, bf16[4,24,3584]{2,1,0:T(8,128)(2,1)S(1)}, u32[]{:S(2)}, u32[]{:S(2)}) collective-permute-start(bf16[4,24,3584]{2,1,0:T(8,128)(2,1)} %get-tuple-element.283), channel_id=1, source_target_pairs={{0,4},{1,5},{2,6},{3,7},{4,0},{5,1},{6,2},{7,3},{8,12},{9,13},{10,... | collective-permute-start | bytes 2064392 | tf_op jit(solution)/shard_map/ppermute | solution.py:50
  246.2 25.4 %collective-permute-start.28 = (bf16[16,24,768]{2,1,0:T(8,128)(2,1)}, bf16[16,24,768]{2,1,0:T(8,128)(2,1)S(1)}, u32[]{:S(2)}, u32[]{:S(2)}) collective-permute-start(bf16[16,24,768]{2,1,0:T(8,128)(2,1)} %get-tuple-element.304), channel_id=1, source_target_pairs={{0,1},{1,0},{2,3},{3,2},{4,5},{5,4},{6,7},{7,6},{8,9},{9,8},{10,11... | collective-permute-start | bytes 1769480 | tf_op jit(solution)/shard_map/ppermute | solution.py:36
  249.8 30.4 %all-to-all-start.3 = ((bf16[4,96,768]{2,1,0:T(8,128)(2,1)}), bf16[4,96,768]{2,1,0:T(8,128)(2,1)S(1)}, u32[]{:S(2)}, u32[]{:S(2)}) async-start(bf16[4,96,768]{2,1,0:T(8,128)(2,1)} %plane_sum.3), calls=%async_computation.3 | async-start | bytes 1179648 | tf_op jit(solution)/shard_map/all_to_all | solution.py:286
  259.2 21.0 %collective-permute-start.29 = (bf16[4,24,3584]{2,1,0:T(8,128)(2,1)}, bf16[4,24,3584]{2,1,0:T(8,128)(2,1)S(1)}, u32[]{:S(2)}, u32[]{:S(2)}) collective-permute-start(bf16[4,24,3584]{2,1,0:T(8,128)(2,1)} %get-tuple-element.310), channel_id=1, source_target_pairs={{0,6},{1,7},{2,4},{3,5},{4,2},{5,3},{6,0},{7,1},{8,14},{9,15},{10,... | collective-permute-start | bytes 2064392 | tf_op jit(solution)/shard_map/ppermute | solution.py:50
  276.6 27.5 %collective-permute-start.32 = (bf16[4,24,2304]{2,1,0:T(8,128)(2,1)}, bf16[4,24,2304]{2,1,0:T(8,128)(2,1)S(1)}, u32[]{:S(2)}, u32[]{:S(2)}) collective-permute-start(bf16[4,24,2304]{2,1,0:T(8,128)(2,1)} %get-tuple-element.325), channel_id=1, source_target_pairs={{0,2},{1,3},{2,0},{3,1},{4,6},{5,7},{6,4},{7,5},{8,10},{9,11},{10,... | collective-permute-start | bytes 1327112 | tf_op jit(solution)/shard_map/ppermute | solution.py:50
  277.9 26.3 %collective-permute-start.33 = (bf16[4,24,2304]{2,1,0:T(8,128)(2,1)}, bf16[4,24,2304]{2,1,0:T(8,128)(2,1)S(1)}, u32[]{:S(2)}, u32[]{:S(2)}) collective-permute-start(bf16[4,24,2304]{2,1,0:T(8,128)(2,1)} %get-tuple-element.326), channel_id=1, source_target_pairs={{0,4},{1,5},{2,6},{3,7},{4,0},{5,1},{6,2},{7,3},{8,12},{9,13},{10,... | collective-permute-start | bytes 1327112 | tf_op jit(solution)/shard_map/ppermute | solution.py:50
  278.5 25.6 %collective-permute-start.34 = (bf16[4,24,2304]{2,1,0:T(8,128)(2,1)}, bf16[4,24,2304]{2,1,0:T(8,128)(2,1)}, u32[]{:S(2)}, u32[]{:S(2)}) collective-permute-start(bf16[4,24,2304]{2,1,0:T(8,128)(2,1)} %get-tuple-element.327), channel_id=1, source_target_pairs={{0,6},{1,7},{2,4},{3,5},{4,2},{5,3},{6,0},{7,1},{8,14},{9,15},{10,... | collective-permute-start | bytes 1327112 | tf_op jit(solution)/shard_map/ppermute | solution.py:50
  280.2 24.0 %collective-permute-start.30 = (bf16[16,24,768]{2,1,0:T(8,128)(2,1)}, bf16[16,24,768]{2,1,0:T(8,128)(2,1)S(1)}, u32[]{:S(2)}, u32[]{:S(2)}) collective-permute-start(bf16[16,24,768]{2,1,0:T(8,128)(2,1)} %get-tuple-element.322), channel_id=1, source_target_pairs={{0,1},{1,0},{2,3},{3,2},{4,5},{5,4},{6,7},{7,6},{8,9},{9,8},{10,11... | collective-permute-start | bytes 1769480 | tf_op jit(solution)/shard_map/ppermute | solution.py:36
  284.0 28.3 %all-to-all-start.4 = ((bf16[4,24,3584]{2,1,0:T(8,128)(2,1)}), bf16[4,24,3584]{2,1,0:T(8,128)(2,1)S(1)}, u32[]{:S(2)}, u32[]{:S(2)}) async-start(bf16[4,24,3584]{2,1,0:T(8,128)(2,1)} %plane_sum.4), calls=%async_computation.4 | async-start | bytes 1376256 | tf_op jit(solution)/shard_map/all_to_all | solution.py:286
  308.7 12.7 %collective-permute-start.35 = (bf16[4,24,1152]{2,1,0:T(8,128)(2,1)}, bf16[4,24,1152]{2,1,0:T(8,128)(2,1)S(1)}, u32[]{:S(2)}, u32[]{:S(2)}) collective-permute-start(bf16[4,24,1152]{2,1,0:T(8,128)(2,1)} %get-tuple-element.332), channel_id=1, source_target_pairs={{0,2},{1,3},{2,0},{3,1},{4,6},{5,7},{6,4},{7,5},{8,10},{9,11},{10,... | collective-permute-start | bytes 663560 | tf_op jit(solution)/shard_map/ppermute | solution.py:50
  (55 other events, 603.6 us)
Sparse Core Ops, SparseCore 0:
  22.5 88.3 all-gather.1

commit v5 on v4

--- a/solution.py
+++ b/solution.py
@@ -926,7 +926,7 @@
     )
     ya = ga.second(packed)
     rest = lax.all_gather(
-        held(jnp.concatenate([fc1_weight, out_weight, dec_weight], axis=1), *za),
+        jnp.concatenate([fc1_weight, out_weight, dec_weight], axis=1),
         "dp",
         axis=0,
         tiled=True,
@@ -955,6 +955,7 @@
     )(meta, held(tokens, za), vecs)
 
     from_a = ga.swap(h_one)
+    zc = gc.along_z(*ga.sent)
 
     wins = 16
     steps = total // wins
@@ -972,7 +973,6 @@
         cost_estimate=cost(1e9, 3e6, weight=0.02),
     )(dec_cot, held(info_got, h_one, *ga.sent))
 
-    zc = gc.along_z(*from_a)
     (w_qkv,) = ga.result(meta, de_send)
     group = 4
     parts = HEADS // group
@@ -997,11 +997,10 @@
         )(meta, h_rows, w_qkv, w_qkv, w_qkv, vecs)
 
     attn = [attend(0, h_one)]
-    gc.first(attn[0][5])
-    attn.append(attend(1, held(h_one, attn[0][5], *gc.sent)))
-    gc.second(attn[1][5])
+    attn.append(attend(1, held(h_one, attn[0][5])))
+    gc.first(attn[1][5])
     attn.append(attend(2, held(h_one, attn[1][5], *gc.sent)))
-    swapped = gc.swap(attn[2][5])
+    gc.second(attn[2][5])
     de_got = lax.all_to_all(
         held(de_send, attn[1][5]).reshape(count, per_peer * LANE_SLOTS, dec_width), "dp", 0, 0, tiled=True
     ).reshape(total * LANE_SLOTS, dec_width)
@@ -1024,6 +1023,7 @@
         compiler_params=params(),
         cost_estimate=cost(2 * R * D * (hidden + D), 2.5e7, 6e6),
     )(*att, rest, vecs, held(x_rows, *gc.sent), rest, bf1)
+    gc.swap(h_two)
 
     ht = hidden // 4
     nz, ny, nx = sizes

time: 357 us -> 352 us (0.986)
  waiting for transfers between devices: 45.8 us -> 35.4 us
    ppermute x29, waiting for transfers between devices: 29.9 us -> 20.5 us  [shift(): return lax.ppermute(values, 'dp', pairs)]
    ppermute x29, starting transfers between devices: 28.8 us -> 34.1 us  [shift(): return lax.ppermute(values, 'dp', pairs)]
where the time goes in v5:
time: 352 us; the launch traced here: 346 us
  Pallas kernels  201 us (57%)
  starting transfers between devices  70.5 us (20%)
  waiting for transfers between devices  35.4 us (10%)
  between operations  15 us (4%)
  other arithmetic  12.6 us (4%)
  local copies, waits for them, and re-layouts  11.2 us (3%)
    ppermute x29, starting transfers between devices, shift(): return lax.ppermute(values, 'dp', pairs)  34.1 us
    pallas_call x3, Pallas kernels, attend_back(): pl.pallas_call(functools.partial(attention_back_kernel, row_dev, lay, chu...  33.2 us
    pallas_call x1, Pallas kernels, local(): pl.pallas_call(functools.partial(feed_back_kernel, row_dev, row_two), nam...  27.3 us
    pallas_call x3, Pallas kernels, attend(): pl.pallas_call(functools.partial(attention_kernel, lay, chunk, head_dim),...  22.9 us
    ppermute x29, waiting for transfers between devices, shift(): return lax.ppermute(values, 'dp', pairs)  20.5 us
    pallas_call x1, Pallas kernels, local(): pl.pallas_call(functools.partial(join_kernel, row_dev, sizes), name='join...  18.9 us
    pallas_call x4, Pallas kernels, add(): pl.pallas_call(functools.partial(chip_sum_kernel, sizes, pairs), name='ch...  17.7 us
    pallas_call x1, Pallas kernels, local(): pl.pallas_call(functools.partial(feed_kernel, parts, R // 24), name='feed...  16 us
  transfers between devices with their start and end apart: 47, of which 15 were waited for; matrix products, arithmetic and copies ran while one was open for 4% of the time, Pallas kernels for 51%

profile of v5, /device:TPU:0, one launch (start us, length us, event | category | flops | bytes accessed | tf_op | source)
XLA Modules:
  0.0 345.7 jit_solution(11569573311050455856)
XLA Ops:
  9.1 4.1 %collective-permute-start.1 = (bf16[24,2304]{1,0:T(8,128)(2,1)}, bf16[24,2304]{1,0:T(8,128)(2,1)S(1)}, u32[]{:S(2)}, u32[]{:S(2)}) collective-permute-start(bf16[24,2304]{1,0:T(8,128)(2,1)} %param.25), channel_id=1, source_target_pairs={{0,16},{1,17},{2,18},{3,19},{4,20},{5,21},{6,22},{7,23},{8,24},{9,... | collective-permute-start | bytes 331784 | tf_op jit(solution)/shard_map/ppermute | solution.py:36
  17.0 5.1 %collective-permute-done.1 = bf16[24,2304]{1,0:T(8,128)(2,1)S(1)} collective-permute-done((bf16[24,2304]{1,0:T(8,128)(2,1)}, bf16[24,2304]{1,0:T(8,128)(2,1)S(1)}, u32[]{:S(2)}, u32[]{:S(2)}) %collective-permute-start.1) | collective-permute-done | bytes 110624 | tf_op jit(solution)/shard_map/ppermute | solution.py:36
  31.2 3.7 %all-to-all-start = ((bf16[32,15,128]{2,1,0:T(8,128)(2,1)}), bf16[32,15,128]{2,1,0:T(8,128)(2,1)S(1)}, u32[]{:S(2)}, u32[]{:S(2)}) async-start(bf16[32,15,128]{2,1,0:T(8,128)(2,1)} %pad_maximum_fusion.12), calls=%async_computation | async-start | bytes 262144 | tf_op jit(solution)/shard_map/all_to_all | solution.py:934
  38.5 4.8 %all-to-all-done = bf16[32,15,128]{2,1,0:T(8,128)(2,1)S(1)} async-done(((bf16[32,15,128]{2,1,0:T(8,128)(2,1)}), bf16[32,15,128]{2,1,0:T(8,128)(2,1)S(1)}, u32[]{:S(2)}, u32[]{:S(2)}) %all-to-all-start) | async-done | bytes 122912 | tf_op jit(solution)/shard_map/all_to_all | solution.py:934
  44.1 6.1 %first_norm.1 = (bf16[960,768]{1,0:T(8,128)(2,1)}, bf16[960,768]{1,0:T(8,128)(2,1)}) custom-call(s32[16]{0:T(128)} %get-tuple-element.191.meta.place.spot, bf16[882,768]{1,0:T(8,128)(2,1)} %tokens, f32[8,768]{1,0:T(8,128)} %reshape.159.vecs.refs_4_.refs_15_), custom_call_target="tpu_custom_call" | custom-call | flops 26011238 | bytes 80000 | tf_op jit(solution)/shard_map/first_norm/pallas_call | solution.py:946
  50.2 4.1 %collective-permute-done.6 = bf16[2,4,24,1152]{3,2,1,0:T(8,128)(2,1)S(1)} collective-permute-done((bf16[2,4,24,1152]{3,2,1,0:T(8,128)(2,1)S(1)}, bf16[2,4,24,1152]{3,2,1,0:T(8,128)(2,1)S(1)}, u32[]{:S(2)}, u32[]{:S(2)}) %collective-permute-start.6) | collective-permute-done | bytes 442400 | tf_op jit(solution)/shard_map/ppermute | solution.py:36
  57.0 3.1 collective-permute-start.11
  62.0 8.4 %owner_side.1 = (bf16[1024,512]{1,0:T(8,128)(2,1)}, f32[8,512]{1,0:T(8,128)}) custom-call(bf16[1792,512]{1,0:T(8,128)(2,1)} %cot.1, bf16[128,128]{1,0:T(8,128)(2,1)} %bitcast.113), custom_call_target="tpu_custom_call" | custom-call | flops 20000000 | bytes 60000 | tf_op jit(solution)/shard_map/owner_side/pallas_call | solution.py:965
  71.7 5.2 %assemble.1 = bf16[4,8,24,2304]{3,2,1,0:T(8,128)(2,1)} custom-call(s32[16]{0:T(128)} %get-tuple-element.191.meta.place.spot, bf16[2,2,4,24,1152]{4,3,2,1,0:T(8,128)(2,1)} %copy-done.1, bf16[2,2,4,24,1152]{4,3,2,1,0:T(8,128)(2,1)} %copy-done, bf16[2,2,4,24,1152]{4,3,2,1,0:T(8,128)(2,1)} %copy-done.6, bf16[2,2,4,24,1152]{4,3,2,1,0:T(8,128)(2,1)} %copy-done.5), custom_call_target="tpu_custom_call" | custom-call | bytes 7077888 | tf_op jit(solution)/shard_map/assemble/pallas_call | solution.py:154
  76.9 7.6 %attention.3 = (bf16[960,256]{1,0:T(8,128)(2,1)}, bf16[960,256]{1,0:T(8,128)(2,1)}, bf16[960,256]{1,0:T(8,128)(2,1)}, bf16[4,400,400]{2,1,0:T(8,128)(2,1)}, bf16...) custom-call(s32[16]{0:T(128)} %get-tuple-element.191.meta.place.spot, bf16[960,768]{1,0:T(8,128)(2,1)} %get-tuple-element.218.h_in, ...), custom_call_target="tpu_custom_call" | custom-call | flops 3132462080 | bytes 8000000 | tf_op jit(solution)/shard_map/attention/pallas_call | solution.py:986
  84.5 7.7 %attention.4 = (bf16[960,256]{1,0:T(8,128)(2,1)}, bf16[960,256]{1,0:T(8,128)(2,1)}, bf16[960,256]{1,0:T(8,128)(2,1)}, bf16[4,400,400]{2,1,0:T(8,128)(2,1)}, bf16...) custom-call(s32[16]{0:T(128)} %get-tuple-element.191.meta.place.spot, bf16[960,768]{1,0:T(8,128)(2,1)} %get-tuple-element.218.h_in, ...), custom_call_target="tpu_custom_call" | custom-call | flops 3132462080 | bytes 8000000 | tf_op jit(solution)/shard_map/attention/pallas_call | solution.py:986
  96.4 3.6 %all-to-all-start.1 = ((bf16[32,32,512]{2,1,0:T(8,128)(2,1)}), bf16[32,32,512]{2,1,0:T(8,128)(2,1)}, u32[]{:S(2)}, u32[]{:S(2)}) async-start(bf16[32,32,512]{2,1,0:T(8,128)(2,1)} %bitcast.42), calls=%async_computation.1 | async-start | bytes 2097152 | tf_op jit(solution)/shard_map/all_to_all | solution.py:1004
  100.0 7.6 %attention.5 = (bf16[960,256]{1,0:T(8,128)(2,1)}, bf16[960,256]{1,0:T(8,128)(2,1)}, bf16[960,256]{1,0:T(8,128)(2,1)}, bf16[4,400,400]{2,1,0:T(8,128)(2,1)}, bf16...) custom-call(s32[16]{0:T(128)} %get-tuple-element.191.meta.place.spot, bf16[960,768]{1,0:T(8,128)(2,1)} %get-tuple-element.218.h_in, ...), custom_call_target="tpu_custom_call" | custom-call | flops 3132462080 | bytes 8000000 | tf_op jit(solution)/shard_map/attention/pallas_call | solution.py:986
  112.7 16.0 %feed.1 = (f32[960,768]{1,0:T(8,128)}, bf16[960,768]{1,0:T(8,128)(2,1)}, bf16[960,3072]{1,0:T(8,128)(2,1)}, bf16[960,3072]{1,0:T(8,128)(2,1)}) custom-call(bf16[960,256]{1,0:T(8,128)(2,1)} %get-tuple-element.210.refs_0_, bf16[960,256]{1,0:T(8,128)(2,1)} %get-tuple-element.212.refs_1_, bf16[960,256]{1,0:T(8,128)(2,1)} %get-tuple-element.219.refs_2_, ...), custom_call_target="tpu_custom_call" | custom-call | flops 5662310400 | bytes 25000000 | tf_op jit(solution)/shard_map/feed/pallas_call | solution.py:1013
  134.1 18.9 %join.1 = (bf16[32,96,768]{2,1,0:T(8,128)(2,1)}, bf16[1024,512]{1,0:T(8,128)(2,1)}, bf16[960,768]{1,0:T(8,128)(2,1)}, bf16[16,24,512]{2,1,0:T(8,128)(2,1)}, bf16...) custom-call(s32[16]{0:T(128)} %get-tuple-element.191.meta.place.spot, bf16[960,3072]{1,0:T(8,128)(2,1)} %get-tuple-element.226.g_in, ...), custom_call_target="tpu_custom_call" | custom-call | flops 8304721920 | bytes 20000000 | tf_op jit(solution)/shard_map/join/pallas_call | solution.py:1034
  153.0 3.9 %all-to-all-start.2 = ((bf16[32,32,512]{2,1,0:T(8,128)(2,1)}), bf16[32,32,512]{2,1,0:T(8,128)(2,1)}, u32[]{:S(2)}, u32[]{:S(2)}) async-start(bf16[32,32,512]{2,1,0:T(8,128)(2,1)} %bitcast.100), calls=%async_computation.2 | async-start | bytes 2097152 | tf_op jit(solution)/shard_map/all_to_all | solution.py:1057
  157.4 27.3 %feed_back.1 = (f32[960,768]{1,0:T(8,128)}, bf16[16,96,768]{2,1,0:T(8,128)(2,1)}, bf16[16,96,768]{2,1,0:T(8,128)(2,1)}, bf16[16,24,3072]{2,1,0:T(8,128)(2,1)}, b...) custom-call(s32[16]{0:T(128)} %get-tuple-element.191.meta.place.spot, bf16[960,768]{1,0:T(8,128)(2,1)} %get-tuple-element.241.dy_in, ...), custom_call_target="tpu_custom_call" | custom-call | flops 362387865600 | bytes 800000000 | tf_op jit(solution)/shard_map/feed_back/pallas_call | solution.py:1064
  185.2 11.4 %out_back.1 = (f32[960,768]{1,0:T(8,128)}, bf16[960,768]{1,0:T(8,128)(2,1)}, bf16[16,24,768]{2,1,0:T(8,128)(2,1)}, bf16[16,24,768]{2,1,0:T(8,128)(2,1)}, f32[8,768]{1,0:T(8,128)}) custom-call(s32[16]{0:T(128)} %get-tuple-element.191.meta.place.spot, f32[960,768]{1,0:T(8,128)} %get-tuple-element.244.dh_in, f32[960,768]{1,0:T(8,128)} %get-tuple-element.232.r_in, ...), custom_call_target="tpu_custom_call" | custom-call | flops 45298483200 | bytes 400000000 | tf_op jit(solution)/shard_map/out_back/pallas_call | solution.py:1082
  196.6 4.8 %chip_sum.4 = (bf16[4,96,768]{2,1,0:T(8,128)(2,1)}, bf16[4,96,768]{2,1,0:T(8,128)(2,1)}, bf16[4,96,768]{2,1,0:T(8,128)(2,1)}, bf16[4,96,768]{2,1,0:T(8,128)(2,1)}) custom-call(s32[16]{0:T(128)} %get-tuple-element.191.meta.place.spot, bf16[16,96,768]{2,1,0:T(8,128)(2,1)} %get-tuple-element.256.refs_0_, bf16[16,96,768]{2,1,0:T(8,128)(2,1)} %collective-permute-done.18.refs_1_), custom_call_target="tpu_custom_call" | custom-call | bytes 7077888 | tf_op jit(solution)/shard_map/chip_sum/pallas_call | solution.py:220
  204.7 11.6 %attention_back.3 = (bf16[960,256]{1,0:T(8,128)(2,1)}, bf16[960,256]{1,0:T(8,128)(2,1)}, bf16[960,256]{1,0:T(8,128)(2,1)}, bf16[16,24,768]{2,1,0:T(8,128)(2,1)},...) custom-call(s32[16]{0:T(128)} %get-tuple-element.191.meta.place.spot, bf16[960,768]{1,0:T(8,128)(2,1)} %get-tuple-element.218.h_in, ...), custom_call_target="tpu_custom_call" | custom-call | flops 82649243648 | bytes 200000000 | tf_op jit(solution)/shard_map/attention_back/pallas_call | solution.py:1101
  218.7 5.4 %chip_sum.5 = (bf16[4,24,3584]{2,1,0:T(8,128)(2,1)}, bf16[4,24,3584]{2,1,0:T(8,128)(2,1)}, bf16[4,24,3584]{2,1,0:T(8,128)(2,1)}, bf16[4,24,3584]{2,1,0:T(8,128)(2,1)}) custom-call(s32[16]{0:T(128)} %get-tuple-element.191.meta.place.spot, bf16[16,24,3072]{2,1,0:T(8,128)(2,1)} %get-tuple-element.265.refs_0_, bf16[16,24,512]{2,1,0:T(8,128)(2,1)} %get-tuple-element.266.refs_1_, ...), custom_call_target="tpu_custom_call" | custom-call | bytes 8257536 | tf_op jit(solution)/shard_map/chip_sum/pallas_call | solution.py:220
  227.8 10.8 %attention_back.4 = (bf16[960,256]{1,0:T(8,128)(2,1)}, bf16[960,256]{1,0:T(8,128)(2,1)}, bf16[960,256]{1,0:T(8,128)(2,1)}, bf16[16,24,768]{2,1,0:T(8,128)(2,1)},...) custom-call(s32[16]{0:T(128)} %get-tuple-element.191.meta.place.spot, bf16[960,768]{1,0:T(8,128)(2,1)} %get-tuple-element.218.h_in, ...), custom_call_target="tpu_custom_call" | custom-call | flops 82649243648 | bytes 200000000 | tf_op jit(solution)/shard_map/attention_back/pallas_call | solution.py:1101
  245.0 4.8 %all-to-all-start.3 = ((bf16[4,96,768]{2,1,0:T(8,128)(2,1)}), bf16[4,96,768]{2,1,0:T(8,128)(2,1)S(1)}, u32[]{:S(2)}, u32[]{:S(2)}) async-start(bf16[4,96,768]{2,1,0:T(8,128)(2,1)} %plane_sum.3), calls=%async_computation.3 | async-start | bytes 1179648 | tf_op jit(solution)/shard_map/all_to_all | solution.py:286
  249.8 4.6 %collective-permute-done.24.refs_1_ = bf16[4,24,3584]{2,1,0:T(8,128)(2,1)S(1)} collective-permute-done((bf16[4,24,3584]{2,1,0:T(8,128)(2,1)}, bf16[4,24,3584]{2,1,0:T(8,128)(2,1)S(1)}, u32[]{:S(2)}, u32[]{:S(2)}) %collective-permute-start.24) | collective-permute-done | bytes 688160 | tf_op jit(solution)/shard_map/ppermute | solution.py:50
  256.1 10.8 %attention_back.5 = (bf16[960,256]{1,0:T(8,128)(2,1)}, bf16[960,256]{1,0:T(8,128)(2,1)}, bf16[960,256]{1,0:T(8,128)(2,1)}, bf16[16,24,768]{2,1,0:T(8,128)(2,1)},...) custom-call(s32[16]{0:T(128)} %get-tuple-element.191.meta.place.spot, bf16[960,768]{1,0:T(8,128)(2,1)} %get-tuple-element.218.h_in, ...), custom_call_target="tpu_custom_call" | custom-call | flops 82649243648 | bytes 200000000 | tf_op jit(solution)/shard_map/attention_back/pallas_call | solution.py:1101
  267.7 4.2 %chip_sum.6 = (bf16[4,24,2304]{2,1,0:T(8,128)(2,1)}, bf16[4,24,2304]{2,1,0:T(8,128)(2,1)}, bf16[4,24,2304]{2,1,0:T(8,128)(2,1)}, bf16[4,24,2304]{2,1,0:T(8,128)(2,1)}) custom-call(s32[16]{0:T(128)} %get-tuple-element.191.meta.place.spot, bf16[16,24,768]{2,1,0:T(8,128)(2,1)} %get-tuple-element.294.refs_0_, bf16[16,24,768]{2,1,0:T(8,128)(2,1)} %get-tuple-element.295.refs_1_, ...), custom_call_target="tpu_custom_call" | custom-call | bytes 5308416 | tf_op jit(solution)/shard_map/chip_sum/pallas_call | solution.py:220
  276.3 2.9 plane_sum.4
  279.3 4.8 %all-to-all-start.4 = ((bf16[4,24,3584]{2,1,0:T(8,128)(2,1)}), bf16[4,24,3584]{2,1,0:T(8,128)(2,1)S(1)}, u32[]{:S(2)}, u32[]{:S(2)}) async-start(bf16[4,24,3584]{2,1,0:T(8,128)(2,1)} %plane_sum.4), calls=%async_computation.4 | async-start | bytes 1376256 | tf_op jit(solution)/shard_map/all_to_all | solution.py:286
  284.1 12.4 %first_back.1 = (bf16[882,768]{1,0:T(8,128)(2,1)}, f32[11,32,128]{2,1,0:T(8,128)}) custom-call(s32[16]{0:T(128)} %get-tuple-element.191.meta.place.spot, bf16[960,256]{1,0:T(8,128)(2,1)} %get-tuple-element.264.refs_0_, bf16[960,256]{1,0:T(8,128)(2,1)} %get-tuple-element.273.refs_1_, bf16[960,256]{1,0:T(8,128)(2,1)} %get-tuple-element.284.refs_2_, ...), custom_call_target="tpu_custom_call" | custom-call | flops 93958963200 | bytes 400000000 | tf_op jit(solution)/shard_map/first_back/pallas_call | solution.py:1135
  300.7 3.3 chip_sum.7
  307.5 9.1 %decode.1 = bf16[1792,512]{1,0:T(8,128)(2,1)} custom-call(bf16[1024,512]{1,0:T(8,128)(2,1)} %bitcast.45.got, bf16[128,128]{1,0:T(8,128)(2,1)} %bitcast.114, f32[2,512]{1,0:T(2,128)} %reshape.161.vec_dec), custom_call_target="tpu_custom_call" | custom-call | flops 20000000000 | bytes 140000000 | tf_op jit(solution)/shard_map/decode/pallas_call | solution.py:1163
  330.9 5.0 %collective-permute-done.39.refs_2_ = bf16[24,3456]{1,0:T(8,128)(2,1)S(1)} collective-permute-done((bf16[24,3456]{1,0:T(8,128)(2,1)}, bf16[24,3456]{1,0:T(8,128)(2,1)S(1)}, u32[]{:S(2)}, u32[]{:S(2)}) %collective-permute-start.39) | collective-permute-done | bytes 165920 | tf_op jit(solution)/shard_map/ppermute | solution.py:36
  (206 shorter events, 87.5 us)
Async XLA Ops:
  7.3 105.4 %all-gather.2.cloned.1.call-start = ((), (), s32[]{:S(2)}) async-start(), calls=%async_computation.5 | async-start | bytes 6893568 | tf_op jit(solution)/shard_map/all_gather | solution.py:928
  9.1 13.0 %collective-permute-start.1 = (bf16[24,2304]{1,0:T(8,128)(2,1)}, bf16[24,2304]{1,0:T(8,128)(2,1)S(1)}, u32[]{:S(2)}, u32[]{:S(2)}) collective-permute-start(bf16[24,2304]{1,0:T(8,128)(2,1)} %param.25), channel_id=1, source_target_pairs={{0,16},{1,17},{2,18},{3,19},{4,20},{5,21},{6,22},{7,23},{8,24},{9,... | collective-permute-start | bytes 331784 | tf_op jit(solution)/shard_map/ppermute | solution.py:36
  35.1 19.2 %collective-permute-start.6 = (bf16[2,4,24,1152]{3,2,1,0:T(8,128)(2,1)S(1)}, bf16[2,4,24,1152]{3,2,1,0:T(8,128)(2,1)S(1)}, u32[]{:S(2)}, u32[]{:S(2)}) collective-permute-start(bf16[2,4,24,1152]{3,2,1,0:T(8,128)(2,1)S(1)} %pad_maximum_fusion.9), channel_id=1, source_target_pairs={{0,2},{1,3},{2,0},{3,1},{4,6},{5,7},{6,4},{7,5},{8,10},{9,11},{10,... | collective-permute-start | bytes 1327112 | tf_op jit(solution)/shard_map/ppermute | solution.py:36
  36.9 17.3 %collective-permute-start.5 = (bf16[2,4,24,1152]{3,2,1,0:T(8,128)(2,1)S(1)}, bf16[2,4,24,1152]{3,2,1,0:T(8,128)(2,1)S(1)}, u32[]{:S(2)}, u32[]{:S(2)}) collective-permute-start(bf16[2,4,24,1152]{3,2,1,0:T(8,128)(2,1)S(1)} %pad_maximum_fusion.8), channel_id=1, source_target_pairs={{0,4},{1,5},{2,6},{3,7},{4,0},{5,1},{6,2},{7,3},{8,12},{9,13},{10,... | collective-permute-start | bytes 1327112 | tf_op jit(solution)/shard_map/ppermute | solution.py:36
  54.4 16.0 %collective-permute-start.8 = (bf16[2,2,4,24,1152]{4,3,2,1,0:T(8,128)(2,1)S(1)}, bf16[2,2,4,24,1152]{4,3,2,1,0:T(8,128)(2,1)S(1)}, u32[]{:S(2)}, u32[]{:S(2)}) collective-permute-start(bf16[2,2,4,24,1152]{4,3,2,1,0:T(8,128)(2,1)S(1)} %pad_maximum_fusion.3.part_b), channel_id=1, source_target_pairs={{0,1},{1,0},{2,3},{3,2},{4,5},{5,4},{6,7},{7,6},{8,9},{9,8},{10,11... | collective-permute-start | bytes 2654216 | tf_op jit(solution)/shard_map/ppermute | solution.py:36
  56.2 14.3 %collective-permute-start.7 = (bf16[2,2,4,24,1152]{4,3,2,1,0:T(8,128)(2,1)S(1)}, bf16[2,2,4,24,1152]{4,3,2,1,0:T(8,128)(2,1)S(1)}, u32[]{:S(2)}, u32[]{:S(2)}) collective-permute-start(bf16[2,2,4,24,1152]{4,3,2,1,0:T(8,128)(2,1)S(1)} %pad_maximum_fusion.2.part_a), channel_id=1, source_target_pairs={{0,1},{1,0},{2,3},{3,2},{4,5},{5,4},{6,7},{7,6},{8,9},{9,8},{10,11... | collective-permute-start | bytes 2654216 | tf_op jit(solution)/shard_map/ppermute | solution.py:36
  57.0 35.1 %collective-permute-start.11 = (bf16[96,768]{1,0:T(8,128)(2,1)S(1)}, bf16[96,768]{1,0:T(8,128)(2,1)S(1)}, u32[]{:S(2)}, u32[]{:S(2)}) collective-permute-start(bf16[96,768]{1,0:T(8,128)(2,1)S(1)} %copy-done.26), channel_id=1, source_target_pairs={{0,24},{1,25},{2,26},{3,27},{4,28},{5,29},{6,30},{7,31},{8,0},{9,1... | collective-permute-start | bytes 442376 | tf_op jit(solution)/shard_map/ppermute | solution.py:36
  60.1 32.0 %collective-permute-start.10 = (bf16[96,768]{1,0:T(8,128)(2,1)S(1)}, bf16[96,768]{1,0:T(8,128)(2,1)}, u32[]{:S(2)}, u32[]{:S(2)}) collective-permute-start(bf16[96,768]{1,0:T(8,128)(2,1)S(1)} %copy-done.26), channel_id=1, source_target_pairs={{0,16},{1,17},{2,18},{3,19},{4,20},{5,21},{6,22},{7,23},{8,24},{9,... | collective-permute-start | bytes 442376 | tf_op jit(solution)/shard_map/ppermute | solution.py:36
  60.1 32.0 %collective-permute-start.9 = (bf16[96,768]{1,0:T(8,128)(2,1)S(1)}, bf16[96,768]{1,0:T(8,128)(2,1)}, u32[]{:S(2)}, u32[]{:S(2)}) collective-permute-start(bf16[96,768]{1,0:T(8,128)(2,1)S(1)} %copy-done.26), channel_id=1, source_target_pairs={{0,8},{1,9},{2,10},{3,11},{4,12},{5,13},{6,14},{7,15},{8,16},{9,17... | collective-permute-start | bytes 442376 | tf_op jit(solution)/shard_map/ppermute | solution.py:36
  93.3 14.3 %collective-permute-start.13 = (bf16[4,96,384]{2,1,0:T(8,128)(2,1)S(1)}, bf16[4,96,384]{2,1,0:T(8,128)(2,1)S(1)}, u32[]{:S(2)}, u32[]{:S(2)}) collective-permute-start(bf16[4,96,384]{2,1,0:T(8,128)(2,1)S(1)} %get-tuple-element.223), channel_id=1, source_target_pairs={{0,4},{1,5},{2,6},{3,7},{4,0},{5,1},{6,2},{7,3},{8,12},{9,13},{10,... | collective-permute-start | bytes 884744 | tf_op jit(solution)/shard_map/ppermute | solution.py:36
  94.8 12.8 %collective-permute-start.12 = (bf16[4,96,384]{2,1,0:T(8,128)(2,1)S(1)}, bf16[4,96,384]{2,1,0:T(8,128)(2,1)S(1)}, u32[]{:S(2)}, u32[]{:S(2)}) collective-permute-start(bf16[4,96,384]{2,1,0:T(8,128)(2,1)S(1)} %get-tuple-element.221), channel_id=1, source_target_pairs={{0,2},{1,3},{2,0},{3,1},{4,6},{5,7},{6,4},{7,5},{8,10},{9,11},{10,... | collective-permute-start | bytes 884744 | tf_op jit(solution)/shard_map/ppermute | solution.py:36
  96.4 35.3 %all-to-all-start.1 = ((bf16[32,32,512]{2,1,0:T(8,128)(2,1)}), bf16[32,32,512]{2,1,0:T(8,128)(2,1)}, u32[]{:S(2)}, u32[]{:S(2)}) async-start(bf16[32,32,512]{2,1,0:T(8,128)(2,1)} %bitcast.42), calls=%async_computation.1 | async-start | bytes 2097152 | tf_op jit(solution)/shard_map/all_to_all | solution.py:1004
  107.7 21.0 %collective-permute-start.15 = (bf16[2,4,96,384]{3,2,1,0:T(8,128)(2,1)S(1)}, bf16[2,4,96,384]{3,2,1,0:T(8,128)(2,1)S(1)}, u32[]{:S(2)}, u32[]{:S(2)}) collective-permute-start(bf16[2,4,96,384]{3,2,1,0:T(8,128)(2,1)S(1)} %pad_maximum_fusion.6), channel_id=1, source_target_pairs={{0,2},{1,3},{2,0},{3,1},{4,6},{5,7},{6,4},{7,5},{8,10},{9,11},{10,... | collective-permute-start | bytes 1769480 | tf_op jit(solution)/shard_map/ppermute | solution.py:36
  109.6 19.6 %collective-permute-start.14 = (bf16[2,4,96,384]{3,2,1,0:T(8,128)(2,1)S(1)}, bf16[2,4,96,384]{3,2,1,0:T(8,128)(2,1)S(1)}, u32[]{:S(2)}, u32[]{:S(2)}) collective-permute-start(bf16[2,4,96,384]{3,2,1,0:T(8,128)(2,1)S(1)} %pad_maximum_fusion.5), channel_id=1, source_target_pairs={{0,4},{1,5},{2,6},{3,7},{4,0},{5,1},{6,2},{7,3},{8,12},{9,13},{10,... | collective-permute-start | bytes 1769480 | tf_op jit(solution)/shard_map/ppermute | solution.py:36
  153.0 51.7 %all-to-all-start.2 = ((bf16[32,32,512]{2,1,0:T(8,128)(2,1)}), bf16[32,32,512]{2,1,0:T(8,128)(2,1)}, u32[]{:S(2)}, u32[]{:S(2)}) async-start(bf16[32,32,512]{2,1,0:T(8,128)(2,1)} %bitcast.100), calls=%async_computation.2 | async-start | bytes 2097152 | tf_op jit(solution)/shard_map/all_to_all | solution.py:1057
  156.9 47.7 %collective-permute-start.20 = (bf16[16,24,512]{2,1,0:T(8,128)(2,1)}, bf16[16,24,512]{2,1,0:T(8,128)(2,1)}, u32[]{:S(2)}, u32[]{:S(2)}) collective-permute-start(bf16[16,24,512]{2,1,0:T(8,128)(2,1)} %get-tuple-element.262), channel_id=1, source_target_pairs={{0,1},{1,0},{2,3},{3,2},{4,5},{5,4},{6,7},{7,6},{8,9},{9,8},{10,11... | collective-permute-start | bytes 1179656 | tf_op jit(solution)/shard_map/ppermute | solution.py:36
  184.9 19.8 %collective-permute-start.19 = (bf16[16,24,3072]{2,1,0:T(8,128)(2,1)}, bf16[16,24,3072]{2,1,0:T(8,128)(2,1)S(1)}, u32[]{:S(2)}, u32[]{:S(2)}) collective-permute-start(bf16[16,24,3072]{2,1,0:T(8,128)(2,1)} %get-tuple-element.261), channel_id=1, source_target_pairs={{0,1},{1,0},{2,3},{3,2},{4,5},{5,4},{6,7},{7,6},{8,9},{9,8},{10,11... | collective-permute-start | bytes 7077896 | tf_op jit(solution)/shard_map/ppermute | solution.py:36
  201.5 15.8 %collective-permute-start.21 = (bf16[4,96,768]{2,1,0:T(8,128)(2,1)}, bf16[4,96,768]{2,1,0:T(8,128)(2,1)S(1)}, u32[]{:S(2)}, u32[]{:S(2)}) collective-permute-start(bf16[4,96,768]{2,1,0:T(8,128)(2,1)} %get-tuple-element.267), channel_id=1, source_target_pairs={{0,2},{1,3},{2,0},{3,1},{4,6},{5,7},{6,4},{7,5},{8,10},{9,11},{10,... | collective-permute-start | bytes 1769480 | tf_op jit(solution)/shard_map/ppermute | solution.py:50
  203.2 15.5 %collective-permute-start.22 = (bf16[4,96,768]{2,1,0:T(8,128)(2,1)}, bf16[4,96,768]{2,1,0:T(8,128)(2,1)S(1)}, u32[]{:S(2)}, u32[]{:S(2)}) collective-permute-start(bf16[4,96,768]{2,1,0:T(8,128)(2,1)} %get-tuple-element.268), channel_id=1, source_target_pairs={{0,4},{1,5},{2,6},{3,7},{4,0},{5,1},{6,2},{7,3},{8,12},{9,13},{10,... | collective-permute-start | bytes 1769480 | tf_op jit(solution)/shard_map/ppermute | solution.py:50
  216.3 50.6 %collective-permute-start.26 = (bf16[16,24,768]{2,1,0:T(8,128)(2,1)}, bf16[16,24,768]{2,1,0:T(8,128)(2,1)}, u32[]{:S(2)}, u32[]{:S(2)}) collective-permute-start(bf16[16,24,768]{2,1,0:T(8,128)(2,1)} %get-tuple-element.299), channel_id=1, source_target_pairs={{0,1},{1,0},{2,3},{3,2},{4,5},{5,4},{6,7},{7,6},{8,9},{9,8},{10,11... | collective-permute-start | bytes 1769480 | tf_op jit(solution)/shard_map/ppermute | solution.py:36
  216.4 50.5 %collective-permute-start.27 = (bf16[16,24,768]{2,1,0:T(8,128)(2,1)}, bf16[16,24,768]{2,1,0:T(8,128)(2,1)}, u32[]{:S(2)}, u32[]{:S(2)}) collective-permute-start(bf16[16,24,768]{2,1,0:T(8,128)(2,1)} %get-tuple-element.300), channel_id=1, source_target_pairs={{0,1},{1,0},{2,3},{3,2},{4,5},{5,4},{6,7},{7,6},{8,9},{9,8},{10,11... | collective-permute-start | bytes 1769480 | tf_op jit(solution)/shard_map/ppermute | solution.py:36
  224.2 17.3 %collective-permute-start.23 = (bf16[4,96,768]{2,1,0:T(8,128)(2,1)S(1)}, bf16[4,96,768]{2,1,0:T(8,128)(2,1)S(1)}, u32[]{:S(2)}, u32[]{:S(2)}) collective-permute-start(bf16[4,96,768]{2,1,0:T(8,128)(2,1)S(1)} %copy-done.37), channel_id=1, source_target_pairs={{0,6},{1,7},{2,4},{3,5},{4,2},{5,3},{6,0},{7,1},{8,14},{9,15},{10,... | collective-permute-start | bytes 1769480 | tf_op jit(solution)/shard_map/ppermute | solution.py:50
  225.7 28.7 %collective-permute-start.24 = (bf16[4,24,3584]{2,1,0:T(8,128)(2,1)}, bf16[4,24,3584]{2,1,0:T(8,128)(2,1)S(1)}, u32[]{:S(2)}, u32[]{:S(2)}) collective-permute-start(bf16[4,24,3584]{2,1,0:T(8,128)(2,1)} %get-tuple-element.280), channel_id=1, source_target_pairs={{0,2},{1,3},{2,0},{3,1},{4,6},{5,7},{6,4},{7,5},{8,10},{9,11},{10,... | collective-permute-start | bytes 2064392 | tf_op jit(solution)/shard_map/ppermute | solution.py:50
  227.2 27.2 %collective-permute-start.25 = (bf16[4,24,3584]{2,1,0:T(8,128)(2,1)}, bf16[4,24,3584]{2,1,0:T(8,128)(2,1)S(1)}, u32[]{:S(2)}, u32[]{:S(2)}) collective-permute-start(bf16[4,24,3584]{2,1,0:T(8,128)(2,1)} %get-tuple-element.281), channel_id=1, source_target_pairs={{0,4},{1,5},{2,6},{3,7},{4,0},{5,1},{6,2},{7,3},{8,12},{9,13},{10,... | collective-permute-start | bytes 2064392 | tf_op jit(solution)/shard_map/ppermute | solution.py:50
  241.5 25.4 %collective-permute-start.28 = (bf16[16,24,768]{2,1,0:T(8,128)(2,1)}, bf16[16,24,768]{2,1,0:T(8,128)(2,1)S(1)}, u32[]{:S(2)}, u32[]{:S(2)}) collective-permute-start(bf16[16,24,768]{2,1,0:T(8,128)(2,1)} %get-tuple-element.302), channel_id=1, source_target_pairs={{0,1},{1,0},{2,3},{3,2},{4,5},{5,4},{6,7},{7,6},{8,9},{9,8},{10,11... | collective-permute-start | bytes 1769480 | tf_op jit(solution)/shard_map/ppermute | solution.py:36
  245.0 30.4 %all-to-all-start.3 = ((bf16[4,96,768]{2,1,0:T(8,128)(2,1)}), bf16[4,96,768]{2,1,0:T(8,128)(2,1)S(1)}, u32[]{:S(2)}, u32[]{:S(2)}) async-start(bf16[4,96,768]{2,1,0:T(8,128)(2,1)} %plane_sum.3), calls=%async_computation.3 | async-start | bytes 1179648 | tf_op jit(solution)/shard_map/all_to_all | solution.py:286
  254.4 21.0 %collective-permute-start.29 = (bf16[4,24,3584]{2,1,0:T(8,128)(2,1)}, bf16[4,24,3584]{2,1,0:T(8,128)(2,1)S(1)}, u32[]{:S(2)}, u32[]{:S(2)}) collective-permute-start(bf16[4,24,3584]{2,1,0:T(8,128)(2,1)} %get-tuple-element.308), channel_id=1, source_target_pairs={{0,6},{1,7},{2,4},{3,5},{4,2},{5,3},{6,0},{7,1},{8,14},{9,15},{10,... | collective-permute-start | bytes 2064392 | tf_op jit(solution)/shard_map/ppermute | solution.py:50
  271.9 27.5 %collective-permute-start.32 = (bf16[4,24,2304]{2,1,0:T(8,128)(2,1)}, bf16[4,24,2304]{2,1,0:T(8,128)(2,1)S(1)}, u32[]{:S(2)}, u32[]{:S(2)}) collective-permute-start(bf16[4,24,2304]{2,1,0:T(8,128)(2,1)} %get-tuple-element.323), channel_id=1, source_target_pairs={{0,2},{1,3},{2,0},{3,1},{4,6},{5,7},{6,4},{7,5},{8,10},{9,11},{10,... | collective-permute-start | bytes 1327112 | tf_op jit(solution)/shard_map/ppermute | solution.py:50
  273.1 26.2 %collective-permute-start.33 = (bf16[4,24,2304]{2,1,0:T(8,128)(2,1)}, bf16[4,24,2304]{2,1,0:T(8,128)(2,1)S(1)}, u32[]{:S(2)}, u32[]{:S(2)}) collective-permute-start(bf16[4,24,2304]{2,1,0:T(8,128)(2,1)} %get-tuple-element.324), channel_id=1, source_target_pairs={{0,4},{1,5},{2,6},{3,7},{4,0},{5,1},{6,2},{7,3},{8,12},{9,13},{10,... | collective-permute-start | bytes 1327112 | tf_op jit(solution)/shard_map/ppermute | solution.py:50
  273.8 25.6 %collective-permute-start.34 = (bf16[4,24,2304]{2,1,0:T(8,128)(2,1)}, bf16[4,24,2304]{2,1,0:T(8,128)(2,1)}, u32[]{:S(2)}, u32[]{:S(2)}) collective-permute-start(bf16[4,24,2304]{2,1,0:T(8,128)(2,1)} %get-tuple-element.325), channel_id=1, source_target_pairs={{0,6},{1,7},{2,4},{3,5},{4,2},{5,3},{6,0},{7,1},{8,14},{9,15},{10,... | collective-permute-start | bytes 1327112 | tf_op jit(solution)/shard_map/ppermute | solution.py:50
  275.4 23.9 %collective-permute-start.30 = (bf16[16,24,768]{2,1,0:T(8,128)(2,1)}, bf16[16,24,768]{2,1,0:T(8,128)(2,1)S(1)}, u32[]{:S(2)}, u32[]{:S(2)}) collective-permute-start(bf16[16,24,768]{2,1,0:T(8,128)(2,1)} %get-tuple-element.320), channel_id=1, source_target_pairs={{0,1},{1,0},{2,3},{3,2},{4,5},{5,4},{6,7},{7,6},{8,9},{9,8},{10,11... | collective-permute-start | bytes 1769480 | tf_op jit(solution)/shard_map/ppermute | solution.py:36
  279.3 28.2 %all-to-all-start.4 = ((bf16[4,24,3584]{2,1,0:T(8,128)(2,1)}), bf16[4,24,3584]{2,1,0:T(8,128)(2,1)S(1)}, u32[]{:S(2)}, u32[]{:S(2)}) async-start(bf16[4,24,3584]{2,1,0:T(8,128)(2,1)} %plane_sum.4), calls=%async_computation.4 | async-start | bytes 1376256 | tf_op jit(solution)/shard_map/all_to_all | solution.py:286
  (55 other events, 564.6 us)
Sparse Core Ops, SparseCore 0:
  11.6 82.5 all-gather.1
